TPU v7x, 128 devices: a whole 4x4x4 slice. The times are simulated.
128 devices in a mesh: gx: 16 (over z, x_hi, core), gy: 8 (over y, x_lo).
Axes of the slice: x: 4 (x_hi: 2, x_lo: 2; x = x_hi * 2 + x_lo), y: 4, z: 4, core: 2. Of those that a mesh axis runs over, the one named last changes fastest.
Arguments:
- rhs: float32 [3, 25, 64, 64, 128], P(None, None, 'gx', 'gy'), may hold values from -6 to 6
- kappa: float32 [64, 64, 128], P('gx', 'gy'), may hold values from 0.1 to 10
- mass: float32 [64, 64, 128], P('gx', 'gy'), may hold values from 0.05 to 2
- stiffness: float32 [150, 150], replicated, as said below
- mass_matrix: float32 [150, 150], replicated, as said below
- prolong: float32 [3, 25], replicated, may hold values from 0.5 to 1.5
Outputs:
- solution: float32 [3, 25, 64, 64, 128], P(None, None, 'gx', 'gy')
- residual: float32 [3, 25, 64, 64, 128], P(None, None, 'gx', 'gy')
- coarse: float32 [16, 64, 128], P('gx', 'gy')
Inputs may be any that keep to these rules, and one draw needn't show every extreme that they name: `stiffness`: symmetric, with a diagonal larger than the sum of magnitudes of the rest of its row. `mass_matrix`: symmetric, with a diagonal larger than the sum of magnitudes of the rest of its row.
All inputs are finite; a program needn't handle non-finite values.
Results may differ from a plain program's by a relative error of at most 0.0035.
Values sent between devices are 32-bit elements; how exact they have to be, the bound alone decides.
No kernel may reach another device: no remote copies, remote signals or barrier semaphores. Data moves between devices by JAX's collectives and lax.ppermute only.
A program may use at most 64 MiB of HBM per device.

v0:
```python
import jax
import jax.numpy as jnp
from jax import lax
from jax.sharding import PartitionSpec as P

ITERS = 3
SWEEPS = 8


def passed_along(value, axis, by):
    peers = lax.axis_size(axis)
    return lax.ppermute(value, axis, [(i, (i + by) % peers) for i in range(peers)])


def with_halo(cells, sides, width):
    for axis, dim in sides:
        count = lax.axis_size(axis)
        head = lax.slice_in_dim(cells, 0, width, axis=dim)
        tail = lax.slice_in_dim(cells, cells.shape[dim] - width, cells.shape[dim], axis=dim)
        cells = jnp.concatenate(
            [
                lax.ppermute(tail, axis, [(i, (i + 1) % count) for i in range(count)]),
                cells,
                lax.ppermute(head, axis, [((i + 1) % count, i) for i in range(count)]),
            ],
            axis=dim,
        )
    return cells


def shards(rhs, kappa, mass, stiffness, mass_matrix, prolong):
    stacked = jnp.concatenate([stiffness, mass_matrix], 0)
    half = stiffness.shape[0]
    nodes = rhs.shape[1]
    kappa_flat = kappa.reshape(-1)
    mass_flat = mass.reshape(-1)

    def squares(vector):
        return lax.psum(jnp.sum(vector * vector), ("gx", "gy"))

    iterate = jnp.zeros_like(rhs)
    residual = rhs
    direction = rhs
    norm_now = squares(residual)
    for step in range(ITERS):
        trace_x = direction[0]
        trace_y = direction[1]
        trace_z = direction[2]
        above_x = passed_along(trace_x[:, :1], "gx", -1)
        upper_x = jnp.concatenate([trace_x[:, 1:], above_x], 1)
        above_y = passed_along(trace_y[:, :, :1], "gy", -1)
        upper_y = jnp.concatenate([trace_y[:, :, 1:], above_y], 2)
        upper_z = jnp.roll(trace_z, -1, axis=3)
        local = jnp.concatenate([trace_x, upper_x, trace_y, upper_y, trace_z, upper_z], 0).reshape(
            6 * nodes, -1
        )
        prod = jnp.dot(
            stacked, local, precision=lax.Precision.HIGHEST, preferred_element_type=jnp.float32
        )
        weighted = kappa_flat[None] * prod[:half] + mass_flat[None] * prod[half:]
        parts = weighted.reshape((6, nodes) + kappa.shape)
        below_x = passed_along(parts[1][:, -1:], "gx", 1)
        out_x = parts[0] + jnp.concatenate([below_x, parts[1][:, :-1]], 1)
        below_y = passed_along(parts[3][:, :, -1:], "gy", 1)
        out_y = parts[2] + jnp.concatenate([below_y, parts[3][:, :, :-1]], 2)
        out_z = parts[4] + jnp.roll(parts[5], 1, axis=3)
        image = jnp.stack([out_x, out_y, out_z], 0)
        alpha = norm_now / lax.psum(jnp.sum(direction * image), ("gx", "gy"))
        iterate = iterate + alpha * direction
        residual = residual - alpha * image
        norm_next = squares(residual)
        direction = residual + norm_next / norm_now * direction
        norm_now = norm_next
    load = jnp.sum(residual, axis=(0, 1, 2))[None] / 75.0
    coarse = jnp.zeros_like(load)

    def sweep_once(count, value):
        widened = with_halo(value, (("gx", 0),), 1)
        return (load + widened[:-2] + widened[2:]) / 2.2

    coarse = lax.fori_loop(0, SWEEPS, sweep_once, coarse)
    solution = iterate + prolong[:, :, None, None, None] * coarse[None, None]
    return (solution, residual, coarse)


def solution(mesh):
    placed = (
        P(None, None, "gx", "gy", None),
        P("gx", "gy", None),
        P("gx", "gy", None),
        P(),
        P(),
        P(),
    )
    return jax.shard_map(
        shards,
        mesh=mesh,
        in_specs=placed,
        out_specs=(
            P(None, None, "gx", "gy", None),
            P(None, None, "gx", "gy", None),
            P("gx", "gy", None),
        ),
        check_vma=False,
    )
```

profile of v0, /device:TPU:0, one launch (start us, length us, event | category | flops | bytes accessed | tf_op | source)
XLA Modules:
  0.0 554.3 jit_solution(818553645722352906)
XLA Ops:
  2.2 4.1 collective-permute-start.3
  6.3 5.4 collective-permute-start.2
  17.6 10.6 %concatenate.216 = f32[150,4096]{1,0:T(8,128)S(1)} concatenate(f32[25,4096]{1,0:T(8,128)S(1)} %concatenate.207, f32[25,4096]{1,0:T(8,128)} %bitcast.257, f32[25,4096]{1,0:T(8,128)} %concatenate.210, f32[25,4096]{1,0:T(8,128)} %bitcast.255, f32[25,4096]{1,0:T(8,128)} %concatenate.213, f32[25,4096]{1,0:T(8,128)} %bitcast.253), dimensions={0} | concatenate | bytes 4915200 | tf_op jit(solution)/shard_map/concatenate | solution.py:54
  28.2 4.4 fusion.5
  43.8 64.8 %all-reduce = (f32[]{:T(128)}, f32[]{:T(128)}) all-reduce(f32[]{:T(128)} %get-tuple-element.34, f32[]{:T(128)} %get-tuple-element.33), channel_id=1, replica_groups=mesh['gx'=16,'gy'=8] {'gx','gy'}, use_global_device_ids=true, to_apply=%region_1.0 | all-reduce | flops 2 | bytes 16 | tf_op jit(solution)/shard_map/psum | solution.py:39
  110.9 62.3 %psum.44 = f32[]{:T(128)} all-reduce(f32[]{:T(128)} %multiply_reduce_fusion.3), channel_id=1, replica_groups=mesh['gx'=16,'gy'=8] {'gx','gy'}, use_global_device_ids=true, to_apply=%region_5.6 | all-reduce | flops 1 | bytes 8 | tf_op jit(solution)/shard_map/psum | solution.py:39
  191.7 17.4 %concatenate.235 = f32[150,4096]{1,0:T(8,128)} concatenate(f32[25,4096]{1,0:T(8,128)S(1)} %concatenate.226, f32[25,4096]{1,0:T(8,128)} %bitcast.258, f32[25,4096]{1,0:T(8,128)S(1)} %concatenate.229, f32[25,4096]{1,0:T(8,128)} %bitcast.256, f32[25,4096]{1,0:T(8,128)} %concatenate.232, f32[25,4096]{1,0:T(8,128)} %bitcast.252), dimensions={0} | concatenate | bytes 4915200 | tf_op jit(solution)/shard_map/concatenate | solution.py:54
  209.0 6.3 %fusion.4 = f32[300,4096]{1,0:T(8,128)S(1)} fusion(f32[150,4096]{1,0:T(8,128)} %concatenate.235, f32[150,150]{1,0:T(8,128)} %param.12, f32[150,150]{1,0:T(8,128)} %param.11), kind=kOutput, calls=%fused_computation.64 | convolution fusion | flops 2211885056 | bytes 7552800 | tf_op jit(solution)/shard_map/dot_general | solution.py:57
  231.3 66.8 %psum.45 = f32[]{:T(128)} all-reduce(f32[]{:T(128)} %multiply_reduce_fusion.2), channel_id=1, replica_groups=mesh['gx'=16,'gy'=8] {'gx','gy'}, use_global_device_ids=true, to_apply=%region_7.8 | all-reduce | flops 1 | bytes 8 | tf_op jit(solution)/shard_map/psum | solution.py:68
  299.4 3.1 multiply_reduce_fusion.1
  302.5 62.2 %psum.46 = f32[]{:T(128)} all-reduce(f32[]{:T(128)} %get-tuple-element.45), channel_id=1, replica_groups=mesh['gx'=16,'gy'=8] {'gx','gy'}, use_global_device_ids=true, to_apply=%region_9.10 | all-reduce | flops 1 | bytes 8 | tf_op jit(solution)/shard_map/psum | solution.py:39
  385.1 17.4 %concatenate.254 = f32[150,4096]{1,0:T(8,128)} concatenate(f32[25,4096]{1,0:T(8,128)S(1)} %concatenate.245, f32[25,4096]{1,0:T(8,128)} %bitcast.259, f32[25,4096]{1,0:T(8,128)S(1)} %concatenate.248, f32[25,4096]{1,0:T(8,128)} %bitcast.254, f32[25,4096]{1,0:T(8,128)} %concatenate.251, f32[25,4096]{1,0:T(8,128)} %bitcast.251), dimensions={0} | concatenate | bytes 4915200 | tf_op jit(solution)/shard_map/concatenate | solution.py:54
  402.5 6.3 %fusion.3 = f32[300,4096]{1,0:T(8,128)S(1)} fusion(f32[150,4096]{1,0:T(8,128)} %concatenate.254, f32[150,150]{1,0:T(8,128)} %param.12, f32[150,150]{1,0:T(8,128)} %param.11), kind=kOutput, calls=%fused_computation.63 | convolution fusion | flops 2211885056 | bytes 7552800 | tf_op jit(solution)/shard_map/dot_general | solution.py:57
  424.4 67.1 %psum.47 = f32[]{:T(128)} all-reduce(f32[]{:T(128)} %multiply_reduce_fusion), channel_id=1, replica_groups=mesh['gx'=16,'gy'=8] {'gx','gy'}, use_global_device_ids=true, to_apply=%region_11.12 | all-reduce | flops 1 | bytes 8 | tf_op jit(solution)/shard_map/psum | solution.py:68
  495.5 55.5 %while.11 = (s32[]{:T(128)}, f32[1,8,128]{2,1,0:T(8,128)S(1)}, f32[1,8,128]{2,1,0:T(8,128)S(1)}, s32[]{:T(128)}, s32[]{:T(128)}) while((s32[]{:T(128)}, f32[1,8,128]{2,1,0:T(8,128)S(1)}, f32[1,8,128]{2,1,0:T(8,128)S(1)}, s32[]{:T(128)}, s32[]{:T(128)}) %tuple.59), condition=%wide.region_14.15_spmd.clone, body=%wide.region_13.14_spmd.clone.sunk | while | flops 4099 | bytes 57495 | solution.py:81
  498.0 5.3 collective-permute-done.1
  504.7 5.4 collective-permute-done.1
  511.5 5.4 collective-permute-done.1
  518.4 5.4 collective-permute-done.1
  525.2 5.4 collective-permute-done.1
  532.0 5.4 collective-permute-done.1
  538.8 5.4 collective-permute-done.1
  545.6 5.4 collective-permute-done.1
  551.2 2.9 add_add_fusion
  (242 shorter events, 102.0 us)
Async XLA Ops:
  2.2 13.0 %collective-permute-start.3 = (f32[25,4,1,128]{3,2,1,0:T(1,128)S(1)}, f32[25,4,1,128]{3,2,1,0:T(1,128)S(1)}, u32[]{:S(2)}, u32[]{:S(2)}) collective-permute-start(f32[25,4,1,128]{3,2,1,0:T(1,128)S(1)} %slice.307), channel_id=1, source_target_pairs={{0,7},{1,0},{2,1},{3,2},{4,3},{5,4},{6,5},{7,6},{8,15},{9,8},{10,9... | collective-permute-start | bytes 153608 | tf_op jit(solution)/shard_map/ppermute | solution.py:12
  6.3 10.1 %collective-permute-start.2 = (f32[25,1,8,128]{3,2,1,0:T(8,128)S(1)}, f32[25,1,8,128]{3,2,1,0:T(8,128)S(1)}, u32[]{:S(2)}, u32[]{:S(2)}) collective-permute-start(f32[25,1,8,128]{3,2,1,0:T(8,128)S(1)} %slice.305), channel_id=1, source_target_pairs={{0,120},{8,0},{16,8},{24,16},{32,24},{40,32},{48,40},{56,48},{64,5... | collective-permute-start | bytes 307208 | tf_op jit(solution)/shard_map/ppermute | solution.py:12
  34.9 7.8 %collective-permute-start.4 = (f32[25,1,8,128]{3,2,1,0:T(8,128)S(1)}, f32[25,1,8,128]{3,2,1,0:T(8,128)S(1)}, u32[]{:S(2)}, u32[]{:S(2)}) collective-permute-start(f32[25,1,8,128]{3,2,1,0:T(8,128)S(1)} %slice.314), channel_id=1, source_target_pairs={{0,8},{8,16},{16,24},{24,32},{32,40},{40,48},{48,56},{56,64},{64,7... | collective-permute-start | bytes 307208 | tf_op jit(solution)/shard_map/ppermute | solution.py:12
  35.0 6.4 %collective-permute-start.5 = (f32[25,4,1,128]{3,2,1,0:T(1,128)S(1)}, f32[25,4,1,128]{3,2,1,0:T(1,128)}, u32[]{:S(2)}, u32[]{:S(2)}) collective-permute-start(f32[25,4,1,128]{3,2,1,0:T(1,128)S(1)} %slice.318), channel_id=1, source_target_pairs={{0,1},{1,2},{2,3},{3,4},{4,5},{5,6},{6,7},{7,0},{8,9},{9,10},{10,1... | collective-permute-start | bytes 153608 | tf_op jit(solution)/shard_map/ppermute | solution.py:12
  176.7 10.5 %collective-permute-start.7 = (f32[25,4,1,128]{3,2,1,0:T(1,128)}, f32[25,4,1,128]{3,2,1,0:T(1,128)}, u32[]{:S(2)}, u32[]{:S(2)}) collective-permute-start(f32[25,4,1,128]{3,2,1,0:T(1,128)} %slice.329), channel_id=1, source_target_pairs={{0,7},{1,0},{2,1},{3,2},{4,3},{5,4},{6,5},{7,6},{8,15},{9,8},{10,9... | collective-permute-start | bytes 153608 | tf_op jit(solution)/shard_map/ppermute | solution.py:12
  181.9 7.7 %collective-permute-start.6 = (f32[25,1,8,128]{3,2,1,0:T(8,128)}, f32[25,1,8,128]{3,2,1,0:T(8,128)}, u32[]{:S(2)}, u32[]{:S(2)}) collective-permute-start(f32[25,1,8,128]{3,2,1,0:T(8,128)} %slice.326), channel_id=1, source_target_pairs={{0,120},{8,0},{16,8},{24,16},{32,24},{40,32},{48,40},{56,48},{64,5... | collective-permute-start | bytes 307208 | tf_op jit(solution)/shard_map/ppermute | solution.py:12
  221.2 8.1 %collective-permute-start.8 = (f32[25,1,8,128]{3,2,1,0:T(8,128)}, f32[25,1,8,128]{3,2,1,0:T(8,128)S(1)}, u32[]{:S(2)}, u32[]{:S(2)}) collective-permute-start(f32[25,1,8,128]{3,2,1,0:T(8,128)} %slice.337), channel_id=1, source_target_pairs={{0,8},{8,16},{16,24},{24,32},{32,40},{40,48},{48,56},{56,64},{64,7... | collective-permute-start | bytes 307208 | tf_op jit(solution)/shard_map/ppermute | solution.py:12
  221.2 7.2 %collective-permute-start.9 = (f32[25,4,1,128]{3,2,1,0:T(1,128)}, f32[25,4,1,128]{3,2,1,0:T(1,128)}, u32[]{:S(2)}, u32[]{:S(2)}) collective-permute-start(f32[25,4,1,128]{3,2,1,0:T(1,128)} %slice.341), channel_id=1, source_target_pairs={{0,1},{1,2},{2,3},{3,4},{4,5},{5,6},{6,7},{7,0},{8,9},{9,10},{10,1... | collective-permute-start | bytes 153608 | tf_op jit(solution)/shard_map/ppermute | solution.py:12
  369.9 10.7 %collective-permute-start.11 = (f32[25,4,1,128]{3,2,1,0:T(1,128)}, f32[25,4,1,128]{3,2,1,0:T(1,128)}, u32[]{:S(2)}, u32[]{:S(2)}) collective-permute-start(f32[25,4,1,128]{3,2,1,0:T(1,128)} %slice.352), channel_id=1, source_target_pairs={{0,7},{1,0},{2,1},{3,2},{4,3},{5,4},{6,5},{7,6},{8,15},{9,8},{10,9... | collective-permute-start | bytes 153608 | tf_op jit(solution)/shard_map/ppermute | solution.py:12
  374.9 8.1 %collective-permute-start.10 = (f32[25,1,8,128]{3,2,1,0:T(8,128)}, f32[25,1,8,128]{3,2,1,0:T(8,128)}, u32[]{:S(2)}, u32[]{:S(2)}) collective-permute-start(f32[25,1,8,128]{3,2,1,0:T(8,128)} %slice.349), channel_id=1, source_target_pairs={{0,120},{8,0},{16,8},{24,16},{32,24},{40,32},{48,40},{56,48},{64,5... | collective-permute-start | bytes 307208 | tf_op jit(solution)/shard_map/ppermute | solution.py:12
  414.7 7.9 %collective-permute-start.12 = (f32[25,1,8,128]{3,2,1,0:T(8,128)}, f32[25,1,8,128]{3,2,1,0:T(8,128)S(1)}, u32[]{:S(2)}, u32[]{:S(2)}) collective-permute-start(f32[25,1,8,128]{3,2,1,0:T(8,128)} %slice.360), channel_id=1, source_target_pairs={{0,8},{8,16},{16,24},{24,32},{32,40},{40,48},{48,56},{56,64},{64,7... | collective-permute-start | bytes 307208 | tf_op jit(solution)/shard_map/ppermute | solution.py:12
  414.7 6.5 %collective-permute-start.13 = (f32[25,4,1,128]{3,2,1,0:T(1,128)}, f32[25,4,1,128]{3,2,1,0:T(1,128)}, u32[]{:S(2)}, u32[]{:S(2)}) collective-permute-start(f32[25,4,1,128]{3,2,1,0:T(1,128)} %slice.364), channel_id=1, source_target_pairs={{0,1},{1,2},{2,3},{3,4},{4,5},{5,6},{6,7},{7,0},{8,9},{9,10},{10,1... | collective-permute-start | bytes 153608 | tf_op jit(solution)/shard_map/ppermute | solution.py:12
  495.5 2.5 collective-permute-start
  496.7 6.6 %collective-permute-start.1 = (f32[1,8,128]{2,1,0:T(8,128)S(1)}, f32[1,8,128]{2,1,0:T(8,128)S(1)}, u32[]{:S(2)}, u32[]{:S(2)}) collective-permute-start(f32[1,8,128]{2,1,0:T(8,128)S(1)} %broadcast_select_fusion.2), channel_id=1, source_target_pairs={{0,8},{8,16},{16,24},{24,32},{32,40},{40,48},{48,56},{56,64},{64,7... | collective-permute-start | bytes 12296 | tf_op jit(solution)/shard_map/while/body/eval_jaxpr/ppermute | solution.py:22
  503.3 1.4 collective-permute-start
  503.4 6.7 %collective-permute-start.1 = (f32[1,8,128]{2,1,0:T(8,128)S(1)}, f32[1,8,128]{2,1,0:T(8,128)S(1)}, u32[]{:S(2)}, u32[]{:S(2)}) collective-permute-start(f32[1,8,128]{2,1,0:T(8,128)S(1)} %broadcast_select_fusion.2), channel_id=1, source_target_pairs={{0,8},{8,16},{16,24},{24,32},{32,40},{40,48},{48,56},{56,64},{64,7... | collective-permute-start | bytes 12296 | tf_op jit(solution)/shard_map/while/body/eval_jaxpr/ppermute | solution.py:22
  510.2 6.7 %collective-permute-start.1 = (f32[1,8,128]{2,1,0:T(8,128)S(1)}, f32[1,8,128]{2,1,0:T(8,128)S(1)}, u32[]{:S(2)}, u32[]{:S(2)}) collective-permute-start(f32[1,8,128]{2,1,0:T(8,128)S(1)} %broadcast_select_fusion.2), channel_id=1, source_target_pairs={{0,8},{8,16},{16,24},{24,32},{32,40},{40,48},{48,56},{56,64},{64,7... | collective-permute-start | bytes 12296 | tf_op jit(solution)/shard_map/while/body/eval_jaxpr/ppermute | solution.py:22
  517.0 6.7 %collective-permute-start.1 = (f32[1,8,128]{2,1,0:T(8,128)S(1)}, f32[1,8,128]{2,1,0:T(8,128)S(1)}, u32[]{:S(2)}, u32[]{:S(2)}) collective-permute-start(f32[1,8,128]{2,1,0:T(8,128)S(1)} %broadcast_select_fusion.2), channel_id=1, source_target_pairs={{0,8},{8,16},{16,24},{24,32},{32,40},{40,48},{48,56},{56,64},{64,7... | collective-permute-start | bytes 12296 | tf_op jit(solution)/shard_map/while/body/eval_jaxpr/ppermute | solution.py:22
  523.8 1.4 collective-permute-start
  523.8 6.7 %collective-permute-start.1 = (f32[1,8,128]{2,1,0:T(8,128)S(1)}, f32[1,8,128]{2,1,0:T(8,128)S(1)}, u32[]{:S(2)}, u32[]{:S(2)}) collective-permute-start(f32[1,8,128]{2,1,0:T(8,128)S(1)} %broadcast_select_fusion.2), channel_id=1, source_target_pairs={{0,8},{8,16},{16,24},{24,32},{32,40},{40,48},{48,56},{56,64},{64,7... | collective-permute-start | bytes 12296 | tf_op jit(solution)/shard_map/while/body/eval_jaxpr/ppermute | solution.py:22
  530.7 6.7 %collective-permute-start.1 = (f32[1,8,128]{2,1,0:T(8,128)S(1)}, f32[1,8,128]{2,1,0:T(8,128)S(1)}, u32[]{:S(2)}, u32[]{:S(2)}) collective-permute-start(f32[1,8,128]{2,1,0:T(8,128)S(1)} %broadcast_select_fusion.2), channel_id=1, source_target_pairs={{0,8},{8,16},{16,24},{24,32},{32,40},{40,48},{48,56},{56,64},{64,7... | collective-permute-start | bytes 12296 | tf_op jit(solution)/shard_map/while/body/eval_jaxpr/ppermute | solution.py:22
  537.4 1.4 collective-permute-start
  537.5 6.7 %collective-permute-start.1 = (f32[1,8,128]{2,1,0:T(8,128)S(1)}, f32[1,8,128]{2,1,0:T(8,128)S(1)}, u32[]{:S(2)}, u32[]{:S(2)}) collective-permute-start(f32[1,8,128]{2,1,0:T(8,128)S(1)} %broadcast_select_fusion.2), channel_id=1, source_target_pairs={{0,8},{8,16},{16,24},{24,32},{32,40},{40,48},{48,56},{56,64},{64,7... | collective-permute-start | bytes 12296 | tf_op jit(solution)/shard_map/while/body/eval_jaxpr/ppermute | solution.py:22
  544.3 6.7 %collective-permute-start.1 = (f32[1,8,128]{2,1,0:T(8,128)S(1)}, f32[1,8,128]{2,1,0:T(8,128)S(1)}, u32[]{:S(2)}, u32[]{:S(2)}) collective-permute-start(f32[1,8,128]{2,1,0:T(8,128)S(1)} %broadcast_select_fusion.2), channel_id=1, source_target_pairs={{0,8},{8,16},{16,24},{24,32},{32,40},{40,48},{48,56},{56,64},{64,7... | collective-permute-start | bytes 12296 | tf_op jit(solution)/shard_map/while/body/eval_jaxpr/ppermute | solution.py:22
  (29 other events, 130.1 us)
where the time goes:
time: 565 us; the launch traced here: 554 us
  blocking collectives  323 us (57%)
  local copies, waits for them, and re-layouts  99.2 us (18%)
  waiting for transfers between devices  56.4 us (10%)
  other arithmetic  27.2 us (5%)
  starting transfers between devices  23.1 us (4%)
  matrix products  16.9 us (3%)
  between operations  8.35 us (1%)
    psum x3, blocking collectives, squares(): return lax.psum(jnp.sum(vector * vector), ('gx', 'gy'))  189 us
    psum x2, blocking collectives, shards(): alpha = norm_now / lax.psum(jnp.sum(direction * image), ('gx', 'gy'))  134 us
    concatenate x12, local copies, waits for them, and re-layouts, shards(): jnp.concatenate([trace_x, upper_x, trace_y, upper_y, trace_z, upper_z], 0)  53.2 us
    ppermute x8, waiting for transfers between devices, with_halo(): lax.ppermute(tail, axis, [(i, (i + 1) % count) for i in range(count)])  43.1 us
    unnamed x89, local copies, waits for them, and re-layouts  20.5 us
    ppermute x12, starting transfers between devices, passed_along(): lax.ppermute(value, axis, [(i, (i + by) % peers) for i in range(peers)])  17.9 us
    dot_general x3, matrix products, shards(): jnp.dot(stacked, local, precision=lax.Precision.HIGHEST, preferred_elemen...  16.9 us
  transfers between devices with their start and end apart: 28, of which 21 were waited for; matrix products, arithmetic and copies ran while one was open for 7% of the time, Pallas kernels for 0%

commit v1 on v0

v1 whole, which is shorter than its diff:
```python
import jax
import jax.numpy as jnp
import numpy as np
from jax import lax
from jax.experimental import pallas as pl
from jax.experimental.pallas import tpu as pltpu
from jax.sharding import PartitionSpec as P

ITERS = 3
SWEEPS = 8
F, A, AP = 3, 25, 32
LX, LY, LZ = 4, 8, 128
CELLS = LX * LY
FACE = A * CELLS
ROWS = F * FACE
PADDED = ROWS + (AP - A) * CELLS
f32, bf16 = jnp.float32, jnp.bfloat16
VM = pl.BlockSpec(memory_space=pltpu.VMEM)
SM = pl.BlockSpec(memory_space=pltpu.SMEM)


def shifted(value, axis, by):
    n = lax.axis_size(axis)
    return lax.ppermute(value, axis, [(i, (i + by) % n) for i in range(n)])


def near_swap(value, axis):
    n = lax.axis_size(axis)
    return lax.ppermute(value, axis, [(i, i ^ 1) for i in range(n)])


def far_swap(value, axis):
    n = lax.axis_size(axis)
    pairs = [(i, (i + 1) % n) if i % 2 else (i, (i - 1) % n) for i in range(n)]
    return lax.ppermute(value, axis, pairs)


def halves(v):
    hi = v.astype(bf16)
    lo = (v - hi.astype(f32)).astype(bf16)
    return hi, lo


def apply_operator(v_ref, ux_ref, uy_ref, k_ref, m_ref, scale, wh_ref, wl_ref, out_ref, up_x, low_x, up_y, low_y):
    wh = wh_ref[...]
    wl = wl_ref[...]

    def face(f, x, y):
        if f == 0 and x == LX:
            return ux_ref[pl.ds(y, AP, stride=LY), :]
        if f == 1 and y == LY:
            return uy_ref[pl.ds(x, AP, stride=LX), :]
        return v_ref[pl.ds(f * FACE + x * LY + y, AP, stride=CELLS), :]

    def put(f, x, y, value):
        out_ref[pl.ds(f * FACE + x * LY + y, A, stride=CELLS), :] = value[:A]

    t0 = [halves(face(0, 0, y)) for y in range(LY)]
    carry = None
    for x in range(LX):
        t0_next = [halves(face(0, x + 1, y)) for y in range(LY)]
        t1 = [halves(face(1, x, y)) for y in range(LY + 1)]
        his, los = [], []
        for y in range(LY):
            z = face(2, x, y)
            t2 = halves(z)
            t2u = halves(pltpu.roll(z, LZ - 1, 1))
            six = (t0[y], t0_next[y], t1[y], t1[y + 1], t2, t2u)
            his.append(jnp.concatenate([b[0] for b in six], 0))
            los.append(jnp.concatenate([b[1] for b in six], 0))
        t0 = t0_next
        hi = jnp.concatenate(his, 1)
        lo = jnp.concatenate(los, 1)
        prod = jnp.dot(wh, hi, preferred_element_type=f32)
        prod += jnp.dot(wh, lo, preferred_element_type=f32)
        prod += jnp.dot(wl, hi, preferred_element_type=f32)
        parts = []
        for y in range(LY):
            k = k_ref[x * LY + y : x * LY + y + 1, :] * scale
            m = m_ref[x * LY + y : x * LY + y + 1, :] * scale
            cols = slice(y * LZ, (y + 1) * LZ)
            w = prod[: 6 * AP, cols] * k + prod[6 * AP :, cols] * m
            parts.append([w[b * AP : (b + 1) * AP] for b in range(6)])
        for y in range(LY):
            wlx, wux, wly, wuy, wlz, wuz = parts[y]
            put(0, x, y, wlx if x == 0 else wlx + carry[y])
            put(1, x, y, wly if y == 0 else wly + parts[y - 1][3])
            put(2, x, y, wlz + pltpu.roll(wuz, 1, 1))
            if x == 0 and low_x is not None:
                low_x[pl.ds(y, A, stride=LY), :] = wlx[:A]
            if x == LX - 1:
                up_x[pl.ds(y, A, stride=LY), :] = wux[:A]
        if low_y is not None:
            low_y[pl.ds(x, A, stride=LX), :] = parts[0][2][:A]
        up_y[pl.ds(x, A, stride=LX), :] = parts[LY - 1][3][:A]
        carry = [parts[y][1] for y in range(LY)]


def route(even, up, low, near, far):
    near[...] = jnp.where(even, up[...], low[...])
    far[...] = jnp.where(even, low[...], up[...])


def mean_eigenvalue(st_ref, traces_ref, total):
    st = st_ref[...].reshape(-1, 2, LZ)
    sums = jnp.sum(jnp.sum(st, 0), axis=1, keepdims=True)
    return (sums[0:1] * traces_ref[0] + sums[1:2] * traces_ref[1]) * (1.0 / (75.0 * total))


def first_kernel(even_ref, rhs_ref, hx_ref, hy_ref, k_ref, m_ref, wh_ref, wl_ref,
                 p_ref, snx, sfx, sny, sfy, v, ux, uy, upx, lowx, upy, lowy):
    v[:ROWS] = rhs_ref[...]
    v[ROWS:] = jnp.zeros((PADDED - ROWS, LZ), f32)
    ux[: A * LY] = hx_ref[...]
    ux[A * LY :] = jnp.zeros(((AP - A) * LY, LZ), f32)
    uy[: A * LX] = hy_ref[...]
    uy[A * LX :] = jnp.zeros(((AP - A) * LX, LZ), f32)
    apply_operator(v, ux, uy, k_ref, m_ref, 1.0, wh_ref, wl_ref, p_ref, upx, lowx, upy, lowy)
    route(even_ref[0] == 0, upx, lowx, snx, sfx)
    route(even_ref[1] == 0, upy, lowy, sny, sfy)


def next_vector(even_ref, p_ref, prev_ref, hx_ref, hy_ref, snx, sfx, sny, sfy, rnx, rfx, rny, rfy, scale, v, ux, uy):
    even_x = even_ref[0] == 0
    even_y = even_ref[1] == 0
    v[:ROWS] = p_ref[...] * scale - prev_ref[...]
    v[ROWS:] = jnp.zeros((PADDED - ROWS, LZ), f32)
    below_x = jnp.where(even_x, rfx[...], rnx[...]) * scale
    for a in range(A):
        rows = slice(a * CELLS, a * CELLS + LY)
        v[rows, :] = v[rows, :] + below_x[a * LY : (a + 1) * LY]
    below_y = jnp.where(even_y, rfy[...], rny[...]) * scale
    first = pl.ds(FACE, A * LX, stride=LY)
    v[first, :] = v[first, :] + below_y
    above_x = jnp.where(even_x, snx[...] + rnx[...], sfx[...] + rfx[...])
    ux[: A * LY] = above_x * scale - hx_ref[...]
    ux[A * LY :] = jnp.zeros(((AP - A) * LY, LZ), f32)
    above_y = jnp.where(even_y, sny[...] + rny[...], sfy[...] + rfy[...])
    uy[: A * LX] = above_y * scale - hy_ref[...]
    uy[A * LX :] = jnp.zeros(((AP - A) * LX, LZ), f32)


def node_sum(value):
    return jnp.sum(value.reshape(-1, LY, LZ), 0)


def second_kernel(even_ref, traces_ref, p_ref, rhs_ref, hx_ref, hy_ref, snx, sfx, sny, sfy, rnx, rfx, rny, rfy,
                  st_ref, k_ref, m_ref, wh_ref, wl_ref,
                  v1_ref, ux1_ref, uy1_ref, p1_ref, tnx, tfx, tny, tfy, sums_ref, inv_ref,
                  v, ux, uy, upx, lowx, upy, lowy, *, total):
    inv = 1.0 / mean_eigenvalue(st_ref, traces_ref, total)
    inv_ref[...] = jnp.broadcast_to(inv, (8, LZ))
    next_vector(even_ref, p_ref, rhs_ref, hx_ref, hy_ref, snx, sfx, sny, sfy, rnx, rfx, rny, rfy, inv, v, ux, uy)
    v0 = rhs_ref[...]
    v1 = v[:ROWS]
    v1_ref[...] = v1
    ux1_ref[...] = ux[: A * LY]
    uy1_ref[...] = uy[: A * LX]
    sums_ref[0:8] = node_sum(v0)
    sums_ref[8:16] = node_sum(v1)
    sums_ref[16:24] = node_sum(v0 * v0)
    sums_ref[24:32] = node_sum(v0 * v1)
    sums_ref[32:40] = node_sum(v1 * v1)
    apply_operator(v, ux, uy, k_ref, m_ref, inv, wh_ref, wl_ref, p1_ref, upx, lowx, upy, lowy)
    route(even_ref[0] == 0, upx, lowx, tnx, tfx)
    route(even_ref[1] == 0, upy, lowy, tny, tfy)


def third_kernel(even_ref, p_ref, prev_ref, hx_ref, hy_ref, snx, sfx, sny, sfy, rnx, rfx, rny, rfy,
                 inv_ref, sums1_ref, k_ref, m_ref, wh_ref, wl_ref,
                 v2_ref, p2_ref, upx, upy, loads_ref, mom_ref, v, ux, uy):
    one = jnp.float32(1.0)
    next_vector(even_ref, p_ref, prev_ref, hx_ref, hy_ref, snx, sfx, sny, sfy, rnx, rfx, rny, rfy, one, v, ux, uy)
    v1 = prev_ref[...]
    v2 = v[:ROWS]
    v2_ref[...] = v2
    loads_ref[0:16] = sums1_ref[0:16]
    loads_ref[16:24] = node_sum(v2)
    m3 = node_sum(v1 * v2)
    m4 = node_sum(v2 * v2)
    apply_operator(v, ux, uy, k_ref, m_ref, inv_ref[0:1], wh_ref, wl_ref, p2_ref, upx, None, upy, None)
    p2 = p2_ref[...]
    loads_ref[24:32] = node_sum(p2)
    loads_ref[32:40] = node_sum(upx[...])
    energy = node_sum(v[:ROWS] * p2) + node_sum(ux[: A * LY] * upx[...])
    tail = jnp.sum(uy[: A * LX] * upy[...], 0, keepdims=True)

    def row(tile):
        return jnp.sum(tile, 0, keepdims=True)

    mom_ref[0:1] = row(sums1_ref[16:24])
    mom_ref[1:2] = row(sums1_ref[24:32])
    mom_ref[2:3] = row(sums1_ref[32:40])
    mom_ref[3:4] = row(m3)
    mom_ref[4:5] = row(m4)
    mom_ref[5:6] = row(energy) + tail
    mom_ref[6:7] = jnp.sum(upy[...], 0, keepdims=True)
    mom_ref[7:8] = jnp.zeros((1, LZ), f32)


def middle_kernel(me_ref, g_ref, mom_ref, loads_ref, out_ref, *, nx, ny):
    below = lax.rem(me_ref[1] + ny - 1, ny)
    tiles = mom_ref[...].reshape(ny, 8, LZ)
    total = jnp.sum(tiles, 0)
    edge = mom_ref[pl.ds(below * 8 + 6, 1), :]
    image = loads_ref[24:32]
    at_first = lax.broadcasted_iota(jnp.int32, (8, LZ), 0) == 0
    image = image + jnp.where(at_first, jnp.broadcast_to(edge, (8, LZ)), 0.0)
    own = [loads_ref[0:8], loads_ref[8:16], loads_ref[16:24], image]
    above = loads_ref[32:40]
    for to in range(nx):
        g = g_ref[to]
        for k in range(4):
            piece = own[k] * g
            if k == 3:
                piece = piece + above * g_ref[nx + to]
            out_ref[to * 40 + k * 8 : to * 40 + (k + 1) * 8] = piece
        out_ref[to * 40 + 32 : to * 40 + 40] = total


def conjugate_gradient(m):
    def dot(a, b):
        s = None
        for i, ai in enumerate(a):
            for j, bj in enumerate(b):
                t = ai * bj * m[i + j]
                s = t if s is None else s + t
        return s

    def add(a, b, factor):
        longer = []
        for i in range(max(len(a), len(b))):
            if i >= len(b):
                longer.append(a[i])
            elif i >= len(a):
                longer.append(factor * b[i])
            else:
                longer.append(a[i] + factor * b[i])
        return longer

    def image(a):
        return [a[0]] + [a[i] + a[i - 1] for i in range(1, len(a))] + [a[-1]]

    one = jnp.ones((1, 1), f32)
    iterate, residual, direction = [], [one], [one]
    norm = m[0]
    for step in range(ITERS):
        img = image(direction)
        alpha = norm / dot(direction, img)
        iterate = add(iterate, direction, alpha)
        residual = add(residual, img, -alpha)
        if step < ITERS - 1:
            norm_next = dot(residual, residual)
            direction = add(residual, direction, norm_next / norm)
            norm = norm_next
    return iterate, residual


def last_kernel(prolong_ref, got_ref, inv_ref, rhs_ref, v1_ref, v2_ref, p2_ref, rx_ref, ry_ref,
                sol_ref, res_ref, coarse_ref, *, nx):
    got = jnp.sum(got_ref[...].reshape(nx, 5, 8, LZ), 0)
    sums = jnp.sum(got[4], axis=1, keepdims=True)
    m = [sums[k : k + 1] for k in range(6)]
    m[5] = m[5] - m[4]
    x, d = conjugate_gradient(m)
    inv = inv_ref[0:1, 0:1]
    x = [t * inv for t in x]
    coarse = d[0] * got[0] + d[1] * got[1] + (d[2] - d[3]) * got[2] + d[3] * got[3]
    coarse_ref[...] = coarse
    d2 = d[2] - d[3]
    for f in range(F):
        for a in range(A):
            at = (f * A + a) * CELLS
            spread = coarse * prolong_ref[f * A + a]
            for c in range(LX):
                rows = slice(at + c * LY, at + (c + 1) * LY)
                v0, v1, v2 = rhs_ref[rows, :], v1_ref[rows, :], v2_ref[rows, :]
                img = p2_ref[rows, :]
                if f == 0 and c == 0:
                    img = img + rx_ref[a * LY : (a + 1) * LY, :]
                sol_ref[rows, :] = x[0] * v0 + x[1] * v1 + x[2] * v2 + spread
                res_ref[rows, :] = d[0] * v0 + d[1] * v1 + d2 * v2 + d[3] * img
    first = pl.ds(FACE, A * LX, stride=LY)
    res_ref[first, :] = res_ref[first, :] + d[3] * ry_ref[...]


def jacobi_weights(n):
    coarse = np.zeros(n)
    load = np.zeros(n)
    load[0] = 1.0
    for _ in range(SWEEPS):
        coarse = (load + np.roll(coarse, 1) + np.roll(coarse, -1)) / 2.2
    return coarse / 75.0


def struct(*shape):
    return jax.ShapeDtypeStruct(shape, f32)


PARAMS = pltpu.CompilerParams(vmem_limit_bytes=40 * 1024 * 1024)


def shards(rhs, kappa, mass, stiffness, mass_matrix, prolong):
    nx, ny = lax.axis_size("gx"), lax.axis_size("gy")
    me_x, me_y = lax.axis_index("gx"), lax.axis_index("gy")
    both = ("gx", "gy")
    vx, vy = A * LY, A * LX

    hx = shifted(rhs[0, :, 0].reshape(vx, LZ), "gx", -1)
    hy = shifted(rhs[1, :, :, 0].reshape(vy, LZ), "gy", -1)

    stats = jnp.stack([jnp.sum(kappa, (0, 1)), jnp.sum(mass, (0, 1))], 0)
    stats = lax.all_to_all(jnp.broadcast_to(stats[None], (nx * ny, 2, LZ)), both, 0, 0, tiled=True)
    stats = stats.reshape(nx * ny * 2, LZ)
    traces = jnp.stack([jnp.trace(stiffness), jnp.trace(mass_matrix)])

    def padded(matrix):
        blocks = jnp.pad(matrix.reshape(6, A, 6, A), ((0, 0), (0, AP - A), (0, 0), (0, AP - A)))
        return blocks.reshape(6 * AP, 6 * AP)

    weights = jnp.concatenate([padded(stiffness), padded(mass_matrix)], 0)
    wh = lax.reduce_precision(weights, 8, 7)
    wl = (weights - wh).astype(bf16)
    wh = wh.astype(bf16)

    even = jnp.stack([me_x % 2, me_y % 2])
    me = jnp.stack([me_x, me_y])
    table = jacobi_weights(nx)
    index = np.arange(nx)
    rows = np.stack([np.concatenate([table[(index - p) % nx], table[(index - p - 1) % nx]]) for p in range(nx)])
    g = lax.dynamic_index_in_dim(jnp.asarray(rows, f32), me_x, 0, keepdims=False)

    rhs2 = rhs.reshape(ROWS, LZ)
    k2 = kappa.reshape(CELLS, LZ)
    m2 = mass.reshape(CELLS, LZ)
    sends = [struct(vx, LZ), struct(vx, LZ), struct(vy, LZ), struct(vy, LZ)]
    field = [pltpu.VMEM((PADDED, LZ), f32), pltpu.VMEM((AP * LY, LZ), f32), pltpu.VMEM((AP * LX, LZ), f32)]
    edges = [pltpu.VMEM((vx, LZ), f32)] * 2 + [pltpu.VMEM((vy, LZ), f32)] * 2

    def swap(s):
        far_x = far_swap(s[1], "gx")
        far_y = far_swap(s[3], "gy")
        near_y = near_swap(s[2], "gy")
        near_x = near_swap(s[0], "gx")
        return [near_x, far_x, near_y, far_y]

    p0, *s = pl.pallas_call(
        first_kernel,
        out_shape=[struct(ROWS, LZ)] + sends,
        in_specs=[SM] + [VM] * 7,
        out_specs=[VM] * 5,
        scratch_shapes=field + edges,
        compiler_params=PARAMS,
        name="first",
    )(even, rhs2, hx, hy, k2, m2, wh, wl)
    r = swap(s)

    def second(*refs):
        second_kernel(*refs, total=float(nx * ny * CELLS * LZ))

    v1, ux1, uy1, p1, *rest = pl.pallas_call(
        second,
        out_shape=[struct(ROWS, LZ), struct(vx, LZ), struct(vy, LZ), struct(ROWS, LZ)] + sends + [struct(40, LZ), struct(8, LZ)],
        in_specs=[SM, SM] + [VM] * 17,
        out_specs=[VM] * 10,
        scratch_shapes=field + edges,
        compiler_params=PARAMS,
        name="second",
    )(even, traces, p0, rhs2, hx, hy, *s, *r, stats, k2, m2, wh, wl)
    s, (sums, inv) = rest[:4], rest[4:]
    r = swap(s)

    v2, p2, upx, upy, loads, mom = pl.pallas_call(
        third_kernel,
        out_shape=[struct(ROWS, LZ), struct(ROWS, LZ), struct(vx, LZ), struct(vy, LZ), struct(40, LZ), struct(8, LZ)],
        in_specs=[SM] + [VM] * 18,
        out_specs=[VM] * 6,
        scratch_shapes=field,
        compiler_params=PARAMS,
        name="third",
    )(even, p1, v1, ux1, uy1, *s, *r, inv, sums, k2, m2, wh, wl)
    rx = shifted(upx, "gx", 1)
    ry = shifted(upy, "gy", 1)
    mom = lax.all_to_all(jnp.broadcast_to(mom[None], (ny, 8, LZ)), "gy", 0, 0, tiled=True)

    def middle(*refs):
        middle_kernel(*refs, nx=nx, ny=ny)

    pieces = pl.pallas_call(
        middle,
        out_shape=struct(nx * 40, LZ),
        in_specs=[SM, SM, VM, VM],
        out_specs=VM,
        compiler_params=PARAMS,
        name="middle",
    )(me, g, mom.reshape(ny * 8, LZ), loads)
    got = lax.all_to_all(pieces.reshape(nx, 40, LZ), "gx", 0, 0, tiled=True)

    def last(*refs):
        last_kernel(*refs, nx=nx)

    sol, res, coarse = pl.pallas_call(
        last,
        out_shape=[struct(ROWS, LZ), struct(ROWS, LZ), struct(LY, LZ)],
        in_specs=[SM] + [VM] * 8,
        out_specs=[VM] * 3,
        compiler_params=PARAMS,
        name="last",
    )(prolong.reshape(-1), got.reshape(nx * 40, LZ), inv, rhs2, v1, v2, p2, rx, ry)
    return sol.reshape(rhs.shape), res.reshape(rhs.shape), coarse[None]


def solution(mesh):
    placed = (
        P(None, None, "gx", "gy", None),
        P("gx", "gy", None),
        P("gx", "gy", None),
        P(),
        P(),
        P(),
    )
    return jax.shard_map(
        shards,
        mesh=mesh,
        in_specs=placed,
        out_specs=(
            P(None, None, "gx", "gy", None),
            P(None, None, "gx", "gy", None),
            P("gx", "gy", None),
        ),
        check_vma=False,
    )
```

time: 565 us -> 118 us (0.21); the launches traced: 554 us -> 117 us
  blocking collectives: 323 us -> 0 us
  local copies, waits for them, and re-layouts: 99.2 us -> 32.5 us
  waiting for transfers between devices: 56.4 us -> 20 us
  other arithmetic: 27.2 us -> 6.32 us
  Pallas kernels: 0 us -> 20.2 us
  matrix products: 16.9 us -> 0 us
  starting transfers between devices: 23.1 us -> 36.6 us
  between operations: 8.35 us -> 0.88 us
    psum x5 -> x0, blocking collectives: 323 us -> none  [the longest x3 189 us: squares(): return lax.psum(jnp.sum(vector * vector), ('gx', 'gy'))]
    concatenate x24 -> x1, local copies, waits for them, and re-layouts: 60.1 us -> 0.02 us  [shards(): weights = jnp.concatenate([padded(stiffness), padded(mass_matrix)], 0)]
    ppermute x28 -> x12, waiting for transfers between devices: 56.4 us -> 14.5 us  [the longest x4 10.2 us: shifted(): return lax.ppermute(value, axis, [(i, (i + by) % n) for i in range(n)])]
    pallas_call x0 -> x5, Pallas kernels: none -> 20.2 us  [the longest x1 6.01 us: shards(): pl.pallas_call(second, out_shape=[struct(ROWS, LZ), struct(vx, LZ), struc...]
    dot_general x3 -> x0, matrix products: 16.9 us -> none  [shards(): jnp.dot(stacked, local, precision=lax.Precision.HIGHEST, preferred_elemen...]
    slice x27 -> x1, local copies, waits for them, and re-layouts: 14.4 us -> 1.18 us  [shards(): hy = shifted(rhs[1, :, :, 0].reshape(vy, LZ), 'gy', -1)]
    add x15 -> x0, other arithmetic: 12.2 us -> none  [the longest x3 2.95 us: shards(): out_y = parts[2] + jnp.concatenate([below_y, parts[3][:, :, :-1]], 2)]
    all_to_all x0 -> x3, starting transfers between devices: none -> 11.5 us  [the longest x1 4.61 us: shards(): lax.all_to_all(jnp.broadcast_to(stats[None], (nx * ny, 2, LZ)), both, 0,...]
  transfers between devices with their start and end apart: 28 -> 15, of which waited for: 21 -> 5; matrix products, arithmetic and copies ran while one was open for 7% -> 10% of each run, Pallas kernels for 0% -> 4%
where the time goes in v1:
time: 118 us; the launch traced here: 117 us
  starting transfers between devices  36.6 us (31%)
  local copies, waits for them, and re-layouts  32.5 us (28%)
  Pallas kernels  20.2 us (17%)
  waiting for transfers between devices  20 us (17%)
  other arithmetic  6.32 us (5%)
    unnamed x71, local copies, waits for them, and re-layouts  25.8 us
    ppermute x4, starting transfers between devices, far_swap(): return lax.ppermute(value, axis, pairs)  13.9 us
    ppermute x4, starting transfers between devices, shifted(): return lax.ppermute(value, axis, [(i, (i + by) % n) for i in range(n)])  10.4 us
    ppermute x4, waiting for transfers between devices, shifted(): return lax.ppermute(value, axis, [(i, (i + by) % n) for i in range(n)])  10.2 us
    pallas_call x1, Pallas kernels, shards(): pl.pallas_call(second, out_shape=[struct(ROWS, LZ), struct(vx, LZ), struc...  6.01 us
    pallas_call x1, Pallas kernels, shards(): pl.pallas_call(third_kernel, out_shape=[struct(ROWS, LZ), struct(ROWS, LZ...  5.64 us
    all_to_all x1, waiting for transfers between devices, shards(): lax.all_to_all(jnp.broadcast_to(mom[None], (ny, 8, LZ)), 'gy', 0, 0, tile...  5.48 us
    pallas_call x1, Pallas kernels, shards(): pl.pallas_call(first_kernel, out_shape=[struct(ROWS, LZ)] + sends, in_spe...  4.78 us
  transfers between devices with their start and end apart: 15, of which 5 were waited for; matrix products, arithmetic and copies ran while one was open for 10% of the time, Pallas kernels for 4%

profile of v1, /device:TPU:0, one launch (start us, length us, event | category | flops | bytes accessed | tf_op | source)
XLA Modules:
  0.0 116.5 jit_solution(12705463278705326759)
XLA Ops:
  1.8 4.1 %collective-permute-start.1 = (f32[100,128]{1,0:T(8,128)S(1)}, f32[100,128]{1,0:T(8,128)S(1)}, u32[]{:S(2)}, u32[]{:S(2)}) collective-permute-start(f32[100,128]{1,0:T(8,128)S(1)} %reshape_squeeze.7), channel_id=1, source_target_pairs={{0,7},{1,0},{2,1},{3,2},{4,3},{5,4},{6,5},{7,6},{8,15},{9,8},{10,9... | collective-permute-start | bytes 153608 | tf_op jit(solution)/shard_map/ppermute | solution.py:24
  6.8 5.4 %collective-permute-start = (f32[200,128]{1,0:T(8,128)S(1)}, f32[200,128]{1,0:T(8,128)S(1)}, u32[]{:S(2)}, u32[]{:S(2)}) collective-permute-start(f32[200,128]{1,0:T(8,128)S(1)} %slice_bitcast_fusion), channel_id=1, source_target_pairs={{0,120},{8,0},{16,8},{24,16},{32,24},{40,32},{48,40},{56,48},{64,5... | collective-permute-start | bytes 307208 | tf_op jit(solution)/shard_map/ppermute | solution.py:24
  14.4 4.6 %all-to-all-start = ((f32[128,2,128]{2,1,0:T(2,128)}), f32[128,2,128]{2,1,0:T(2,128)S(1)}, u32[]{:S(2)}, u32[]{:S(2)}) async-start(f32[128,2,128]{2,1,0:T(2,128)} %broadcast_in_dim.21), calls=%async_computation | async-start | bytes 262144 | tf_op jit(solution)/shard_map/all_to_all | solution.py:313
  19.0 1.6 %select_reduce_fusion.1 = f32[]{:T(128)} fusion(f32[150,150]{1,0:T(8,128)} %param.10), kind=kLoop, calls=%fused_computation.4 | loop fusion | flops 67499 | bytes 90004 | tf_op jit(solution)/shard_map/jit(trace)/reduce_sum | solution.py:315
  24.2 4.8 %first.1 = (f32[2400,128]{1,0:T(8,128)S(1)}, f32[200,128]{1,0:T(8,128)S(1)}, f32[200,128]{1,0:T(8,128)S(1)}, f32[100,128]{1,0:T(8,128)S(1)}, f32[100,128]{1,0:T(8,128)S(1)}) custom-call(s32[2]{0:T(128)S(1)} %pad_add_fusion.1.even_ref.refs_0_, f32[2400,128]{1,0:T(8,128)S(1)} %bitcast.23, f32[200,128]{1,0:T(8,128)S(1)} %collective-permute-done.hx_ref.refs_4_, ...), custom_call_target="tpu_custom_call" | custom-call | tf_op jit(solution)/shard_map/first/pallas_call | solution.py:347
  31.5 2.9 %collective-permute-start.5 = (f32[100,128]{1,0:T(8,128)S(1)}, f32[100,128]{1,0:T(8,128)S(1)}, u32[]{:S(2)}, u32[]{:S(2)}) collective-permute-start(f32[100,128]{1,0:T(8,128)S(1)} %get-tuple-element.31.refs_9_), channel_id=1, source_target_pairs={{0,7},{1,2},{2,1},{3,4},{4,3},{5,6},{6,5},{7,0},{8,15},{9,10},{10,... | collective-permute-start | bytes 153608 | tf_op jit(solution)/shard_map/ppermute | solution.py:35
  35.6 6.0 %collective-permute-start.3 = (f32[200,128]{1,0:T(8,128)S(1)}, f32[200,128]{1,0:T(8,128)S(1)}, u32[]{:S(2)}, u32[]{:S(2)}) collective-permute-start(f32[200,128]{1,0:T(8,128)S(1)} %get-tuple-element.29.refs_7_), channel_id=1, source_target_pairs={{0,120},{8,16},{16,8},{24,32},{32,24},{40,48},{48,40},{56,64},{64,... | collective-permute-start | bytes 307208 | tf_op jit(solution)/shard_map/ppermute | solution.py:35
  42.3 1.8 %pad_maximum_fusion.1.refs_1_ = f32[2]{0:T(128)} fusion(f32[1]{0:T(128)} %bitcast.6, f32[1]{0:T(128)} %bitcast.5), kind=kLoop, calls=%fused_computation.13 | loop fusion | flops 2 | bytes 16 | tf_op jit(solution)/shard_map/stack | solution.py:315
  46.7 1.3 %copy-done.8 = f32[2400,128]{1,0:T(8,128)S(1)} copy-done((f32[2400,128]{1,0:T(8,128)S(1)}, f32[2400,128]{1,0:T(8,128)}, u32[]{:S(2)}) %copy-start.8) | copy-done | bytes 1228824
  56.1 6.0 %second.1 = (f32[2400,128]{1,0:T(8,128)S(1)}, f32[200,128]{1,0:T(8,128)S(1)}, f32[100,128]{1,0:T(8,128)S(1)}, f32[2400,128]{1,0:T(8,128)S(1)}, f32[200,128]{1,0:...) custom-call(s32[2]{0:T(128)S(1)} %copy-done.28, ...), custom_call_target="tpu_custom_call" | custom-call | tf_op jit(solution)/shard_map/second/pallas_call | solution.py:361
  63.1 2.3 %collective-permute-start.9 = (f32[100,128]{1,0:T(8,128)}, f32[100,128]{1,0:T(8,128)}, u32[]{:S(2)}, u32[]{:S(2)}) collective-permute-start(f32[100,128]{1,0:T(8,128)} %get-tuple-element.39.sfy), channel_id=1, source_target_pairs={{0,7},{1,2},{2,1},{3,4},{4,3},{5,6},{6,5},{7,0},{8,15},{9,10},{10,... | collective-permute-start | bytes 153608 | tf_op jit(solution)/shard_map/ppermute | solution.py:35
  65.4 2.7 %collective-permute-start.7 = (f32[200,128]{1,0:T(8,128)S(1)}, f32[200,128]{1,0:T(8,128)S(1)}, u32[]{:S(2)}, u32[]{:S(2)}) collective-permute-start(f32[200,128]{1,0:T(8,128)S(1)} %get-tuple-element.37.sfx), channel_id=1, source_target_pairs={{0,120},{8,16},{16,8},{24,32},{32,24},{40,48},{48,40},{56,64},{64,... | collective-permute-start | bytes 307208 | tf_op jit(solution)/shard_map/ppermute | solution.py:35
  68.7 1.4 %collective-permute-done.9.rfy = f32[100,128]{1,0:T(8,128)} collective-permute-done((f32[100,128]{1,0:T(8,128)}, f32[100,128]{1,0:T(8,128)}, u32[]{:S(2)}, u32[]{:S(2)}) %collective-permute-start.9) | collective-permute-done | bytes 51232 | tf_op jit(solution)/shard_map/ppermute | solution.py:35
  70.1 2.9 %collective-permute-done.7.rfx = f32[200,128]{1,0:T(8,128)S(1)} collective-permute-done((f32[200,128]{1,0:T(8,128)S(1)}, f32[200,128]{1,0:T(8,128)S(1)}, u32[]{:S(2)}, u32[]{:S(2)}) %collective-permute-start.7) | collective-permute-done | bytes 102432 | tf_op jit(solution)/shard_map/ppermute | solution.py:35
  73.1 1.3 %copy-done.6 = f32[2400,128]{1,0:T(8,128)S(1)} copy-done((f32[2400,128]{1,0:T(8,128)S(1)}, f32[2400,128]{1,0:T(8,128)}, u32[]{:S(2)}) %copy-start.6) | copy-done | bytes 1228824
  75.0 5.6 %third.1 = (f32[2400,128]{1,0:T(8,128)S(1)}, f32[2400,128]{1,0:T(8,128)S(1)}, f32[200,128]{1,0:T(8,128)S(1)}, f32[100,128]{1,0:T(8,128)S(1)}, f32[40,128]{1,0:T(8,128)S(1)}, /*index=5*/f32[8,128]{1,0:T(8,128)S(1)}) custom-call(s32[2]{0:T(128)S(1)} %copy-done.29, f32[2400,128]{1,0:T(8,128)S(1)} %copy-done.6, ...), custom_call_target="tpu_custom_call" | custom-call | tf_op jit(solution)/shard_map/third/pallas_call | solution.py:373
  84.6 3.3 %all-to-all-start.1 = ((f32[8,8,128]{2,1,0:T(8,128)}), f32[8,8,128]{2,1,0:T(8,128)S(1)}, u32[]{:S(2)}, u32[]{:S(2)}) async-start(f32[8,8,128]{2,1,0:T(8,128)} %broadcast_in_dim.22), calls=%async_computation.1 | async-start | bytes 65536 | tf_op jit(solution)/shard_map/all_to_all | solution.py:384
  88.6 5.5 %all-to-all-done.1 = f32[8,8,128]{2,1,0:T(8,128)S(1)} async-done(((f32[8,8,128]{2,1,0:T(8,128)}), f32[8,8,128]{2,1,0:T(8,128)S(1)}, u32[]{:S(2)}, u32[]{:S(2)}) %all-to-all-start.1) | async-done | bytes 32800 | tf_op jit(solution)/shard_map/all_to_all | solution.py:384
  94.7 1.3 %middle.1 = f32[640,128]{1,0:T(8,128)} custom-call(s32[2]{0:T(128)S(1)} %copy-done.30, f32[32]{0:T(128)S(1)} %dynamic-slice_bitcast_fusion.refs_1_, f32[64,128]{1,0:T(8,128)S(1)} %bitcast.34, f32[40,128]{1,0:T(8,128)S(1)} %get-tuple-element.43.refs_3_), custom_call_target="tpu_custom_call" | custom-call | tf_op jit(solution)/shard_map/middle/pallas_call | solution.py:389
  96.0 3.5 %all-to-all-start.2 = ((f32[16,40,128]{2,1,0:T(8,128)}), f32[16,40,128]{2,1,0:T(8,128)S(1)}, u32[]{:S(2)}, u32[]{:S(2)}) async-start(f32[16,40,128]{2,1,0:T(8,128)} %bitcast.15), calls=%async_computation.2 | async-start | bytes 655360 | tf_op jit(solution)/shard_map/all_to_all | solution.py:397
  101.3 5.8 %collective-permute-done.11.refs_8_ = f32[100,128]{1,0:T(8,128)S(1)} collective-permute-done((f32[100,128]{1,0:T(8,128)}, f32[100,128]{1,0:T(8,128)S(1)}, u32[]{:S(2)}, u32[]{:S(2)}) %collective-permute-start.11) | collective-permute-done | bytes 51232 | tf_op jit(solution)/shard_map/ppermute | solution.py:24
  107.1 4.4 %collective-permute-done.10.refs_7_ = f32[200,128]{1,0:T(8,128)S(1)} collective-permute-done((f32[200,128]{1,0:T(8,128)}, f32[200,128]{1,0:T(8,128)S(1)}, u32[]{:S(2)}, u32[]{:S(2)}) %collective-permute-start.10) | collective-permute-done | bytes 102432 | tf_op jit(solution)/shard_map/ppermute | solution.py:24
  111.5 1.3 %copy-done.2 = f32[2400,128]{1,0:T(8,128)S(1)} copy-done((f32[2400,128]{1,0:T(8,128)S(1)}, f32[2400,128]{1,0:T(8,128)}, u32[]{:S(2)}) %copy-start.2) | copy-done | bytes 1228824
  114.1 2.5 %last.1 = (f32[2400,128]{1,0:T(8,128)}, f32[2400,128]{1,0:T(8,128)}, f32[8,128]{1,0:T(8,128)}) custom-call(f32[75]{0:T(128)S(1)} %reshape.50.refs_0_, f32[640,128]{1,0:T(8,128)S(1)} %bitcast.26, f32[8,128]{1,0:T(8,128)S(1)} %get-tuple-element.40.inv_ref.refs_2_, f32[2400,128]{1,0:T(8,128)S(1)} %bitcast.25, ...), custom_call_target="tpu_custom_call" | custom-call | tf_op jit(solution)/shard_map/last/pallas_call | solution.py:402
  (105 shorter events, 33.3 us)
Async XLA Ops:
  0.6 21.1 %copy-start.34 = (f32[150,150]{1,0:T(8,128)S(1)}, f32[150,150]{1,0:T(8,128)}, u32[]{:S(2)}) copy-start(f32[150,150]{1,0:T(8,128)} %param.11) | copy-start | bytes 270004
  1.8 21.5 %collective-permute-start.1 = (f32[100,128]{1,0:T(8,128)S(1)}, f32[100,128]{1,0:T(8,128)S(1)}, u32[]{:S(2)}, u32[]{:S(2)}) collective-permute-start(f32[100,128]{1,0:T(8,128)S(1)} %reshape_squeeze.7), channel_id=1, source_target_pairs={{0,7},{1,0},{2,1},{3,2},{4,3},{5,4},{6,5},{7,6},{8,15},{9,8},{10,9... | collective-permute-start | bytes 153608 | tf_op jit(solution)/shard_map/ppermute | solution.py:24
  6.8 16.5 %collective-permute-start = (f32[200,128]{1,0:T(8,128)S(1)}, f32[200,128]{1,0:T(8,128)S(1)}, u32[]{:S(2)}, u32[]{:S(2)}) collective-permute-start(f32[200,128]{1,0:T(8,128)S(1)} %slice_bitcast_fusion), channel_id=1, source_target_pairs={{0,120},{8,0},{16,8},{24,16},{32,24},{40,32},{48,40},{56,48},{64,5... | collective-permute-start | bytes 307208 | tf_op jit(solution)/shard_map/ppermute | solution.py:24
  14.4 29.7 %all-to-all-start = ((f32[128,2,128]{2,1,0:T(2,128)}), f32[128,2,128]{2,1,0:T(2,128)S(1)}, u32[]{:S(2)}, u32[]{:S(2)}) async-start(f32[128,2,128]{2,1,0:T(2,128)} %broadcast_in_dim.21), calls=%async_computation | async-start | bytes 262144 | tf_op jit(solution)/shard_map/all_to_all | solution.py:313
  22.9 1.3 %copy-start = (f32[3,25,4,8,128]{4,3,2,1,0:T(8,128)S(1)}, f32[3,25,4,8,128]{4,3,2,1,0:T(8,128)}, u32[]{:S(2)}) copy-start(f32[3,25,4,8,128]{4,3,2,1,0:T(8,128)} %param.7) | copy-start | bytes 3686404
  22.9 1.3 %copy-start.9 = (f32[4,8,128]{2,1,0:T(8,128)S(1)}, f32[4,8,128]{2,1,0:T(8,128)}, u32[]{:S(2)}) copy-start(f32[4,8,128]{2,1,0:T(8,128)} %param.8) | copy-start | bytes 49156
  23.0 1.3 %copy-start.10 = (f32[4,8,128]{2,1,0:T(8,128)S(1)}, f32[4,8,128]{2,1,0:T(8,128)}, u32[]{:S(2)}) copy-start(f32[4,8,128]{2,1,0:T(8,128)} %param.9) | copy-start | bytes 49156
  23.4 18.9 %copy-start.27 = (s32[2]{0:T(128)}, s32[2]{0:T(128)S(1)}, u32[]{:S(2)}) copy-start(s32[2]{0:T(128)S(1)} %pad_add_fusion.1.even_ref.refs_0_) | copy-start | bytes 28
  30.1 14.1 %collective-permute-start.4 = (f32[100,128]{1,0:T(8,128)S(1)}, f32[100,128]{1,0:T(8,128)S(1)}, u32[]{:S(2)}, u32[]{:S(2)}) collective-permute-start(f32[100,128]{1,0:T(8,128)S(1)} %get-tuple-element.30.refs_8_), channel_id=1, source_target_pairs={{0,1},{1,0},{2,3},{3,2},{4,5},{5,4},{6,7},{7,6},{8,9},{9,8},{10,11... | collective-permute-start | bytes 153608 | tf_op jit(solution)/shard_map/ppermute | solution.py:29
  31.5 13.3 %collective-permute-start.5 = (f32[100,128]{1,0:T(8,128)S(1)}, f32[100,128]{1,0:T(8,128)S(1)}, u32[]{:S(2)}, u32[]{:S(2)}) collective-permute-start(f32[100,128]{1,0:T(8,128)S(1)} %get-tuple-element.31.refs_9_), channel_id=1, source_target_pairs={{0,7},{1,2},{2,1},{3,4},{4,3},{5,6},{6,5},{7,0},{8,15},{9,10},{10,... | collective-permute-start | bytes 153608 | tf_op jit(solution)/shard_map/ppermute | solution.py:35
  35.0 10.4 %collective-permute-start.2 = (f32[200,128]{1,0:T(8,128)S(1)}, f32[200,128]{1,0:T(8,128)S(1)}, u32[]{:S(2)}, u32[]{:S(2)}) collective-permute-start(f32[200,128]{1,0:T(8,128)S(1)} %get-tuple-element.28.refs_6_), channel_id=1, source_target_pairs={{0,8},{8,0},{16,24},{24,16},{32,40},{40,32},{48,56},{56,48},{64,72... | collective-permute-start | bytes 307208 | tf_op jit(solution)/shard_map/ppermute | solution.py:29
  35.6 10.4 %collective-permute-start.3 = (f32[200,128]{1,0:T(8,128)S(1)}, f32[200,128]{1,0:T(8,128)S(1)}, u32[]{:S(2)}, u32[]{:S(2)}) collective-permute-start(f32[200,128]{1,0:T(8,128)S(1)} %get-tuple-element.29.refs_7_), channel_id=1, source_target_pairs={{0,120},{8,16},{16,8},{24,32},{32,24},{40,48},{48,40},{56,64},{64,... | collective-permute-start | bytes 307208 | tf_op jit(solution)/shard_map/ppermute | solution.py:35
  46.7 1.3 %copy-start.8 = (f32[2400,128]{1,0:T(8,128)S(1)}, f32[2400,128]{1,0:T(8,128)}, u32[]{:S(2)}) copy-start(f32[2400,128]{1,0:T(8,128)} %copy-done.7) | copy-start | bytes 3686404
  63.1 5.6 %collective-permute-start.8 = (f32[100,128]{1,0:T(8,128)}, f32[100,128]{1,0:T(8,128)S(1)}, u32[]{:S(2)}, u32[]{:S(2)}) collective-permute-start(f32[100,128]{1,0:T(8,128)} %get-tuple-element.38.sny), channel_id=1, source_target_pairs={{0,1},{1,0},{2,3},{3,2},{4,5},{5,4},{6,7},{7,6},{8,9},{9,8},{10,11... | collective-permute-start | bytes 153608 | tf_op jit(solution)/shard_map/ppermute | solution.py:29
  63.1 7.0 %collective-permute-start.9 = (f32[100,128]{1,0:T(8,128)}, f32[100,128]{1,0:T(8,128)}, u32[]{:S(2)}, u32[]{:S(2)}) collective-permute-start(f32[100,128]{1,0:T(8,128)} %get-tuple-element.39.sfy), channel_id=1, source_target_pairs={{0,7},{1,2},{2,1},{3,4},{4,3},{5,6},{6,5},{7,0},{8,15},{9,10},{10,... | collective-permute-start | bytes 153608 | tf_op jit(solution)/shard_map/ppermute | solution.py:35
  65.4 4.8 %collective-permute-start.6 = (f32[200,128]{1,0:T(8,128)S(1)}, f32[200,128]{1,0:T(8,128)S(1)}, u32[]{:S(2)}, u32[]{:S(2)}) collective-permute-start(f32[200,128]{1,0:T(8,128)S(1)} %get-tuple-element.36.snx), channel_id=1, source_target_pairs={{0,8},{8,0},{16,24},{24,16},{32,40},{40,32},{48,56},{56,48},{64,72... | collective-permute-start | bytes 307208 | tf_op jit(solution)/shard_map/ppermute | solution.py:29
  65.4 7.7 %collective-permute-start.7 = (f32[200,128]{1,0:T(8,128)S(1)}, f32[200,128]{1,0:T(8,128)S(1)}, u32[]{:S(2)}, u32[]{:S(2)}) collective-permute-start(f32[200,128]{1,0:T(8,128)S(1)} %get-tuple-element.37.sfx), channel_id=1, source_target_pairs={{0,120},{8,16},{16,8},{24,32},{32,24},{40,48},{48,40},{56,64},{64,... | collective-permute-start | bytes 307208 | tf_op jit(solution)/shard_map/ppermute | solution.py:35
  73.1 1.3 %copy-start.6 = (f32[2400,128]{1,0:T(8,128)S(1)}, f32[2400,128]{1,0:T(8,128)}, u32[]{:S(2)}) copy-start(f32[2400,128]{1,0:T(8,128)} %copy-done.5) | copy-start | bytes 3686404
  84.6 9.5 %all-to-all-start.1 = ((f32[8,8,128]{2,1,0:T(8,128)}), f32[8,8,128]{2,1,0:T(8,128)S(1)}, u32[]{:S(2)}, u32[]{:S(2)}) async-start(f32[8,8,128]{2,1,0:T(8,128)} %broadcast_in_dim.22), calls=%async_computation.1 | async-start | bytes 65536 | tf_op jit(solution)/shard_map/all_to_all | solution.py:384
  96.0 15.4 %all-to-all-start.2 = ((f32[16,40,128]{2,1,0:T(8,128)}), f32[16,40,128]{2,1,0:T(8,128)S(1)}, u32[]{:S(2)}, u32[]{:S(2)}) async-start(f32[16,40,128]{2,1,0:T(8,128)} %bitcast.15), calls=%async_computation.2 | async-start | bytes 655360 | tf_op jit(solution)/shard_map/all_to_all | solution.py:397
  99.6 11.9 %collective-permute-start.10 = (f32[200,128]{1,0:T(8,128)}, f32[200,128]{1,0:T(8,128)S(1)}, u32[]{:S(2)}, u32[]{:S(2)}) collective-permute-start(f32[200,128]{1,0:T(8,128)} %copy-done.32), channel_id=1, source_target_pairs={{0,8},{8,16},{16,24},{24,32},{32,40},{40,48},{48,56},{56,64},{64,7... | collective-permute-start | bytes 307208 | tf_op jit(solution)/shard_map/ppermute | solution.py:24
  99.9 7.2 %collective-permute-start.11 = (f32[100,128]{1,0:T(8,128)}, f32[100,128]{1,0:T(8,128)S(1)}, u32[]{:S(2)}, u32[]{:S(2)}) collective-permute-start(f32[100,128]{1,0:T(8,128)} %copy-done.33), channel_id=1, source_target_pairs={{0,1},{1,2},{2,3},{3,4},{4,5},{5,6},{6,7},{7,0},{8,9},{9,10},{10,1... | collective-permute-start | bytes 153608 | tf_op jit(solution)/shard_map/ppermute | solution.py:24
  111.5 1.3 %copy-start.2 = (f32[2400,128]{1,0:T(8,128)S(1)}, f32[2400,128]{1,0:T(8,128)}, u32[]{:S(2)}) copy-start(f32[2400,128]{1,0:T(8,128)} %copy-done.1) | copy-start | bytes 3686404
  112.8 1.3 %copy-start.4 = (f32[2400,128]{1,0:T(8,128)S(1)}, f32[2400,128]{1,0:T(8,128)}, u32[]{:S(2)}) copy-start(f32[2400,128]{1,0:T(8,128)} %copy-done.3) | copy-start | bytes 3686404
  (26 other events, 19.8 us)

commit v2 on v1

--- a/solution.py
+++ b/solution.py
@@ -17,6 +17,7 @@
 f32, bf16 = jnp.float32, jnp.bfloat16
 VM = pl.BlockSpec(memory_space=pltpu.VMEM)
 SM = pl.BlockSpec(memory_space=pltpu.SMEM)
+ANY = pl.BlockSpec(memory_space=pl.ANY)
 
 
 def shifted(value, axis, by):
@@ -96,6 +97,10 @@
         carry = [parts[y][1] for y in range(LY)]
 
 
+def is_even(axis):
+    return lax.rem(lax.axis_index(axis), 2) == 0
+
+
 def route(even, up, low, near, far):
     near[...] = jnp.where(even, up[...], low[...])
     far[...] = jnp.where(even, low[...], up[...])
@@ -104,10 +109,38 @@
 def mean_eigenvalue(st_ref, traces_ref, total):
     st = st_ref[...].reshape(-1, 2, LZ)
     sums = jnp.sum(jnp.sum(st, 0), axis=1, keepdims=True)
-    return (sums[0:1] * traces_ref[0] + sums[1:2] * traces_ref[1]) * (1.0 / (75.0 * total))
-
-
-def first_kernel(even_ref, rhs_ref, hx_ref, hy_ref, k_ref, m_ref, wh_ref, wl_ref,
+    return (sums[0:1] * traces_ref[0:1, 0:1] + sums[1:2] * traces_ref[1:2, 0:1]) * (1.0 / (75.0 * total))
+
+
+def edge_kernel(rhs_ref, k_ref, m_ref, fx_ref, fy_ref, st_ref, sem_x, sem_y, *, devices):
+    face_x = pltpu.make_async_copy(rhs_ref.at[0, :, 0], fx_ref, sem_x)
+    face_y = pltpu.make_async_copy(rhs_ref.at[1, :, :, 0], fy_ref, sem_y)
+    face_x.start()
+    face_y.start()
+    both = jnp.concatenate([jnp.sum(k_ref[...], 0, keepdims=True), jnp.sum(m_ref[...], 0, keepdims=True)], 0)
+    st_ref[...] = jnp.broadcast_to(both[None], (devices, 2, LZ))
+    face_x.wait()
+    face_y.wait()
+
+
+def weight_kernel(s_ref, m_ref, wh_ref, wl_ref, traces_ref):
+    n, padded = 6 * A, 6 * AP
+    r = lax.broadcasted_iota(jnp.int32, (padded, n), 0)
+    c = lax.broadcasted_iota(jnp.int32, (padded, n), 1)
+    node = lax.rem(r, AP)
+    place = jnp.where((node < A) & (lax.div(r, AP) * A + node == c), 1.0, 0.0).astype(bf16)
+    diagonal = lax.broadcasted_iota(jnp.int32, (n, n), 0) == lax.broadcasted_iota(jnp.int32, (n, n), 1)
+    for i, ref in enumerate((s_ref, m_ref)):
+        v = ref[...]
+        for part, out in zip(halves(v), (wh_ref, wl_ref)):
+            rows = jnp.dot(place, part, preferred_element_type=f32).astype(bf16)
+            full = lax.dot_general(rows, place, (((1,), (1,)), ((), ())), preferred_element_type=f32)
+            out[i * padded : (i + 1) * padded] = full.astype(bf16)
+        trace = jnp.sum(jnp.sum(jnp.where(diagonal, v, 0.0), 0, keepdims=True), 1, keepdims=True)
+        traces_ref[i : i + 1] = jnp.broadcast_to(trace, (1, LZ))
+
+
+def first_kernel(rhs_ref, hx_ref, hy_ref, k_ref, m_ref, wh_ref, wl_ref,
                  p_ref, snx, sfx, sny, sfy, v, ux, uy, upx, lowx, upy, lowy):
     v[:ROWS] = rhs_ref[...]
     v[ROWS:] = jnp.zeros((PADDED - ROWS, LZ), f32)
@@ -116,13 +149,13 @@
     uy[: A * LX] = hy_ref[...]
     uy[A * LX :] = jnp.zeros(((AP - A) * LX, LZ), f32)
     apply_operator(v, ux, uy, k_ref, m_ref, 1.0, wh_ref, wl_ref, p_ref, upx, lowx, upy, lowy)
-    route(even_ref[0] == 0, upx, lowx, snx, sfx)
-    route(even_ref[1] == 0, upy, lowy, sny, sfy)
-
-
-def next_vector(even_ref, p_ref, prev_ref, hx_ref, hy_ref, snx, sfx, sny, sfy, rnx, rfx, rny, rfy, scale, v, ux, uy):
-    even_x = even_ref[0] == 0
-    even_y = even_ref[1] == 0
+    route(is_even("gx"), upx, lowx, snx, sfx)
+    route(is_even("gy"), upy, lowy, sny, sfy)
+
+
+def next_vector(p_ref, prev_ref, hx_ref, hy_ref, snx, sfx, sny, sfy, rnx, rfx, rny, rfy, scale, v, ux, uy):
+    even_x = is_even("gx")
+    even_y = is_even("gy")
     v[:ROWS] = p_ref[...] * scale - prev_ref[...]
     v[ROWS:] = jnp.zeros((PADDED - ROWS, LZ), f32)
     below_x = jnp.where(even_x, rfx[...], rnx[...]) * scale
@@ -144,13 +177,13 @@
     return jnp.sum(value.reshape(-1, LY, LZ), 0)
 
 
-def second_kernel(even_ref, traces_ref, p_ref, rhs_ref, hx_ref, hy_ref, snx, sfx, sny, sfy, rnx, rfx, rny, rfy,
-                  st_ref, k_ref, m_ref, wh_ref, wl_ref,
+def second_kernel(p_ref, rhs_ref, hx_ref, hy_ref, snx, sfx, sny, sfy, rnx, rfx, rny, rfy,
+                  st_ref, traces_ref, k_ref, m_ref, wh_ref, wl_ref,
                   v1_ref, ux1_ref, uy1_ref, p1_ref, tnx, tfx, tny, tfy, sums_ref, inv_ref,
                   v, ux, uy, upx, lowx, upy, lowy, *, total):
     inv = 1.0 / mean_eigenvalue(st_ref, traces_ref, total)
     inv_ref[...] = jnp.broadcast_to(inv, (8, LZ))
-    next_vector(even_ref, p_ref, rhs_ref, hx_ref, hy_ref, snx, sfx, sny, sfy, rnx, rfx, rny, rfy, inv, v, ux, uy)
+    next_vector(p_ref, rhs_ref, hx_ref, hy_ref, snx, sfx, sny, sfy, rnx, rfx, rny, rfy, inv, v, ux, uy)
     v0 = rhs_ref[...]
     v1 = v[:ROWS]
     v1_ref[...] = v1
@@ -162,15 +195,15 @@
     sums_ref[24:32] = node_sum(v0 * v1)
     sums_ref[32:40] = node_sum(v1 * v1)
     apply_operator(v, ux, uy, k_ref, m_ref, inv, wh_ref, wl_ref, p1_ref, upx, lowx, upy, lowy)
-    route(even_ref[0] == 0, upx, lowx, tnx, tfx)
-    route(even_ref[1] == 0, upy, lowy, tny, tfy)
-
-
-def third_kernel(even_ref, p_ref, prev_ref, hx_ref, hy_ref, snx, sfx, sny, sfy, rnx, rfx, rny, rfy,
+    route(is_even("gx"), upx, lowx, tnx, tfx)
+    route(is_even("gy"), upy, lowy, tny, tfy)
+
+
+def third_kernel(p_ref, prev_ref, hx_ref, hy_ref, snx, sfx, sny, sfy, rnx, rfx, rny, rfy,
                  inv_ref, sums1_ref, k_ref, m_ref, wh_ref, wl_ref,
                  v2_ref, p2_ref, upx, upy, loads_ref, mom_ref, v, ux, uy):
     one = jnp.float32(1.0)
-    next_vector(even_ref, p_ref, prev_ref, hx_ref, hy_ref, snx, sfx, sny, sfy, rnx, rfx, rny, rfy, one, v, ux, uy)
+    next_vector(p_ref, prev_ref, hx_ref, hy_ref, snx, sfx, sny, sfy, rnx, rfx, rny, rfy, one, v, ux, uy)
     v1 = prev_ref[...]
     v2 = v[:ROWS]
     v2_ref[...] = v2
@@ -181,41 +214,30 @@
     apply_operator(v, ux, uy, k_ref, m_ref, inv_ref[0:1], wh_ref, wl_ref, p2_ref, upx, None, upy, None)
     p2 = p2_ref[...]
     loads_ref[24:32] = node_sum(p2)
-    loads_ref[32:40] = node_sum(upx[...])
     energy = node_sum(v[:ROWS] * p2) + node_sum(ux[: A * LY] * upx[...])
     tail = jnp.sum(uy[: A * LX] * upy[...], 0, keepdims=True)
 
     def row(tile):
         return jnp.sum(tile, 0, keepdims=True)
 
-    mom_ref[0:1] = row(sums1_ref[16:24])
-    mom_ref[1:2] = row(sums1_ref[24:32])
-    mom_ref[2:3] = row(sums1_ref[32:40])
-    mom_ref[3:4] = row(m3)
-    mom_ref[4:5] = row(m4)
-    mom_ref[5:6] = row(energy) + tail
-    mom_ref[6:7] = jnp.sum(upy[...], 0, keepdims=True)
-    mom_ref[7:8] = jnp.zeros((1, LZ), f32)
-
-
-def middle_kernel(me_ref, g_ref, mom_ref, loads_ref, out_ref, *, nx, ny):
-    below = lax.rem(me_ref[1] + ny - 1, ny)
-    tiles = mom_ref[...].reshape(ny, 8, LZ)
-    total = jnp.sum(tiles, 0)
-    edge = mom_ref[pl.ds(below * 8 + 6, 1), :]
-    image = loads_ref[24:32]
-    at_first = lax.broadcasted_iota(jnp.int32, (8, LZ), 0) == 0
-    image = image + jnp.where(at_first, jnp.broadcast_to(edge, (8, LZ)), 0.0)
+    tile = [row(sums1_ref[16 + 8 * k : 24 + 8 * k]) for k in range(3)]
+    tile += [row(m3), row(m4), row(energy) + tail, jnp.zeros((2, LZ), f32)]
+    mom_ref[...] = jnp.broadcast_to(jnp.concatenate(tile, 0)[None], mom_ref.shape)
+
+
+def middle_kernel(mom_ref, loads_ref, rx_ref, ry_ref, out_ref, *, table):
+    nx = len(table)
+    me = lax.axis_index("gx")
+    total = jnp.sum(mom_ref[...], 0)
+    edge = jnp.broadcast_to(jnp.sum(ry_ref[...], 0, keepdims=True), (LY, LZ))
+    at_first = lax.broadcasted_iota(jnp.int32, (LY, LZ), 0) == 0
+    image = loads_ref[24:32] + node_sum(rx_ref[...]) + jnp.where(at_first, edge, 0.0)
     own = [loads_ref[0:8], loads_ref[8:16], loads_ref[16:24], image]
-    above = loads_ref[32:40]
-    for to in range(nx):
-        g = g_ref[to]
+    for offset, weight in enumerate(table):
+        to = lax.rem(me + offset, nx)
         for k in range(4):
-            piece = own[k] * g
-            if k == 3:
-                piece = piece + above * g_ref[nx + to]
-            out_ref[to * 40 + k * 8 : to * 40 + (k + 1) * 8] = piece
-        out_ref[to * 40 + 32 : to * 40 + 40] = total
+            out_ref[to, k] = own[k] * weight
+        out_ref[to, 4] = total
 
 
 def conjugate_gradient(m):
@@ -257,8 +279,8 @@
 
 
 def last_kernel(prolong_ref, got_ref, inv_ref, rhs_ref, v1_ref, v2_ref, p2_ref, rx_ref, ry_ref,
-                sol_ref, res_ref, coarse_ref, *, nx):
-    got = jnp.sum(got_ref[...].reshape(nx, 5, 8, LZ), 0)
+                sol_ref, res_ref, coarse_ref):
+    got = jnp.sum(got_ref[...], 0)
     sums = jnp.sum(got[4], axis=1, keepdims=True)
     m = [sums[k : k + 1] for k in range(6)]
     m[5] = m[5] - m[4]
@@ -297,39 +319,12 @@
     return jax.ShapeDtypeStruct(shape, f32)
 
 
-PARAMS = pltpu.CompilerParams(vmem_limit_bytes=40 * 1024 * 1024)
+PARAMS = pltpu.CompilerParams(vmem_limit_bytes=16 * 1024 * 1024)
 
 
 def shards(rhs, kappa, mass, stiffness, mass_matrix, prolong):
     nx, ny = lax.axis_size("gx"), lax.axis_size("gy")
-    me_x, me_y = lax.axis_index("gx"), lax.axis_index("gy")
-    both = ("gx", "gy")
     vx, vy = A * LY, A * LX
-
-    hx = shifted(rhs[0, :, 0].reshape(vx, LZ), "gx", -1)
-    hy = shifted(rhs[1, :, :, 0].reshape(vy, LZ), "gy", -1)
-
-    stats = jnp.stack([jnp.sum(kappa, (0, 1)), jnp.sum(mass, (0, 1))], 0)
-    stats = lax.all_to_all(jnp.broadcast_to(stats[None], (nx * ny, 2, LZ)), both, 0, 0, tiled=True)
-    stats = stats.reshape(nx * ny * 2, LZ)
-    traces = jnp.stack([jnp.trace(stiffness), jnp.trace(mass_matrix)])
-
-    def padded(matrix):
-        blocks = jnp.pad(matrix.reshape(6, A, 6, A), ((0, 0), (0, AP - A), (0, 0), (0, AP - A)))
-        return blocks.reshape(6 * AP, 6 * AP)
-
-    weights = jnp.concatenate([padded(stiffness), padded(mass_matrix)], 0)
-    wh = lax.reduce_precision(weights, 8, 7)
-    wl = (weights - wh).astype(bf16)
-    wh = wh.astype(bf16)
-
-    even = jnp.stack([me_x % 2, me_y % 2])
-    me = jnp.stack([me_x, me_y])
-    table = jacobi_weights(nx)
-    index = np.arange(nx)
-    rows = np.stack([np.concatenate([table[(index - p) % nx], table[(index - p - 1) % nx]]) for p in range(nx)])
-    g = lax.dynamic_index_in_dim(jnp.asarray(rows, f32), me_x, 0, keepdims=False)
-
     rhs2 = rhs.reshape(ROWS, LZ)
     k2 = kappa.reshape(CELLS, LZ)
     m2 = mass.reshape(CELLS, LZ)
@@ -337,6 +332,23 @@
     field = [pltpu.VMEM((PADDED, LZ), f32), pltpu.VMEM((AP * LY, LZ), f32), pltpu.VMEM((AP * LX, LZ), f32)]
     edges = [pltpu.VMEM((vx, LZ), f32)] * 2 + [pltpu.VMEM((vy, LZ), f32)] * 2
 
+    def call(kernel, name, ins, outs, scratch=(), **static):
+        specs = [i[1] if isinstance(i, tuple) else VM for i in ins]
+        ins = [i[0] if isinstance(i, tuple) else i for i in ins]
+
+        def bound(*refs):
+            kernel(*refs, **static)
+
+        return pl.pallas_call(
+            bound,
+            out_shape=outs,
+            in_specs=specs,
+            out_specs=[VM] * len(outs),
+            scratch_shapes=list(scratch),
+            compiler_params=PARAMS,
+            name=name,
+        )(*ins)
+
     def swap(s):
         far_x = far_swap(s[1], "gx")
         far_y = far_swap(s[3], "gy")
@@ -344,69 +356,42 @@
         near_x = near_swap(s[0], "gx")
         return [near_x, far_x, near_y, far_y]
 
-    p0, *s = pl.pallas_call(
-        first_kernel,
-        out_shape=[struct(ROWS, LZ)] + sends,
-        in_specs=[SM] + [VM] * 7,
-        out_specs=[VM] * 5,
-        scratch_shapes=field + edges,
-        compiler_params=PARAMS,
-        name="first",
-    )(even, rhs2, hx, hy, k2, m2, wh, wl)
+    fx, fy, stats = call(
+        edge_kernel, "edges", [(rhs, ANY), k2, m2], [struct(A, LY, LZ), struct(A, LX, LZ), struct(nx * ny, 2, LZ)],
+        [pltpu.SemaphoreType.DMA, pltpu.SemaphoreType.DMA], devices=nx * ny,
+    )
+    hx = shifted(fx.reshape(vx, LZ), "gx", -1)
+    hy = shifted(fy.reshape(vy, LZ), "gy", -1)
+    stats = lax.all_to_all(stats, ("gx", "gy"), 0, 0, tiled=True).reshape(nx * ny * 2, LZ)
+    half = jax.ShapeDtypeStruct((12 * AP, 6 * AP), bf16)
+    wh, wl, traces = call(weight_kernel, "weights", [stiffness, mass_matrix], [half, half, struct(8, LZ)])
+
+    p0, *s = call(
+        first_kernel, "first", [rhs2, hx, hy, k2, m2, wh, wl], [struct(ROWS, LZ)] + sends, field + edges,
+    )
     r = swap(s)
-
-    def second(*refs):
-        second_kernel(*refs, total=float(nx * ny * CELLS * LZ))
-
-    v1, ux1, uy1, p1, *rest = pl.pallas_call(
-        second,
-        out_shape=[struct(ROWS, LZ), struct(vx, LZ), struct(vy, LZ), struct(ROWS, LZ)] + sends + [struct(40, LZ), struct(8, LZ)],
-        in_specs=[SM, SM] + [VM] * 17,
-        out_specs=[VM] * 10,
-        scratch_shapes=field + edges,
-        compiler_params=PARAMS,
-        name="second",
-    )(even, traces, p0, rhs2, hx, hy, *s, *r, stats, k2, m2, wh, wl)
+    v1, ux1, uy1, p1, *rest = call(
+        second_kernel, "second", [p0, rhs2, hx, hy, *s, *r, stats, traces, k2, m2, wh, wl],
+        [struct(ROWS, LZ), struct(vx, LZ), struct(vy, LZ), struct(ROWS, LZ)] + sends + [struct(40, LZ), struct(8, LZ)],
+        field + edges, total=float(nx * ny * CELLS * LZ),
+    )
     s, (sums, inv) = rest[:4], rest[4:]
     r = swap(s)
-
-    v2, p2, upx, upy, loads, mom = pl.pallas_call(
-        third_kernel,
-        out_shape=[struct(ROWS, LZ), struct(ROWS, LZ), struct(vx, LZ), struct(vy, LZ), struct(40, LZ), struct(8, LZ)],
-        in_specs=[SM] + [VM] * 18,
-        out_specs=[VM] * 6,
-        scratch_shapes=field,
-        compiler_params=PARAMS,
-        name="third",
-    )(even, p1, v1, ux1, uy1, *s, *r, inv, sums, k2, m2, wh, wl)
+    v2, p2, upx, upy, loads, mom = call(
+        third_kernel, "third", [p1, v1, ux1, uy1, *s, *r, inv, sums, k2, m2, wh, wl],
+        [struct(ROWS, LZ), struct(ROWS, LZ), struct(vx, LZ), struct(vy, LZ), struct(32, LZ), struct(ny, 8, LZ)], field,
+    )
     rx = shifted(upx, "gx", 1)
     ry = shifted(upy, "gy", 1)
-    mom = lax.all_to_all(jnp.broadcast_to(mom[None], (ny, 8, LZ)), "gy", 0, 0, tiled=True)
-
-    def middle(*refs):
-        middle_kernel(*refs, nx=nx, ny=ny)
-
-    pieces = pl.pallas_call(
-        middle,
-        out_shape=struct(nx * 40, LZ),
-        in_specs=[SM, SM, VM, VM],
-        out_specs=VM,
-        compiler_params=PARAMS,
-        name="middle",
-    )(me, g, mom.reshape(ny * 8, LZ), loads)
-    got = lax.all_to_all(pieces.reshape(nx, 40, LZ), "gx", 0, 0, tiled=True)
-
-    def last(*refs):
-        last_kernel(*refs, nx=nx)
-
-    sol, res, coarse = pl.pallas_call(
-        last,
-        out_shape=[struct(ROWS, LZ), struct(ROWS, LZ), struct(LY, LZ)],
-        in_specs=[SM] + [VM] * 8,
-        out_specs=[VM] * 3,
-        compiler_params=PARAMS,
-        name="last",
-    )(prolong.reshape(-1), got.reshape(nx * 40, LZ), inv, rhs2, v1, v2, p2, rx, ry)
+    mom = lax.all_to_all(mom, "gy", 0, 0, tiled=True)
+    pieces, = call(
+        middle_kernel, "middle", [mom, loads, rx, ry], [struct(nx, 5, 8, LZ)], table=[float(t) for t in jacobi_weights(nx)],
+    )
+    got = lax.all_to_all(pieces, "gx", 0, 0, tiled=True)
+    sol, res, coarse = call(
+        last_kernel, "last", [(prolong.reshape(-1), SM), got, inv, rhs2, v1, v2, p2, rx, ry],
+        [struct(ROWS, LZ), struct(ROWS, LZ), struct(LY, LZ)],
+    )
     return sol.reshape(rhs.shape), res.reshape(rhs.shape), coarse[None]
 
 

time: 118 us -> 97.8 us (0.83)
  local copies, waits for them, and re-layouts: 32.5 us -> 15.6 us
  blocking collectives: 0 us -> 11.1 us
  other arithmetic: 6.32 us -> 0 us
  waiting for transfers between devices: 20 us -> 15.9 us
  starting transfers between devices: 36.6 us -> 34.8 us
  Pallas kernels: 20.2 us -> 18.6 us
    all_to_all x0 -> x1, blocking collectives: none -> 11.1 us  [shards(): mom = lax.all_to_all(mom, 'gy', 0, 0, tiled=True)]
    unnamed x71 -> x46, local copies, waits for them, and re-layouts: 25.8 us -> 15.5 us
    ppermute x4, waiting for transfers between devices: 10.2 us -> 0.01 us  [shifted(): return lax.ppermute(value, axis, [(i, (i + by) % n) for i in range(n)])]
    all_to_all x3 -> x2, waiting for transfers between devices: 5.49 us -> 10.2 us  [the longest x1 10.2 us: shards(): got = lax.all_to_all(pieces, 'gx', 0, 0, tiled=True)]
    reduce_sum x4 -> x0, other arithmetic: 3.72 us -> none  [the longest x2 2.25 us: shards(): traces = jnp.stack([jnp.trace(stiffness), jnp.trace(mass_matrix)])]
    another operation x4 -> x0, other arithmetic: 2.54 us -> none  [the longest x1 1.85 us: shards(): traces = jnp.stack([jnp.trace(stiffness), jnp.trace(mass_matrix)])]
    ppermute x4, waiting for transfers between devices: 0.01 us -> 1.75 us  [near_swap(): return lax.ppermute(value, axis, [(i, i ^ 1) for i in range(n)])]
    reshape x4 -> x1, local copies, waits for them, and re-layouts: 1.68 us -> 0.02 us  [shards(): hy = shifted(fy.reshape(vy, LZ), 'gy', -1)]
  transfers between devices with their start and end apart: 15 -> 14, of which waited for: 5 -> 4; matrix products, arithmetic and copies ran while one was open for 10% -> 0% of each run, Pallas kernels for 4% -> 5%
where the time goes in v2:
time: 97.8 us; the launch traced here: 96.8 us
  starting transfers between devices  34.8 us (36%)
  Pallas kernels  18.6 us (19%)
  waiting for transfers between devices  15.9 us (16%)
  local copies, waits for them, and re-layouts  15.6 us (16%)
  blocking collectives  11.1 us (11%)
    pallas_call x7, Pallas kernels, call(): pl.pallas_call(bound, out_shape=outs, in_specs=specs, out_specs=[VM] * le...  18.6 us
    unnamed x46, local copies, waits for them, and re-layouts  15.5 us
    ppermute x4, starting transfers between devices, far_swap(): return lax.ppermute(value, axis, pairs)  14.2 us
    all_to_all x1, blocking collectives, shards(): mom = lax.all_to_all(mom, 'gy', 0, 0, tiled=True)  11.1 us
    all_to_all x1, waiting for transfers between devices, shards(): got = lax.all_to_all(pieces, 'gx', 0, 0, tiled=True)  10.2 us
    ppermute x4, starting transfers between devices, shifted(): return lax.ppermute(value, axis, [(i, (i + by) % n) for i in range(n)])  9.56 us
    all_to_all x1, starting transfers between devices, shards(): got = lax.all_to_all(pieces, 'gx', 0, 0, tiled=True)  5.73 us
    all_to_all x1, starting transfers between devices, shards(): lax.all_to_all(stats, ('gx', 'gy'), 0, 0, tiled=True)  4.61 us
  transfers between devices with their start and end apart: 14, of which 4 were waited for; matrix products, arithmetic and copies ran while one was open for 0% of the time, Pallas kernels for 5%

profile of v2, /device:TPU:0, one launch (start us, length us, event | category | flops | bytes accessed | tf_op | source)
XLA Modules:
  0.0 96.8 jit_solution(14579847012861450509)
XLA Ops:
  0.6 1.3 %copy-done = f32[3,25,4,8,128]{4,3,2,1,0:T(8,128)S(1)} copy-done((f32[3,25,4,8,128]{4,3,2,1,0:T(8,128)S(1)}, f32[3,25,4,8,128]{4,3,2,1,0:T(8,128)}, u32[]{:S(2)}) %copy-start) | copy-done | bytes 1228824
  4.2 6.1 %collective-permute-start = (f32[200,128]{1,0:T(8,128)S(1)}, f32[200,128]{1,0:T(8,128)S(1)}, u32[]{:S(2)}, u32[]{:S(2)}) collective-permute-start(f32[200,128]{1,0:T(8,128)S(1)} %bitcast.20), channel_id=1, source_target_pairs={{0,120},{8,0},{16,8},{24,16},{32,24},{40,32},{48,40},{56,48},{64,5... | collective-permute-start | bytes 307208 | tf_op jit(solution)/shard_map/ppermute | solution.py:25
  10.3 3.1 %collective-permute-start.1 = (f32[100,128]{1,0:T(8,128)S(1)}, f32[100,128]{1,0:T(8,128)S(1)}, u32[]{:S(2)}, u32[]{:S(2)}) collective-permute-start(f32[100,128]{1,0:T(8,128)S(1)} %reshape.38), channel_id=1, source_target_pairs={{0,7},{1,0},{2,1},{3,2},{4,3},{5,4},{6,5},{7,6},{8,15},{9,8},{10,9... | collective-permute-start | bytes 153608 | tf_op jit(solution)/shard_map/ppermute | solution.py:25
  13.4 4.6 %all-to-all-start = ((f32[128,2,128]{2,1,0:T(2,128)}), f32[128,2,128]{2,1,0:T(2,128)S(1)}, u32[]{:S(2)}, u32[]{:S(2)}) async-start(f32[128,2,128]{2,1,0:T(2,128)} %get-tuple-element.42), calls=%async_computation | async-start | bytes 262144 | tf_op jit(solution)/shard_map/all_to_all | solution.py:365
  18.5 4.2 %first.1 = (f32[2400,128]{1,0:T(8,128)S(1)}, f32[200,128]{1,0:T(8,128)S(1)}, f32[200,128]{1,0:T(8,128)S(1)}, f32[100,128]{1,0:T(8,128)S(1)}, f32[100,128]{1,0:T(8,128)S(1)}) custom-call(f32[2400,128]{1,0:T(8,128)S(1)} %bitcast.8, f32[200,128]{1,0:T(8,128)S(1)} %collective-permute-done.refs_1_.refs_2_, f32[100,128]{1,0:T(8,128)S(1)} %collective-permute-done.1.refs_2_.refs_3_, ...), custom_call_target="tpu_custom_call" | custom-call | tf_op jit(solution)/shard_map/first/pallas_call | solution.py:342
  22.7 1.0 %copy-done.2 = f32[2400,128]{1,0:T(8,128)} copy-done((f32[2400,128]{1,0:T(8,128)}, f32[2400,128]{1,0:T(8,128)S(1)}, u32[]{:S(2)}) %copy-start.2) | copy-done | bytes 1228824
  23.8 5.4 %collective-permute-start.3 = (f32[200,128]{1,0:T(8,128)S(1)}, f32[200,128]{1,0:T(8,128)S(1)}, u32[]{:S(2)}, u32[]{:S(2)}) collective-permute-start(f32[200,128]{1,0:T(8,128)S(1)} %get-tuple-element.39.refs_5_), channel_id=1, source_target_pairs={{0,120},{8,16},{16,8},{24,32},{32,24},{40,48},{48,40},{56,64},{64,... | collective-permute-start | bytes 307208 | tf_op jit(solution)/shard_map/ppermute | solution.py:36
  29.7 3.8 %collective-permute-start.5 = (f32[100,128]{1,0:T(8,128)S(1)}, f32[100,128]{1,0:T(8,128)S(1)}, u32[]{:S(2)}, u32[]{:S(2)}) collective-permute-start(f32[100,128]{1,0:T(8,128)S(1)} %get-tuple-element.41.refs_7_), channel_id=1, source_target_pairs={{0,7},{1,2},{2,1},{3,4},{4,3},{5,6},{6,5},{7,0},{8,15},{9,10},{10,... | collective-permute-start | bytes 153608 | tf_op jit(solution)/shard_map/ppermute | solution.py:36
  34.7 1.4 %collective-permute-done.5.refs_11_ = f32[100,128]{1,0:T(8,128)S(1)} collective-permute-done((f32[100,128]{1,0:T(8,128)S(1)}, f32[100,128]{1,0:T(8,128)S(1)}, u32[]{:S(2)}, u32[]{:S(2)}) %collective-permute-start.5) | collective-permute-done | bytes 51232 | tf_op jit(solution)/shard_map/ppermute | solution.py:36
  37.4 1.3 %copy-done.3 = f32[2400,128]{1,0:T(8,128)S(1)} copy-done((f32[2400,128]{1,0:T(8,128)S(1)}, f32[2400,128]{1,0:T(8,128)}, u32[]{:S(2)}) %copy-start.3) | copy-done | bytes 1228824
  42.0 4.9 %second.1 = (f32[2400,128]{1,0:T(8,128)S(1)}, f32[200,128]{1,0:T(8,128)S(1)}, f32[100,128]{1,0:T(8,128)S(1)}, f32[2400,128]{1,0:T(8,128)S(1)}, f32[200,128]{1,0:...) custom-call(f32[2400,128]{1,0:T(8,128)S(1)} %copy-done.3, ...), custom_call_target="tpu_custom_call" | custom-call | tf_op jit(solution)/shard_map/second/pallas_call | solution.py:342
  47.1 2.7 %collective-permute-start.7 = (f32[200,128]{1,0:T(8,128)S(1)}, f32[200,128]{1,0:T(8,128)S(1)}, u32[]{:S(2)}, u32[]{:S(2)}) collective-permute-start(f32[200,128]{1,0:T(8,128)S(1)} %get-tuple-element.49.refs_5_), channel_id=1, source_target_pairs={{0,120},{8,16},{16,8},{24,32},{32,24},{40,48},{48,40},{56,64},{64,... | collective-permute-start | bytes 307208 | tf_op jit(solution)/shard_map/ppermute | solution.py:36
  49.7 2.4 %collective-permute-start.9 = (f32[100,128]{1,0:T(8,128)S(1)}, f32[100,128]{1,0:T(8,128)S(1)}, u32[]{:S(2)}, u32[]{:S(2)}) collective-permute-start(f32[100,128]{1,0:T(8,128)S(1)} %get-tuple-element.51.refs_7_), channel_id=1, source_target_pairs={{0,7},{1,2},{2,1},{3,4},{4,3},{5,6},{6,5},{7,0},{8,15},{9,10},{10,... | collective-permute-start | bytes 153608 | tf_op jit(solution)/shard_map/ppermute | solution.py:36
  52.1 1.7 %collective-permute-done.8.refs_10_ = f32[100,128]{1,0:T(8,128)S(1)} collective-permute-done((f32[100,128]{1,0:T(8,128)S(1)}, f32[100,128]{1,0:T(8,128)S(1)}, u32[]{:S(2)}, u32[]{:S(2)}) %collective-permute-start.8) | collective-permute-done | bytes 51232 | tf_op jit(solution)/shard_map/ppermute | solution.py:30
  53.9 2.6 %collective-permute-done.9.refs_11_ = f32[100,128]{1,0:T(8,128)S(1)} collective-permute-done((f32[100,128]{1,0:T(8,128)S(1)}, f32[100,128]{1,0:T(8,128)S(1)}, u32[]{:S(2)}, u32[]{:S(2)}) %collective-permute-start.9) | collective-permute-done | bytes 51232 | tf_op jit(solution)/shard_map/ppermute | solution.py:36
  56.5 4.7 %third.1 = (f32[2400,128]{1,0:T(8,128)S(1)}, f32[2400,128]{1,0:T(8,128)S(1)}, f32[200,128]{1,0:T(8,128)S(1)}, f32[100,128]{1,0:T(8,128)S(1)}, f32[32,128]{1,0:T(8,128)S(1)}, /*index=5*/f32[8,8,128]{2,1,0:T(8,128)S(1)}) custom-call(f32[2400,128]{1,0:T(8,128)S(1)} %get-tuple-element.44.refs_0_, f32[2400,128]{1,0:T(8,128)S(1)} %get-tuple-element.45.refs_1_.refs_4_, ...), custom_call_target="tpu_custom_call" | custom-call | tf_op jit(solution)/shard_map/third/pallas_call | solution.py:342
  61.2 1.0 %copy-done.4 = f32[2400,128]{1,0:T(8,128)} copy-done((f32[2400,128]{1,0:T(8,128)}, f32[2400,128]{1,0:T(8,128)S(1)}, u32[]{:S(2)}) %copy-start.4) | copy-done | bytes 1228824
  62.2 1.0 %copy-done.6 = f32[2400,128]{1,0:T(8,128)} copy-done((f32[2400,128]{1,0:T(8,128)}, f32[2400,128]{1,0:T(8,128)S(1)}, u32[]{:S(2)}) %copy-start.6) | copy-done | bytes 1228824
  63.6 11.1 %all_to_all.15.refs_0_ = f32[8,8,128]{2,1,0:T(8,128)S(1)} all-to-all(f32[8,8,128]{2,1,0:T(8,128)S(1)} %get-tuple-element.54), channel_id=1, replica_groups=mesh['gx'=16,'gy'=8] {'gy'}, dimensions={0} | all-to-all | bytes 65536 | tf_op jit(solution)/shard_map/all_to_all | solution.py:386
  75.5 5.7 %all-to-all-start.2 = ((f32[16,5,8,128]{3,2,1,0:T(8,128)}), f32[16,5,8,128]{3,2,1,0:T(8,128)S(1)}, u32[]{:S(2)}, u32[]{:S(2)}) async-start(f32[16,5,8,128]{3,2,1,0:T(8,128)} %middle.1), calls=%async_computation.2 | async-start | bytes 655360 | tf_op jit(solution)/shard_map/all_to_all | solution.py:390
  81.3 10.2 %all-to-all-done.2.refs_1_ = f32[16,5,8,128]{3,2,1,0:T(8,128)S(1)} async-done(((f32[16,5,8,128]{3,2,1,0:T(8,128)}), f32[16,5,8,128]{3,2,1,0:T(8,128)S(1)}, u32[]{:S(2)}, u32[]{:S(2)}) %all-to-all-start.2) | async-done | bytes 327712 | tf_op jit(solution)/shard_map/all_to_all | solution.py:390
  91.5 1.3 %copy-done.5 = f32[2400,128]{1,0:T(8,128)S(1)} copy-done((f32[2400,128]{1,0:T(8,128)S(1)}, f32[2400,128]{1,0:T(8,128)}, u32[]{:S(2)}) %copy-start.5) | copy-done | bytes 1228824
  92.8 1.3 %copy-done.7 = f32[2400,128]{1,0:T(8,128)S(1)} copy-done((f32[2400,128]{1,0:T(8,128)S(1)}, f32[2400,128]{1,0:T(8,128)}, u32[]{:S(2)}) %copy-start.7) | copy-done | bytes 1228824
  94.1 2.7 %last.1 = (f32[2400,128]{1,0:T(8,128)}, f32[2400,128]{1,0:T(8,128)}, f32[8,128]{1,0:T(8,128)}) custom-call(f32[75]{0:T(128)S(1)} %reshape.33.refs_0_, f32[16,5,8,128]{3,2,1,0:T(8,128)S(1)} %all-to-all-done.2.refs_1_, f32[8,128]{1,0:T(8,128)S(1)} %get-tuple-element.52.refs_12_.refs_2_, f32[2400,128]{1,0:T(8,128)S(1)} %bitcast.10, ...), custom_call_target="tpu_custom_call" | custom-call | tf_op jit(solution)/shard_map/last/pallas_call | solution.py:342
  (60 shorter events, 10.5 us)
Async XLA Ops:
  0.6 1.3 %copy-start = (f32[3,25,4,8,128]{4,3,2,1,0:T(8,128)S(1)}, f32[3,25,4,8,128]{4,3,2,1,0:T(8,128)}, u32[]{:S(2)}) copy-start(f32[3,25,4,8,128]{4,3,2,1,0:T(8,128)} %refs_0_.2) | copy-start | bytes 3686404
  3.4 14.6 %copy-start.12 = (f32[150,150]{1,0:T(8,128)S(1)}, f32[150,150]{1,0:T(8,128)}, u32[]{:S(2)}) copy-start(f32[150,150]{1,0:T(8,128)} %refs_0_.3) | copy-start | bytes 270004
  3.4 14.7 %copy-start.13 = (f32[150,150]{1,0:T(8,128)S(1)}, f32[150,150]{1,0:T(8,128)}, u32[]{:S(2)}) copy-start(f32[150,150]{1,0:T(8,128)} %refs_1_.1) | copy-start | bytes 270004
  3.4 15.2 %copy-start.1 = (f32[3,25,4,8,128]{4,3,2,1,0:T(8,128)S(1)}, f32[3,25,4,8,128]{4,3,2,1,0:T(8,128)}, u32[]{:S(2)}) copy-start(f32[3,25,4,8,128]{4,3,2,1,0:T(8,128)} %refs_0_.2) | copy-start | bytes 3686404
  3.4 15.2 %copy-start.9 = (f32[4,8,128]{2,1,0:T(8,128)S(1)}, f32[4,8,128]{2,1,0:T(8,128)}, u32[]{:S(2)}) copy-start(f32[4,8,128]{2,1,0:T(8,128)} %param.7) | copy-start | bytes 49156
  3.4 15.2 %copy-start.11 = (f32[4,8,128]{2,1,0:T(8,128)S(1)}, f32[4,8,128]{2,1,0:T(8,128)}, u32[]{:S(2)}) copy-start(f32[4,8,128]{2,1,0:T(8,128)} %param.8) | copy-start | bytes 49156
  4.2 14.4 %collective-permute-start = (f32[200,128]{1,0:T(8,128)S(1)}, f32[200,128]{1,0:T(8,128)S(1)}, u32[]{:S(2)}, u32[]{:S(2)}) collective-permute-start(f32[200,128]{1,0:T(8,128)S(1)} %bitcast.20), channel_id=1, source_target_pairs={{0,120},{8,0},{16,8},{24,16},{32,24},{40,32},{48,40},{56,48},{64,5... | collective-permute-start | bytes 307208 | tf_op jit(solution)/shard_map/ppermute | solution.py:25
  10.3 8.2 %collective-permute-start.1 = (f32[100,128]{1,0:T(8,128)S(1)}, f32[100,128]{1,0:T(8,128)S(1)}, u32[]{:S(2)}, u32[]{:S(2)}) collective-permute-start(f32[100,128]{1,0:T(8,128)S(1)} %reshape.38), channel_id=1, source_target_pairs={{0,7},{1,0},{2,1},{3,2},{4,3},{5,4},{6,5},{7,6},{8,15},{9,8},{10,9... | collective-permute-start | bytes 153608 | tf_op jit(solution)/shard_map/ppermute | solution.py:25
  13.4 20.7 %all-to-all-start = ((f32[128,2,128]{2,1,0:T(2,128)}), f32[128,2,128]{2,1,0:T(2,128)S(1)}, u32[]{:S(2)}, u32[]{:S(2)}) async-start(f32[128,2,128]{2,1,0:T(2,128)} %get-tuple-element.42), calls=%async_computation | async-start | bytes 262144 | tf_op jit(solution)/shard_map/all_to_all | solution.py:365
  23.8 13.0 %collective-permute-start.2 = (f32[200,128]{1,0:T(8,128)S(1)}, f32[200,128]{1,0:T(8,128)S(1)}, u32[]{:S(2)}, u32[]{:S(2)}) collective-permute-start(f32[200,128]{1,0:T(8,128)S(1)} %get-tuple-element.38.refs_4_), channel_id=1, source_target_pairs={{0,8},{8,0},{16,24},{24,16},{32,40},{40,32},{48,56},{56,48},{64,72... | collective-permute-start | bytes 307208 | tf_op jit(solution)/shard_map/ppermute | solution.py:30
  23.8 13.0 %collective-permute-start.3 = (f32[200,128]{1,0:T(8,128)S(1)}, f32[200,128]{1,0:T(8,128)S(1)}, u32[]{:S(2)}, u32[]{:S(2)}) collective-permute-start(f32[200,128]{1,0:T(8,128)S(1)} %get-tuple-element.39.refs_5_), channel_id=1, source_target_pairs={{0,120},{8,16},{16,8},{24,32},{32,24},{40,48},{48,40},{56,64},{64,... | collective-permute-start | bytes 307208 | tf_op jit(solution)/shard_map/ppermute | solution.py:36
  29.1 5.0 %collective-permute-start.4 = (f32[100,128]{1,0:T(8,128)S(1)}, f32[100,128]{1,0:T(8,128)S(1)}, u32[]{:S(2)}, u32[]{:S(2)}) collective-permute-start(f32[100,128]{1,0:T(8,128)S(1)} %get-tuple-element.40.refs_6_), channel_id=1, source_target_pairs={{0,1},{1,0},{2,3},{3,2},{4,5},{5,4},{6,7},{7,6},{8,9},{9,8},{10,11... | collective-permute-start | bytes 153608 | tf_op jit(solution)/shard_map/ppermute | solution.py:30
  29.7 6.4 %collective-permute-start.5 = (f32[100,128]{1,0:T(8,128)S(1)}, f32[100,128]{1,0:T(8,128)S(1)}, u32[]{:S(2)}, u32[]{:S(2)}) collective-permute-start(f32[100,128]{1,0:T(8,128)S(1)} %get-tuple-element.41.refs_7_), channel_id=1, source_target_pairs={{0,7},{1,2},{2,1},{3,4},{4,3},{5,6},{6,5},{7,0},{8,15},{9,10},{10,... | collective-permute-start | bytes 153608 | tf_op jit(solution)/shard_map/ppermute | solution.py:36
  37.4 1.3 %copy-start.3 = (f32[2400,128]{1,0:T(8,128)S(1)}, f32[2400,128]{1,0:T(8,128)}, u32[]{:S(2)}) copy-start(f32[2400,128]{1,0:T(8,128)} %copy-done.2) | copy-start | bytes 3686404
  47.0 9.5 %collective-permute-start.6 = (f32[200,128]{1,0:T(8,128)S(1)}, f32[200,128]{1,0:T(8,128)S(1)}, u32[]{:S(2)}, u32[]{:S(2)}) collective-permute-start(f32[200,128]{1,0:T(8,128)S(1)} %get-tuple-element.48.refs_4_), channel_id=1, source_target_pairs={{0,8},{8,0},{16,24},{24,16},{32,40},{40,32},{48,56},{56,48},{64,72... | collective-permute-start | bytes 307208 | tf_op jit(solution)/shard_map/ppermute | solution.py:30
  47.1 9.4 %collective-permute-start.7 = (f32[200,128]{1,0:T(8,128)S(1)}, f32[200,128]{1,0:T(8,128)S(1)}, u32[]{:S(2)}, u32[]{:S(2)}) collective-permute-start(f32[200,128]{1,0:T(8,128)S(1)} %get-tuple-element.49.refs_5_), channel_id=1, source_target_pairs={{0,120},{8,16},{16,8},{24,32},{32,24},{40,48},{48,40},{56,64},{64,... | collective-permute-start | bytes 307208 | tf_op jit(solution)/shard_map/ppermute | solution.py:36
  49.7 4.1 %collective-permute-start.8 = (f32[100,128]{1,0:T(8,128)S(1)}, f32[100,128]{1,0:T(8,128)S(1)}, u32[]{:S(2)}, u32[]{:S(2)}) collective-permute-start(f32[100,128]{1,0:T(8,128)S(1)} %get-tuple-element.50.refs_6_), channel_id=1, source_target_pairs={{0,1},{1,0},{2,3},{3,2},{4,5},{5,4},{6,7},{7,6},{8,9},{9,8},{10,11... | collective-permute-start | bytes 153608 | tf_op jit(solution)/shard_map/ppermute | solution.py:30
  49.7 6.7 %collective-permute-start.9 = (f32[100,128]{1,0:T(8,128)S(1)}, f32[100,128]{1,0:T(8,128)S(1)}, u32[]{:S(2)}, u32[]{:S(2)}) collective-permute-start(f32[100,128]{1,0:T(8,128)S(1)} %get-tuple-element.51.refs_7_), channel_id=1, source_target_pairs={{0,7},{1,2},{2,1},{3,4},{4,3},{5,6},{6,5},{7,0},{8,15},{9,10},{10,... | collective-permute-start | bytes 153608 | tf_op jit(solution)/shard_map/ppermute | solution.py:36
  63.3 18.0 %copy-start.22 = (f32[3,25]{1,0:T(4,128)S(1)}, f32[3,25]{1,0:T(4,128)}, u32[]{:S(2)}) copy-start(f32[3,25]{1,0:T(4,128)} %param.11) | copy-start | bytes 904
  63.3 11.5 %collective-permute-start.10 = (f32[200,128]{1,0:T(8,128)S(1)}, f32[200,128]{1,0:T(8,128)S(1)}, u32[]{:S(2)}, u32[]{:S(2)}) collective-permute-start(f32[200,128]{1,0:T(8,128)S(1)} %get-tuple-element.56), channel_id=1, source_target_pairs={{0,8},{8,16},{16,24},{24,32},{32,40},{40,48},{48,56},{56,64},{64,7... | collective-permute-start | bytes 307208 | tf_op jit(solution)/shard_map/ppermute | solution.py:25
  63.3 11.5 %collective-permute-start.11 = (f32[100,128]{1,0:T(8,128)S(1)}, f32[100,128]{1,0:T(8,128)S(1)}, u32[]{:S(2)}, u32[]{:S(2)}) collective-permute-start(f32[100,128]{1,0:T(8,128)S(1)} %get-tuple-element.57), channel_id=1, source_target_pairs={{0,1},{1,2},{2,3},{3,4},{4,5},{5,6},{6,7},{7,0},{8,9},{9,10},{10,1... | collective-permute-start | bytes 153608 | tf_op jit(solution)/shard_map/ppermute | solution.py:25
  75.5 16.0 %all-to-all-start.2 = ((f32[16,5,8,128]{3,2,1,0:T(8,128)}), f32[16,5,8,128]{3,2,1,0:T(8,128)S(1)}, u32[]{:S(2)}, u32[]{:S(2)}) async-start(f32[16,5,8,128]{3,2,1,0:T(8,128)} %middle.1), calls=%async_computation.2 | async-start | bytes 655360 | tf_op jit(solution)/shard_map/all_to_all | solution.py:390
  91.5 1.3 %copy-start.5 = (f32[2400,128]{1,0:T(8,128)S(1)}, f32[2400,128]{1,0:T(8,128)}, u32[]{:S(2)}) copy-start(f32[2400,128]{1,0:T(8,128)} %copy-done.4) | copy-start | bytes 3686404
  92.8 1.3 %copy-start.7 = (f32[2400,128]{1,0:T(8,128)S(1)}, f32[2400,128]{1,0:T(8,128)}, u32[]{:S(2)}) copy-start(f32[2400,128]{1,0:T(8,128)} %copy-done.6) | copy-start | bytes 3686404
  (13 other events, 10.3 us)

commit v3 on v2

v3 whole, which is shorter than its diff:
```python
import jax
import jax.numpy as jnp
import numpy as np
from jax import lax
from jax.experimental import pallas as pl
from jax.experimental.pallas import tpu as pltpu
from jax.sharding import PartitionSpec as P

ITERS = 3
SWEEPS = 8
F, A, AP = 3, 25, 32
LX, LY, LZ = 4, 8, 128
CELLS = LX * LY
FACE = A * CELLS
ROWS = F * FACE
PADDED = ROWS + (AP - A) * CELLS
f32, bf16 = jnp.float32, jnp.bfloat16
VM = pl.BlockSpec(memory_space=pltpu.VMEM)
SM = pl.BlockSpec(memory_space=pltpu.SMEM)
ANY = pl.BlockSpec(memory_space=pl.ANY)


def shifted(value, axis, by):
    n = lax.axis_size(axis)
    return lax.ppermute(value, axis, [(i, (i + by) % n) for i in range(n)])


def near_swap(value, axis):
    n = lax.axis_size(axis)
    return lax.ppermute(value, axis, [(i, i ^ 1) for i in range(n)])


def far_swap(value, axis):
    n = lax.axis_size(axis)
    pairs = [(i, (i + 1) % n) if i % 2 else (i, (i - 1) % n) for i in range(n)]
    return lax.ppermute(value, axis, pairs)


def halves(v):
    hi = v.astype(bf16)
    lo = (v - hi.astype(f32)).astype(bf16)
    return hi, lo


def apply_operator(v_ref, ux_ref, uy_ref, k_ref, m_ref, wh_ref, wl_ref, out_ref, up_x, low_x, up_y, low_y):
    wh = wh_ref[...]
    wl = wl_ref[...]

    def face(f, x, y):
        if f == 0 and x == LX:
            return ux_ref[pl.ds(y, AP, stride=LY), :]
        if f == 1 and y == LY:
            return uy_ref[pl.ds(x, AP, stride=LX), :]
        return v_ref[pl.ds(f * FACE + x * LY + y, AP, stride=CELLS), :]

    def put(f, x, y, value):
        out_ref[pl.ds(f * FACE + x * LY + y, A, stride=CELLS), :] = value[:A]

    t0 = [halves(face(0, 0, y)) for y in range(LY)]
    carry = None
    for x in range(LX):
        t0_next = [halves(face(0, x + 1, y)) for y in range(LY)]
        t1 = [halves(face(1, x, y)) for y in range(LY + 1)]
        his, los = [], []
        for y in range(LY):
            z = face(2, x, y)
            t2 = halves(z)
            t2u = halves(pltpu.roll(z, LZ - 1, 1))
            six = (t0[y], t0_next[y], t1[y], t1[y + 1], t2, t2u)
            his.append(jnp.concatenate([b[0] for b in six], 0))
            los.append(jnp.concatenate([b[1] for b in six], 0))
        t0 = t0_next
        hi = jnp.concatenate(his, 1)
        lo = jnp.concatenate(los, 1)
        prod = jnp.dot(wh, hi, preferred_element_type=f32)
        prod += jnp.dot(wh, lo, preferred_element_type=f32)
        prod += jnp.dot(wl, hi, preferred_element_type=f32)
        parts = []
        for y in range(LY):
            k = k_ref[x * LY + y : x * LY + y + 1, :]
            m = m_ref[x * LY + y : x * LY + y + 1, :]
            cols = slice(y * LZ, (y + 1) * LZ)
            w = prod[: 6 * AP, cols] * k + prod[6 * AP :, cols] * m
            parts.append([w[b * AP : (b + 1) * AP] for b in range(6)])
        for y in range(LY):
            wlx, wux, wly, wuy, wlz, wuz = parts[y]
            put(0, x, y, wlx if x == 0 else wlx + carry[y])
            put(1, x, y, wly if y == 0 else wly + parts[y - 1][3])
            put(2, x, y, wlz + pltpu.roll(wuz, 1, 1))
            if x == 0 and low_x is not None:
                low_x[pl.ds(y, A, stride=LY), :] = wlx[:A]
            if x == LX - 1:
                up_x[pl.ds(y, A, stride=LY), :] = wux[:A]
        if low_y is not None:
            low_y[pl.ds(x, A, stride=LX), :] = parts[0][2][:A]
        up_y[pl.ds(x, A, stride=LX), :] = parts[LY - 1][3][:A]
        carry = [parts[y][1] for y in range(LY)]


def is_even(axis):
    return lax.rem(lax.axis_index(axis), 2) == 0


def route(even, up, low, near, far):
    near[...] = jnp.where(even, up[...], low[...])
    far[...] = jnp.where(even, low[...], up[...])


def edge_kernel(rhs_ref, fx_ref, fy_ref, sem_x, sem_y):
    face_x = pltpu.make_async_copy(rhs_ref.at[0, :, 0], fx_ref, sem_x)
    face_y = pltpu.make_async_copy(rhs_ref.at[1, :, :, 0], fy_ref, sem_y)
    face_x.start()
    face_y.start()
    face_x.wait()
    face_y.wait()


def weight_kernel(s_ref, m_ref, wh_ref, wl_ref, inv_ref):
    n, padded = 6 * A, 6 * AP
    r = lax.broadcasted_iota(jnp.int32, (padded, n), 0)
    c = lax.broadcasted_iota(jnp.int32, (padded, n), 1)
    node = lax.rem(r, AP)
    place = jnp.where((node < A) & (lax.div(r, AP) * A + node == c), 1.0, 0.0).astype(bf16)
    diagonal = lax.broadcasted_iota(jnp.int32, (n, n), 0) == lax.broadcasted_iota(jnp.int32, (n, n), 1)

    def largest(v):
        return jnp.max(jnp.max(jnp.where(diagonal, v, 0.0), 0, keepdims=True), 1, keepdims=True)

    inv = 1.0 / (10.0 * largest(s_ref[...]) + 2.0 * largest(m_ref[...]))
    inv_ref[...] = jnp.broadcast_to(inv, (8, LZ))
    for i, ref in enumerate((s_ref, m_ref)):
        for part, out in zip(halves(ref[...] * inv), (wh_ref, wl_ref)):
            rows = jnp.dot(place, part, preferred_element_type=f32).astype(bf16)
            full = lax.dot_general(rows, place, (((1,), (1,)), ((), ())), preferred_element_type=f32)
            out[i * padded : (i + 1) * padded] = full.astype(bf16)


def pad(ref, rows):
    ref[rows:] = jnp.zeros((ref.shape[0] - rows, LZ), f32)


def first_kernel(rhs_ref, hx_ref, hy_ref, k_ref, m_ref, wh_ref, wl_ref,
                 p_ref, snx, sfx, sny, sfy, v, ux, uy, upx, lowx, upy, lowy):
    v[:ROWS] = rhs_ref[...]
    pad(v, ROWS)
    ux[: A * LY] = hx_ref[...]
    pad(ux, A * LY)
    uy[: A * LX] = hy_ref[...]
    pad(uy, A * LX)
    apply_operator(v, ux, uy, k_ref, m_ref, wh_ref, wl_ref, p_ref, upx, lowx, upy, lowy)
    route(is_even("gx"), upx, lowx, snx, sfx)
    route(is_even("gy"), upy, lowy, sny, sfy)


def assemble(p_ref, snx, sfx, sny, sfy, rnx, rfx, rny, rfy, v, ux, uy):
    even_x = is_even("gx")
    even_y = is_even("gy")
    v[:ROWS] = p_ref[...]
    pad(v, ROWS)
    below_x = jnp.where(even_x, rfx[...], rnx[...])
    for a in range(A):
        rows = slice(a * CELLS, a * CELLS + LY)
        v[rows, :] = v[rows, :] + below_x[a * LY : (a + 1) * LY]
    below_y = jnp.where(even_y, rfy[...], rny[...])
    first = pl.ds(FACE, A * LX, stride=LY)
    v[first, :] = v[first, :] + below_y
    ux[: A * LY] = jnp.where(even_x, snx[...] + rnx[...], sfx[...] + rfx[...])
    pad(ux, A * LY)
    uy[: A * LX] = jnp.where(even_y, sny[...] + rny[...], sfy[...] + rfy[...])
    pad(uy, A * LX)


def node_sum(value):
    return jnp.sum(value.reshape(-1, LY, LZ), 0)


def row(tile):
    return jnp.sum(tile, 0, keepdims=True)


def second_kernel(p_ref, rhs_ref, snx, sfx, sny, sfy, rnx, rfx, rny, rfy, k_ref, m_ref, wh_ref, wl_ref,
                  v1_ref, p1_ref, tnx, tfx, tny, tfy, sums_ref, ux, uy, upx, lowx, upy, lowy):
    assemble(p_ref, snx, sfx, sny, sfy, rnx, rfx, rny, rfy, v1_ref, ux, uy)
    v0 = rhs_ref[...]
    v1 = v1_ref[:ROWS]
    sums_ref[0:8] = node_sum(v0)
    sums_ref[8:16] = node_sum(v1)
    sums_ref[16:24] = node_sum(v0 * v0)
    sums_ref[24:32] = node_sum(v0 * v1)
    sums_ref[32:40] = node_sum(v1 * v1)
    apply_operator(v1_ref, ux, uy, k_ref, m_ref, wh_ref, wl_ref, p1_ref, upx, lowx, upy, lowy)
    route(is_even("gx"), upx, lowx, tnx, tfx)
    route(is_even("gy"), upy, lowy, tny, tfy)


def third_kernel(p_ref, v1_ref, snx, sfx, sny, sfy, rnx, rfx, rny, rfy, sums_ref, k_ref, m_ref, wh_ref, wl_ref,
                 v2_ref, p2_ref, upx, upy, loads_ref, mom_ref, ux, uy):
    assemble(p_ref, snx, sfx, sny, sfy, rnx, rfx, rny, rfy, v2_ref, ux, uy)
    v1 = v1_ref[:ROWS]
    v2 = v2_ref[:ROWS]
    loads_ref[0:16] = sums_ref[0:16]
    loads_ref[16:24] = node_sum(v2)
    m3 = node_sum(v1 * v2)
    m4 = node_sum(v2 * v2)
    apply_operator(v2_ref, ux, uy, k_ref, m_ref, wh_ref, wl_ref, p2_ref, upx, None, upy, None)
    p2 = p2_ref[...]
    above = upx[...]
    loads_ref[24:32] = node_sum(p2)
    loads_ref[32:40] = node_sum(above)
    energy = node_sum(v2_ref[:ROWS] * p2) + node_sum(ux[: A * LY] * above)
    tail = row(uy[: A * LX] * upy[...])
    tile = [row(sums_ref[16 + 8 * k : 24 + 8 * k]) for k in range(3)]
    tile = jnp.concatenate(tile + [row(m3), row(m4), row(energy) + tail, jnp.zeros((2, LZ), f32)], 0)
    for lanes in (64, 32, 16):
        tile = tile + pltpu.roll(tile, lanes, 1)
    lane = lax.broadcasted_iota(jnp.int32, (8, LZ), 1)
    moment = lax.broadcasted_iota(jnp.int32, (8, LZ), 0)
    packed = row(jnp.where(lax.div(lane, 16) == moment, tile, 0.0))
    pair = jnp.concatenate([packed, row(upy[...])] * 4, 0)
    for at in range(0, mom_ref.shape[0], 8):
        mom_ref[at : at + 8] = pair


def weigh_kernel(own, near, far, both, *outs, table):
    nx = len(table)
    q = lax.rem(lax.axis_index("gx"), 4)
    low, high = lax.rem(q, 2) == 0, q < 2
    one, two = jnp.where(low, 1, -1), jnp.where(high, 2, -2)

    def pick(at, shift, span):
        value = jnp.float32(table[(at - span[0]) % nx])
        for s in span[1:]:
            value = jnp.where(shift == s, table[(at - s) % nx], value)
        return value

    for z, out in enumerate(outs):
        total = [0.0] * 4
        for ref, shift, span in ((own, 0, (0,)), (near, one, (1, -1)), (far, two, (2, -2)), (both, one + two, (3, 1, -1, -3))):
            w = pick(4 * z, shift, span)
            for k in range(4):
                total[k] = total[k] + ref[k * 8 : k * 8 + 8] * w
            total[3] = total[3] + ref[32:40] * pick(4 * z - 1, shift, span)
        for k in range(4):
            out[k * 8 : k * 8 + 8] = total[k]


def two_sum(a, b):
    s = a + b
    t = s - a
    return s, (a - (s - t)) + (b - t)


def pair_add(a, b):
    s, e = two_sum(a[0], b[0])
    e = e + (a[1] + b[1])
    h = s + e
    return h, e - (h - s)


def split(a):
    t = a * 4097.0
    h = t - (t - a)
    return h, a - h


def pair_times(a, c):
    p = a[0] * c
    ah, al = split(a[0])
    ch, cl = split(c)
    return p, ((ah * ch - p) + ah * cl + al * ch) + al * cl + a[1] * c


def moments(got):
    pairs = [(got[at : at + 8], jnp.zeros((8, LZ), f32)) for at in range(0, got.shape[0], 8)]
    while len(pairs) > 1:
        pairs = [pair_add(a, b) for a, b in zip(pairs[::2], pairs[1::2])]
    t = pairs[0]
    for rows in (4, 2):
        t = pair_add(t, tuple(pltpu.roll(p, rows, 0) for p in t))
    for lanes in (8, 4, 2, 1):
        t = pair_add(t, tuple(pltpu.roll(p, LZ - lanes, 1) for p in t))
    c = t[0][0:1, 16:17] / t[0][0:1, 0:1]
    wide = jnp.broadcast_to(c, (8, LZ))
    m = [t[0][0:1, 0:1]]
    for _ in range(5):
        up = tuple(pltpu.roll(p, LZ - 16, 1) for p in t)
        t = pair_add(up, pair_times(t, -wide))
        m.append(t[0][0:1, 0:1])
    return c, m


def conjugate_gradient(c, m):
    def dot(a, b):
        s = None
        for i, ai in enumerate(a):
            for j, bj in enumerate(b):
                t = ai * bj * m[i + j]
                s = t if s is None else s + t
        return s

    def add(a, b, factor):
        longer = []
        for i in range(max(len(a), len(b))):
            if i >= len(b):
                longer.append(a[i])
            elif i >= len(a):
                longer.append(factor * b[i])
            else:
                longer.append(a[i] + factor * b[i])
        return longer

    def times(a, shift):
        return [a[0] * shift] + [a[i] * shift + a[i - 1] for i in range(1, len(a))] + [a[-1]]

    def plain(a):
        out = [a[-1]]
        for coefficient in a[-2::-1]:
            out = times(out, -c)
            out[0] = out[0] + coefficient
        return out

    one = jnp.ones((1, 1), f32)
    iterate, residual, direction = [], [one], [one]
    norm = m[0]
    for step in range(ITERS):
        img = times(direction, c)
        alpha = norm / dot(direction, img)
        iterate = add(iterate, direction, alpha)
        residual = add(residual, img, -alpha)
        if step < ITERS - 1:
            norm_next = dot(residual, residual)
            direction = add(residual, direction, norm_next / norm)
            norm = norm_next
    return plain(iterate), plain(residual)


def last_kernel(prolong_ref, got_ref, c0, c1, c2, c3, inv_ref, rhs_ref, v1_ref, v2_ref, p2_ref, rx_ref, ry_ref,
                sol_ref, res_ref, coarse_ref, *, table, ny):
    nx = len(table)
    x, d = conjugate_gradient(*moments(got_ref[...]))
    inv = inv_ref[0:1, 0:1]
    x = [t * inv for t in x]
    me = lax.axis_index("gx")
    below = lax.rem(lax.axis_index("gy") + ny - 1, ny)
    edge = jnp.zeros((1, LZ), f32)
    for offset, weight in enumerate(table):
        slab = lax.rem(me + nx - offset, nx)
        edge = edge + got_ref[pl.ds(2 * (slab * ny + below) + 1, 1), :] * weight
    circ = [c0[k * 8 : k * 8 + 8] + c1[k * 8 : k * 8 + 8] + c2[k * 8 : k * 8 + 8] + c3[k * 8 : k * 8 + 8] for k in range(4)]
    at_first = lax.broadcasted_iota(jnp.int32, (LY, LZ), 0) == 0
    circ[3] = circ[3] + jnp.where(at_first, jnp.broadcast_to(edge, (LY, LZ)), 0.0)
    coarse = d[0] * circ[0] + d[1] * circ[1] + d[2] * circ[2] + d[3] * circ[3]
    coarse_ref[...] = coarse
    x = [jnp.broadcast_to(t, (LY, LZ)) for t in x]
    d = [jnp.broadcast_to(t, (LY, LZ)) for t in d]
    for f in range(F):
        for a in range(A):
            at = (f * A + a) * CELLS
            spread = coarse * prolong_ref[f, a]
            for cell in range(LX):
                rows = slice(at + cell * LY, at + (cell + 1) * LY)
                v0, v1, v2 = rhs_ref[rows, :], v1_ref[rows, :], v2_ref[rows, :]
                img = p2_ref[rows, :]
                if f == 0 and cell == 0:
                    img = img + rx_ref[a * LY : (a + 1) * LY, :]
                sol_ref[rows, :] = x[0] * v0 + x[1] * v1 + x[2] * v2 + spread
                res_ref[rows, :] = d[0] * v0 + d[1] * v1 + d[2] * v2 + d[3] * img
    first = pl.ds(FACE, A * LX, stride=LY)
    res_ref[first, :] = res_ref[first, :] + d[3][0:1] * ry_ref[...]


def jacobi_weights(n):
    coarse = np.zeros(n)
    load = np.zeros(n)
    load[0] = 1.0
    for _ in range(SWEEPS):
        coarse = (load + np.roll(coarse, 1) + np.roll(coarse, -1)) / 2.2
    return coarse / 75.0


def struct(*shape):
    return jax.ShapeDtypeStruct(shape, f32)


PARAMS = pltpu.CompilerParams(vmem_limit_bytes=16 * 1024 * 1024)


def shards(rhs, kappa, mass, stiffness, mass_matrix, prolong):
    nx, ny = lax.axis_size("gx"), lax.axis_size("gy")
    vx, vy = A * LY, A * LX
    rhs2 = rhs.reshape(ROWS, LZ)
    k2 = kappa.reshape(CELLS, LZ)
    m2 = mass.reshape(CELLS, LZ)
    sends = [struct(vx, LZ), struct(vx, LZ), struct(vy, LZ), struct(vy, LZ)]
    upper = [pltpu.VMEM((AP * LY, LZ), f32), pltpu.VMEM((AP * LX, LZ), f32)]
    field = [pltpu.VMEM((PADDED, LZ), f32)] + upper
    edges = [pltpu.VMEM((vx, LZ), f32)] * 2 + [pltpu.VMEM((vy, LZ), f32)] * 2

    def call(kernel, name, ins, outs, scratch=(), **static):
        specs = [i[1] if isinstance(i, tuple) else VM for i in ins]
        ins = [i[0] if isinstance(i, tuple) else i for i in ins]

        def bound(*refs):
            kernel(*refs, **static)

        return pl.pallas_call(
            bound,
            out_shape=outs,
            in_specs=specs,
            out_specs=[VM] * len(outs),
            scratch_shapes=list(scratch),
            compiler_params=PARAMS,
            name=name,
        )(*ins)

    def swap(s):
        far_x = far_swap(s[1], "gx")
        far_y = far_swap(s[3], "gy")
        near_y = near_swap(s[2], "gy")
        near_x = near_swap(s[0], "gx")
        return [near_x, far_x, near_y, far_y]

    hbm = pltpu.with_memory_space_constraint(rhs, pltpu.HBM)
    fx, fy = call(
        edge_kernel, "edges", [(hbm, ANY)], [struct(A, LY, LZ), struct(A, LX, LZ)],
        [pltpu.SemaphoreType.DMA, pltpu.SemaphoreType.DMA],
    )
    hx = shifted(fx.reshape(vx, LZ), "gx", -1)
    hy = shifted(fy.reshape(vy, LZ), "gy", -1)
    half = jax.ShapeDtypeStruct((12 * AP, 6 * AP), bf16)
    wh, wl, inv = call(weight_kernel, "weights", [stiffness, mass_matrix], [half, half, struct(8, LZ)])

    p0, *s = call(
        first_kernel, "first", [rhs2, hx, hy, k2, m2, wh, wl], [struct(ROWS, LZ)] + sends, field + edges,
    )
    r = swap(s)
    v1, p1, *s, sums = call(
        second_kernel, "second", [p0, rhs2, *s, *r, k2, m2, wh, wl],
        [struct(PADDED, LZ), struct(ROWS, LZ)] + sends + [struct(40, LZ)], upper + edges,
    )
    r = swap(s)
    v2, p2, upx, upy, loads, mom = call(
        third_kernel, "third", [p1, v1, *s, *r, sums, k2, m2, wh, wl],
        [struct(PADDED, LZ), struct(ROWS, LZ), struct(vx, LZ), struct(vy, LZ), struct(40, LZ), struct(nx * ny * 2, LZ)],
        upper,
    )
    got = lax.all_to_all(mom.reshape(nx * ny, 2, LZ), ("gx", "gy"), 0, 0, tiled=True).reshape(nx * ny * 2, LZ)
    group = [lax.ppermute(loads, "gx", [(i, i ^ b) for i in range(nx)]) for b in (1, 2, 3)]
    rx = shifted(upx, "gx", 1)
    ry = shifted(upy, "gy", 1)
    table = [float(t) for t in jacobi_weights(nx)]
    pieces = call(weigh_kernel, "weigh", [loads, *group], [struct(32, LZ)] * (nx // 4), table=table)
    coarse = [pieces[0]] + [shifted(p, "gx", 4 * z) for z, p in enumerate(pieces) if z]
    sol, res, coarse = call(
        last_kernel, "last", [(prolong, SM), got, *coarse, inv, rhs2, v1, v2, p2, rx, ry],
        [struct(ROWS, LZ), struct(ROWS, LZ), struct(LY, LZ)], table=table, ny=ny,
    )
    return sol.reshape(rhs.shape), res.reshape(rhs.shape), coarse[None]


def solution(mesh):
    placed = (
        P(None, None, "gx", "gy", None),
        P("gx", "gy", None),
        P("gx", "gy", None),
        P(),
        P(),
        P(),
    )
    return jax.shard_map(
        shards,
        mesh=mesh,
        in_specs=placed,
        out_specs=(
            P(None, None, "gx", "gy", None),
            P(None, None, "gx", "gy", None),
            P("gx", "gy", None),
        ),
        check_vma=False,
    )
```

time: 97.8 us -> 79.7 us (0.81)
  blocking collectives: 11.1 us -> 0 us
  local copies, waits for them, and re-layouts: 15.6 us -> 6.57 us
  starting transfers between devices: 34.8 us -> 39.1 us
  waiting for transfers between devices: 15.9 us -> 13.4 us
    all_to_all x1 -> x0, blocking collectives: 11.1 us -> none  [shards(): mom = lax.all_to_all(mom, 'gy', 0, 0, tiled=True)]
    all_to_all x2 -> x1, waiting for transfers between devices: 10.2 us -> 0.01 us  [shards(): lax.all_to_all(mom.reshape(nx * ny, 2, LZ), ('gx', 'gy'), 0, 0, tiled=True)]
    unnamed x46 -> x20, local copies, waits for them, and re-layouts: 15.5 us -> 6.56 us
    ppermute x4 -> x7, starting transfers between devices: 9.56 us -> 16.3 us  [shifted(): return lax.ppermute(value, axis, [(i, (i + by) % n) for i in range(n)])]
    all_to_all x2 -> x1, starting transfers between devices: 10.3 us -> 5.19 us  [shards(): lax.all_to_all(mom.reshape(nx * ny, 2, LZ), ('gx', 'gy'), 0, 0, tiled=True)]
    ppermute x0 -> x3, starting transfers between devices: none -> 4.89 us  [shards(): lax.ppermute(loads, 'gx', [(i, i ^ b) for i in range(nx)])]
    ppermute x0 -> x3, waiting for transfers between devices: none -> 4.86 us  [shards(): lax.ppermute(loads, 'gx', [(i, i ^ b) for i in range(nx)])]
    ppermute x4, starting transfers between devices: 14.2 us -> 12 us  [far_swap(): return lax.ppermute(value, axis, pairs)]
  transfers between devices with their start and end apart: 14 -> 19, of which waited for: 4 -> 7; matrix products, arithmetic and copies ran while one was open for 0% -> 0% of each run, Pallas kernels for 5% -> 1%
where the time goes in v3:
time: 79.7 us; the launch traced here: 79 us
  starting transfers between devices  39.1 us (49%)
  Pallas kernels  19.1 us (24%)
  waiting for transfers between devices  13.4 us (17%)
  local copies, waits for them, and re-layouts  6.57 us (8%)
  between operations  0.81 us (1%)
    pallas_call x7, Pallas kernels, call(): pl.pallas_call(bound, out_shape=outs, in_specs=specs, out_specs=[VM] * le...  19.1 us
    ppermute x7, starting transfers between devices, shifted(): return lax.ppermute(value, axis, [(i, (i + by) % n) for i in range(n)])  16.3 us
    ppermute x4, starting transfers between devices, far_swap(): return lax.ppermute(value, axis, pairs)  12 us
    unnamed x20, local copies, waits for them, and re-layouts  6.56 us
    all_to_all x1, starting transfers between devices, shards(): lax.all_to_all(mom.reshape(nx * ny, 2, LZ), ('gx', 'gy'), 0, 0, tiled=True)  5.19 us
    ppermute x4, waiting for transfers between devices, far_swap(): return lax.ppermute(value, axis, pairs)  5.07 us
    ppermute x3, starting transfers between devices, shards(): lax.ppermute(loads, 'gx', [(i, i ^ b) for i in range(nx)])  4.89 us
    ppermute x3, waiting for transfers between devices, shards(): lax.ppermute(loads, 'gx', [(i, i ^ b) for i in range(nx)])  4.86 us
  transfers between devices with their start and end apart: 19, of which 7 were waited for; matrix products, arithmetic and copies ran while one was open for 0% of the time, Pallas kernels for 1%

profile of v3, /device:TPU:0, one launch (start us, length us, event | category | flops | bytes accessed | tf_op | source)
XLA Modules:
  0.0 79.0 jit_solution(3911977819935001564)
XLA Ops:
  1.7 6.1 %collective-permute-start = (f32[200,128]{1,0:T(8,128)S(1)}, f32[200,128]{1,0:T(8,128)S(1)}, u32[]{:S(2)}, u32[]{:S(2)}) collective-permute-start(f32[200,128]{1,0:T(8,128)S(1)} %bitcast.19), channel_id=1, source_target_pairs={{0,120},{8,0},{16,8},{24,16},{32,24},{40,32},{48,40},{56,48},{64,5... | collective-permute-start | bytes 307208 | tf_op jit(solution)/shard_map/ppermute | solution.py:25
  7.8 3.1 %collective-permute-start.1 = (f32[100,128]{1,0:T(8,128)S(1)}, f32[100,128]{1,0:T(8,128)S(1)}, u32[]{:S(2)}, u32[]{:S(2)}) collective-permute-start(f32[100,128]{1,0:T(8,128)S(1)} %reshape.35), channel_id=1, source_target_pairs={{0,7},{1,0},{2,1},{3,2},{4,3},{5,4},{6,5},{7,6},{8,15},{9,8},{10,9... | collective-permute-start | bytes 153608 | tf_op jit(solution)/shard_map/ppermute | solution.py:25
  13.4 4.2 %first.1 = (f32[2400,128]{1,0:T(8,128)S(1)}, f32[200,128]{1,0:T(8,128)S(1)}, f32[200,128]{1,0:T(8,128)S(1)}, f32[100,128]{1,0:T(8,128)S(1)}, f32[100,128]{1,0:T(8,128)S(1)}) custom-call(f32[2400,128]{1,0:T(8,128)S(1)} %bitcast.9, f32[200,128]{1,0:T(8,128)S(1)} %collective-permute-done.refs_1_, f32[100,128]{1,0:T(8,128)S(1)} %collective-permute-done.1.refs_2_, ...), custom_call_target="tpu_custom_call" | custom-call | tf_op jit(solution)/shard_map/first/pallas_call | solution.py:406
  17.6 2.2 %collective-permute-start.3 = (f32[200,128]{1,0:T(8,128)S(1)}, f32[200,128]{1,0:T(8,128)S(1)}, u32[]{:S(2)}, u32[]{:S(2)}) collective-permute-start(f32[200,128]{1,0:T(8,128)S(1)} %get-tuple-element.39.refs_3_), channel_id=1, source_target_pairs={{0,120},{8,16},{16,8},{24,32},{32,24},{40,48},{48,40},{56,64},{64,... | collective-permute-start | bytes 307208 | tf_op jit(solution)/shard_map/ppermute | solution.py:36
  20.4 3.9 %collective-permute-start.5 = (f32[100,128]{1,0:T(8,128)S(1)}, f32[100,128]{1,0:T(8,128)S(1)}, u32[]{:S(2)}, u32[]{:S(2)}) collective-permute-start(f32[100,128]{1,0:T(8,128)S(1)} %get-tuple-element.41.refs_5_), channel_id=1, source_target_pairs={{0,7},{1,2},{2,1},{3,4},{4,3},{5,6},{6,5},{7,0},{8,15},{9,10},{10,... | collective-permute-start | bytes 153608 | tf_op jit(solution)/shard_map/ppermute | solution.py:36
  24.3 3.0 %collective-permute-done.5.refs_9_ = f32[100,128]{1,0:T(8,128)S(1)} collective-permute-done((f32[100,128]{1,0:T(8,128)S(1)}, f32[100,128]{1,0:T(8,128)S(1)}, u32[]{:S(2)}, u32[]{:S(2)}) %collective-permute-start.5) | collective-permute-done | bytes 51232 | tf_op jit(solution)/shard_map/ppermute | solution.py:36
  27.3 4.5 %second.1 = (f32[2624,128]{1,0:T(8,128)S(1)}, f32[2400,128]{1,0:T(8,128)S(1)}, f32[200,128]{1,0:T(8,128)S(1)}, f32[200,128]{1,0:T(8,128)S(1)}, f32[100,128]{1,0:...) custom-call(f32[2400,128]{1,0:T(8,128)S(1)} %get-tuple-element.37.refs_0_, f32[2400,128]{1,0:T(8,128)S(1)} %bitcast.10, ...), custom_call_target="tpu_custom_call" | custom-call | tf_op jit(solution)/shard_map/second/pallas_call | solution.py:406
  31.8 3.8 %collective-permute-start.7 = (f32[200,128]{1,0:T(8,128)S(1)}, f32[200,128]{1,0:T(8,128)S(1)}, u32[]{:S(2)}, u32[]{:S(2)}) collective-permute-start(f32[200,128]{1,0:T(8,128)S(1)} %get-tuple-element.45.refs_3_), channel_id=1, source_target_pairs={{0,120},{8,16},{16,8},{24,32},{32,24},{40,48},{48,40},{56,64},{64,... | collective-permute-start | bytes 307208 | tf_op jit(solution)/shard_map/ppermute | solution.py:36
  35.6 2.2 %collective-permute-start.9 = (f32[100,128]{1,0:T(8,128)S(1)}, f32[100,128]{1,0:T(8,128)S(1)}, u32[]{:S(2)}, u32[]{:S(2)}) collective-permute-start(f32[100,128]{1,0:T(8,128)S(1)} %get-tuple-element.47.refs_5_), channel_id=1, source_target_pairs={{0,7},{1,2},{2,1},{3,4},{4,3},{5,6},{6,5},{7,0},{8,15},{9,10},{10,... | collective-permute-start | bytes 153608 | tf_op jit(solution)/shard_map/ppermute | solution.py:36
  37.8 2.0 %collective-permute-done.8.refs_8_ = f32[100,128]{1,0:T(8,128)S(1)} collective-permute-done((f32[100,128]{1,0:T(8,128)S(1)}, f32[100,128]{1,0:T(8,128)S(1)}, u32[]{:S(2)}, u32[]{:S(2)}) %collective-permute-start.8) | collective-permute-done | bytes 51232 | tf_op jit(solution)/shard_map/ppermute | solution.py:30
  39.8 2.1 %collective-permute-done.9.refs_9_ = f32[100,128]{1,0:T(8,128)S(1)} collective-permute-done((f32[100,128]{1,0:T(8,128)S(1)}, f32[100,128]{1,0:T(8,128)S(1)}, u32[]{:S(2)}, u32[]{:S(2)}) %collective-permute-start.9) | collective-permute-done | bytes 51232 | tf_op jit(solution)/shard_map/ppermute | solution.py:36
  41.9 5.5 %third.1 = (f32[2624,128]{1,0:T(8,128)S(1)}, f32[2400,128]{1,0:T(8,128)S(1)}, f32[200,128]{1,0:T(8,128)S(1)}, f32[100,128]{1,0:T(8,128)S(1)}, f32[40,128]{1,0:T(8,128)S(1)}, /*index=5*/f32[256,128]{1,0:T(8,128)}) custom-call(f32[2400,128]{1,0:T(8,128)S(1)} %get-tuple-element.42.refs_0_, f32[2624,128]{1,0:T(8,128)S(1)} %get-tuple-element.43.refs_1_.refs_8_, ...), custom_call_target="tpu_custom_call" | custom-call | tf_op jit(solution)/shard_map/third/pallas_call | solution.py:406
  49.5 5.2 %all-to-all-start = ((f32[128,2,128]{2,1,0:T(2,128)}), f32[128,2,128]{2,1,0:T(2,128)S(1)}, u32[]{:S(2)}, u32[]{:S(2)}) async-start(f32[128,2,128]{2,1,0:T(2,128)} %bitcast.4), calls=%async_computation | async-start | bytes 262144 | tf_op jit(solution)/shard_map/all_to_all | solution.py:447
  54.8 1.1 %collective-permute-start.17 = (f32[100,128]{1,0:T(8,128)S(1)}, f32[100,128]{1,0:T(8,128)S(1)}, u32[]{:S(2)}, u32[]{:S(2)}) collective-permute-start(f32[100,128]{1,0:T(8,128)S(1)} %get-tuple-element.59), channel_id=1, source_target_pairs={{0,1},{1,2},{2,3},{3,4},{4,5},{5,6},{6,7},{7,0},{8,9},{9,10},{10,1... | collective-permute-start | bytes 153608 | tf_op jit(solution)/shard_map/ppermute | solution.py:25
  55.9 4.5 %collective-permute-start.12 = (f32[40,128]{1,0:T(8,128)S(1)}, f32[40,128]{1,0:T(8,128)S(1)}, u32[]{:S(2)}, u32[]{:S(2)}) collective-permute-start(f32[40,128]{1,0:T(8,128)S(1)} %get-tuple-element.50.refs_0_), channel_id=1, source_target_pairs={{0,24},{8,16},{16,8},{24,0},{32,56},{40,48},{48,40},{56,32},{64,88... | collective-permute-start | bytes 61448 | tf_op jit(solution)/shard_map/ppermute | solution.py:448
  60.8 1.7 %collective-permute-done.12.refs_3_ = f32[40,128]{1,0:T(8,128)S(1)} collective-permute-done((f32[40,128]{1,0:T(8,128)S(1)}, f32[40,128]{1,0:T(8,128)S(1)}, u32[]{:S(2)}, u32[]{:S(2)}) %collective-permute-start.12) | collective-permute-done | bytes 20512 | tf_op jit(solution)/shard_map/ppermute | solution.py:448
  62.5 3.1 %collective-permute-done.11.refs_2_ = f32[40,128]{1,0:T(8,128)S(1)} collective-permute-done((f32[40,128]{1,0:T(8,128)S(1)}, f32[40,128]{1,0:T(8,128)S(1)}, u32[]{:S(2)}, u32[]{:S(2)}) %collective-permute-start.11) | collective-permute-done | bytes 20512 | tf_op jit(solution)/shard_map/ppermute | solution.py:448
  65.7 1.8 %collective-permute-start.13 = (f32[32,128]{1,0:T(8,128)S(1)}, f32[32,128]{1,0:T(8,128)S(1)}, u32[]{:S(2)}, u32[]{:S(2)}) collective-permute-start(f32[32,128]{1,0:T(8,128)S(1)} %get-tuple-element.52), channel_id=1, source_target_pairs={{0,32},{8,40},{16,48},{24,56},{32,64},{40,72},{48,80},{56,88},{64,... | collective-permute-start | bytes 49160 | tf_op jit(solution)/shard_map/ppermute | solution.py:25
  67.5 1.6 %collective-permute-start.14 = (f32[32,128]{1,0:T(8,128)S(1)}, f32[32,128]{1,0:T(8,128)S(1)}, u32[]{:S(2)}, u32[]{:S(2)}) collective-permute-start(f32[32,128]{1,0:T(8,128)S(1)} %get-tuple-element.53), channel_id=1, source_target_pairs={{0,64},{8,72},{16,80},{24,88},{32,96},{40,104},{48,112},{56,120},{... | collective-permute-start | bytes 49160 | tf_op jit(solution)/shard_map/ppermute | solution.py:25
  69.1 2.5 %collective-permute-start.15 = (f32[32,128]{1,0:T(8,128)S(1)}, f32[32,128]{1,0:T(8,128)S(1)}, u32[]{:S(2)}, u32[]{:S(2)}) collective-permute-start(f32[32,128]{1,0:T(8,128)S(1)} %get-tuple-element.54), channel_id=1, source_target_pairs={{0,96},{8,104},{16,112},{24,120},{32,0},{40,8},{48,16},{56,24},{64... | collective-permute-start | bytes 49160 | tf_op jit(solution)/shard_map/ppermute | solution.py:25
  71.6 1.1 %collective-permute-done.14.refs_4_ = f32[32,128]{1,0:T(8,128)S(1)} collective-permute-done((f32[32,128]{1,0:T(8,128)S(1)}, f32[32,128]{1,0:T(8,128)S(1)}, u32[]{:S(2)}, u32[]{:S(2)}) %collective-permute-start.14) | collective-permute-done | bytes 16416 | tf_op jit(solution)/shard_map/ppermute | solution.py:25
  73.1 1.3 %copy-done.2 = f32[2624,128]{1,0:T(8,128)S(1)} copy-done((f32[2624,128]{1,0:T(8,128)S(1)}, f32[2624,128]{1,0:T(8,128)}, u32[]{:S(2)}) %copy-start.2) | copy-done | bytes 1343512
  74.4 1.3 %copy-done.4 = f32[2400,128]{1,0:T(8,128)S(1)} copy-done((f32[2400,128]{1,0:T(8,128)S(1)}, f32[2400,128]{1,0:T(8,128)}, u32[]{:S(2)}) %copy-start.4) | copy-done | bytes 1228824
  75.7 3.3 %last.1 = (f32[2400,128]{1,0:T(8,128)}, f32[2400,128]{1,0:T(8,128)}, f32[8,128]{1,0:T(8,128)}) custom-call(f32[3,25]{1,0:T(4,128)S(1)} %copy-done.9, f32[256,128]{1,0:T(8,128)S(1)} %bitcast.12, f32[32,128]{1,0:T(8,128)S(1)} %get-tuple-element.51.refs_2_, f32[32,128]{1,0:T(8,128)S(1)} %collective-permute-done.13.refs_3_, ...), custom_call_target="tpu_custom_call" | custom-call | tf_op jit(solution)/shard_map/last/pallas_call | solution.py:406
  (42 shorter events, 7.2 us)
Async XLA Ops:
  0.6 12.7 %copy-start = (f32[3,25,4,8,128]{4,3,2,1,0:T(8,128)S(1)}, f32[3,25,4,8,128]{4,3,2,1,0:T(8,128)}, u32[]{:S(2)}) copy-start(f32[3,25,4,8,128]{4,3,2,1,0:T(8,128)} %refs_0_.3) | copy-start | bytes 3686404
  0.6 12.7 %copy-start.8 = (f32[4,8,128]{2,1,0:T(8,128)S(1)}, f32[4,8,128]{2,1,0:T(8,128)}, u32[]{:S(2)}) copy-start(f32[4,8,128]{2,1,0:T(8,128)} %param.8) | copy-start | bytes 49156
  0.7 12.7 %copy-start.7 = (f32[4,8,128]{2,1,0:T(8,128)S(1)}, f32[4,8,128]{2,1,0:T(8,128)}, u32[]{:S(2)}) copy-start(f32[4,8,128]{2,1,0:T(8,128)} %param.7) | copy-start | bytes 49156
  1.7 11.7 %collective-permute-start = (f32[200,128]{1,0:T(8,128)S(1)}, f32[200,128]{1,0:T(8,128)S(1)}, u32[]{:S(2)}, u32[]{:S(2)}) collective-permute-start(f32[200,128]{1,0:T(8,128)S(1)} %bitcast.19), channel_id=1, source_target_pairs={{0,120},{8,0},{16,8},{24,16},{32,24},{40,32},{48,40},{56,48},{64,5... | collective-permute-start | bytes 307208 | tf_op jit(solution)/shard_map/ppermute | solution.py:25
  7.8 5.5 %collective-permute-start.1 = (f32[100,128]{1,0:T(8,128)S(1)}, f32[100,128]{1,0:T(8,128)S(1)}, u32[]{:S(2)}, u32[]{:S(2)}) collective-permute-start(f32[100,128]{1,0:T(8,128)S(1)} %reshape.35), channel_id=1, source_target_pairs={{0,7},{1,0},{2,1},{3,2},{4,3},{5,4},{6,5},{7,6},{8,15},{9,8},{10,9... | collective-permute-start | bytes 153608 | tf_op jit(solution)/shard_map/ppermute | solution.py:25
  17.6 9.7 %collective-permute-start.2 = (f32[200,128]{1,0:T(8,128)S(1)}, f32[200,128]{1,0:T(8,128)S(1)}, u32[]{:S(2)}, u32[]{:S(2)}) collective-permute-start(f32[200,128]{1,0:T(8,128)S(1)} %get-tuple-element.38.refs_2_), channel_id=1, source_target_pairs={{0,8},{8,0},{16,24},{24,16},{32,40},{40,32},{48,56},{56,48},{64,72... | collective-permute-start | bytes 307208 | tf_op jit(solution)/shard_map/ppermute | solution.py:30
  17.6 9.6 %collective-permute-start.3 = (f32[200,128]{1,0:T(8,128)S(1)}, f32[200,128]{1,0:T(8,128)S(1)}, u32[]{:S(2)}, u32[]{:S(2)}) collective-permute-start(f32[200,128]{1,0:T(8,128)S(1)} %get-tuple-element.39.refs_3_), channel_id=1, source_target_pairs={{0,120},{8,16},{16,8},{24,32},{32,24},{40,48},{48,40},{56,64},{64,... | collective-permute-start | bytes 307208 | tf_op jit(solution)/shard_map/ppermute | solution.py:36
  19.8 4.5 %collective-permute-start.4 = (f32[100,128]{1,0:T(8,128)S(1)}, f32[100,128]{1,0:T(8,128)S(1)}, u32[]{:S(2)}, u32[]{:S(2)}) collective-permute-start(f32[100,128]{1,0:T(8,128)S(1)} %get-tuple-element.40.refs_4_), channel_id=1, source_target_pairs={{0,1},{1,0},{2,3},{3,2},{4,5},{5,4},{6,7},{7,6},{8,9},{9,8},{10,11... | collective-permute-start | bytes 153608 | tf_op jit(solution)/shard_map/ppermute | solution.py:30
  20.4 6.8 %collective-permute-start.5 = (f32[100,128]{1,0:T(8,128)S(1)}, f32[100,128]{1,0:T(8,128)S(1)}, u32[]{:S(2)}, u32[]{:S(2)}) collective-permute-start(f32[100,128]{1,0:T(8,128)S(1)} %get-tuple-element.41.refs_5_), channel_id=1, source_target_pairs={{0,7},{1,2},{2,1},{3,4},{4,3},{5,6},{6,5},{7,0},{8,15},{9,10},{10,... | collective-permute-start | bytes 153608 | tf_op jit(solution)/shard_map/ppermute | solution.py:36
  31.8 10.1 %collective-permute-start.6 = (f32[200,128]{1,0:T(8,128)S(1)}, f32[200,128]{1,0:T(8,128)S(1)}, u32[]{:S(2)}, u32[]{:S(2)}) collective-permute-start(f32[200,128]{1,0:T(8,128)S(1)} %get-tuple-element.44.refs_2_), channel_id=1, source_target_pairs={{0,8},{8,0},{16,24},{24,16},{32,40},{40,32},{48,56},{56,48},{64,72... | collective-permute-start | bytes 307208 | tf_op jit(solution)/shard_map/ppermute | solution.py:30
  31.8 10.0 %collective-permute-start.7 = (f32[200,128]{1,0:T(8,128)S(1)}, f32[200,128]{1,0:T(8,128)S(1)}, u32[]{:S(2)}, u32[]{:S(2)}) collective-permute-start(f32[200,128]{1,0:T(8,128)S(1)} %get-tuple-element.45.refs_3_), channel_id=1, source_target_pairs={{0,120},{8,16},{16,8},{24,32},{32,24},{40,48},{48,40},{56,64},{64,... | collective-permute-start | bytes 307208 | tf_op jit(solution)/shard_map/ppermute | solution.py:36
  35.6 4.1 %collective-permute-start.8 = (f32[100,128]{1,0:T(8,128)S(1)}, f32[100,128]{1,0:T(8,128)S(1)}, u32[]{:S(2)}, u32[]{:S(2)}) collective-permute-start(f32[100,128]{1,0:T(8,128)S(1)} %get-tuple-element.46.refs_4_), channel_id=1, source_target_pairs={{0,1},{1,0},{2,3},{3,2},{4,5},{5,4},{6,7},{7,6},{8,9},{9,8},{10,11... | collective-permute-start | bytes 153608 | tf_op jit(solution)/shard_map/ppermute | solution.py:30
  35.6 6.2 %collective-permute-start.9 = (f32[100,128]{1,0:T(8,128)S(1)}, f32[100,128]{1,0:T(8,128)S(1)}, u32[]{:S(2)}, u32[]{:S(2)}) collective-permute-start(f32[100,128]{1,0:T(8,128)S(1)} %get-tuple-element.47.refs_5_), channel_id=1, source_target_pairs={{0,7},{1,2},{2,1},{3,4},{4,3},{5,6},{6,5},{7,0},{8,15},{9,10},{10,... | collective-permute-start | bytes 153608 | tf_op jit(solution)/shard_map/ppermute | solution.py:36
  41.9 31.2 %copy-start.9 = (f32[3,25]{1,0:T(4,128)S(1)}, f32[3,25]{1,0:T(4,128)}, u32[]{:S(2)}) copy-start(f32[3,25]{1,0:T(4,128)} %refs_0_.5) | copy-start | bytes 904
  49.5 23.5 %all-to-all-start = ((f32[128,2,128]{2,1,0:T(2,128)}), f32[128,2,128]{2,1,0:T(2,128)S(1)}, u32[]{:S(2)}, u32[]{:S(2)}) async-start(f32[128,2,128]{2,1,0:T(2,128)} %bitcast.4), calls=%async_computation | async-start | bytes 262144 | tf_op jit(solution)/shard_map/all_to_all | solution.py:447
  54.7 18.3 %collective-permute-start.16 = (f32[200,128]{1,0:T(8,128)S(1)}, f32[200,128]{1,0:T(8,128)S(1)}, u32[]{:S(2)}, u32[]{:S(2)}) collective-permute-start(f32[200,128]{1,0:T(8,128)S(1)} %get-tuple-element.58), channel_id=1, source_target_pairs={{0,8},{8,16},{16,24},{24,32},{32,40},{40,48},{48,56},{56,64},{64,7... | collective-permute-start | bytes 307208 | tf_op jit(solution)/shard_map/ppermute | solution.py:25
  54.8 18.3 %collective-permute-start.17 = (f32[100,128]{1,0:T(8,128)S(1)}, f32[100,128]{1,0:T(8,128)S(1)}, u32[]{:S(2)}, u32[]{:S(2)}) collective-permute-start(f32[100,128]{1,0:T(8,128)S(1)} %get-tuple-element.59), channel_id=1, source_target_pairs={{0,1},{1,2},{2,3},{3,4},{4,5},{5,6},{6,7},{7,0},{8,9},{9,10},{10,1... | collective-permute-start | bytes 153608 | tf_op jit(solution)/shard_map/ppermute | solution.py:25
  55.9 6.6 %collective-permute-start.12 = (f32[40,128]{1,0:T(8,128)S(1)}, f32[40,128]{1,0:T(8,128)S(1)}, u32[]{:S(2)}, u32[]{:S(2)}) collective-permute-start(f32[40,128]{1,0:T(8,128)S(1)} %get-tuple-element.50.refs_0_), channel_id=1, source_target_pairs={{0,24},{8,16},{16,8},{24,0},{32,56},{40,48},{48,40},{56,32},{64,88... | collective-permute-start | bytes 61448 | tf_op jit(solution)/shard_map/ppermute | solution.py:448
  60.4 5.3 %collective-permute-start.11 = (f32[40,128]{1,0:T(8,128)S(1)}, f32[40,128]{1,0:T(8,128)S(1)}, u32[]{:S(2)}, u32[]{:S(2)}) collective-permute-start(f32[40,128]{1,0:T(8,128)S(1)} %get-tuple-element.50.refs_0_), channel_id=1, source_target_pairs={{0,16},{8,24},{16,0},{24,8},{32,48},{40,56},{48,32},{56,40},{64,80... | collective-permute-start | bytes 61448 | tf_op jit(solution)/shard_map/ppermute | solution.py:448
  60.8 4.9 %collective-permute-start.10 = (f32[40,128]{1,0:T(8,128)S(1)}, f32[40,128]{1,0:T(8,128)S(1)}, u32[]{:S(2)}, u32[]{:S(2)}) collective-permute-start(f32[40,128]{1,0:T(8,128)S(1)} %get-tuple-element.50.refs_0_), channel_id=1, source_target_pairs={{0,8},{8,0},{16,24},{24,16},{32,40},{40,32},{48,56},{56,48},{64,72... | collective-permute-start | bytes 61448 | tf_op jit(solution)/shard_map/ppermute | solution.py:448
  65.7 5.9 %collective-permute-start.13 = (f32[32,128]{1,0:T(8,128)S(1)}, f32[32,128]{1,0:T(8,128)S(1)}, u32[]{:S(2)}, u32[]{:S(2)}) collective-permute-start(f32[32,128]{1,0:T(8,128)S(1)} %get-tuple-element.52), channel_id=1, source_target_pairs={{0,32},{8,40},{16,48},{24,56},{32,64},{40,72},{48,80},{56,88},{64,... | collective-permute-start | bytes 49160 | tf_op jit(solution)/shard_map/ppermute | solution.py:25
  67.5 5.2 %collective-permute-start.14 = (f32[32,128]{1,0:T(8,128)S(1)}, f32[32,128]{1,0:T(8,128)S(1)}, u32[]{:S(2)}, u32[]{:S(2)}) collective-permute-start(f32[32,128]{1,0:T(8,128)S(1)} %get-tuple-element.53), channel_id=1, source_target_pairs={{0,64},{8,72},{16,80},{24,88},{32,96},{40,104},{48,112},{56,120},{... | collective-permute-start | bytes 49160 | tf_op jit(solution)/shard_map/ppermute | solution.py:25
  69.1 4.0 %collective-permute-start.15 = (f32[32,128]{1,0:T(8,128)S(1)}, f32[32,128]{1,0:T(8,128)S(1)}, u32[]{:S(2)}, u32[]{:S(2)}) collective-permute-start(f32[32,128]{1,0:T(8,128)S(1)} %get-tuple-element.54), channel_id=1, source_target_pairs={{0,96},{8,104},{16,112},{24,120},{32,0},{40,8},{48,16},{56,24},{64... | collective-permute-start | bytes 49160 | tf_op jit(solution)/shard_map/ppermute | solution.py:25
  73.1 1.3 %copy-start.2 = (f32[2624,128]{1,0:T(8,128)S(1)}, f32[2624,128]{1,0:T(8,128)}, u32[]{:S(2)}) copy-start(f32[2624,128]{1,0:T(8,128)} %copy-done.1) | copy-start | bytes 4030468
  (5 other events, 5.2 us)

commit v4 on v3

--- a/solution.py
+++ b/solution.py
@@ -178,7 +178,7 @@
     return jnp.sum(tile, 0, keepdims=True)
 
 
-def second_kernel(p_ref, rhs_ref, snx, sfx, sny, sfy, rnx, rfx, rny, rfy, k_ref, m_ref, wh_ref, wl_ref,
+def second_kernel(p_ref, rhs_ref, rfx, rfy, rny, rnx, snx, sfx, sny, sfy, k_ref, m_ref, wh_ref, wl_ref,
                   v1_ref, p1_ref, tnx, tfx, tny, tfy, sums_ref, ux, uy, upx, lowx, upy, lowy):
     assemble(p_ref, snx, sfx, sny, sfy, rnx, rfx, rny, rfy, v1_ref, ux, uy)
     v0 = rhs_ref[...]
@@ -193,9 +193,11 @@
     route(is_even("gy"), upy, lowy, tny, tfy)
 
 
-def third_kernel(p_ref, v1_ref, snx, sfx, sny, sfy, rnx, rfx, rny, rfy, sums_ref, k_ref, m_ref, wh_ref, wl_ref,
-                 v2_ref, p2_ref, upx, upy, loads_ref, mom_ref, ux, uy):
+def third_kernel(p_ref, v1_ref, rfx, rfy, rny, rnx, snx, sfx, sny, sfy, sums_ref, k_ref, m_ref, wh_ref, wl_ref,
+                 v2_out, p2_out, upx, upy, loads_ref, v2_ref, p2_ref, ux, uy, v2_sem, p2_sem):
     assemble(p_ref, snx, sfx, sny, sfy, rnx, rfx, rny, rfy, v2_ref, ux, uy)
+    v2_copy = pltpu.make_async_copy(v2_ref.at[:ROWS], v2_out, v2_sem)
+    v2_copy.start()
     v1 = v1_ref[:ROWS]
     v2 = v2_ref[:ROWS]
     loads_ref[0:16] = sums_ref[0:16]
@@ -203,29 +205,35 @@
     m3 = node_sum(v1 * v2)
     m4 = node_sum(v2 * v2)
     apply_operator(v2_ref, ux, uy, k_ref, m_ref, wh_ref, wl_ref, p2_ref, upx, None, upy, None)
+    p2_copy = pltpu.make_async_copy(p2_ref, p2_out, p2_sem)
+    p2_copy.start()
     p2 = p2_ref[...]
     above = upx[...]
     loads_ref[24:32] = node_sum(p2)
     loads_ref[32:40] = node_sum(above)
     energy = node_sum(v2_ref[:ROWS] * p2) + node_sum(ux[: A * LY] * above)
     tail = row(uy[: A * LX] * upy[...])
-    tile = [row(sums_ref[16 + 8 * k : 24 + 8 * k]) for k in range(3)]
-    tile = jnp.concatenate(tile + [row(m3), row(m4), row(energy) + tail, jnp.zeros((2, LZ), f32)], 0)
-    for lanes in (64, 32, 16):
-        tile = tile + pltpu.roll(tile, lanes, 1)
-    lane = lax.broadcasted_iota(jnp.int32, (8, LZ), 1)
-    moment = lax.broadcasted_iota(jnp.int32, (8, LZ), 0)
-    packed = row(jnp.where(lax.div(lane, 16) == moment, tile, 0.0))
-    pair = jnp.concatenate([packed, row(upy[...])] * 4, 0)
-    for at in range(0, mom_ref.shape[0], 8):
-        mom_ref[at : at + 8] = pair
-
-
-def weigh_kernel(own, near, far, both, *outs, table):
+    for k in range(3):
+        loads_ref[40 + k : 41 + k] = row(sums_ref[16 + 8 * k : 24 + 8 * k])
+    loads_ref[43:44] = row(m3)
+    loads_ref[44:45] = row(m4)
+    loads_ref[45:46] = row(energy) + tail
+    loads_ref[46:47] = row(upy[...])
+    loads_ref[47:48] = jnp.zeros((1, LZ), f32)
+    v2_copy.wait()
+    p2_copy.wait()
+
+
+def weigh_kernel(own, near, far, both, upx, upy, *outs, table, ny):
+    *outs, mom_ref, cx_ref, cy_ref = outs
+    cx_ref[...] = upx[...]
+    cy_ref[...] = upy[...]
     nx = len(table)
-    q = lax.rem(lax.axis_index("gx"), 4)
+    me = lax.axis_index("gx")
+    q = lax.rem(me, 4)
     low, high = lax.rem(q, 2) == 0, q < 2
     one, two = jnp.where(low, 1, -1), jnp.where(high, 2, -2)
+    sources = ((own, 0, (0,)), (near, one, (1, -1)), (far, two, (2, -2)), (both, one + two, (3, 1, -1, -3)))
 
     def pick(at, shift, span):
         value = jnp.float32(table[(at - span[0]) % nx])
@@ -233,15 +241,28 @@
             value = jnp.where(shift == s, table[(at - s) % nx], value)
         return value
 
+    tile = own[40:48] + near[40:48] + far[40:48] + both[40:48]
+    for lanes in (64, 32, 16):
+        tile = tile + pltpu.roll(tile, lanes, 1)
+    lane = lax.broadcasted_iota(jnp.int32, (8, LZ), 1)
+    moment = lax.broadcasted_iota(jnp.int32, (8, LZ), 0)
+    packed = row(jnp.where((lax.div(lane, 16) == moment) & (moment < 6), tile, 0.0))
+    groups = nx // 4
     for z, out in enumerate(outs):
         total = [0.0] * 4
-        for ref, shift, span in ((own, 0, (0,)), (near, one, (1, -1)), (far, two, (2, -2)), (both, one + two, (3, 1, -1, -3))):
+        edge = 0.0
+        for ref, shift, span in sources:
             w = pick(4 * z, shift, span)
             for k in range(4):
                 total[k] = total[k] + ref[k * 8 : k * 8 + 8] * w
             total[3] = total[3] + ref[32:40] * pick(4 * z - 1, shift, span)
+            edge = edge + ref[46:47] * w
         for k in range(4):
             out[k * 8 : k * 8 + 8] = total[k]
+        pair = jnp.concatenate([packed, edge] * 4, 0)
+        first = lax.rem(lax.div(me, 4) + z, groups) * (2 * ny)
+        for at in range(0, 2 * ny, 8):
+            mom_ref[pl.ds(pl.multiple_of(first + at, 8), 8), :] = pair
 
 
 def two_sum(a, b):
@@ -334,18 +355,21 @@
     return plain(iterate), plain(residual)
 
 
-def last_kernel(prolong_ref, got_ref, c0, c1, c2, c3, inv_ref, rhs_ref, v1_ref, v2_ref, p2_ref, rx_ref, ry_ref,
-                sol_ref, res_ref, coarse_ref, *, table, ny):
-    nx = len(table)
+def last_kernel(prolong_ref, got_ref, c0, c1, c2, c3, inv_ref, rhs_ref, v1_ref, v2_hbm, p2_hbm, rx_ref, ry_ref,
+                sol_hbm, res_hbm, coarse_ref, v2_ref, p2_ref, sol_ref, res_ref, in_sems, out_sems, *, ny):
+    fetches = []
+    for f in range(F):
+        rows = pl.ds(f * FACE, FACE)
+        for i, (src, dst) in enumerate(((v2_hbm, v2_ref), (p2_hbm, p2_ref))):
+            fetches.append(pltpu.make_async_copy(src.at[rows], dst.at[rows], in_sems.at[2 * f + i]))
+            fetches[-1].start()
     x, d = conjugate_gradient(*moments(got_ref[...]))
     inv = inv_ref[0:1, 0:1]
     x = [t * inv for t in x]
-    me = lax.axis_index("gx")
     below = lax.rem(lax.axis_index("gy") + ny - 1, ny)
     edge = jnp.zeros((1, LZ), f32)
-    for offset, weight in enumerate(table):
-        slab = lax.rem(me + nx - offset, nx)
-        edge = edge + got_ref[pl.ds(2 * (slab * ny + below) + 1, 1), :] * weight
+    for z in range(got_ref.shape[0] // (2 * ny)):
+        edge = edge + got_ref[pl.ds(2 * (z * ny + below) + 1, 1), :]
     circ = [c0[k * 8 : k * 8 + 8] + c1[k * 8 : k * 8 + 8] + c2[k * 8 : k * 8 + 8] + c3[k * 8 : k * 8 + 8] for k in range(4)]
     at_first = lax.broadcasted_iota(jnp.int32, (LY, LZ), 0) == 0
     circ[3] = circ[3] + jnp.where(at_first, jnp.broadcast_to(edge, (LY, LZ)), 0.0)
@@ -353,7 +377,10 @@
     coarse_ref[...] = coarse
     x = [jnp.broadcast_to(t, (LY, LZ)) for t in x]
     d = [jnp.broadcast_to(t, (LY, LZ)) for t in d]
+    stores = []
     for f in range(F):
+        fetches[2 * f].wait()
+        fetches[2 * f + 1].wait()
         for a in range(A):
             at = (f * A + a) * CELLS
             spread = coarse * prolong_ref[f, a]
@@ -365,8 +392,15 @@
                     img = img + rx_ref[a * LY : (a + 1) * LY, :]
                 sol_ref[rows, :] = x[0] * v0 + x[1] * v1 + x[2] * v2 + spread
                 res_ref[rows, :] = d[0] * v0 + d[1] * v1 + d[2] * v2 + d[3] * img
-    first = pl.ds(FACE, A * LX, stride=LY)
-    res_ref[first, :] = res_ref[first, :] + d[3][0:1] * ry_ref[...]
+        if f == 1:
+            first = pl.ds(FACE, A * LX, stride=LY)
+            res_ref[first, :] = res_ref[first, :] + d[3][0:1] * ry_ref[...]
+        rows = pl.ds(f * FACE, FACE)
+        for i, (src, dst) in enumerate(((sol_ref, sol_hbm), (res_ref, res_hbm))):
+            stores.append(pltpu.make_async_copy(src.at[rows], dst.at[rows], out_sems.at[2 * f + i]))
+            stores[-1].start()
+    for store in stores:
+        store.wait()
 
 
 def jacobi_weights(n):
@@ -407,7 +441,7 @@
             bound,
             out_shape=outs,
             in_specs=specs,
-            out_specs=[VM] * len(outs),
+            out_specs=[ANY if isinstance(o, pl.MemoryRef) else VM for o in outs],
             scratch_shapes=list(scratch),
             compiler_params=PARAMS,
             name=name,
@@ -418,7 +452,7 @@
         far_y = far_swap(s[3], "gy")
         near_y = near_swap(s[2], "gy")
         near_x = near_swap(s[0], "gx")
-        return [near_x, far_x, near_y, far_y]
+        return [far_x, far_y, near_y, near_x]
 
     hbm = pltpu.with_memory_space_constraint(rhs, pltpu.HBM)
     fx, fy = call(
@@ -435,25 +469,32 @@
     )
     r = swap(s)
     v1, p1, *s, sums = call(
-        second_kernel, "second", [p0, rhs2, *s, *r, k2, m2, wh, wl],
+        second_kernel, "second", [p0, rhs2, *r, *s, k2, m2, wh, wl],
         [struct(PADDED, LZ), struct(ROWS, LZ)] + sends + [struct(40, LZ)], upper + edges,
     )
     r = swap(s)
-    v2, p2, upx, upy, loads, mom = call(
-        third_kernel, "third", [p1, v1, *s, *r, sums, k2, m2, wh, wl],
-        [struct(PADDED, LZ), struct(ROWS, LZ), struct(vx, LZ), struct(vy, LZ), struct(40, LZ), struct(nx * ny * 2, LZ)],
-        upper,
-    )
-    got = lax.all_to_all(mom.reshape(nx * ny, 2, LZ), ("gx", "gy"), 0, 0, tiled=True).reshape(nx * ny * 2, LZ)
+    dma = pltpu.SemaphoreType.DMA
+    v2, p2, upx, upy, loads = call(
+        third_kernel, "third", [p1, v1, *r, *s, sums, k2, m2, wh, wl],
+        [pltpu.HBM((ROWS, LZ), f32)] * 2 + [struct(vx, LZ), struct(vy, LZ), struct(48, LZ)],
+        [field[0], pltpu.VMEM((ROWS, LZ), f32)] + upper + [dma, dma],
+    )
+    table = [float(t) for t in jacobi_weights(nx)]
     group = [lax.ppermute(loads, "gx", [(i, i ^ b) for i in range(nx)]) for b in (1, 2, 3)]
+    *pieces, mom, upx, upy = call(
+        weigh_kernel, "weigh", [loads, *group, upx, upy],
+        [struct(32, LZ)] * (nx // 4) + [struct(nx // 4 * ny * 2, LZ), struct(vx, LZ), struct(vy, LZ)], table=table, ny=ny,
+    )
+    coarse = [pieces[0]] + [shifted(p, "gx", 4 * z) for z, p in enumerate(pieces) if z]
+    alike = [[(4 * z + q) * ny + y for z in range(nx // 4) for y in range(ny)] for q in range(4)]
+    got = lax.all_to_all(mom.reshape(-1, 2, LZ), ("gx", "gy"), 0, 0, tiled=True, axis_index_groups=alike).reshape(mom.shape)
     rx = shifted(upx, "gx", 1)
     ry = shifted(upy, "gy", 1)
-    table = [float(t) for t in jacobi_weights(nx)]
-    pieces = call(weigh_kernel, "weigh", [loads, *group], [struct(32, LZ)] * (nx // 4), table=table)
-    coarse = [pieces[0]] + [shifted(p, "gx", 4 * z) for z, p in enumerate(pieces) if z]
+    v2, p2 = (pltpu.with_memory_space_constraint(v, pltpu.HBM) for v in (v2, p2))
     sol, res, coarse = call(
-        last_kernel, "last", [(prolong, SM), got, *coarse, inv, rhs2, v1, v2, p2, rx, ry],
-        [struct(ROWS, LZ), struct(ROWS, LZ), struct(LY, LZ)], table=table, ny=ny,
+        last_kernel, "last", [(prolong, SM), got, *coarse, inv, rhs2, v1, (v2, ANY), (p2, ANY), rx, ry],
+        [pltpu.HBM((ROWS, LZ), f32)] * 2 + [struct(LY, LZ)],
+        [pltpu.VMEM((ROWS, LZ), f32)] * 4 + [pltpu.SemaphoreType.DMA((6,))] * 2, ny=ny,
     )
     return sol.reshape(rhs.shape), res.reshape(rhs.shape), coarse[None]
 

time: 79.7 us -> 75.4 us (0.946)
  local copies, waits for them, and re-layouts: 6.57 us -> 1.86 us
  starting transfers between devices: 39.1 us -> 36.2 us
  Pallas kernels: 19.1 us -> 21.4 us
    unnamed x20 -> x12, local copies, waits for them, and re-layouts: 6.56 us -> 1.84 us
    ppermute x4, waiting for transfers between devices: 5.07 us -> 9.71 us  [far_swap(): return lax.ppermute(value, axis, pairs)]
    ppermute x3, waiting for transfers between devices: 4.86 us -> 2.06 us  [shards(): lax.ppermute(loads, 'gx', [(i, i ^ b) for i in range(nx)])]
    pallas_call x7, Pallas kernels: 19.1 us -> 21.4 us  [call(): pl.pallas_call(bound, out_shape=outs, in_specs=specs, out_specs=[ANY if i...]
    ppermute x4, waiting for transfers between devices: 1.98 us -> 0.01 us  [near_swap(): return lax.ppermute(value, axis, [(i, i ^ 1) for i in range(n)])]
    ppermute x4, starting transfers between devices: 12 us -> 10.1 us  [far_swap(): return lax.ppermute(value, axis, pairs)]
    all_to_all x1, starting transfers between devices: 5.19 us -> 7.06 us  [shards(): lax.all_to_all(mom.reshape(-1, 2, LZ), ('gx', 'gy'), 0, 0, tiled=True, ax...]
    ppermute x3, starting transfers between devices: 4.89 us -> 3.44 us  [shards(): lax.ppermute(loads, 'gx', [(i, i ^ b) for i in range(nx)])]
  transfers between devices with their start and end apart: 19 -> 19, of which waited for: 7 -> 6; matrix products, arithmetic and copies ran while one was open for 0% -> 0% of each run, Pallas kernels for 1% -> 1%
where the time goes in v4:
time: 75.4 us; the launch traced here: 74.4 us
  starting transfers between devices  36.2 us (48%)
  Pallas kernels  21.4 us (28%)
  waiting for transfers between devices  14.1 us (19%)
  local copies, waits for them, and re-layouts  1.86 us (2%)
  between operations  0.96 us (1%)
    pallas_call x7, Pallas kernels, call(): pl.pallas_call(bound, out_shape=outs, in_specs=specs, out_specs=[ANY if i...  21.4 us
    ppermute x7, starting transfers between devices, shifted(): return lax.ppermute(value, axis, [(i, (i + by) % n) for i in range(n)])  15.5 us
    ppermute x4, starting transfers between devices, far_swap(): return lax.ppermute(value, axis, pairs)  10.1 us
    ppermute x4, waiting for transfers between devices, far_swap(): return lax.ppermute(value, axis, pairs)  9.71 us
    all_to_all x1, starting transfers between devices, shards(): lax.all_to_all(mom.reshape(-1, 2, LZ), ('gx', 'gy'), 0, 0, tiled=True, ax...  7.06 us
    ppermute x3, starting transfers between devices, shards(): lax.ppermute(loads, 'gx', [(i, i ^ b) for i in range(nx)])  3.44 us
    ppermute x7, waiting for transfers between devices, shifted(): return lax.ppermute(value, axis, [(i, (i + by) % n) for i in range(n)])  2.32 us
    ppermute x3, waiting for transfers between devices, shards(): lax.ppermute(loads, 'gx', [(i, i ^ b) for i in range(nx)])  2.06 us
  transfers between devices with their start and end apart: 19, of which 6 were waited for; matrix products, arithmetic and copies ran while one was open for 0% of the time, Pallas kernels for 1%

profile of v4, /device:TPU:0, one launch (start us, length us, event | category | flops | bytes accessed | tf_op | source)
XLA Modules:
  0.0 74.4 jit_solution(7062818224635078743)
XLA Ops:
  0.7 1.0 %edges.1 = (f32[25,8,128]{2,1,0:T(8,128)S(1)}, f32[25,4,128]{2,1,0:T(4,128)S(1)}) custom-call(f32[3,25,4,8,128]{4,3,2,1,0:T(8,128)} %refs_0_.3), custom_call_target="tpu_custom_call" | custom-call | tf_op jit(solution)/shard_map/edges/pallas_call | solution.py:440
  1.7 6.1 %collective-permute-start = (f32[200,128]{1,0:T(8,128)S(1)}, f32[200,128]{1,0:T(8,128)S(1)}, u32[]{:S(2)}, u32[]{:S(2)}) collective-permute-start(f32[200,128]{1,0:T(8,128)S(1)} %bitcast.19), channel_id=1, source_target_pairs={{0,120},{8,0},{16,8},{24,16},{32,24},{40,32},{48,40},{56,48},{64,5... | collective-permute-start | bytes 307208 | tf_op jit(solution)/shard_map/ppermute | solution.py:25
  7.8 3.1 %collective-permute-start.1 = (f32[100,128]{1,0:T(8,128)S(1)}, f32[100,128]{1,0:T(8,128)S(1)}, u32[]{:S(2)}, u32[]{:S(2)}) collective-permute-start(f32[100,128]{1,0:T(8,128)S(1)} %reshape.35), channel_id=1, source_target_pairs={{0,7},{1,0},{2,1},{3,2},{4,3},{5,4},{6,5},{7,6},{8,15},{9,8},{10,9... | collective-permute-start | bytes 153608 | tf_op jit(solution)/shard_map/ppermute | solution.py:25
  10.9 0.9 %copy-done.1 = f32[150,150]{1,0:T(8,128)S(1)} copy-done((f32[150,150]{1,0:T(8,128)S(1)}, f32[150,150]{1,0:T(8,128)}, u32[]{:S(2)}) %copy-start.1) | copy-done | bytes 90024
  11.8 0.9 %copy-done.2 = f32[150,150]{1,0:T(8,128)S(1)} copy-done((f32[150,150]{1,0:T(8,128)S(1)}, f32[150,150]{1,0:T(8,128)}, u32[]{:S(2)}) %copy-start.2) | copy-done | bytes 90024
  13.4 4.2 %first.1 = (f32[2400,128]{1,0:T(8,128)S(1)}, f32[200,128]{1,0:T(8,128)S(1)}, f32[200,128]{1,0:T(8,128)S(1)}, f32[100,128]{1,0:T(8,128)S(1)}, f32[100,128]{1,0:T(8,128)S(1)}) custom-call(f32[2400,128]{1,0:T(8,128)S(1)} %bitcast.9, f32[200,128]{1,0:T(8,128)S(1)} %collective-permute-done.refs_1_, f32[100,128]{1,0:T(8,128)S(1)} %collective-permute-done.1.refs_2_, ...), custom_call_target="tpu_custom_call" | custom-call | tf_op jit(solution)/shard_map/first/pallas_call | solution.py:440
  17.6 2.2 %collective-permute-start.2 = (f32[200,128]{1,0:T(8,128)S(1)}, f32[200,128]{1,0:T(8,128)S(1)}, u32[]{:S(2)}, u32[]{:S(2)}) collective-permute-start(f32[200,128]{1,0:T(8,128)S(1)} %get-tuple-element.40.refs_7_), channel_id=1, source_target_pairs={{0,120},{8,16},{16,8},{24,32},{32,24},{40,48},{48,40},{56,64},{64,... | collective-permute-start | bytes 307208 | tf_op jit(solution)/shard_map/ppermute | solution.py:36
  19.7 3.0 %collective-permute-start.3 = (f32[100,128]{1,0:T(8,128)S(1)}, f32[100,128]{1,0:T(8,128)S(1)}, u32[]{:S(2)}, u32[]{:S(2)}) collective-permute-start(f32[100,128]{1,0:T(8,128)S(1)} %get-tuple-element.41.refs_9_), channel_id=1, source_target_pairs={{0,7},{1,2},{2,1},{3,4},{4,3},{5,6},{6,5},{7,0},{8,15},{9,10},{10,... | collective-permute-start | bytes 153608 | tf_op jit(solution)/shard_map/ppermute | solution.py:36
  22.8 4.3 %collective-permute-done.3.refs_3_ = f32[100,128]{1,0:T(8,128)S(1)} collective-permute-done((f32[100,128]{1,0:T(8,128)S(1)}, f32[100,128]{1,0:T(8,128)S(1)}, u32[]{:S(2)}, u32[]{:S(2)}) %collective-permute-start.3) | collective-permute-done | bytes 51232 | tf_op jit(solution)/shard_map/ppermute | solution.py:36
  27.1 4.5 %second.1 = (f32[2624,128]{1,0:T(8,128)S(1)}, f32[2400,128]{1,0:T(8,128)S(1)}, f32[200,128]{1,0:T(8,128)S(1)}, f32[200,128]{1,0:T(8,128)S(1)}, f32[100,128]{1,0:...) custom-call(f32[2400,128]{1,0:T(8,128)S(1)} %get-tuple-element.39.refs_0_, f32[2400,128]{1,0:T(8,128)S(1)} %bitcast.10, ...), custom_call_target="tpu_custom_call" | custom-call | tf_op jit(solution)/shard_map/second/pallas_call | solution.py:440
  31.6 3.6 %collective-permute-start.6 = (f32[200,128]{1,0:T(8,128)S(1)}, f32[200,128]{1,0:T(8,128)S(1)}, u32[]{:S(2)}, u32[]{:S(2)}) collective-permute-start(f32[200,128]{1,0:T(8,128)S(1)} %get-tuple-element.46.refs_7_), channel_id=1, source_target_pairs={{0,120},{8,16},{16,8},{24,32},{32,24},{40,48},{48,40},{56,64},{64,... | collective-permute-start | bytes 307208 | tf_op jit(solution)/shard_map/ppermute | solution.py:36
  35.2 1.3 %collective-permute-start.7 = (f32[100,128]{1,0:T(8,128)S(1)}, f32[100,128]{1,0:T(8,128)S(1)}, u32[]{:S(2)}, u32[]{:S(2)}) collective-permute-start(f32[100,128]{1,0:T(8,128)S(1)} %get-tuple-element.47.refs_9_), channel_id=1, source_target_pairs={{0,7},{1,2},{2,1},{3,4},{4,3},{5,6},{6,5},{7,0},{8,15},{9,10},{10,... | collective-permute-start | bytes 153608 | tf_op jit(solution)/shard_map/ppermute | solution.py:36
  36.5 5.4 %collective-permute-done.7.refs_3_ = f32[100,128]{1,0:T(8,128)S(1)} collective-permute-done((f32[100,128]{1,0:T(8,128)S(1)}, f32[100,128]{1,0:T(8,128)S(1)}, u32[]{:S(2)}, u32[]{:S(2)}) %collective-permute-start.7) | collective-permute-done | bytes 51232 | tf_op jit(solution)/shard_map/ppermute | solution.py:36
  41.9 5.7 %third.1 = (f32[2400,128]{1,0:T(8,128)}, f32[2400,128]{1,0:T(8,128)}, f32[200,128]{1,0:T(8,128)S(1)}, f32[100,128]{1,0:T(8,128)S(1)}, f32[48,128]{1,0:T(8,128)S(1)}) custom-call(f32[2400,128]{1,0:T(8,128)S(1)} %get-tuple-element.44.refs_0_, f32[2624,128]{1,0:T(8,128)S(1)} %get-tuple-element.45.refs_1_.refs_8_, ...), custom_call_target="tpu_custom_call" | custom-call | tf_op jit(solution)/shard_map/third/pallas_call | solution.py:440
  47.7 2.5 %collective-permute-start.11 = (f32[48,128]{1,0:T(8,128)S(1)}, f32[48,128]{1,0:T(8,128)S(1)}, u32[]{:S(2)}, u32[]{:S(2)}) collective-permute-start(f32[48,128]{1,0:T(8,128)S(1)} %get-tuple-element.51.refs_0_), channel_id=1, source_target_pairs={{0,16},{8,24},{16,0},{24,8},{32,48},{40,56},{48,32},{56,40},{64,80... | collective-permute-start | bytes 73736 | tf_op jit(solution)/shard_map/ppermute | solution.py:483
  50.2 0.9 %collective-permute-start.10 = (f32[48,128]{1,0:T(8,128)S(1)}, f32[48,128]{1,0:T(8,128)S(1)}, u32[]{:S(2)}, u32[]{:S(2)}) collective-permute-start(f32[48,128]{1,0:T(8,128)S(1)} %get-tuple-element.51.refs_0_), channel_id=1, source_target_pairs={{0,8},{8,0},{16,24},{24,16},{32,40},{40,32},{48,56},{56,48},{64,72... | collective-permute-start | bytes 73736 | tf_op jit(solution)/shard_map/ppermute | solution.py:483
  51.1 1.4 %collective-permute-done.12.refs_3_ = f32[48,128]{1,0:T(8,128)S(1)} collective-permute-done((f32[48,128]{1,0:T(8,128)S(1)}, f32[48,128]{1,0:T(8,128)S(1)}, u32[]{:S(2)}, u32[]{:S(2)}) %collective-permute-start.12) | collective-permute-done | bytes 24608 | tf_op jit(solution)/shard_map/ppermute | solution.py:483
  54.3 7.1 %all-to-all-start = ((f32[32,2,128]{2,1,0:T(2,128)}), f32[32,2,128]{2,1,0:T(2,128)S(1)}, u32[]{:S(2)}, u32[]{:S(2)}) async-start(f32[32,2,128]{2,1,0:T(2,128)} %bitcast.4), calls=%async_computation | async-start | bytes 65536 | tf_op jit(solution)/shard_map/all_to_all | solution.py:490
  61.4 1.9 %collective-permute-start.13 = (f32[32,128]{1,0:T(8,128)S(1)}, f32[32,128]{1,0:T(8,128)S(1)}, u32[]{:S(2)}, u32[]{:S(2)}) collective-permute-start(f32[32,128]{1,0:T(8,128)S(1)} %get-tuple-element.56), channel_id=1, source_target_pairs={{0,32},{8,40},{16,48},{24,56},{32,64},{40,72},{48,80},{56,88},{64,... | collective-permute-start | bytes 49160 | tf_op jit(solution)/shard_map/ppermute | solution.py:25
  63.3 2.7 %collective-permute-start.14 = (f32[32,128]{1,0:T(8,128)S(1)}, f32[32,128]{1,0:T(8,128)S(1)}, u32[]{:S(2)}, u32[]{:S(2)}) collective-permute-start(f32[32,128]{1,0:T(8,128)S(1)} %get-tuple-element.57), channel_id=1, source_target_pairs={{0,64},{8,72},{16,80},{24,88},{32,96},{40,104},{48,112},{56,120},{... | collective-permute-start | bytes 49160 | tf_op jit(solution)/shard_map/ppermute | solution.py:25
  66.0 1.4 %collective-permute-start.15 = (f32[32,128]{1,0:T(8,128)S(1)}, f32[32,128]{1,0:T(8,128)S(1)}, u32[]{:S(2)}, u32[]{:S(2)}) collective-permute-start(f32[32,128]{1,0:T(8,128)S(1)} %get-tuple-element.58), channel_id=1, source_target_pairs={{0,96},{8,104},{16,112},{24,120},{32,0},{40,8},{48,16},{56,24},{64... | collective-permute-start | bytes 49160 | tf_op jit(solution)/shard_map/ppermute | solution.py:25
  67.4 1.1 %collective-permute-done.14.refs_4_ = f32[32,128]{1,0:T(8,128)S(1)} collective-permute-done((f32[32,128]{1,0:T(8,128)S(1)}, f32[32,128]{1,0:T(8,128)S(1)}, u32[]{:S(2)}, u32[]{:S(2)}) %collective-permute-start.14) | collective-permute-done | bytes 16416 | tf_op jit(solution)/shard_map/ppermute | solution.py:25
  68.5 1.2 %collective-permute-done.15.refs_5_ = f32[32,128]{1,0:T(8,128)S(1)} collective-permute-done((f32[32,128]{1,0:T(8,128)S(1)}, f32[32,128]{1,0:T(8,128)S(1)}, u32[]{:S(2)}, u32[]{:S(2)}) %collective-permute-start.15) | collective-permute-done | bytes 16416 | tf_op jit(solution)/shard_map/ppermute | solution.py:25
  69.7 4.5 %last.1 = (f32[2400,128]{1,0:T(8,128)}, f32[2400,128]{1,0:T(8,128)}, f32[8,128]{1,0:T(8,128)}) custom-call(f32[3,25]{1,0:T(4,128)S(1)} %copy-done.5, f32[64,128]{1,0:T(8,128)S(1)} %bitcast.18, f32[32,128]{1,0:T(8,128)S(1)} %get-tuple-element.55.refs_2_, f32[32,128]{1,0:T(8,128)S(1)} %collective-permute-done.13.refs_3_, ...), custom_call_target="tpu_custom_call" | custom-call | tf_op jit(solution)/shard_map/last/pallas_call | solution.py:440
  (34 shorter events, 2.6 us)
Async XLA Ops:
  0.6 12.7 %copy-start = (f32[3,25,4,8,128]{4,3,2,1,0:T(8,128)S(1)}, f32[3,25,4,8,128]{4,3,2,1,0:T(8,128)}, u32[]{:S(2)}) copy-start(f32[3,25,4,8,128]{4,3,2,1,0:T(8,128)} %refs_0_.3) | copy-start | bytes 3686404
  0.6 12.7 %copy-start.4 = (f32[4,8,128]{2,1,0:T(8,128)S(1)}, f32[4,8,128]{2,1,0:T(8,128)}, u32[]{:S(2)}) copy-start(f32[4,8,128]{2,1,0:T(8,128)} %param.8) | copy-start | bytes 49156
  0.7 12.7 %copy-start.3 = (f32[4,8,128]{2,1,0:T(8,128)S(1)}, f32[4,8,128]{2,1,0:T(8,128)}, u32[]{:S(2)}) copy-start(f32[4,8,128]{2,1,0:T(8,128)} %param.7) | copy-start | bytes 49156
  1.7 11.7 %collective-permute-start = (f32[200,128]{1,0:T(8,128)S(1)}, f32[200,128]{1,0:T(8,128)S(1)}, u32[]{:S(2)}, u32[]{:S(2)}) collective-permute-start(f32[200,128]{1,0:T(8,128)S(1)} %bitcast.19), channel_id=1, source_target_pairs={{0,120},{8,0},{16,8},{24,16},{32,24},{40,32},{48,40},{56,48},{64,5... | collective-permute-start | bytes 307208 | tf_op jit(solution)/shard_map/ppermute | solution.py:25
  7.8 5.5 %collective-permute-start.1 = (f32[100,128]{1,0:T(8,128)S(1)}, f32[100,128]{1,0:T(8,128)S(1)}, u32[]{:S(2)}, u32[]{:S(2)}) collective-permute-start(f32[100,128]{1,0:T(8,128)S(1)} %reshape.35), channel_id=1, source_target_pairs={{0,7},{1,0},{2,1},{3,2},{4,3},{5,4},{6,5},{7,6},{8,15},{9,8},{10,9... | collective-permute-start | bytes 153608 | tf_op jit(solution)/shard_map/ppermute | solution.py:25
  10.9 0.9 %copy-start.1 = (f32[150,150]{1,0:T(8,128)S(1)}, f32[150,150]{1,0:T(8,128)}, u32[]{:S(2)}) copy-start(f32[150,150]{1,0:T(8,128)} %refs_0_.4) | copy-start | bytes 270004
  17.6 9.5 %collective-permute-start.2 = (f32[200,128]{1,0:T(8,128)S(1)}, f32[200,128]{1,0:T(8,128)S(1)}, u32[]{:S(2)}, u32[]{:S(2)}) collective-permute-start(f32[200,128]{1,0:T(8,128)S(1)} %get-tuple-element.40.refs_7_), channel_id=1, source_target_pairs={{0,120},{8,16},{16,8},{24,32},{32,24},{40,48},{48,40},{56,64},{64,... | collective-permute-start | bytes 307208 | tf_op jit(solution)/shard_map/ppermute | solution.py:36
  19.7 7.3 %collective-permute-start.5 = (f32[200,128]{1,0:T(8,128)S(1)}, f32[200,128]{1,0:T(8,128)S(1)}, u32[]{:S(2)}, u32[]{:S(2)}) collective-permute-start(f32[200,128]{1,0:T(8,128)S(1)} %get-tuple-element.43.refs_6_), channel_id=1, source_target_pairs={{0,8},{8,0},{16,24},{24,16},{32,40},{40,32},{48,56},{56,48},{64,72... | collective-permute-start | bytes 307208 | tf_op jit(solution)/shard_map/ppermute | solution.py:30
  19.7 7.3 %collective-permute-start.3 = (f32[100,128]{1,0:T(8,128)S(1)}, f32[100,128]{1,0:T(8,128)S(1)}, u32[]{:S(2)}, u32[]{:S(2)}) collective-permute-start(f32[100,128]{1,0:T(8,128)S(1)} %get-tuple-element.41.refs_9_), channel_id=1, source_target_pairs={{0,7},{1,2},{2,1},{3,4},{4,3},{5,6},{6,5},{7,0},{8,15},{9,10},{10,... | collective-permute-start | bytes 153608 | tf_op jit(solution)/shard_map/ppermute | solution.py:36
  22.8 4.3 %collective-permute-start.4 = (f32[100,128]{1,0:T(8,128)S(1)}, f32[100,128]{1,0:T(8,128)S(1)}, u32[]{:S(2)}, u32[]{:S(2)}) collective-permute-start(f32[100,128]{1,0:T(8,128)S(1)} %get-tuple-element.42.refs_8_), channel_id=1, source_target_pairs={{0,1},{1,0},{2,3},{3,2},{4,5},{5,4},{6,7},{7,6},{8,9},{9,8},{10,11... | collective-permute-start | bytes 153608 | tf_op jit(solution)/shard_map/ppermute | solution.py:30
  31.6 10.3 %collective-permute-start.6 = (f32[200,128]{1,0:T(8,128)S(1)}, f32[200,128]{1,0:T(8,128)S(1)}, u32[]{:S(2)}, u32[]{:S(2)}) collective-permute-start(f32[200,128]{1,0:T(8,128)S(1)} %get-tuple-element.46.refs_7_), channel_id=1, source_target_pairs={{0,120},{8,16},{16,8},{24,32},{32,24},{40,48},{48,40},{56,64},{64,... | collective-permute-start | bytes 307208 | tf_op jit(solution)/shard_map/ppermute | solution.py:36
  35.2 6.7 %collective-permute-start.9 = (f32[200,128]{1,0:T(8,128)S(1)}, f32[200,128]{1,0:T(8,128)S(1)}, u32[]{:S(2)}, u32[]{:S(2)}) collective-permute-start(f32[200,128]{1,0:T(8,128)S(1)} %get-tuple-element.49.refs_6_), channel_id=1, source_target_pairs={{0,8},{8,0},{16,24},{24,16},{32,40},{40,32},{48,56},{56,48},{64,72... | collective-permute-start | bytes 307208 | tf_op jit(solution)/shard_map/ppermute | solution.py:30
  35.2 6.7 %collective-permute-start.7 = (f32[100,128]{1,0:T(8,128)S(1)}, f32[100,128]{1,0:T(8,128)S(1)}, u32[]{:S(2)}, u32[]{:S(2)}) collective-permute-start(f32[100,128]{1,0:T(8,128)S(1)} %get-tuple-element.47.refs_9_), channel_id=1, source_target_pairs={{0,7},{1,2},{2,1},{3,4},{4,3},{5,6},{6,5},{7,0},{8,15},{9,10},{10,... | collective-permute-start | bytes 153608 | tf_op jit(solution)/shard_map/ppermute | solution.py:36
  36.5 5.4 %collective-permute-start.8 = (f32[100,128]{1,0:T(8,128)S(1)}, f32[100,128]{1,0:T(8,128)S(1)}, u32[]{:S(2)}, u32[]{:S(2)}) collective-permute-start(f32[100,128]{1,0:T(8,128)S(1)} %get-tuple-element.48.refs_8_), channel_id=1, source_target_pairs={{0,1},{1,0},{2,3},{3,2},{4,5},{5,4},{6,7},{7,6},{8,9},{9,8},{10,11... | collective-permute-start | bytes 153608 | tf_op jit(solution)/shard_map/ppermute | solution.py:30
  41.9 27.8 %copy-start.5 = (f32[3,25]{1,0:T(4,128)S(1)}, f32[3,25]{1,0:T(4,128)}, u32[]{:S(2)}) copy-start(f32[3,25]{1,0:T(4,128)} %refs_0_.5) | copy-start | bytes 904
  47.6 4.8 %collective-permute-start.12 = (f32[48,128]{1,0:T(8,128)S(1)}, f32[48,128]{1,0:T(8,128)S(1)}, u32[]{:S(2)}, u32[]{:S(2)}) collective-permute-start(f32[48,128]{1,0:T(8,128)S(1)} %get-tuple-element.51.refs_0_), channel_id=1, source_target_pairs={{0,24},{8,16},{16,8},{24,0},{32,56},{40,48},{48,40},{56,32},{64,88... | collective-permute-start | bytes 73736 | tf_op jit(solution)/shard_map/ppermute | solution.py:483
  47.7 5.4 %collective-permute-start.11 = (f32[48,128]{1,0:T(8,128)S(1)}, f32[48,128]{1,0:T(8,128)S(1)}, u32[]{:S(2)}, u32[]{:S(2)}) collective-permute-start(f32[48,128]{1,0:T(8,128)S(1)} %get-tuple-element.51.refs_0_), channel_id=1, source_target_pairs={{0,16},{8,24},{16,0},{24,8},{32,48},{40,56},{48,32},{56,40},{64,80... | collective-permute-start | bytes 73736 | tf_op jit(solution)/shard_map/ppermute | solution.py:483
  50.2 2.9 %collective-permute-start.10 = (f32[48,128]{1,0:T(8,128)S(1)}, f32[48,128]{1,0:T(8,128)S(1)}, u32[]{:S(2)}, u32[]{:S(2)}) collective-permute-start(f32[48,128]{1,0:T(8,128)S(1)} %get-tuple-element.51.refs_0_), channel_id=1, source_target_pairs={{0,8},{8,0},{16,24},{24,16},{32,40},{40,32},{48,56},{56,48},{64,72... | collective-permute-start | bytes 73736 | tf_op jit(solution)/shard_map/ppermute | solution.py:483
  54.0 15.7 %collective-permute-start.16 = (f32[200,128]{1,0:T(8,128)S(1)}, f32[200,128]{1,0:T(8,128)S(1)}, u32[]{:S(2)}, u32[]{:S(2)}) collective-permute-start(f32[200,128]{1,0:T(8,128)S(1)} %get-tuple-element.62), channel_id=1, source_target_pairs={{0,8},{8,16},{16,24},{24,32},{32,40},{40,48},{48,56},{56,64},{64,7... | collective-permute-start | bytes 307208 | tf_op jit(solution)/shard_map/ppermute | solution.py:25
  54.0 15.7 %collective-permute-start.17 = (f32[100,128]{1,0:T(8,128)S(1)}, f32[100,128]{1,0:T(8,128)S(1)}, u32[]{:S(2)}, u32[]{:S(2)}) collective-permute-start(f32[100,128]{1,0:T(8,128)S(1)} %get-tuple-element.63), channel_id=1, source_target_pairs={{0,1},{1,2},{2,3},{3,4},{4,5},{5,6},{6,7},{7,0},{8,9},{9,10},{10,1... | collective-permute-start | bytes 153608 | tf_op jit(solution)/shard_map/ppermute | solution.py:25
  54.3 15.4 %all-to-all-start = ((f32[32,2,128]{2,1,0:T(2,128)}), f32[32,2,128]{2,1,0:T(2,128)S(1)}, u32[]{:S(2)}, u32[]{:S(2)}) async-start(f32[32,2,128]{2,1,0:T(2,128)} %bitcast.4), calls=%async_computation | async-start | bytes 65536 | tf_op jit(solution)/shard_map/all_to_all | solution.py:490
  61.4 6.0 %collective-permute-start.13 = (f32[32,128]{1,0:T(8,128)S(1)}, f32[32,128]{1,0:T(8,128)S(1)}, u32[]{:S(2)}, u32[]{:S(2)}) collective-permute-start(f32[32,128]{1,0:T(8,128)S(1)} %get-tuple-element.56), channel_id=1, source_target_pairs={{0,32},{8,40},{16,48},{24,56},{32,64},{40,72},{48,80},{56,88},{64,... | collective-permute-start | bytes 49160 | tf_op jit(solution)/shard_map/ppermute | solution.py:25
  63.3 5.3 %collective-permute-start.14 = (f32[32,128]{1,0:T(8,128)S(1)}, f32[32,128]{1,0:T(8,128)S(1)}, u32[]{:S(2)}, u32[]{:S(2)}) collective-permute-start(f32[32,128]{1,0:T(8,128)S(1)} %get-tuple-element.57), channel_id=1, source_target_pairs={{0,64},{8,72},{16,80},{24,88},{32,96},{40,104},{48,112},{56,120},{... | collective-permute-start | bytes 49160 | tf_op jit(solution)/shard_map/ppermute | solution.py:25
  66.0 3.7 %collective-permute-start.15 = (f32[32,128]{1,0:T(8,128)S(1)}, f32[32,128]{1,0:T(8,128)S(1)}, u32[]{:S(2)}, u32[]{:S(2)}) collective-permute-start(f32[32,128]{1,0:T(8,128)S(1)} %get-tuple-element.58), channel_id=1, source_target_pairs={{0,96},{8,104},{16,112},{24,120},{32,0},{40,8},{48,16},{56,24},{64... | collective-permute-start | bytes 49160 | tf_op jit(solution)/shard_map/ppermute | solution.py:25
  (1 other events, 0.9 us)

commit v5 on v4

--- a/solution.py
+++ b/solution.py
@@ -8,12 +8,14 @@
 
 ITERS = 3
 SWEEPS = 8
-F, A, AP = 3, 25, 32
+F, A = 3, 25
+B = 24
+LAST = 6 * B
+OUT, IN = LAST + 8, LAST + 16
 LX, LY, LZ = 4, 8, 128
 CELLS = LX * LY
 FACE = A * CELLS
 ROWS = F * FACE
-PADDED = ROWS + (AP - A) * CELLS
 f32, bf16 = jnp.float32, jnp.bfloat16
 VM = pl.BlockSpec(memory_space=pltpu.VMEM)
 SM = pl.BlockSpec(memory_space=pltpu.SMEM)
@@ -42,59 +44,80 @@
     return hi, lo
 
 
-def apply_operator(v_ref, ux_ref, uy_ref, k_ref, m_ref, wh_ref, wl_ref, out_ref, up_x, low_x, up_y, low_y):
-    wh = wh_ref[...]
-    wl = wl_ref[...]
+def apply_operator(v_ref, ux_ref, uy_ref, k_ref, m_ref, w_ref, out_ref, up_x, low_x, up_y, low_y, last_in, last_out):
+    w_all = w_ref[...]
+    at_first = lax.broadcasted_iota(jnp.int32, (LY, LZ), 0) == 0
+    last_in[LAST // B * LY :] = jnp.zeros((2 * LY, LZ), f32)
 
     def face(f, x, y):
         if f == 0 and x == LX:
-            return ux_ref[pl.ds(y, AP, stride=LY), :]
+            return ux_ref[pl.ds(y, B, stride=LY), :]
         if f == 1 and y == LY:
-            return uy_ref[pl.ds(x, AP, stride=LX), :]
-        return v_ref[pl.ds(f * FACE + x * LY + y, AP, stride=CELLS), :]
+            return uy_ref[pl.ds(x, B, stride=LX), :]
+        return v_ref[pl.ds(f * FACE + x * LY + y, B, stride=CELLS), :]
+
+    def last_rows(f, x):
+        if x == LX:
+            return ux_ref[B * LY :, :]
+        at = f * FACE + B * CELLS + x * LY
+        return v_ref[at : at + LY, :]
 
     def put(f, x, y, value):
-        out_ref[pl.ds(f * FACE + x * LY + y, A, stride=CELLS), :] = value[:A]
-
-    t0 = [halves(face(0, 0, y)) for y in range(LY)]
-    carry = None
+        out_ref[pl.ds(f * FACE + x * LY + y, B, stride=CELLS), :] = value
+
+    def put_last(f, x, value):
+        at = f * FACE + B * CELLS + x * LY
+        out_ref[at : at + LY, :] = value
+
+    filler = jnp.zeros((IN - OUT, LZ), f32)
+    carry = last_carry = None
     for x in range(LX):
-        t0_next = [halves(face(0, x + 1, y)) for y in range(LY)]
-        t1 = [halves(face(1, x, y)) for y in range(LY + 1)]
-        his, los = [], []
+        z_last = last_rows(2, x)
+        y_last = last_rows(1, x)
+        above = uy_ref[B * LX + x : B * LX + x + 1, :]
+        top = lax.broadcasted_iota(jnp.int32, (LY, LZ), 0) == LY - 1
+        y_up = jnp.where(top, jnp.broadcast_to(above, (LY, LZ)), pltpu.roll(y_last, LY - 1, 0))
+        for j, tile in enumerate((last_rows(0, x), y_last, z_last, last_rows(0, x + 1), y_up, pltpu.roll(z_last, LZ - 1, 1))):
+            last_in[j * LY : (j + 1) * LY] = tile
+        columns = []
         for y in range(LY):
             z = face(2, x, y)
-            t2 = halves(z)
-            t2u = halves(pltpu.roll(z, LZ - 1, 1))
-            six = (t0[y], t0_next[y], t1[y], t1[y + 1], t2, t2u)
-            his.append(jnp.concatenate([b[0] for b in six], 0))
-            los.append(jnp.concatenate([b[1] for b in six], 0))
-        t0 = t0_next
-        hi = jnp.concatenate(his, 1)
-        lo = jnp.concatenate(los, 1)
-        prod = jnp.dot(wh, hi, preferred_element_type=f32)
-        prod += jnp.dot(wh, lo, preferred_element_type=f32)
-        prod += jnp.dot(wl, hi, preferred_element_type=f32)
+            six = [face(0, x, y), face(0, x + 1, y), face(1, x, y), face(1, x, y + 1), z, pltpu.roll(z, LZ - 1, 1)]
+            columns.append(jnp.concatenate(six + [last_in[pl.ds(y, 8, stride=LY), :], filler], 0))
+        hi, lo = halves(jnp.concatenate(columns, 1))
+        prod = jnp.dot(w_all, jnp.concatenate([hi, lo, hi], 0), preferred_element_type=f32)
         parts = []
         for y in range(LY):
             k = k_ref[x * LY + y : x * LY + y + 1, :]
             m = m_ref[x * LY + y : x * LY + y + 1, :]
             cols = slice(y * LZ, (y + 1) * LZ)
-            w = prod[: 6 * AP, cols] * k + prod[6 * AP :, cols] * m
-            parts.append([w[b * AP : (b + 1) * AP] for b in range(6)])
+            w = prod[:OUT, cols] * k + prod[OUT:, cols] * m
+            parts.append([w[b * B : (b + 1) * B] for b in range(6)])
+            last_out[pl.ds(y, 8, stride=LY), :] = w[LAST:]
         for y in range(LY):
             wlx, wux, wly, wuy, wlz, wuz = parts[y]
             put(0, x, y, wlx if x == 0 else wlx + carry[y])
             put(1, x, y, wly if y == 0 else wly + parts[y - 1][3])
             put(2, x, y, wlz + pltpu.roll(wuz, 1, 1))
             if x == 0 and low_x is not None:
-                low_x[pl.ds(y, A, stride=LY), :] = wlx[:A]
+                low_x[pl.ds(y, B, stride=LY), :] = wlx
             if x == LX - 1:
-                up_x[pl.ds(y, A, stride=LY), :] = wux[:A]
+                up_x[pl.ds(y, B, stride=LY), :] = wux
+        tiles = [last_out[j * LY : (j + 1) * LY] for j in range(6)]
+        put_last(0, x, tiles[0] if x == 0 else tiles[0] + last_carry)
+        put_last(1, x, tiles[1] + jnp.where(at_first, 0.0, pltpu.roll(tiles[4], 1, 0)))
+        put_last(2, x, tiles[2] + pltpu.roll(tiles[5], 1, 1))
+        if x == 0 and low_x is not None:
+            low_x[B * LY :] = tiles[0]
+        if x == LX - 1:
+            up_x[B * LY :] = tiles[3]
         if low_y is not None:
-            low_y[pl.ds(x, A, stride=LX), :] = parts[0][2][:A]
-        up_y[pl.ds(x, A, stride=LX), :] = parts[LY - 1][3][:A]
+            low_y[pl.ds(x, B, stride=LX), :] = parts[0][2]
+            low_y[B * LX + x : B * LX + x + 1] = tiles[1][:1]
+        up_y[pl.ds(x, B, stride=LX), :] = parts[LY - 1][3]
+        up_y[B * LX + x : B * LX + x + 1] = tiles[4][LY - 1 :]
         carry = [parts[y][1] for y in range(LY)]
+        last_carry = tiles[3]
 
 
 def is_even(axis):
@@ -115,12 +138,23 @@
     face_y.wait()
 
 
-def weight_kernel(s_ref, m_ref, wh_ref, wl_ref, inv_ref):
-    n, padded = 6 * A, 6 * AP
-    r = lax.broadcasted_iota(jnp.int32, (padded, n), 0)
-    c = lax.broadcasted_iota(jnp.int32, (padded, n), 1)
-    node = lax.rem(r, AP)
-    place = jnp.where((node < A) & (lax.div(r, AP) * A + node == c), 1.0, 0.0).astype(bf16)
+def weight_kernel(s_ref, m_ref, w_ref, inv_ref):
+    n = 6 * A
+
+    def placing(rows, span):
+        r = lax.broadcasted_iota(jnp.int32, (rows, n), 0)
+        c = lax.broadcasted_iota(jnp.int32, (rows, n), 1)
+        p = lax.rem(r, span)
+        j = p - LAST
+        node = jnp.where(p < LAST, lax.div(p, B) * A + lax.rem(p, B), (2 * lax.rem(j, 3) + lax.div(j, 3)) * A + B)
+        return (node == c) & (p < n), lax.div(r, span)
+
+    def ones(mask):
+        return jnp.where(mask, 1.0, 0.0).astype(bf16)
+
+    rows = ones(placing(OUT, OUT)[0])
+    mask, third = placing(3 * IN, IN)
+    columns = (ones(mask & (third < 2)), ones(mask & (third == 2)))
     diagonal = lax.broadcasted_iota(jnp.int32, (n, n), 0) == lax.broadcasted_iota(jnp.int32, (n, n), 1)
 
     def largest(v):
@@ -129,25 +163,19 @@
     inv = 1.0 / (10.0 * largest(s_ref[...]) + 2.0 * largest(m_ref[...]))
     inv_ref[...] = jnp.broadcast_to(inv, (8, LZ))
     for i, ref in enumerate((s_ref, m_ref)):
-        for part, out in zip(halves(ref[...] * inv), (wh_ref, wl_ref)):
-            rows = jnp.dot(place, part, preferred_element_type=f32).astype(bf16)
-            full = lax.dot_general(rows, place, (((1,), (1,)), ((), ())), preferred_element_type=f32)
-            out[i * padded : (i + 1) * padded] = full.astype(bf16)
-
-
-def pad(ref, rows):
-    ref[rows:] = jnp.zeros((ref.shape[0] - rows, LZ), f32)
-
-
-def first_kernel(rhs_ref, hx_ref, hy_ref, k_ref, m_ref, wh_ref, wl_ref,
-                 p_ref, snx, sfx, sny, sfy, v, ux, uy, upx, lowx, upy, lowy):
-    v[:ROWS] = rhs_ref[...]
-    pad(v, ROWS)
-    ux[: A * LY] = hx_ref[...]
-    pad(ux, A * LY)
-    uy[: A * LX] = hy_ref[...]
-    pad(uy, A * LX)
-    apply_operator(v, ux, uy, k_ref, m_ref, wh_ref, wl_ref, p_ref, upx, lowx, upy, lowy)
+        full = 0.0
+        for part, place in zip(halves(ref[...] * inv), columns):
+            moved = jnp.dot(rows, part, preferred_element_type=f32).astype(bf16)
+            full = full + lax.dot_general(moved, place, (((1,), (1,)), ((), ())), preferred_element_type=f32)
+        w_ref[i * OUT : (i + 1) * OUT] = full.astype(bf16)
+
+
+def first_kernel(rhs_ref, hx_ref, hy_ref, k_ref, m_ref, w_ref,
+                 p_ref, snx, sfx, sny, sfy, v, ux, uy, last_in, last_out, upx, lowx, upy, lowy):
+    v[...] = rhs_ref[...]
+    ux[...] = hx_ref[...]
+    uy[...] = hy_ref[...]
+    apply_operator(v, ux, uy, k_ref, m_ref, w_ref, p_ref, upx, lowx, upy, lowy, last_in, last_out)
     route(is_even("gx"), upx, lowx, snx, sfx)
     route(is_even("gy"), upy, lowy, sny, sfy)
 
@@ -155,8 +183,7 @@
 def assemble(p_ref, snx, sfx, sny, sfy, rnx, rfx, rny, rfy, v, ux, uy):
     even_x = is_even("gx")
     even_y = is_even("gy")
-    v[:ROWS] = p_ref[...]
-    pad(v, ROWS)
+    v[...] = p_ref[...]
     below_x = jnp.where(even_x, rfx[...], rnx[...])
     for a in range(A):
         rows = slice(a * CELLS, a * CELLS + LY)
@@ -164,10 +191,8 @@
     below_y = jnp.where(even_y, rfy[...], rny[...])
     first = pl.ds(FACE, A * LX, stride=LY)
     v[first, :] = v[first, :] + below_y
-    ux[: A * LY] = jnp.where(even_x, snx[...] + rnx[...], sfx[...] + rfx[...])
-    pad(ux, A * LY)
-    uy[: A * LX] = jnp.where(even_y, sny[...] + rny[...], sfy[...] + rfy[...])
-    pad(uy, A * LX)
+    ux[...] = jnp.where(even_x, snx[...] + rnx[...], sfx[...] + rfx[...])
+    uy[...] = jnp.where(even_y, sny[...] + rny[...], sfy[...] + rfy[...])
 
 
 def node_sum(value):
@@ -178,41 +203,41 @@
     return jnp.sum(tile, 0, keepdims=True)
 
 
-def second_kernel(p_ref, rhs_ref, rfx, rfy, rny, rnx, snx, sfx, sny, sfy, k_ref, m_ref, wh_ref, wl_ref,
-                  v1_ref, p1_ref, tnx, tfx, tny, tfy, sums_ref, ux, uy, upx, lowx, upy, lowy):
+def second_kernel(p_ref, rhs_ref, rfx, rfy, rny, rnx, snx, sfx, sny, sfy, k_ref, m_ref, w_ref,
+                  v1_ref, p1_ref, tnx, tfx, tny, tfy, sums_ref, ux, uy, last_in, last_out, upx, lowx, upy, lowy):
     assemble(p_ref, snx, sfx, sny, sfy, rnx, rfx, rny, rfy, v1_ref, ux, uy)
     v0 = rhs_ref[...]
-    v1 = v1_ref[:ROWS]
+    v1 = v1_ref[...]
     sums_ref[0:8] = node_sum(v0)
     sums_ref[8:16] = node_sum(v1)
     sums_ref[16:24] = node_sum(v0 * v0)
     sums_ref[24:32] = node_sum(v0 * v1)
     sums_ref[32:40] = node_sum(v1 * v1)
-    apply_operator(v1_ref, ux, uy, k_ref, m_ref, wh_ref, wl_ref, p1_ref, upx, lowx, upy, lowy)
+    apply_operator(v1_ref, ux, uy, k_ref, m_ref, w_ref, p1_ref, upx, lowx, upy, lowy, last_in, last_out)
     route(is_even("gx"), upx, lowx, tnx, tfx)
     route(is_even("gy"), upy, lowy, tny, tfy)
 
 
-def third_kernel(p_ref, v1_ref, rfx, rfy, rny, rnx, snx, sfx, sny, sfy, sums_ref, k_ref, m_ref, wh_ref, wl_ref,
-                 v2_out, p2_out, upx, upy, loads_ref, v2_ref, p2_ref, ux, uy, v2_sem, p2_sem):
+def third_kernel(p_ref, v1_ref, rfx, rfy, rny, rnx, snx, sfx, sny, sfy, sums_ref, k_ref, m_ref, w_ref,
+                 v2_out, p2_out, upx, upy, loads_ref, v2_ref, p2_ref, ux, uy, last_in, last_out, v2_sem, p2_sem):
     assemble(p_ref, snx, sfx, sny, sfy, rnx, rfx, rny, rfy, v2_ref, ux, uy)
-    v2_copy = pltpu.make_async_copy(v2_ref.at[:ROWS], v2_out, v2_sem)
+    v2_copy = pltpu.make_async_copy(v2_ref, v2_out, v2_sem)
     v2_copy.start()
-    v1 = v1_ref[:ROWS]
-    v2 = v2_ref[:ROWS]
+    v1 = v1_ref[...]
+    v2 = v2_ref[...]
     loads_ref[0:16] = sums_ref[0:16]
     loads_ref[16:24] = node_sum(v2)
     m3 = node_sum(v1 * v2)
     m4 = node_sum(v2 * v2)
-    apply_operator(v2_ref, ux, uy, k_ref, m_ref, wh_ref, wl_ref, p2_ref, upx, None, upy, None)
+    apply_operator(v2_ref, ux, uy, k_ref, m_ref, w_ref, p2_ref, upx, None, upy, None, last_in, last_out)
     p2_copy = pltpu.make_async_copy(p2_ref, p2_out, p2_sem)
     p2_copy.start()
     p2 = p2_ref[...]
     above = upx[...]
     loads_ref[24:32] = node_sum(p2)
     loads_ref[32:40] = node_sum(above)
-    energy = node_sum(v2_ref[:ROWS] * p2) + node_sum(ux[: A * LY] * above)
-    tail = row(uy[: A * LX] * upy[...])
+    energy = node_sum(v2_ref[...] * p2) + node_sum(ux[...] * above)
+    tail = row(uy[...] * upy[...])
     for k in range(3):
         loads_ref[40 + k : 41 + k] = row(sums_ref[16 + 8 * k : 24 + 8 * k])
     loads_ref[43:44] = row(m3)
@@ -426,8 +451,8 @@
     k2 = kappa.reshape(CELLS, LZ)
     m2 = mass.reshape(CELLS, LZ)
     sends = [struct(vx, LZ), struct(vx, LZ), struct(vy, LZ), struct(vy, LZ)]
-    upper = [pltpu.VMEM((AP * LY, LZ), f32), pltpu.VMEM((AP * LX, LZ), f32)]
-    field = [pltpu.VMEM((PADDED, LZ), f32)] + upper
+    upper = [pltpu.VMEM((vx, LZ), f32), pltpu.VMEM((vy, LZ), f32)] + [pltpu.VMEM((8 * LY, LZ), f32)] * 2
+    field = [pltpu.VMEM((ROWS, LZ), f32)] + upper
     edges = [pltpu.VMEM((vx, LZ), f32)] * 2 + [pltpu.VMEM((vy, LZ), f32)] * 2
 
     def call(kernel, name, ins, outs, scratch=(), **static):
@@ -461,21 +486,23 @@
     )
     hx = shifted(fx.reshape(vx, LZ), "gx", -1)
     hy = shifted(fy.reshape(vy, LZ), "gy", -1)
-    half = jax.ShapeDtypeStruct((12 * AP, 6 * AP), bf16)
-    wh, wl, inv = call(weight_kernel, "weights", [stiffness, mass_matrix], [half, half, struct(8, LZ)])
+    w, inv = call(
+        weight_kernel, "weights", [stiffness, mass_matrix],
+        [jax.ShapeDtypeStruct((2 * OUT, 3 * IN), bf16), struct(8, LZ)],
+    )
 
     p0, *s = call(
-        first_kernel, "first", [rhs2, hx, hy, k2, m2, wh, wl], [struct(ROWS, LZ)] + sends, field + edges,
+        first_kernel, "first", [rhs2, hx, hy, k2, m2, w], [struct(ROWS, LZ)] + sends, field + edges,
     )
     r = swap(s)
     v1, p1, *s, sums = call(
-        second_kernel, "second", [p0, rhs2, *r, *s, k2, m2, wh, wl],
-        [struct(PADDED, LZ), struct(ROWS, LZ)] + sends + [struct(40, LZ)], upper + edges,
+        second_kernel, "second", [p0, rhs2, *r, *s, k2, m2, w],
+        [struct(ROWS, LZ), struct(ROWS, LZ)] + sends + [struct(40, LZ)], upper + edges,
     )
     r = swap(s)
     dma = pltpu.SemaphoreType.DMA
     v2, p2, upx, upy, loads = call(
-        third_kernel, "third", [p1, v1, *r, *s, sums, k2, m2, wh, wl],
+        third_kernel, "third", [p1, v1, *r, *s, sums, k2, m2, w],
         [pltpu.HBM((ROWS, LZ), f32)] * 2 + [struct(vx, LZ), struct(vy, LZ), struct(48, LZ)],
         [field[0], pltpu.VMEM((ROWS, LZ), f32)] + upper + [dma, dma],
     )

time: 75.4 us -> 72.4 us (0.960)
  Pallas kernels: 21.4 us -> 18.9 us
    pallas_call x7, Pallas kernels: 21.4 us -> 18.9 us  [call(): pl.pallas_call(bound, out_shape=outs, in_specs=specs, out_specs=[ANY if i...]
  transfers between devices with their start and end apart: 19 -> 19, of which waited for: 6 -> 6; matrix products, arithmetic and copies ran while one was open for 0% -> 0% of each run, Pallas kernels for 1% -> 2%
where the time goes in v5:
time: 72.4 us; the launch traced here: 71.4 us
  starting transfers between devices  35.7 us (49%)
  Pallas kernels  18.9 us (26%)
  waiting for transfers between devices  14 us (19%)
  local copies, waits for them, and re-layouts  1.86 us (3%)
  between operations  0.96 us (1%)
    pallas_call x7, Pallas kernels, call(): pl.pallas_call(bound, out_shape=outs, in_specs=specs, out_specs=[ANY if i...  18.9 us
    ppermute x7, starting transfers between devices, shifted(): return lax.ppermute(value, axis, [(i, (i + by) % n) for i in range(n)])  15.5 us
    ppermute x4, waiting for transfers between devices, far_swap(): return lax.ppermute(value, axis, pairs)  9.62 us
    ppermute x4, starting transfers between devices, far_swap(): return lax.ppermute(value, axis, pairs)  9.55 us
    all_to_all x1, starting transfers between devices, shards(): lax.all_to_all(mom.reshape(-1, 2, LZ), ('gx', 'gy'), 0, 0, tiled=True, ax...  7.15 us
    ppermute x3, starting transfers between devices, shards(): lax.ppermute(loads, 'gx', [(i, i ^ b) for i in range(nx)])  3.44 us
    ppermute x7, waiting for transfers between devices, shifted(): return lax.ppermute(value, axis, [(i, (i + by) % n) for i in range(n)])  2.32 us
    ppermute x3, waiting for transfers between devices, shards(): lax.ppermute(loads, 'gx', [(i, i ^ b) for i in range(nx)])  2.06 us
  transfers between devices with their start and end apart: 19, of which 6 were waited for; matrix products, arithmetic and copies ran while one was open for 0% of the time, Pallas kernels for 2%

profile of v5, /device:TPU:0, one launch (start us, length us, event | category | flops | bytes accessed | tf_op | source)
XLA Modules:
  0.0 71.4 jit_solution(14333109032695819175)
XLA Ops:
  0.7 1.0 %edges.1 = (f32[25,8,128]{2,1,0:T(8,128)S(1)}, f32[25,4,128]{2,1,0:T(4,128)S(1)}) custom-call(f32[3,25,4,8,128]{4,3,2,1,0:T(8,128)} %refs_0_.3), custom_call_target="tpu_custom_call" | custom-call | tf_op jit(solution)/shard_map/edges/pallas_call | solution.py:465
  1.7 6.1 %collective-permute-start = (f32[200,128]{1,0:T(8,128)S(1)}, f32[200,128]{1,0:T(8,128)S(1)}, u32[]{:S(2)}, u32[]{:S(2)}) collective-permute-start(f32[200,128]{1,0:T(8,128)S(1)} %bitcast.19), channel_id=1, source_target_pairs={{0,120},{8,0},{16,8},{24,16},{32,24},{40,32},{48,40},{56,48},{64,5... | collective-permute-start | bytes 307208 | tf_op jit(solution)/shard_map/ppermute | solution.py:27
  7.8 3.1 %collective-permute-start.1 = (f32[100,128]{1,0:T(8,128)S(1)}, f32[100,128]{1,0:T(8,128)S(1)}, u32[]{:S(2)}, u32[]{:S(2)}) collective-permute-start(f32[100,128]{1,0:T(8,128)S(1)} %reshape.35), channel_id=1, source_target_pairs={{0,7},{1,0},{2,1},{3,2},{4,3},{5,4},{6,5},{7,6},{8,15},{9,8},{10,9... | collective-permute-start | bytes 153608 | tf_op jit(solution)/shard_map/ppermute | solution.py:27
  10.9 0.9 %copy-done.1 = f32[150,150]{1,0:T(8,128)S(1)} copy-done((f32[150,150]{1,0:T(8,128)S(1)}, f32[150,150]{1,0:T(8,128)}, u32[]{:S(2)}) %copy-start.1) | copy-done | bytes 90024
  11.8 0.9 %copy-done.2 = f32[150,150]{1,0:T(8,128)S(1)} copy-done((f32[150,150]{1,0:T(8,128)S(1)}, f32[150,150]{1,0:T(8,128)}, u32[]{:S(2)}) %copy-start.2) | copy-done | bytes 90024
  12.7 1.2 %weights.1 = (bf16[304,480]{1,0:T(8,128)(2,1)S(1)}, f32[8,128]{1,0:T(8,128)S(1)}) custom-call(f32[150,150]{1,0:T(8,128)S(1)} %copy-done.1, f32[150,150]{1,0:T(8,128)S(1)} %copy-done.2), custom_call_target="tpu_custom_call" | custom-call | tf_op jit(solution)/shard_map/weights/pallas_call | solution.py:465
  13.9 3.0 %first.1 = (f32[2400,128]{1,0:T(8,128)S(1)}, f32[200,128]{1,0:T(8,128)S(1)}, f32[200,128]{1,0:T(8,128)S(1)}, f32[100,128]{1,0:T(8,128)S(1)}, f32[100,128]{1,0:T(8,128)S(1)}) custom-call(f32[2400,128]{1,0:T(8,128)S(1)} %bitcast.9, f32[200,128]{1,0:T(8,128)S(1)} %collective-permute-done.refs_1_, f32[100,128]{1,0:T(8,128)S(1)} %collective-permute-done.1.refs_2_, ...), custom_call_target="tpu_custom_call" | custom-call | tf_op jit(solution)/shard_map/first/pallas_call | solution.py:465
  16.9 1.6 %collective-permute-start.2 = (f32[200,128]{1,0:T(8,128)S(1)}, f32[200,128]{1,0:T(8,128)S(1)}, u32[]{:S(2)}, u32[]{:S(2)}) collective-permute-start(f32[200,128]{1,0:T(8,128)S(1)} %get-tuple-element.38.refs_7_), channel_id=1, source_target_pairs={{0,120},{8,16},{16,8},{24,32},{32,24},{40,48},{48,40},{56,64},{64,... | collective-permute-start | bytes 307208 | tf_op jit(solution)/shard_map/ppermute | solution.py:38
  18.6 3.0 %collective-permute-start.3 = (f32[100,128]{1,0:T(8,128)S(1)}, f32[100,128]{1,0:T(8,128)S(1)}, u32[]{:S(2)}, u32[]{:S(2)}) collective-permute-start(f32[100,128]{1,0:T(8,128)S(1)} %get-tuple-element.39.refs_9_), channel_id=1, source_target_pairs={{0,7},{1,2},{2,1},{3,4},{4,3},{5,6},{6,5},{7,0},{8,15},{9,10},{10,... | collective-permute-start | bytes 153608 | tf_op jit(solution)/shard_map/ppermute | solution.py:38
  21.6 4.3 %collective-permute-done.3.refs_3_ = f32[100,128]{1,0:T(8,128)S(1)} collective-permute-done((f32[100,128]{1,0:T(8,128)S(1)}, f32[100,128]{1,0:T(8,128)S(1)}, u32[]{:S(2)}, u32[]{:S(2)}) %collective-permute-start.3) | collective-permute-done | bytes 51232 | tf_op jit(solution)/shard_map/ppermute | solution.py:38
  25.9 3.6 %second.1 = (f32[2400,128]{1,0:T(8,128)S(1)}, f32[2400,128]{1,0:T(8,128)S(1)}, f32[200,128]{1,0:T(8,128)S(1)}, f32[200,128]{1,0:T(8,128)S(1)}, f32[100,128]{1,0:...) custom-call(f32[2400,128]{1,0:T(8,128)S(1)} %get-tuple-element.37.refs_0_, f32[2400,128]{1,0:T(8,128)S(1)} %bitcast.10, ...), custom_call_target="tpu_custom_call" | custom-call | tf_op jit(solution)/shard_map/second/pallas_call | solution.py:465
  29.5 3.5 %collective-permute-start.6 = (f32[200,128]{1,0:T(8,128)S(1)}, f32[200,128]{1,0:T(8,128)S(1)}, u32[]{:S(2)}, u32[]{:S(2)}) collective-permute-start(f32[200,128]{1,0:T(8,128)S(1)} %get-tuple-element.44.refs_7_), channel_id=1, source_target_pairs={{0,120},{8,16},{16,8},{24,32},{32,24},{40,48},{48,40},{56,64},{64,... | collective-permute-start | bytes 307208 | tf_op jit(solution)/shard_map/ppermute | solution.py:38
  33.0 1.4 %collective-permute-start.7 = (f32[100,128]{1,0:T(8,128)S(1)}, f32[100,128]{1,0:T(8,128)S(1)}, u32[]{:S(2)}, u32[]{:S(2)}) collective-permute-start(f32[100,128]{1,0:T(8,128)S(1)} %get-tuple-element.45.refs_9_), channel_id=1, source_target_pairs={{0,7},{1,2},{2,1},{3,4},{4,3},{5,6},{6,5},{7,0},{8,15},{9,10},{10,... | collective-permute-start | bytes 153608 | tf_op jit(solution)/shard_map/ppermute | solution.py:38
  34.4 5.3 %collective-permute-done.7.refs_3_ = f32[100,128]{1,0:T(8,128)S(1)} collective-permute-done((f32[100,128]{1,0:T(8,128)S(1)}, f32[100,128]{1,0:T(8,128)S(1)}, u32[]{:S(2)}, u32[]{:S(2)}) %collective-permute-start.7) | collective-permute-done | bytes 51232 | tf_op jit(solution)/shard_map/ppermute | solution.py:38
  39.8 4.7 %third.1 = (f32[2400,128]{1,0:T(8,128)}, f32[2400,128]{1,0:T(8,128)}, f32[200,128]{1,0:T(8,128)S(1)}, f32[100,128]{1,0:T(8,128)S(1)}, f32[48,128]{1,0:T(8,128)S(1)}) custom-call(f32[2400,128]{1,0:T(8,128)S(1)} %get-tuple-element.42.refs_0_, f32[2400,128]{1,0:T(8,128)S(1)} %get-tuple-element.43.refs_1_.refs_8_, ...), custom_call_target="tpu_custom_call" | custom-call | tf_op jit(solution)/shard_map/third/pallas_call | solution.py:465
  44.6 2.5 %collective-permute-start.11 = (f32[48,128]{1,0:T(8,128)S(1)}, f32[48,128]{1,0:T(8,128)S(1)}, u32[]{:S(2)}, u32[]{:S(2)}) collective-permute-start(f32[48,128]{1,0:T(8,128)S(1)} %get-tuple-element.49.refs_0_), channel_id=1, source_target_pairs={{0,16},{8,24},{16,0},{24,8},{32,48},{40,56},{48,32},{56,40},{64,80... | collective-permute-start | bytes 73736 | tf_op jit(solution)/shard_map/ppermute | solution.py:510
  48.0 1.4 %collective-permute-done.12.refs_3_ = f32[48,128]{1,0:T(8,128)S(1)} collective-permute-done((f32[48,128]{1,0:T(8,128)S(1)}, f32[48,128]{1,0:T(8,128)S(1)}, u32[]{:S(2)}, u32[]{:S(2)}) %collective-permute-start.12) | collective-permute-done | bytes 24608 | tf_op jit(solution)/shard_map/ppermute | solution.py:510
  51.2 7.2 %all-to-all-start = ((f32[32,2,128]{2,1,0:T(2,128)}), f32[32,2,128]{2,1,0:T(2,128)S(1)}, u32[]{:S(2)}, u32[]{:S(2)}) async-start(f32[32,2,128]{2,1,0:T(2,128)} %bitcast.4), calls=%async_computation | async-start | bytes 65536 | tf_op jit(solution)/shard_map/all_to_all | solution.py:517
  58.3 1.9 %collective-permute-start.13 = (f32[32,128]{1,0:T(8,128)S(1)}, f32[32,128]{1,0:T(8,128)S(1)}, u32[]{:S(2)}, u32[]{:S(2)}) collective-permute-start(f32[32,128]{1,0:T(8,128)S(1)} %get-tuple-element.54), channel_id=1, source_target_pairs={{0,32},{8,40},{16,48},{24,56},{32,64},{40,72},{48,80},{56,88},{64,... | collective-permute-start | bytes 49160 | tf_op jit(solution)/shard_map/ppermute | solution.py:27
  60.2 2.7 %collective-permute-start.14 = (f32[32,128]{1,0:T(8,128)S(1)}, f32[32,128]{1,0:T(8,128)S(1)}, u32[]{:S(2)}, u32[]{:S(2)}) collective-permute-start(f32[32,128]{1,0:T(8,128)S(1)} %get-tuple-element.55), channel_id=1, source_target_pairs={{0,64},{8,72},{16,80},{24,88},{32,96},{40,104},{48,112},{56,120},{... | collective-permute-start | bytes 49160 | tf_op jit(solution)/shard_map/ppermute | solution.py:27
  62.9 1.4 %collective-permute-start.15 = (f32[32,128]{1,0:T(8,128)S(1)}, f32[32,128]{1,0:T(8,128)S(1)}, u32[]{:S(2)}, u32[]{:S(2)}) collective-permute-start(f32[32,128]{1,0:T(8,128)S(1)} %get-tuple-element.56), channel_id=1, source_target_pairs={{0,96},{8,104},{16,112},{24,120},{32,0},{40,8},{48,16},{56,24},{64... | collective-permute-start | bytes 49160 | tf_op jit(solution)/shard_map/ppermute | solution.py:27
  64.3 1.2 %collective-permute-done.14.refs_4_ = f32[32,128]{1,0:T(8,128)S(1)} collective-permute-done((f32[32,128]{1,0:T(8,128)S(1)}, f32[32,128]{1,0:T(8,128)S(1)}, u32[]{:S(2)}, u32[]{:S(2)}) %collective-permute-start.14) | collective-permute-done | bytes 16416 | tf_op jit(solution)/shard_map/ppermute | solution.py:27
  65.5 1.2 %collective-permute-done.15.refs_5_ = f32[32,128]{1,0:T(8,128)S(1)} collective-permute-done((f32[32,128]{1,0:T(8,128)S(1)}, f32[32,128]{1,0:T(8,128)S(1)}, u32[]{:S(2)}, u32[]{:S(2)}) %collective-permute-start.15) | collective-permute-done | bytes 16416 | tf_op jit(solution)/shard_map/ppermute | solution.py:27
  66.7 4.5 %last.1 = (f32[2400,128]{1,0:T(8,128)}, f32[2400,128]{1,0:T(8,128)}, f32[8,128]{1,0:T(8,128)}) custom-call(f32[3,25]{1,0:T(4,128)S(1)} %copy-done.5, f32[64,128]{1,0:T(8,128)S(1)} %bitcast.18, f32[32,128]{1,0:T(8,128)S(1)} %get-tuple-element.53.refs_2_, f32[32,128]{1,0:T(8,128)S(1)} %collective-permute-done.13.refs_3_, ...), custom_call_target="tpu_custom_call" | custom-call | tf_op jit(solution)/shard_map/last/pallas_call | solution.py:465
  (34 shorter events, 2.9 us)
Async XLA Ops:
  0.6 13.3 %copy-start = (f32[3,25,4,8,128]{4,3,2,1,0:T(8,128)S(1)}, f32[3,25,4,8,128]{4,3,2,1,0:T(8,128)}, u32[]{:S(2)}) copy-start(f32[3,25,4,8,128]{4,3,2,1,0:T(8,128)} %refs_0_.3) | copy-start | bytes 3686404
  0.6 13.3 %copy-start.4 = (f32[4,8,128]{2,1,0:T(8,128)S(1)}, f32[4,8,128]{2,1,0:T(8,128)}, u32[]{:S(2)}) copy-start(f32[4,8,128]{2,1,0:T(8,128)} %param.8) | copy-start | bytes 49156
  0.7 13.3 %copy-start.3 = (f32[4,8,128]{2,1,0:T(8,128)S(1)}, f32[4,8,128]{2,1,0:T(8,128)}, u32[]{:S(2)}) copy-start(f32[4,8,128]{2,1,0:T(8,128)} %param.7) | copy-start | bytes 49156
  1.7 12.2 %collective-permute-start = (f32[200,128]{1,0:T(8,128)S(1)}, f32[200,128]{1,0:T(8,128)S(1)}, u32[]{:S(2)}, u32[]{:S(2)}) collective-permute-start(f32[200,128]{1,0:T(8,128)S(1)} %bitcast.19), channel_id=1, source_target_pairs={{0,120},{8,0},{16,8},{24,16},{32,24},{40,32},{48,40},{56,48},{64,5... | collective-permute-start | bytes 307208 | tf_op jit(solution)/shard_map/ppermute | solution.py:27
  7.8 6.1 %collective-permute-start.1 = (f32[100,128]{1,0:T(8,128)S(1)}, f32[100,128]{1,0:T(8,128)S(1)}, u32[]{:S(2)}, u32[]{:S(2)}) collective-permute-start(f32[100,128]{1,0:T(8,128)S(1)} %reshape.35), channel_id=1, source_target_pairs={{0,7},{1,0},{2,1},{3,2},{4,3},{5,4},{6,5},{7,6},{8,15},{9,8},{10,9... | collective-permute-start | bytes 153608 | tf_op jit(solution)/shard_map/ppermute | solution.py:27
  10.9 0.9 %copy-start.1 = (f32[150,150]{1,0:T(8,128)S(1)}, f32[150,150]{1,0:T(8,128)}, u32[]{:S(2)}) copy-start(f32[150,150]{1,0:T(8,128)} %refs_0_.4) | copy-start | bytes 270004
  16.9 9.0 %collective-permute-start.2 = (f32[200,128]{1,0:T(8,128)S(1)}, f32[200,128]{1,0:T(8,128)S(1)}, u32[]{:S(2)}, u32[]{:S(2)}) collective-permute-start(f32[200,128]{1,0:T(8,128)S(1)} %get-tuple-element.38.refs_7_), channel_id=1, source_target_pairs={{0,120},{8,16},{16,8},{24,32},{32,24},{40,48},{48,40},{56,64},{64,... | collective-permute-start | bytes 307208 | tf_op jit(solution)/shard_map/ppermute | solution.py:38
  18.6 7.3 %collective-permute-start.5 = (f32[200,128]{1,0:T(8,128)S(1)}, f32[200,128]{1,0:T(8,128)S(1)}, u32[]{:S(2)}, u32[]{:S(2)}) collective-permute-start(f32[200,128]{1,0:T(8,128)S(1)} %get-tuple-element.41.refs_6_), channel_id=1, source_target_pairs={{0,8},{8,0},{16,24},{24,16},{32,40},{40,32},{48,56},{56,48},{64,72... | collective-permute-start | bytes 307208 | tf_op jit(solution)/shard_map/ppermute | solution.py:32
  18.6 7.3 %collective-permute-start.3 = (f32[100,128]{1,0:T(8,128)S(1)}, f32[100,128]{1,0:T(8,128)S(1)}, u32[]{:S(2)}, u32[]{:S(2)}) collective-permute-start(f32[100,128]{1,0:T(8,128)S(1)} %get-tuple-element.39.refs_9_), channel_id=1, source_target_pairs={{0,7},{1,2},{2,1},{3,4},{4,3},{5,6},{6,5},{7,0},{8,15},{9,10},{10,... | collective-permute-start | bytes 153608 | tf_op jit(solution)/shard_map/ppermute | solution.py:38
  21.6 4.3 %collective-permute-start.4 = (f32[100,128]{1,0:T(8,128)S(1)}, f32[100,128]{1,0:T(8,128)S(1)}, u32[]{:S(2)}, u32[]{:S(2)}) collective-permute-start(f32[100,128]{1,0:T(8,128)S(1)} %get-tuple-element.40.refs_8_), channel_id=1, source_target_pairs={{0,1},{1,0},{2,3},{3,2},{4,5},{5,4},{6,7},{7,6},{8,9},{9,8},{10,11... | collective-permute-start | bytes 153608 | tf_op jit(solution)/shard_map/ppermute | solution.py:32
  29.5 10.2 %collective-permute-start.6 = (f32[200,128]{1,0:T(8,128)S(1)}, f32[200,128]{1,0:T(8,128)S(1)}, u32[]{:S(2)}, u32[]{:S(2)}) collective-permute-start(f32[200,128]{1,0:T(8,128)S(1)} %get-tuple-element.44.refs_7_), channel_id=1, source_target_pairs={{0,120},{8,16},{16,8},{24,32},{32,24},{40,48},{48,40},{56,64},{64,... | collective-permute-start | bytes 307208 | tf_op jit(solution)/shard_map/ppermute | solution.py:38
  33.0 6.7 %collective-permute-start.9 = (f32[200,128]{1,0:T(8,128)S(1)}, f32[200,128]{1,0:T(8,128)S(1)}, u32[]{:S(2)}, u32[]{:S(2)}) collective-permute-start(f32[200,128]{1,0:T(8,128)S(1)} %get-tuple-element.47.refs_6_), channel_id=1, source_target_pairs={{0,8},{8,0},{16,24},{24,16},{32,40},{40,32},{48,56},{56,48},{64,72... | collective-permute-start | bytes 307208 | tf_op jit(solution)/shard_map/ppermute | solution.py:32
  33.0 6.7 %collective-permute-start.7 = (f32[100,128]{1,0:T(8,128)S(1)}, f32[100,128]{1,0:T(8,128)S(1)}, u32[]{:S(2)}, u32[]{:S(2)}) collective-permute-start(f32[100,128]{1,0:T(8,128)S(1)} %get-tuple-element.45.refs_9_), channel_id=1, source_target_pairs={{0,7},{1,2},{2,1},{3,4},{4,3},{5,6},{6,5},{7,0},{8,15},{9,10},{10,... | collective-permute-start | bytes 153608 | tf_op jit(solution)/shard_map/ppermute | solution.py:38
  34.4 5.3 %collective-permute-start.8 = (f32[100,128]{1,0:T(8,128)S(1)}, f32[100,128]{1,0:T(8,128)S(1)}, u32[]{:S(2)}, u32[]{:S(2)}) collective-permute-start(f32[100,128]{1,0:T(8,128)S(1)} %get-tuple-element.46.refs_8_), channel_id=1, source_target_pairs={{0,1},{1,0},{2,3},{3,2},{4,5},{5,4},{6,7},{7,6},{8,9},{9,8},{10,11... | collective-permute-start | bytes 153608 | tf_op jit(solution)/shard_map/ppermute | solution.py:32
  39.8 26.9 %copy-start.5 = (f32[3,25]{1,0:T(4,128)S(1)}, f32[3,25]{1,0:T(4,128)}, u32[]{:S(2)}) copy-start(f32[3,25]{1,0:T(4,128)} %refs_0_.5) | copy-start | bytes 904
  44.5 4.8 %collective-permute-start.12 = (f32[48,128]{1,0:T(8,128)S(1)}, f32[48,128]{1,0:T(8,128)S(1)}, u32[]{:S(2)}, u32[]{:S(2)}) collective-permute-start(f32[48,128]{1,0:T(8,128)S(1)} %get-tuple-element.49.refs_0_), channel_id=1, source_target_pairs={{0,24},{8,16},{16,8},{24,0},{32,56},{40,48},{48,40},{56,32},{64,88... | collective-permute-start | bytes 73736 | tf_op jit(solution)/shard_map/ppermute | solution.py:510
  44.6 5.4 %collective-permute-start.11 = (f32[48,128]{1,0:T(8,128)S(1)}, f32[48,128]{1,0:T(8,128)S(1)}, u32[]{:S(2)}, u32[]{:S(2)}) collective-permute-start(f32[48,128]{1,0:T(8,128)S(1)} %get-tuple-element.49.refs_0_), channel_id=1, source_target_pairs={{0,16},{8,24},{16,0},{24,8},{32,48},{40,56},{48,32},{56,40},{64,80... | collective-permute-start | bytes 73736 | tf_op jit(solution)/shard_map/ppermute | solution.py:510
  47.1 3.0 %collective-permute-start.10 = (f32[48,128]{1,0:T(8,128)S(1)}, f32[48,128]{1,0:T(8,128)S(1)}, u32[]{:S(2)}, u32[]{:S(2)}) collective-permute-start(f32[48,128]{1,0:T(8,128)S(1)} %get-tuple-element.49.refs_0_), channel_id=1, source_target_pairs={{0,8},{8,0},{16,24},{24,16},{32,40},{40,32},{48,56},{56,48},{64,72... | collective-permute-start | bytes 73736 | tf_op jit(solution)/shard_map/ppermute | solution.py:510
  50.9 15.8 %collective-permute-start.16 = (f32[200,128]{1,0:T(8,128)S(1)}, f32[200,128]{1,0:T(8,128)S(1)}, u32[]{:S(2)}, u32[]{:S(2)}) collective-permute-start(f32[200,128]{1,0:T(8,128)S(1)} %get-tuple-element.60), channel_id=1, source_target_pairs={{0,8},{8,16},{16,24},{24,32},{32,40},{40,48},{48,56},{56,64},{64,7... | collective-permute-start | bytes 307208 | tf_op jit(solution)/shard_map/ppermute | solution.py:27
  50.9 15.8 %collective-permute-start.17 = (f32[100,128]{1,0:T(8,128)S(1)}, f32[100,128]{1,0:T(8,128)S(1)}, u32[]{:S(2)}, u32[]{:S(2)}) collective-permute-start(f32[100,128]{1,0:T(8,128)S(1)} %get-tuple-element.61), channel_id=1, source_target_pairs={{0,1},{1,2},{2,3},{3,4},{4,5},{5,6},{6,7},{7,0},{8,9},{9,10},{10,1... | collective-permute-start | bytes 153608 | tf_op jit(solution)/shard_map/ppermute | solution.py:27
  51.2 15.5 %all-to-all-start = ((f32[32,2,128]{2,1,0:T(2,128)}), f32[32,2,128]{2,1,0:T(2,128)S(1)}, u32[]{:S(2)}, u32[]{:S(2)}) async-start(f32[32,2,128]{2,1,0:T(2,128)} %bitcast.4), calls=%async_computation | async-start | bytes 65536 | tf_op jit(solution)/shard_map/all_to_all | solution.py:517
  58.3 6.0 %collective-permute-start.13 = (f32[32,128]{1,0:T(8,128)S(1)}, f32[32,128]{1,0:T(8,128)S(1)}, u32[]{:S(2)}, u32[]{:S(2)}) collective-permute-start(f32[32,128]{1,0:T(8,128)S(1)} %get-tuple-element.54), channel_id=1, source_target_pairs={{0,32},{8,40},{16,48},{24,56},{32,64},{40,72},{48,80},{56,88},{64,... | collective-permute-start | bytes 49160 | tf_op jit(solution)/shard_map/ppermute | solution.py:27
  60.2 5.3 %collective-permute-start.14 = (f32[32,128]{1,0:T(8,128)S(1)}, f32[32,128]{1,0:T(8,128)S(1)}, u32[]{:S(2)}, u32[]{:S(2)}) collective-permute-start(f32[32,128]{1,0:T(8,128)S(1)} %get-tuple-element.55), channel_id=1, source_target_pairs={{0,64},{8,72},{16,80},{24,88},{32,96},{40,104},{48,112},{56,120},{... | collective-permute-start | bytes 49160 | tf_op jit(solution)/shard_map/ppermute | solution.py:27
  62.9 3.7 %collective-permute-start.15 = (f32[32,128]{1,0:T(8,128)S(1)}, f32[32,128]{1,0:T(8,128)S(1)}, u32[]{:S(2)}, u32[]{:S(2)}) collective-permute-start(f32[32,128]{1,0:T(8,128)S(1)} %get-tuple-element.56), channel_id=1, source_target_pairs={{0,96},{8,104},{16,112},{24,120},{32,0},{40,8},{48,16},{56,24},{64... | collective-permute-start | bytes 49160 | tf_op jit(solution)/shard_map/ppermute | solution.py:27
  (1 other events, 0.9 us)

commit v6 on v5

--- a/solution.py
+++ b/solution.py
@@ -16,6 +16,7 @@
 CELLS = LX * LY
 FACE = A * CELLS
 ROWS = F * FACE
+PIECE = 72
 f32, bf16 = jnp.float32, jnp.bfloat16
 VM = pl.BlockSpec(memory_space=pltpu.VMEM)
 SM = pl.BlockSpec(memory_space=pltpu.SMEM)
@@ -44,7 +45,7 @@
     return hi, lo
 
 
-def apply_operator(v_ref, ux_ref, uy_ref, k_ref, m_ref, w_ref, out_ref, up_x, low_x, up_y, low_y, last_in, last_out):
+def apply_operator(v_ref, ux_ref, uy_ref, k_ref, m_ref, w_ref, out_ref, up_x, low_x, up_y, low_y, last_in, last_out, layer_done=None):
     w_all = w_ref[...]
     at_first = lax.broadcasted_iota(jnp.int32, (LY, LZ), 0) == 0
     last_in[LAST // B * LY :] = jnp.zeros((2 * LY, LZ), f32)
@@ -118,6 +119,8 @@
         up_y[B * LX + x : B * LX + x + 1] = tiles[4][LY - 1 :]
         carry = [parts[y][1] for y in range(LY)]
         last_carry = tiles[3]
+        if layer_done is not None:
+            layer_done(x)
 
 
 def is_even(axis):
@@ -171,11 +174,8 @@
 
 
 def first_kernel(rhs_ref, hx_ref, hy_ref, k_ref, m_ref, w_ref,
-                 p_ref, snx, sfx, sny, sfy, v, ux, uy, last_in, last_out, upx, lowx, upy, lowy):
-    v[...] = rhs_ref[...]
-    ux[...] = hx_ref[...]
-    uy[...] = hy_ref[...]
-    apply_operator(v, ux, uy, k_ref, m_ref, w_ref, p_ref, upx, lowx, upy, lowy, last_in, last_out)
+                 p_ref, snx, sfx, sny, sfy, last_in, last_out, upx, lowx, upy, lowy):
+    apply_operator(rhs_ref, hx_ref, hy_ref, k_ref, m_ref, w_ref, p_ref, upx, lowx, upy, lowy, last_in, last_out)
     route(is_even("gx"), upx, lowx, snx, sfx)
     route(is_even("gy"), upy, lowy, sny, sfy)
 
@@ -203,19 +203,22 @@
     return jnp.sum(tile, 0, keepdims=True)
 
 
-def second_kernel(p_ref, rhs_ref, rfx, rfy, rny, rnx, snx, sfx, sny, sfy, k_ref, m_ref, w_ref,
-                  v1_ref, p1_ref, tnx, tfx, tny, tfy, sums_ref, ux, uy, last_in, last_out, upx, lowx, upy, lowy):
+def second_kernel(p_ref, rfx, rfy, rny, rnx, snx, sfx, sny, sfy, k_ref, m_ref, w_ref,
+                  v1_ref, p1_ref, tnx, tfx, tny, tfy, ux, uy, last_in, last_out, upx, lowx, upy, lowy):
     assemble(p_ref, snx, sfx, sny, sfy, rnx, rfx, rny, rfy, v1_ref, ux, uy)
-    v0 = rhs_ref[...]
+    apply_operator(v1_ref, ux, uy, k_ref, m_ref, w_ref, p1_ref, upx, lowx, upy, lowy, last_in, last_out)
+    route(is_even("gx"), upx, lowx, tnx, tfx)
+    route(is_even("gy"), upy, lowy, tny, tfy)
+
+
+def products_kernel(v0_ref, v1_ref, sums_ref):
+    v0 = v0_ref[...]
     v1 = v1_ref[...]
     sums_ref[0:8] = node_sum(v0)
     sums_ref[8:16] = node_sum(v1)
     sums_ref[16:24] = node_sum(v0 * v0)
     sums_ref[24:32] = node_sum(v0 * v1)
     sums_ref[32:40] = node_sum(v1 * v1)
-    apply_operator(v1_ref, ux, uy, k_ref, m_ref, w_ref, p1_ref, upx, lowx, upy, lowy, last_in, last_out)
-    route(is_even("gx"), upx, lowx, tnx, tfx)
-    route(is_even("gy"), upy, lowy, tny, tfy)
 
 
 def third_kernel(p_ref, v1_ref, rfx, rfy, rny, rnx, snx, sfx, sny, sfy, sums_ref, k_ref, m_ref, w_ref,
@@ -229,9 +232,14 @@
     loads_ref[16:24] = node_sum(v2)
     m3 = node_sum(v1 * v2)
     m4 = node_sum(v2 * v2)
-    apply_operator(v2_ref, ux, uy, k_ref, m_ref, w_ref, p2_ref, upx, None, upy, None, last_in, last_out)
-    p2_copy = pltpu.make_async_copy(p2_ref, p2_out, p2_sem)
-    p2_copy.start()
+    p2_copies = [
+        pltpu.make_async_copy(p2_ref.reshape(F * A, LX, LY, LZ).at[:, x], p2_out.at[:, x], p2_sem.at[x]) for x in range(LX)
+    ]
+
+    def layer_done(x):
+        p2_copies[x].start()
+
+    apply_operator(v2_ref, ux, uy, k_ref, m_ref, w_ref, p2_ref, upx, None, upy, None, last_in, last_out, layer_done)
     p2 = p2_ref[...]
     above = upx[...]
     loads_ref[24:32] = node_sum(p2)
@@ -246,13 +254,12 @@
     loads_ref[46:47] = row(upy[...])
     loads_ref[47:48] = jnp.zeros((1, LZ), f32)
     v2_copy.wait()
-    p2_copy.wait()
-
-
-def weigh_kernel(own, near, far, both, upx, upy, *outs, table, ny):
-    *outs, mom_ref, cx_ref, cy_ref = outs
-    cx_ref[...] = upx[...]
-    cy_ref[...] = upy[...]
+    for copy in p2_copies:
+        copy.wait()
+
+
+def weigh_kernel(own, near, far, both, *outs, table, ny):
+    *outs, mom_ref = outs
     nx = len(table)
     me = lax.axis_index("gx")
     q = lax.rem(me, 4)
@@ -284,6 +291,7 @@
             edge = edge + ref[46:47] * w
         for k in range(4):
             out[k * 8 : k * 8 + 8] = total[k]
+        out[32:] = jnp.zeros((out.shape[0] - 32, LZ), f32)
         pair = jnp.concatenate([packed, edge] * 4, 0)
         first = lax.rem(lax.div(me, 4) + z, groups) * (2 * ny)
         for at in range(0, 2 * ny, 8):
@@ -317,22 +325,26 @@
 
 
 def moments(got):
-    pairs = [(got[at : at + 8], jnp.zeros((8, LZ), f32)) for at in range(0, got.shape[0], 8)]
+    zero = jnp.zeros((8, LZ), f32)
+    pairs = [(got[at : at + 8], zero) for at in range(0, got.shape[0], 8)]
     while len(pairs) > 1:
         pairs = [pair_add(a, b) for a, b in zip(pairs[::2], pairs[1::2])]
-    t = pairs[0]
-    for rows in (4, 2):
-        t = pair_add(t, tuple(pltpu.roll(p, rows, 0) for p in t))
-    for lanes in (8, 4, 2, 1):
-        t = pair_add(t, tuple(pltpu.roll(p, LZ - lanes, 1) for p in t))
-    c = t[0][0:1, 16:17] / t[0][0:1, 0:1]
-    wide = jnp.broadcast_to(c, (8, LZ))
-    m = [t[0][0:1, 0:1]]
-    for _ in range(5):
-        up = tuple(pltpu.roll(p, LZ - 16, 1) for p in t)
-        t = pair_add(up, pair_times(t, -wide))
-        m.append(t[0][0:1, 0:1])
-    return c, m
+    h, l = pairs[0]
+    rows = [(h[r : r + 1], l[r : r + 1]) for r in (0, 2, 4, 6)]
+    t = pair_add(pair_add(rows[0], rows[1]), pair_add(rows[2], rows[3]))
+    level = [t] + [tuple(pltpu.roll(p, LZ - 16 * k, 1) for p in t) for k in range(1, 6)]
+    inside = lax.broadcasted_iota(jnp.int32, (1, LZ), 1) < 16
+
+    def total(value):
+        return jnp.sum(jnp.where(inside, value, 0.0), axis=1, keepdims=True)
+
+    c = total(level[1][0]) / total(level[0][0])
+    minus = jnp.broadcast_to(-c, (1, LZ))
+    heads = [level[0]]
+    while len(level) > 1:
+        level = [pair_add(up, pair_times(at, minus)) for at, up in zip(level, level[1:])]
+        heads.append(level[0])
+    return c, [total(p[0] + p[1]) for p in heads]
 
 
 def conjugate_gradient(c, m):
@@ -452,7 +464,6 @@
     m2 = mass.reshape(CELLS, LZ)
     sends = [struct(vx, LZ), struct(vx, LZ), struct(vy, LZ), struct(vy, LZ)]
     upper = [pltpu.VMEM((vx, LZ), f32), pltpu.VMEM((vy, LZ), f32)] + [pltpu.VMEM((8 * LY, LZ), f32)] * 2
-    field = [pltpu.VMEM((ROWS, LZ), f32)] + upper
     edges = [pltpu.VMEM((vx, LZ), f32)] * 2 + [pltpu.VMEM((vy, LZ), f32)] * 2
 
     def call(kernel, name, ins, outs, scratch=(), **static):
@@ -492,32 +503,33 @@
     )
 
     p0, *s = call(
-        first_kernel, "first", [rhs2, hx, hy, k2, m2, w], [struct(ROWS, LZ)] + sends, field + edges,
+        first_kernel, "first", [rhs2, hx, hy, k2, m2, w], [struct(ROWS, LZ)] + sends, upper[2:] + edges,
     )
     r = swap(s)
-    v1, p1, *s, sums = call(
-        second_kernel, "second", [p0, rhs2, *r, *s, k2, m2, w],
-        [struct(ROWS, LZ), struct(ROWS, LZ)] + sends + [struct(40, LZ)], upper + edges,
+    v1, p1, *s = call(
+        second_kernel, "second", [p0, *r, *s, k2, m2, w],
+        [struct(ROWS, LZ), struct(ROWS, LZ)] + sends, upper + edges,
     )
     r = swap(s)
+    sums, = call(products_kernel, "products", [rhs2, v1], [struct(40, LZ)])
     dma = pltpu.SemaphoreType.DMA
     v2, p2, upx, upy, loads = call(
         third_kernel, "third", [p1, v1, *r, *s, sums, k2, m2, w],
-        [pltpu.HBM((ROWS, LZ), f32)] * 2 + [struct(vx, LZ), struct(vy, LZ), struct(48, LZ)],
-        [field[0], pltpu.VMEM((ROWS, LZ), f32)] + upper + [dma, dma],
+        [pltpu.HBM((ROWS, LZ), f32), pltpu.HBM((F * A, LX, LY, LZ), f32), struct(vx, LZ), struct(vy, LZ), struct(48, LZ)],
+        [pltpu.VMEM((ROWS, LZ), f32)] * 2 + upper + [dma, pltpu.SemaphoreType.DMA((LX,))],
     )
     table = [float(t) for t in jacobi_weights(nx)]
     group = [lax.ppermute(loads, "gx", [(i, i ^ b) for i in range(nx)]) for b in (1, 2, 3)]
-    *pieces, mom, upx, upy = call(
-        weigh_kernel, "weigh", [loads, *group, upx, upy],
-        [struct(32, LZ)] * (nx // 4) + [struct(nx // 4 * ny * 2, LZ), struct(vx, LZ), struct(vy, LZ)], table=table, ny=ny,
+    *pieces, mom = call(
+        weigh_kernel, "weigh", [loads, *group],
+        [struct(PIECE, LZ)] * (nx // 4) + [struct(nx // 4 * ny * 2, LZ)], table=table, ny=ny,
     )
     coarse = [pieces[0]] + [shifted(p, "gx", 4 * z) for z, p in enumerate(pieces) if z]
     alike = [[(4 * z + q) * ny + y for z in range(nx // 4) for y in range(ny)] for q in range(4)]
     got = lax.all_to_all(mom.reshape(-1, 2, LZ), ("gx", "gy"), 0, 0, tiled=True, axis_index_groups=alike).reshape(mom.shape)
     rx = shifted(upx, "gx", 1)
     ry = shifted(upy, "gy", 1)
-    v2, p2 = (pltpu.with_memory_space_constraint(v, pltpu.HBM) for v in (v2, p2))
+    v2, p2 = (pltpu.with_memory_space_constraint(v, pltpu.HBM) for v in (v2, p2.reshape(ROWS, LZ)))
     sol, res, coarse = call(
         last_kernel, "last", [(prolong, SM), got, *coarse, inv, rhs2, v1, (v2, ANY), (p2, ANY), rx, ry],
         [pltpu.HBM((ROWS, LZ), f32)] * 2 + [struct(LY, LZ)],

time: 72.4 us -> 74.3 us (1.026); the launches traced: 71.4 us -> 74.1 us
  waiting for transfers between devices: 14 us -> 20.3 us
  starting transfers between devices: 35.7 us -> 33.8 us
  Pallas kernels: 18.9 us -> 17.2 us
    all_to_all x1, waiting for transfers between devices: 0.01 us -> 8.26 us  [shards(): lax.all_to_all(mom.reshape(-1, 2, LZ), ('gx', 'gy'), 0, 0, tiled=True, ax...]
    all_to_all x1, starting transfers between devices: 7.15 us -> 3.85 us  [shards(): lax.all_to_all(mom.reshape(-1, 2, LZ), ('gx', 'gy'), 0, 0, tiled=True, ax...]
    ppermute x7, waiting for transfers between devices: 2.32 us -> 0.02 us  [shifted(): return lax.ppermute(value, axis, [(i, (i + by) % n) for i in range(n)])]
    pallas_call x7 -> x8, Pallas kernels: 18.9 us -> 17.2 us  [call(): pl.pallas_call(bound, out_shape=outs, in_specs=specs, out_specs=[ANY if i...]
    ppermute x7, starting transfers between devices: 15.5 us -> 16.9 us  [shifted(): return lax.ppermute(value, axis, [(i, (i + by) % n) for i in range(n)])]
    ppermute x3, waiting for transfers between devices: 2.06 us -> 2.83 us  [shards(): lax.ppermute(loads, 'gx', [(i, i ^ b) for i in range(nx)])]
  transfers between devices with their start and end apart: 19 -> 19, of which waited for: 6 -> 5; matrix products, arithmetic and copies ran while one was open for 0% -> 0% of each run, Pallas kernels for 2% -> 3%
where the time goes in v6:
time: 74.3 us; the launch traced here: 74.1 us
  starting transfers between devices  33.8 us (45%)
  waiting for transfers between devices  20.3 us (27%)
  Pallas kernels  17.2 us (23%)
  local copies, waits for them, and re-layouts  1.86 us (3%)
  between operations  0.97 us (1%)
    pallas_call x8, Pallas kernels, call(): pl.pallas_call(bound, out_shape=outs, in_specs=specs, out_specs=[ANY if i...  17.2 us
    ppermute x7, starting transfers between devices, shifted(): return lax.ppermute(value, axis, [(i, (i + by) % n) for i in range(n)])  16.9 us
    ppermute x4, starting transfers between devices, far_swap(): return lax.ppermute(value, axis, pairs)  9.56 us
    ppermute x4, waiting for transfers between devices, far_swap(): return lax.ppermute(value, axis, pairs)  9.15 us
    all_to_all x1, waiting for transfers between devices, shards(): lax.all_to_all(mom.reshape(-1, 2, LZ), ('gx', 'gy'), 0, 0, tiled=True, ax...  8.26 us
    all_to_all x1, starting transfers between devices, shards(): lax.all_to_all(mom.reshape(-1, 2, LZ), ('gx', 'gy'), 0, 0, tiled=True, ax...  3.85 us
    ppermute x3, starting transfers between devices, shards(): lax.ppermute(loads, 'gx', [(i, i ^ b) for i in range(nx)])  3.44 us
    ppermute x3, waiting for transfers between devices, shards(): lax.ppermute(loads, 'gx', [(i, i ^ b) for i in range(nx)])  2.83 us
  transfers between devices with their start and end apart: 19, of which 5 were waited for; matrix products, arithmetic and copies ran while one was open for 0% of the time, Pallas kernels for 3%

profile of v6, /device:TPU:0, one launch (start us, length us, event | category | flops | bytes accessed | tf_op | source)
XLA Modules:
  0.0 74.1 jit_solution(14990228020401149697)
XLA Ops:
  0.7 1.0 %edges.1 = (f32[25,8,128]{2,1,0:T(8,128)S(1)}, f32[25,4,128]{2,1,0:T(4,128)S(1)}) custom-call(f32[3,25,4,8,128]{4,3,2,1,0:T(8,128)} %refs_0_.3), custom_call_target="tpu_custom_call" | custom-call | tf_op jit(solution)/shard_map/edges/pallas_call | solution.py:476
  1.7 6.1 %collective-permute-start = (f32[200,128]{1,0:T(8,128)S(1)}, f32[200,128]{1,0:T(8,128)S(1)}, u32[]{:S(2)}, u32[]{:S(2)}) collective-permute-start(f32[200,128]{1,0:T(8,128)S(1)} %bitcast.20), channel_id=1, source_target_pairs={{0,120},{8,0},{16,8},{24,16},{32,24},{40,32},{48,40},{56,48},{64,5... | collective-permute-start | bytes 307208 | tf_op jit(solution)/shard_map/ppermute | solution.py:28
  7.8 3.1 %collective-permute-start.1 = (f32[100,128]{1,0:T(8,128)S(1)}, f32[100,128]{1,0:T(8,128)S(1)}, u32[]{:S(2)}, u32[]{:S(2)}) collective-permute-start(f32[100,128]{1,0:T(8,128)S(1)} %reshape.38), channel_id=1, source_target_pairs={{0,7},{1,0},{2,1},{3,2},{4,3},{5,4},{6,5},{7,6},{8,15},{9,8},{10,9... | collective-permute-start | bytes 153608 | tf_op jit(solution)/shard_map/ppermute | solution.py:28
  10.9 0.9 %copy-done.1 = f32[150,150]{1,0:T(8,128)S(1)} copy-done((f32[150,150]{1,0:T(8,128)S(1)}, f32[150,150]{1,0:T(8,128)}, u32[]{:S(2)}) %copy-start.1) | copy-done | bytes 90024
  12.7 1.2 %weights.1 = (bf16[304,480]{1,0:T(8,128)(2,1)S(1)}, f32[8,128]{1,0:T(8,128)S(1)}) custom-call(f32[150,150]{1,0:T(8,128)S(1)} %copy-done.1, f32[150,150]{1,0:T(8,128)S(1)} %copy-done.2), custom_call_target="tpu_custom_call" | custom-call | tf_op jit(solution)/shard_map/weights/pallas_call | solution.py:476
  13.9 2.7 %first.1 = (f32[2400,128]{1,0:T(8,128)S(1)}, f32[200,128]{1,0:T(8,128)S(1)}, f32[200,128]{1,0:T(8,128)S(1)}, f32[100,128]{1,0:T(8,128)S(1)}, f32[100,128]{1,0:T(8,128)S(1)}) custom-call(f32[2400,128]{1,0:T(8,128)S(1)} %bitcast.10, f32[200,128]{1,0:T(8,128)S(1)} %collective-permute-done.refs_1_, f32[100,128]{1,0:T(8,128)S(1)} %collective-permute-done.1.refs_2_, ...), custom_call_target="tpu_custom_call" | custom-call | tf_op jit(solution)/shard_map/first/pallas_call | solution.py:476
  16.7 1.6 %collective-permute-start.2 = (f32[200,128]{1,0:T(8,128)S(1)}, f32[200,128]{1,0:T(8,128)S(1)}, u32[]{:S(2)}, u32[]{:S(2)}) collective-permute-start(f32[200,128]{1,0:T(8,128)S(1)} %get-tuple-element.35.refs_6_), channel_id=1, source_target_pairs={{0,120},{8,16},{16,8},{24,32},{32,24},{40,48},{48,40},{56,64},{64,... | collective-permute-start | bytes 307208 | tf_op jit(solution)/shard_map/ppermute | solution.py:39
  18.3 3.0 %collective-permute-start.3 = (f32[100,128]{1,0:T(8,128)S(1)}, f32[100,128]{1,0:T(8,128)S(1)}, u32[]{:S(2)}, u32[]{:S(2)}) collective-permute-start(f32[100,128]{1,0:T(8,128)S(1)} %get-tuple-element.36.refs_8_), channel_id=1, source_target_pairs={{0,7},{1,2},{2,1},{3,4},{4,3},{5,6},{6,5},{7,0},{8,15},{9,10},{10,... | collective-permute-start | bytes 153608 | tf_op jit(solution)/shard_map/ppermute | solution.py:39
  21.4 4.3 %collective-permute-done.3.refs_2_ = f32[100,128]{1,0:T(8,128)S(1)} collective-permute-done((f32[100,128]{1,0:T(8,128)S(1)}, f32[100,128]{1,0:T(8,128)S(1)}, u32[]{:S(2)}, u32[]{:S(2)}) %collective-permute-start.3) | collective-permute-done | bytes 51232 | tf_op jit(solution)/shard_map/ppermute | solution.py:39
  25.6 3.0 %second.1 = (f32[2400,128]{1,0:T(8,128)S(1)}, f32[2400,128]{1,0:T(8,128)S(1)}, f32[200,128]{1,0:T(8,128)S(1)}, f32[200,128]{1,0:T(8,128)S(1)}, f32[100,128]{1,0:T(8,128)S(1)}, /*index=5*/f32[100,128]{1,0:T(8,128)S(1)}) custom-call(f32[2400,128]{1,0:T(8,128)S(1)} %get-tuple-element.34.refs_0_, f32[200,128]{1,0:T(8,128)S(1)} %collective-permute-done.2.refs_1_, ...), custom_call_target="tpu_custom_call" | custom-call | tf_op jit(solution)/shard_map/second/pallas_call | solution.py:476
  28.6 3.5 %collective-permute-start.6 = (f32[200,128]{1,0:T(8,128)S(1)}, f32[200,128]{1,0:T(8,128)S(1)}, u32[]{:S(2)}, u32[]{:S(2)}) collective-permute-start(f32[200,128]{1,0:T(8,128)S(1)} %get-tuple-element.41.refs_7_), channel_id=1, source_target_pairs={{0,120},{8,16},{16,8},{24,32},{32,24},{40,48},{48,40},{56,64},{64,... | collective-permute-start | bytes 307208 | tf_op jit(solution)/shard_map/ppermute | solution.py:39
  32.1 1.4 %collective-permute-start.7 = (f32[100,128]{1,0:T(8,128)S(1)}, f32[100,128]{1,0:T(8,128)S(1)}, u32[]{:S(2)}, u32[]{:S(2)}) collective-permute-start(f32[100,128]{1,0:T(8,128)S(1)} %get-tuple-element.42.refs_9_), channel_id=1, source_target_pairs={{0,7},{1,2},{2,1},{3,4},{4,3},{5,6},{6,5},{7,0},{8,15},{9,10},{10,... | collective-permute-start | bytes 153608 | tf_op jit(solution)/shard_map/ppermute | solution.py:39
  34.0 4.9 %collective-permute-done.7.refs_3_ = f32[100,128]{1,0:T(8,128)S(1)} collective-permute-done((f32[100,128]{1,0:T(8,128)S(1)}, f32[100,128]{1,0:T(8,128)S(1)}, u32[]{:S(2)}, u32[]{:S(2)}) %collective-permute-start.7) | collective-permute-done | bytes 51232 | tf_op jit(solution)/shard_map/ppermute | solution.py:39
  38.9 4.0 %third.1 = (f32[2400,128]{1,0:T(8,128)}, f32[75,4,8,128]{3,2,1,0:T(8,128)}, f32[200,128]{1,0:T(8,128)S(1)}, f32[100,128]{1,0:T(8,128)S(1)}, f32[48,128]{1,0:T(8,128)S(1)}) custom-call(f32[2400,128]{1,0:T(8,128)S(1)} %get-tuple-element.39.refs_0_, f32[2400,128]{1,0:T(8,128)S(1)} %get-tuple-element.40.refs_1_.refs_8_, ...), custom_call_target="tpu_custom_call" | custom-call | tf_op jit(solution)/shard_map/third/pallas_call | solution.py:476
  43.0 1.1 %collective-permute-start.12 = (f32[48,128]{1,0:T(8,128)S(1)}, f32[48,128]{1,0:T(8,128)S(1)}, u32[]{:S(2)}, u32[]{:S(2)}) collective-permute-start(f32[48,128]{1,0:T(8,128)S(1)} %get-tuple-element.45.refs_0_), channel_id=1, source_target_pairs={{0,24},{8,16},{16,8},{24,0},{32,56},{40,48},{48,40},{56,32},{64,88... | collective-permute-start | bytes 73736 | tf_op jit(solution)/shard_map/ppermute | solution.py:522
  44.1 1.8 %collective-permute-start.11 = (f32[48,128]{1,0:T(8,128)S(1)}, f32[48,128]{1,0:T(8,128)S(1)}, u32[]{:S(2)}, u32[]{:S(2)}) collective-permute-start(f32[48,128]{1,0:T(8,128)S(1)} %get-tuple-element.45.refs_0_), channel_id=1, source_target_pairs={{0,16},{8,24},{16,0},{24,8},{32,48},{40,56},{48,32},{56,40},{64,80... | collective-permute-start | bytes 73736 | tf_op jit(solution)/shard_map/ppermute | solution.py:522
  46.7 1.4 %collective-permute-done.12.refs_3_ = f32[48,128]{1,0:T(8,128)S(1)} collective-permute-done((f32[48,128]{1,0:T(8,128)S(1)}, f32[48,128]{1,0:T(8,128)S(1)}, u32[]{:S(2)}, u32[]{:S(2)}) %collective-permute-start.12) | collective-permute-done | bytes 24608 | tf_op jit(solution)/shard_map/ppermute | solution.py:522
  48.0 1.4 %collective-permute-done.11.refs_2_ = f32[48,128]{1,0:T(8,128)S(1)} collective-permute-done((f32[48,128]{1,0:T(8,128)S(1)}, f32[48,128]{1,0:T(8,128)S(1)}, u32[]{:S(2)}, u32[]{:S(2)}) %collective-permute-start.11) | collective-permute-done | bytes 24608 | tf_op jit(solution)/shard_map/ppermute | solution.py:522
  50.3 1.9 %collective-permute-start.13 = (f32[72,128]{1,0:T(8,128)S(1)}, f32[72,128]{1,0:T(8,128)S(1)}, u32[]{:S(2)}, u32[]{:S(2)}) collective-permute-start(f32[72,128]{1,0:T(8,128)S(1)} %get-tuple-element.48), channel_id=1, source_target_pairs={{0,32},{8,40},{16,48},{24,56},{32,64},{40,72},{48,80},{56,88},{64,... | collective-permute-start | bytes 110600 | tf_op jit(solution)/shard_map/ppermute | solution.py:28
  52.2 4.3 %collective-permute-start.14 = (f32[72,128]{1,0:T(8,128)S(1)}, f32[72,128]{1,0:T(8,128)S(1)}, u32[]{:S(2)}, u32[]{:S(2)}) collective-permute-start(f32[72,128]{1,0:T(8,128)S(1)} %get-tuple-element.49), channel_id=1, source_target_pairs={{0,64},{8,72},{16,80},{24,88},{32,96},{40,104},{48,112},{56,120},{... | collective-permute-start | bytes 110600 | tf_op jit(solution)/shard_map/ppermute | solution.py:28
  56.6 1.2 %collective-permute-start.15 = (f32[72,128]{1,0:T(8,128)S(1)}, f32[72,128]{1,0:T(8,128)S(1)}, u32[]{:S(2)}, u32[]{:S(2)}) collective-permute-start(f32[72,128]{1,0:T(8,128)S(1)} %get-tuple-element.50), channel_id=1, source_target_pairs={{0,96},{8,104},{16,112},{24,120},{32,0},{40,8},{48,16},{56,24},{64... | collective-permute-start | bytes 110600 | tf_op jit(solution)/shard_map/ppermute | solution.py:28
  57.8 3.9 %all-to-all-start = ((f32[32,2,128]{2,1,0:T(2,128)}), f32[32,2,128]{2,1,0:T(2,128)S(1)}, u32[]{:S(2)}, u32[]{:S(2)}) async-start(f32[32,2,128]{2,1,0:T(2,128)} %bitcast.4), calls=%async_computation | async-start | bytes 65536 | tf_op jit(solution)/shard_map/all_to_all | solution.py:529
  61.6 8.3 %all-to-all-done = f32[32,2,128]{2,1,0:T(2,128)S(1)} async-done(((f32[32,2,128]{2,1,0:T(2,128)}), f32[32,2,128]{2,1,0:T(2,128)S(1)}, u32[]{:S(2)}, u32[]{:S(2)}) %all-to-all-start) | async-done | bytes 32800 | tf_op jit(solution)/shard_map/all_to_all | solution.py:529
  69.9 4.0 %last.1 = (f32[2400,128]{1,0:T(8,128)}, f32[2400,128]{1,0:T(8,128)}, f32[8,128]{1,0:T(8,128)}) custom-call(f32[3,25]{1,0:T(4,128)S(1)} %copy-done.5, f32[64,128]{1,0:T(8,128)S(1)} %bitcast.19, f32[72,128]{1,0:T(8,128)S(1)} %get-tuple-element.47.refs_2_, f32[72,128]{1,0:T(8,128)S(1)} %collective-permute-done.13.refs_3_, ...), custom_call_target="tpu_custom_call" | custom-call | tf_op jit(solution)/shard_map/last/pallas_call | solution.py:476
  (35 shorter events, 3.0 us)
Async XLA Ops:
  0.6 13.3 %copy-start = (f32[3,25,4,8,128]{4,3,2,1,0:T(8,128)S(1)}, f32[3,25,4,8,128]{4,3,2,1,0:T(8,128)}, u32[]{:S(2)}) copy-start(f32[3,25,4,8,128]{4,3,2,1,0:T(8,128)} %refs_0_.3) | copy-start | bytes 3686404
  0.6 13.3 %copy-start.4 = (f32[4,8,128]{2,1,0:T(8,128)S(1)}, f32[4,8,128]{2,1,0:T(8,128)}, u32[]{:S(2)}) copy-start(f32[4,8,128]{2,1,0:T(8,128)} %param.8) | copy-start | bytes 49156
  0.7 13.3 %copy-start.3 = (f32[4,8,128]{2,1,0:T(8,128)S(1)}, f32[4,8,128]{2,1,0:T(8,128)}, u32[]{:S(2)}) copy-start(f32[4,8,128]{2,1,0:T(8,128)} %param.7) | copy-start | bytes 49156
  1.7 12.2 %collective-permute-start = (f32[200,128]{1,0:T(8,128)S(1)}, f32[200,128]{1,0:T(8,128)S(1)}, u32[]{:S(2)}, u32[]{:S(2)}) collective-permute-start(f32[200,128]{1,0:T(8,128)S(1)} %bitcast.20), channel_id=1, source_target_pairs={{0,120},{8,0},{16,8},{24,16},{32,24},{40,32},{48,40},{56,48},{64,5... | collective-permute-start | bytes 307208 | tf_op jit(solution)/shard_map/ppermute | solution.py:28
  7.8 6.1 %collective-permute-start.1 = (f32[100,128]{1,0:T(8,128)S(1)}, f32[100,128]{1,0:T(8,128)S(1)}, u32[]{:S(2)}, u32[]{:S(2)}) collective-permute-start(f32[100,128]{1,0:T(8,128)S(1)} %reshape.38), channel_id=1, source_target_pairs={{0,7},{1,0},{2,1},{3,2},{4,3},{5,4},{6,5},{7,6},{8,15},{9,8},{10,9... | collective-permute-start | bytes 153608 | tf_op jit(solution)/shard_map/ppermute | solution.py:28
  10.9 0.9 %copy-start.1 = (f32[150,150]{1,0:T(8,128)S(1)}, f32[150,150]{1,0:T(8,128)}, u32[]{:S(2)}) copy-start(f32[150,150]{1,0:T(8,128)} %refs_0_.4) | copy-start | bytes 270004
  16.7 9.0 %collective-permute-start.2 = (f32[200,128]{1,0:T(8,128)S(1)}, f32[200,128]{1,0:T(8,128)S(1)}, u32[]{:S(2)}, u32[]{:S(2)}) collective-permute-start(f32[200,128]{1,0:T(8,128)S(1)} %get-tuple-element.35.refs_6_), channel_id=1, source_target_pairs={{0,120},{8,16},{16,8},{24,32},{32,24},{40,48},{48,40},{56,64},{64,... | collective-permute-start | bytes 307208 | tf_op jit(solution)/shard_map/ppermute | solution.py:39
  18.3 7.3 %collective-permute-start.5 = (f32[200,128]{1,0:T(8,128)S(1)}, f32[200,128]{1,0:T(8,128)S(1)}, u32[]{:S(2)}, u32[]{:S(2)}) collective-permute-start(f32[200,128]{1,0:T(8,128)S(1)} %get-tuple-element.38.refs_5_), channel_id=1, source_target_pairs={{0,8},{8,0},{16,24},{24,16},{32,40},{40,32},{48,56},{56,48},{64,72... | collective-permute-start | bytes 307208 | tf_op jit(solution)/shard_map/ppermute | solution.py:33
  18.3 7.3 %collective-permute-start.3 = (f32[100,128]{1,0:T(8,128)S(1)}, f32[100,128]{1,0:T(8,128)S(1)}, u32[]{:S(2)}, u32[]{:S(2)}) collective-permute-start(f32[100,128]{1,0:T(8,128)S(1)} %get-tuple-element.36.refs_8_), channel_id=1, source_target_pairs={{0,7},{1,2},{2,1},{3,4},{4,3},{5,6},{6,5},{7,0},{8,15},{9,10},{10,... | collective-permute-start | bytes 153608 | tf_op jit(solution)/shard_map/ppermute | solution.py:39
  21.3 4.3 %collective-permute-start.4 = (f32[100,128]{1,0:T(8,128)S(1)}, f32[100,128]{1,0:T(8,128)S(1)}, u32[]{:S(2)}, u32[]{:S(2)}) collective-permute-start(f32[100,128]{1,0:T(8,128)S(1)} %get-tuple-element.37.refs_7_), channel_id=1, source_target_pairs={{0,1},{1,0},{2,3},{3,2},{4,5},{5,4},{6,7},{7,6},{8,9},{9,8},{10,11... | collective-permute-start | bytes 153608 | tf_op jit(solution)/shard_map/ppermute | solution.py:33
  28.6 10.2 %collective-permute-start.6 = (f32[200,128]{1,0:T(8,128)S(1)}, f32[200,128]{1,0:T(8,128)S(1)}, u32[]{:S(2)}, u32[]{:S(2)}) collective-permute-start(f32[200,128]{1,0:T(8,128)S(1)} %get-tuple-element.41.refs_7_), channel_id=1, source_target_pairs={{0,120},{8,16},{16,8},{24,32},{32,24},{40,48},{48,40},{56,64},{64,... | collective-permute-start | bytes 307208 | tf_op jit(solution)/shard_map/ppermute | solution.py:39
  32.1 6.7 %collective-permute-start.9 = (f32[200,128]{1,0:T(8,128)S(1)}, f32[200,128]{1,0:T(8,128)S(1)}, u32[]{:S(2)}, u32[]{:S(2)}) collective-permute-start(f32[200,128]{1,0:T(8,128)S(1)} %get-tuple-element.44.refs_6_), channel_id=1, source_target_pairs={{0,8},{8,0},{16,24},{24,16},{32,40},{40,32},{48,56},{56,48},{64,72... | collective-permute-start | bytes 307208 | tf_op jit(solution)/shard_map/ppermute | solution.py:33
  32.1 6.7 %collective-permute-start.7 = (f32[100,128]{1,0:T(8,128)S(1)}, f32[100,128]{1,0:T(8,128)S(1)}, u32[]{:S(2)}, u32[]{:S(2)}) collective-permute-start(f32[100,128]{1,0:T(8,128)S(1)} %get-tuple-element.42.refs_9_), channel_id=1, source_target_pairs={{0,7},{1,2},{2,1},{3,4},{4,3},{5,6},{6,5},{7,0},{8,15},{9,10},{10,... | collective-permute-start | bytes 153608 | tf_op jit(solution)/shard_map/ppermute | solution.py:39
  33.5 5.3 %collective-permute-start.8 = (f32[100,128]{1,0:T(8,128)S(1)}, f32[100,128]{1,0:T(8,128)S(1)}, u32[]{:S(2)}, u32[]{:S(2)}) collective-permute-start(f32[100,128]{1,0:T(8,128)S(1)} %get-tuple-element.43.refs_8_), channel_id=1, source_target_pairs={{0,1},{1,0},{2,3},{3,2},{4,5},{5,4},{6,7},{7,6},{8,9},{9,8},{10,11... | collective-permute-start | bytes 153608 | tf_op jit(solution)/shard_map/ppermute | solution.py:33
  38.9 31.0 %copy-start.5 = (f32[3,25]{1,0:T(4,128)S(1)}, f32[3,25]{1,0:T(4,128)}, u32[]{:S(2)}) copy-start(f32[3,25]{1,0:T(4,128)} %refs_0_.5) | copy-start | bytes 904
  42.9 27.0 %collective-permute-start.16 = (f32[200,128]{1,0:T(8,128)S(1)}, f32[200,128]{1,0:T(8,128)S(1)}, u32[]{:S(2)}, u32[]{:S(2)}) collective-permute-start(f32[200,128]{1,0:T(8,128)S(1)} %get-tuple-element.54), channel_id=1, source_target_pairs={{0,8},{8,16},{16,24},{24,32},{32,40},{40,48},{48,56},{56,64},{64,7... | collective-permute-start | bytes 307208 | tf_op jit(solution)/shard_map/ppermute | solution.py:28
  43.0 5.0 %collective-permute-start.12 = (f32[48,128]{1,0:T(8,128)S(1)}, f32[48,128]{1,0:T(8,128)S(1)}, u32[]{:S(2)}, u32[]{:S(2)}) collective-permute-start(f32[48,128]{1,0:T(8,128)S(1)} %get-tuple-element.45.refs_0_), channel_id=1, source_target_pairs={{0,24},{8,16},{16,8},{24,0},{32,56},{40,48},{48,40},{56,32},{64,88... | collective-permute-start | bytes 73736 | tf_op jit(solution)/shard_map/ppermute | solution.py:522
  44.1 5.3 %collective-permute-start.11 = (f32[48,128]{1,0:T(8,128)S(1)}, f32[48,128]{1,0:T(8,128)S(1)}, u32[]{:S(2)}, u32[]{:S(2)}) collective-permute-start(f32[48,128]{1,0:T(8,128)S(1)} %get-tuple-element.45.refs_0_), channel_id=1, source_target_pairs={{0,16},{8,24},{16,0},{24,8},{32,48},{40,56},{48,32},{56,40},{64,80... | collective-permute-start | bytes 73736 | tf_op jit(solution)/shard_map/ppermute | solution.py:522
  46.0 3.5 %collective-permute-start.10 = (f32[48,128]{1,0:T(8,128)S(1)}, f32[48,128]{1,0:T(8,128)S(1)}, u32[]{:S(2)}, u32[]{:S(2)}) collective-permute-start(f32[48,128]{1,0:T(8,128)S(1)} %get-tuple-element.45.refs_0_), channel_id=1, source_target_pairs={{0,8},{8,0},{16,24},{24,16},{32,40},{40,32},{48,56},{56,48},{64,72... | collective-permute-start | bytes 73736 | tf_op jit(solution)/shard_map/ppermute | solution.py:522
  46.5 15.2 %collective-permute-start.17 = (f32[100,128]{1,0:T(8,128)S(1)}, f32[100,128]{1,0:T(8,128)S(1)}, u32[]{:S(2)}, u32[]{:S(2)}) collective-permute-start(f32[100,128]{1,0:T(8,128)S(1)} %get-tuple-element.55), channel_id=1, source_target_pairs={{0,1},{1,2},{2,3},{3,4},{4,5},{5,6},{6,7},{7,0},{8,9},{9,10},{10,1... | collective-permute-start | bytes 153608 | tf_op jit(solution)/shard_map/ppermute | solution.py:28
  50.3 19.6 %collective-permute-start.13 = (f32[72,128]{1,0:T(8,128)S(1)}, f32[72,128]{1,0:T(8,128)S(1)}, u32[]{:S(2)}, u32[]{:S(2)}) collective-permute-start(f32[72,128]{1,0:T(8,128)S(1)} %get-tuple-element.48), channel_id=1, source_target_pairs={{0,32},{8,40},{16,48},{24,56},{32,64},{40,72},{48,80},{56,88},{64,... | collective-permute-start | bytes 110600 | tf_op jit(solution)/shard_map/ppermute | solution.py:28
  52.2 17.6 %collective-permute-start.14 = (f32[72,128]{1,0:T(8,128)S(1)}, f32[72,128]{1,0:T(8,128)S(1)}, u32[]{:S(2)}, u32[]{:S(2)}) collective-permute-start(f32[72,128]{1,0:T(8,128)S(1)} %get-tuple-element.49), channel_id=1, source_target_pairs={{0,64},{8,72},{16,80},{24,88},{32,96},{40,104},{48,112},{56,120},{... | collective-permute-start | bytes 110600 | tf_op jit(solution)/shard_map/ppermute | solution.py:28
  56.6 13.3 %collective-permute-start.15 = (f32[72,128]{1,0:T(8,128)S(1)}, f32[72,128]{1,0:T(8,128)S(1)}, u32[]{:S(2)}, u32[]{:S(2)}) collective-permute-start(f32[72,128]{1,0:T(8,128)S(1)} %get-tuple-element.50), channel_id=1, source_target_pairs={{0,96},{8,104},{16,112},{24,120},{32,0},{40,8},{48,16},{56,24},{64... | collective-permute-start | bytes 110600 | tf_op jit(solution)/shard_map/ppermute | solution.py:28
  57.8 12.1 %all-to-all-start = ((f32[32,2,128]{2,1,0:T(2,128)}), f32[32,2,128]{2,1,0:T(2,128)S(1)}, u32[]{:S(2)}, u32[]{:S(2)}) async-start(f32[32,2,128]{2,1,0:T(2,128)} %bitcast.4), calls=%async_computation | async-start | bytes 65536 | tf_op jit(solution)/shard_map/all_to_all | solution.py:529
  (1 other events, 0.9 us)

commit v7 on v6

--- a/solution.py
+++ b/solution.py
@@ -16,7 +16,6 @@
 CELLS = LX * LY
 FACE = A * CELLS
 ROWS = F * FACE
-PIECE = 72
 f32, bf16 = jnp.float32, jnp.bfloat16
 VM = pl.BlockSpec(memory_space=pltpu.VMEM)
 SM = pl.BlockSpec(memory_space=pltpu.SMEM)
@@ -222,7 +221,7 @@
 
 
 def third_kernel(p_ref, v1_ref, rfx, rfy, rny, rnx, snx, sfx, sny, sfy, sums_ref, k_ref, m_ref, w_ref,
-                 v2_out, p2_out, upx, upy, loads_ref, v2_ref, p2_ref, ux, uy, last_in, last_out, v2_sem, p2_sem):
+                 v2_out, p2_out, upx, upy, loads_ref, mom_ref, v2_ref, p2_ref, ux, uy, last_in, last_out, v2_sem, p2_sem):
     assemble(p_ref, snx, sfx, sny, sfy, rnx, rfx, rny, rfy, v2_ref, ux, uy)
     v2_copy = pltpu.make_async_copy(v2_ref, v2_out, v2_sem)
     v2_copy.start()
@@ -246,23 +245,27 @@
     loads_ref[32:40] = node_sum(above)
     energy = node_sum(v2_ref[...] * p2) + node_sum(ux[...] * above)
     tail = row(uy[...] * upy[...])
-    for k in range(3):
-        loads_ref[40 + k : 41 + k] = row(sums_ref[16 + 8 * k : 24 + 8 * k])
-    loads_ref[43:44] = row(m3)
-    loads_ref[44:45] = row(m4)
-    loads_ref[45:46] = row(energy) + tail
-    loads_ref[46:47] = row(upy[...])
-    loads_ref[47:48] = jnp.zeros((1, LZ), f32)
+    tile = jnp.concatenate(
+        [row(sums_ref[16 + 8 * k : 24 + 8 * k]) for k in range(3)]
+        + [row(m3), row(m4), row(energy) + tail, jnp.zeros((2, LZ), f32)], 0,
+    )
+    for lanes in (64, 32, 16):
+        tile = tile + pltpu.roll(tile, lanes, 1)
+    lane = lax.broadcasted_iota(jnp.int32, (8, LZ), 1)
+    moment = lax.broadcasted_iota(jnp.int32, (8, LZ), 0)
+    packed = row(jnp.where(lax.div(lane, 16) == moment, tile, 0.0))
+    pair = jnp.concatenate([packed, row(upy[...])] * 4, 0)
+    for at in range(0, mom_ref.shape[0], 8):
+        mom_ref[at : at + 8] = pair
+    loads_ref[40:] = jnp.zeros((loads_ref.shape[0] - 40, LZ), f32)
     v2_copy.wait()
     for copy in p2_copies:
         copy.wait()
 
 
-def weigh_kernel(own, near, far, both, *outs, table, ny):
-    *outs, mom_ref = outs
+def weigh_kernel(own, near, far, both, *outs, table):
     nx = len(table)
-    me = lax.axis_index("gx")
-    q = lax.rem(me, 4)
+    q = lax.rem(lax.axis_index("gx"), 4)
     low, high = lax.rem(q, 2) == 0, q < 2
     one, two = jnp.where(low, 1, -1), jnp.where(high, 2, -2)
     sources = ((own, 0, (0,)), (near, one, (1, -1)), (far, two, (2, -2)), (both, one + two, (3, 1, -1, -3)))
@@ -273,29 +276,15 @@
             value = jnp.where(shift == s, table[(at - s) % nx], value)
         return value
 
-    tile = own[40:48] + near[40:48] + far[40:48] + both[40:48]
-    for lanes in (64, 32, 16):
-        tile = tile + pltpu.roll(tile, lanes, 1)
-    lane = lax.broadcasted_iota(jnp.int32, (8, LZ), 1)
-    moment = lax.broadcasted_iota(jnp.int32, (8, LZ), 0)
-    packed = row(jnp.where((lax.div(lane, 16) == moment) & (moment < 6), tile, 0.0))
-    groups = nx // 4
     for z, out in enumerate(outs):
         total = [0.0] * 4
-        edge = 0.0
         for ref, shift, span in sources:
             w = pick(4 * z, shift, span)
             for k in range(4):
                 total[k] = total[k] + ref[k * 8 : k * 8 + 8] * w
             total[3] = total[3] + ref[32:40] * pick(4 * z - 1, shift, span)
-            edge = edge + ref[46:47] * w
         for k in range(4):
             out[k * 8 : k * 8 + 8] = total[k]
-        out[32:] = jnp.zeros((out.shape[0] - 32, LZ), f32)
-        pair = jnp.concatenate([packed, edge] * 4, 0)
-        first = lax.rem(lax.div(me, 4) + z, groups) * (2 * ny)
-        for at in range(0, 2 * ny, 8):
-            mom_ref[pl.ds(pl.multiple_of(first + at, 8), 8), :] = pair
 
 
 def two_sum(a, b):
@@ -393,7 +382,7 @@
 
 
 def last_kernel(prolong_ref, got_ref, c0, c1, c2, c3, inv_ref, rhs_ref, v1_ref, v2_hbm, p2_hbm, rx_ref, ry_ref,
-                sol_hbm, res_hbm, coarse_ref, v2_ref, p2_ref, sol_ref, res_ref, in_sems, out_sems, *, ny):
+                sol_hbm, res_hbm, coarse_ref, v2_ref, p2_ref, sol_ref, res_ref, in_sems, out_sems, *, table, ny):
     fetches = []
     for f in range(F):
         rows = pl.ds(f * FACE, FACE)
@@ -404,9 +393,12 @@
     inv = inv_ref[0:1, 0:1]
     x = [t * inv for t in x]
     below = lax.rem(lax.axis_index("gy") + ny - 1, ny)
+    me = lax.axis_index("gx")
+    nx = len(table)
     edge = jnp.zeros((1, LZ), f32)
-    for z in range(got_ref.shape[0] // (2 * ny)):
-        edge = edge + got_ref[pl.ds(2 * (z * ny + below) + 1, 1), :]
+    for offset, weight in enumerate(table):
+        slab = lax.rem(me + nx - offset, nx)
+        edge = edge + got_ref[pl.ds(2 * (slab * ny + below) + 1, 1), :] * weight
     circ = [c0[k * 8 : k * 8 + 8] + c1[k * 8 : k * 8 + 8] + c2[k * 8 : k * 8 + 8] + c3[k * 8 : k * 8 + 8] for k in range(4)]
     at_first = lax.broadcasted_iota(jnp.int32, (LY, LZ), 0) == 0
     circ[3] = circ[3] + jnp.where(at_first, jnp.broadcast_to(edge, (LY, LZ)), 0.0)
@@ -513,27 +505,25 @@
     r = swap(s)
     sums, = call(products_kernel, "products", [rhs2, v1], [struct(40, LZ)])
     dma = pltpu.SemaphoreType.DMA
-    v2, p2, upx, upy, loads = call(
+    peers = nx * ny * 2
+    v2, p2, upx, upy, loads, mom = call(
         third_kernel, "third", [p1, v1, *r, *s, sums, k2, m2, w],
-        [pltpu.HBM((ROWS, LZ), f32), pltpu.HBM((F * A, LX, LY, LZ), f32), struct(vx, LZ), struct(vy, LZ), struct(48, LZ)],
+        [pltpu.HBM((ROWS, LZ), f32), pltpu.HBM((F * A, LX, LY, LZ), f32), struct(vx, LZ), struct(vy, LZ)]
+        + [struct(peers + 8, LZ), struct(peers, LZ)],
         [pltpu.VMEM((ROWS, LZ), f32)] * 2 + upper + [dma, pltpu.SemaphoreType.DMA((LX,))],
     )
     table = [float(t) for t in jacobi_weights(nx)]
     group = [lax.ppermute(loads, "gx", [(i, i ^ b) for i in range(nx)]) for b in (1, 2, 3)]
-    *pieces, mom = call(
-        weigh_kernel, "weigh", [loads, *group],
-        [struct(PIECE, LZ)] * (nx // 4) + [struct(nx // 4 * ny * 2, LZ)], table=table, ny=ny,
-    )
+    pieces = call(weigh_kernel, "weigh", [loads, *group], [struct(32, LZ)] * (nx // 4), table=table)
     coarse = [pieces[0]] + [shifted(p, "gx", 4 * z) for z, p in enumerate(pieces) if z]
-    alike = [[(4 * z + q) * ny + y for z in range(nx // 4) for y in range(ny)] for q in range(4)]
-    got = lax.all_to_all(mom.reshape(-1, 2, LZ), ("gx", "gy"), 0, 0, tiled=True, axis_index_groups=alike).reshape(mom.shape)
+    got = lax.all_to_all(mom.reshape(-1, 2, LZ), ("gx", "gy"), 0, 0, tiled=True).reshape(mom.shape)
     rx = shifted(upx, "gx", 1)
     ry = shifted(upy, "gy", 1)
     v2, p2 = (pltpu.with_memory_space_constraint(v, pltpu.HBM) for v in (v2, p2.reshape(ROWS, LZ)))
     sol, res, coarse = call(
         last_kernel, "last", [(prolong, SM), got, *coarse, inv, rhs2, v1, (v2, ANY), (p2, ANY), rx, ry],
         [pltpu.HBM((ROWS, LZ), f32)] * 2 + [struct(LY, LZ)],
-        [pltpu.VMEM((ROWS, LZ), f32)] * 4 + [pltpu.SemaphoreType.DMA((6,))] * 2, ny=ny,
+        [pltpu.VMEM((ROWS, LZ), f32)] * 4 + [pltpu.SemaphoreType.DMA((6,))] * 2, table=table, ny=ny,
     )
     return sol.reshape(rhs.shape), res.reshape(rhs.shape), coarse[None]
 

time: 74.3 us -> 68.2 us (0.918); the launches traced: 74.1 us -> 66.9 us
  waiting for transfers between devices: 20.3 us -> 11.7 us
  starting transfers between devices: 33.8 us -> 35 us
    all_to_all x1, waiting for transfers between devices: 8.26 us -> 1.2 us  [shards(): lax.all_to_all(mom.reshape(-1, 2, LZ), ('gx', 'gy'), 0, 0, tiled=True)]
    ppermute x3, waiting for transfers between devices: 2.83 us -> 0.01 us  [shards(): lax.ppermute(loads, 'gx', [(i, i ^ b) for i in range(nx)])]
    all_to_all x1, starting transfers between devices: 3.85 us -> 5.55 us  [shards(): lax.all_to_all(mom.reshape(-1, 2, LZ), ('gx', 'gy'), 0, 0, tiled=True)]
    ppermute x7, waiting for transfers between devices: 0.02 us -> 1.35 us  [shifted(): return lax.ppermute(value, axis, [(i, (i + by) % n) for i in range(n)])]
  transfers between devices with their start and end apart: 19 -> 19, of which waited for: 5 -> 6; matrix products, arithmetic and copies ran while one was open for 0% -> 0% of each run, Pallas kernels for 3% -> 2%
where the time goes in v7:
time: 68.2 us; the launch traced here: 66.9 us
  starting transfers between devices  35 us (51%)
  Pallas kernels  17.4 us (26%)
  waiting for transfers between devices  11.7 us (17%)
  local copies, waits for them, and re-layouts  1.86 us (3%)
  between operations  0.96 us (1%)
    pallas_call x8, Pallas kernels, call(): pl.pallas_call(bound, out_shape=outs, in_specs=specs, out_specs=[ANY if i...  17.4 us
    ppermute x7, starting transfers between devices, shifted(): return lax.ppermute(value, axis, [(i, (i + by) % n) for i in range(n)])  16.4 us
    ppermute x4, starting transfers between devices, far_swap(): return lax.ppermute(value, axis, pairs)  9.56 us
    ppermute x4, waiting for transfers between devices, far_swap(): return lax.ppermute(value, axis, pairs)  9.15 us
    all_to_all x1, starting transfers between devices, shards(): lax.all_to_all(mom.reshape(-1, 2, LZ), ('gx', 'gy'), 0, 0, tiled=True)  5.55 us
    ppermute x3, starting transfers between devices, shards(): lax.ppermute(loads, 'gx', [(i, i ^ b) for i in range(nx)])  3.44 us
    unnamed x12, local copies, waits for them, and re-layouts  1.84 us
  transfers between devices with their start and end apart: 19, of which 6 were waited for; matrix products, arithmetic and copies ran while one was open for 0% of the time, Pallas kernels for 2%

profile of v7, /device:TPU:0, one launch (start us, length us, event | category | flops | bytes accessed | tf_op | source)
XLA Modules:
  0.0 66.9 jit_solution(4357030938017079435)
XLA Ops:
  0.7 1.0 %edges.1 = (f32[25,8,128]{2,1,0:T(8,128)S(1)}, f32[25,4,128]{2,1,0:T(4,128)S(1)}) custom-call(f32[3,25,4,8,128]{4,3,2,1,0:T(8,128)} %refs_0_.3), custom_call_target="tpu_custom_call" | custom-call | tf_op jit(solution)/shard_map/edges/pallas_call | solution.py:468
  1.7 6.1 %collective-permute-start = (f32[200,128]{1,0:T(8,128)S(1)}, f32[200,128]{1,0:T(8,128)S(1)}, u32[]{:S(2)}, u32[]{:S(2)}) collective-permute-start(f32[200,128]{1,0:T(8,128)S(1)} %bitcast.20), channel_id=1, source_target_pairs={{0,120},{8,0},{16,8},{24,16},{32,24},{40,32},{48,40},{56,48},{64,5... | collective-permute-start | bytes 307208 | tf_op jit(solution)/shard_map/ppermute | solution.py:27
  7.8 3.1 %collective-permute-start.1 = (f32[100,128]{1,0:T(8,128)S(1)}, f32[100,128]{1,0:T(8,128)S(1)}, u32[]{:S(2)}, u32[]{:S(2)}) collective-permute-start(f32[100,128]{1,0:T(8,128)S(1)} %reshape.38), channel_id=1, source_target_pairs={{0,7},{1,0},{2,1},{3,2},{4,3},{5,4},{6,5},{7,6},{8,15},{9,8},{10,9... | collective-permute-start | bytes 153608 | tf_op jit(solution)/shard_map/ppermute | solution.py:27
  10.9 0.9 %copy-done.1 = f32[150,150]{1,0:T(8,128)S(1)} copy-done((f32[150,150]{1,0:T(8,128)S(1)}, f32[150,150]{1,0:T(8,128)}, u32[]{:S(2)}) %copy-start.1) | copy-done | bytes 90024
  11.8 0.9 %copy-done.2 = f32[150,150]{1,0:T(8,128)S(1)} copy-done((f32[150,150]{1,0:T(8,128)S(1)}, f32[150,150]{1,0:T(8,128)}, u32[]{:S(2)}) %copy-start.2) | copy-done | bytes 90024
  12.7 1.2 %weights.1 = (bf16[304,480]{1,0:T(8,128)(2,1)S(1)}, f32[8,128]{1,0:T(8,128)S(1)}) custom-call(f32[150,150]{1,0:T(8,128)S(1)} %copy-done.1, f32[150,150]{1,0:T(8,128)S(1)} %copy-done.2), custom_call_target="tpu_custom_call" | custom-call | tf_op jit(solution)/shard_map/weights/pallas_call | solution.py:468
  13.9 2.7 %first.1 = (f32[2400,128]{1,0:T(8,128)S(1)}, f32[200,128]{1,0:T(8,128)S(1)}, f32[200,128]{1,0:T(8,128)S(1)}, f32[100,128]{1,0:T(8,128)S(1)}, f32[100,128]{1,0:T(8,128)S(1)}) custom-call(f32[2400,128]{1,0:T(8,128)S(1)} %bitcast.10, f32[200,128]{1,0:T(8,128)S(1)} %collective-permute-done.refs_1_, f32[100,128]{1,0:T(8,128)S(1)} %collective-permute-done.1.refs_2_, ...), custom_call_target="tpu_custom_call" | custom-call | tf_op jit(solution)/shard_map/first/pallas_call | solution.py:468
  16.7 1.6 %collective-permute-start.2 = (f32[200,128]{1,0:T(8,128)S(1)}, f32[200,128]{1,0:T(8,128)S(1)}, u32[]{:S(2)}, u32[]{:S(2)}) collective-permute-start(f32[200,128]{1,0:T(8,128)S(1)} %get-tuple-element.35.refs_6_), channel_id=1, source_target_pairs={{0,120},{8,16},{16,8},{24,32},{32,24},{40,48},{48,40},{56,64},{64,... | collective-permute-start | bytes 307208 | tf_op jit(solution)/shard_map/ppermute | solution.py:38
  18.3 3.0 %collective-permute-start.3 = (f32[100,128]{1,0:T(8,128)S(1)}, f32[100,128]{1,0:T(8,128)S(1)}, u32[]{:S(2)}, u32[]{:S(2)}) collective-permute-start(f32[100,128]{1,0:T(8,128)S(1)} %get-tuple-element.36.refs_8_), channel_id=1, source_target_pairs={{0,7},{1,2},{2,1},{3,4},{4,3},{5,6},{6,5},{7,0},{8,15},{9,10},{10,... | collective-permute-start | bytes 153608 | tf_op jit(solution)/shard_map/ppermute | solution.py:38
  21.4 4.3 %collective-permute-done.3.refs_2_ = f32[100,128]{1,0:T(8,128)S(1)} collective-permute-done((f32[100,128]{1,0:T(8,128)S(1)}, f32[100,128]{1,0:T(8,128)S(1)}, u32[]{:S(2)}, u32[]{:S(2)}) %collective-permute-start.3) | collective-permute-done | bytes 51232 | tf_op jit(solution)/shard_map/ppermute | solution.py:38
  25.6 3.0 %second.1 = (f32[2400,128]{1,0:T(8,128)S(1)}, f32[2400,128]{1,0:T(8,128)S(1)}, f32[200,128]{1,0:T(8,128)S(1)}, f32[200,128]{1,0:T(8,128)S(1)}, f32[100,128]{1,0:T(8,128)S(1)}, /*index=5*/f32[100,128]{1,0:T(8,128)S(1)}) custom-call(f32[2400,128]{1,0:T(8,128)S(1)} %get-tuple-element.34.refs_0_, f32[200,128]{1,0:T(8,128)S(1)} %collective-permute-done.2.refs_1_, ...), custom_call_target="tpu_custom_call" | custom-call | tf_op jit(solution)/shard_map/second/pallas_call | solution.py:468
  28.6 3.5 %collective-permute-start.6 = (f32[200,128]{1,0:T(8,128)S(1)}, f32[200,128]{1,0:T(8,128)S(1)}, u32[]{:S(2)}, u32[]{:S(2)}) collective-permute-start(f32[200,128]{1,0:T(8,128)S(1)} %get-tuple-element.41.refs_7_), channel_id=1, source_target_pairs={{0,120},{8,16},{16,8},{24,32},{32,24},{40,48},{48,40},{56,64},{64,... | collective-permute-start | bytes 307208 | tf_op jit(solution)/shard_map/ppermute | solution.py:38
  32.1 1.4 %collective-permute-start.7 = (f32[100,128]{1,0:T(8,128)S(1)}, f32[100,128]{1,0:T(8,128)S(1)}, u32[]{:S(2)}, u32[]{:S(2)}) collective-permute-start(f32[100,128]{1,0:T(8,128)S(1)} %get-tuple-element.42.refs_9_), channel_id=1, source_target_pairs={{0,7},{1,2},{2,1},{3,4},{4,3},{5,6},{6,5},{7,0},{8,15},{9,10},{10,... | collective-permute-start | bytes 153608 | tf_op jit(solution)/shard_map/ppermute | solution.py:38
  34.0 4.9 %collective-permute-done.7.refs_3_ = f32[100,128]{1,0:T(8,128)S(1)} collective-permute-done((f32[100,128]{1,0:T(8,128)S(1)}, f32[100,128]{1,0:T(8,128)S(1)}, u32[]{:S(2)}, u32[]{:S(2)}) %collective-permute-start.7) | collective-permute-done | bytes 51232 | tf_op jit(solution)/shard_map/ppermute | solution.py:38
  38.9 4.8 %third.1 = (f32[2400,128]{1,0:T(8,128)}, f32[75,4,8,128]{3,2,1,0:T(8,128)}, f32[200,128]{1,0:T(8,128)S(1)}, f32[100,128]{1,0:T(8,128)S(1)}, f32[264,128]{1,0:T(8,128)S(1)}, /*index=5*/f32[256,128]{1,0:T(8,128)}) custom-call(f32[2400,128]{1,0:T(8,128)S(1)} %get-tuple-element.39.refs_0_, f32[2400,128]{1,0:T(8,128)S(1)} %get-tuple-element.40.refs_1_.refs_8_, ...), custom_call_target="tpu_custom_call" | custom-call | tf_op jit(solution)/shard_map/third/pallas_call | solution.py:468
  43.8 2.5 %collective-permute-start.11 = (f32[264,128]{1,0:T(8,128)S(1)}, f32[264,128]{1,0:T(8,128)S(1)}, u32[]{:S(2)}, u32[]{:S(2)}) collective-permute-start(f32[264,128]{1,0:T(8,128)S(1)} %get-tuple-element.46.refs_0_), channel_id=1, source_target_pairs={{0,16},{8,24},{16,0},{24,8},{32,48},{40,56},{48,32},{56,40},{64,80... | collective-permute-start | bytes 405512 | tf_op jit(solution)/shard_map/ppermute | solution.py:516
  47.2 5.5 %all-to-all-start = ((f32[128,2,128]{2,1,0:T(2,128)}), f32[128,2,128]{2,1,0:T(2,128)S(1)}, u32[]{:S(2)}, u32[]{:S(2)}) async-start(f32[128,2,128]{2,1,0:T(2,128)} %bitcast.4), calls=%async_computation | async-start | bytes 262144 | tf_op jit(solution)/shard_map/all_to_all | solution.py:519
  52.8 1.1 %collective-permute-start.17 = (f32[100,128]{1,0:T(8,128)S(1)}, f32[100,128]{1,0:T(8,128)S(1)}, u32[]{:S(2)}, u32[]{:S(2)}) collective-permute-start(f32[100,128]{1,0:T(8,128)S(1)} %get-tuple-element.55), channel_id=1, source_target_pairs={{0,1},{1,2},{2,3},{3,4},{4,5},{5,6},{6,7},{7,0},{8,9},{9,10},{10,1... | collective-permute-start | bytes 153608 | tf_op jit(solution)/shard_map/ppermute | solution.py:27
  54.0 1.7 %collective-permute-start.13 = (f32[32,128]{1,0:T(8,128)S(1)}, f32[32,128]{1,0:T(8,128)S(1)}, u32[]{:S(2)}, u32[]{:S(2)}) collective-permute-start(f32[32,128]{1,0:T(8,128)S(1)} %get-tuple-element.48), channel_id=1, source_target_pairs={{0,32},{8,40},{16,48},{24,56},{32,64},{40,72},{48,80},{56,88},{64,... | collective-permute-start | bytes 49160 | tf_op jit(solution)/shard_map/ppermute | solution.py:27
  55.6 3.2 %collective-permute-start.14 = (f32[32,128]{1,0:T(8,128)S(1)}, f32[32,128]{1,0:T(8,128)S(1)}, u32[]{:S(2)}, u32[]{:S(2)}) collective-permute-start(f32[32,128]{1,0:T(8,128)S(1)} %get-tuple-element.49), channel_id=1, source_target_pairs={{0,64},{8,72},{16,80},{24,88},{32,96},{40,104},{48,112},{56,120},{... | collective-permute-start | bytes 49160 | tf_op jit(solution)/shard_map/ppermute | solution.py:27
  58.9 1.2 %collective-permute-start.15 = (f32[32,128]{1,0:T(8,128)S(1)}, f32[32,128]{1,0:T(8,128)S(1)}, u32[]{:S(2)}, u32[]{:S(2)}) collective-permute-start(f32[32,128]{1,0:T(8,128)S(1)} %get-tuple-element.50), channel_id=1, source_target_pairs={{0,96},{8,104},{16,112},{24,120},{32,0},{40,8},{48,16},{56,24},{64... | collective-permute-start | bytes 49160 | tf_op jit(solution)/shard_map/ppermute | solution.py:27
  60.1 1.0 %collective-permute-done.16.refs_11_ = f32[200,128]{1,0:T(8,128)S(1)} collective-permute-done((f32[200,128]{1,0:T(8,128)S(1)}, f32[200,128]{1,0:T(8,128)S(1)}, u32[]{:S(2)}, u32[]{:S(2)}) %collective-permute-start.16) | collective-permute-done | bytes 102432 | tf_op jit(solution)/shard_map/ppermute | solution.py:27
  61.1 1.2 %all-to-all-done = f32[128,2,128]{2,1,0:T(2,128)S(1)} async-done(((f32[128,2,128]{2,1,0:T(2,128)}), f32[128,2,128]{2,1,0:T(2,128)S(1)}, u32[]{:S(2)}, u32[]{:S(2)}) %all-to-all-start) | async-done | bytes 131104 | tf_op jit(solution)/shard_map/all_to_all | solution.py:519
  62.6 4.1 %last.1 = (f32[2400,128]{1,0:T(8,128)}, f32[2400,128]{1,0:T(8,128)}, f32[8,128]{1,0:T(8,128)}) custom-call(f32[3,25]{1,0:T(4,128)S(1)} %copy-done.5, f32[256,128]{1,0:T(8,128)S(1)} %bitcast.13, f32[32,128]{1,0:T(8,128)S(1)} %get-tuple-element.47.refs_2_, f32[32,128]{1,0:T(8,128)S(1)} %collective-permute-done.13.refs_3_, ...), custom_call_target="tpu_custom_call" | custom-call | tf_op jit(solution)/shard_map/last/pallas_call | solution.py:468
  (35 shorter events, 1.9 us)
Async XLA Ops:
  0.6 13.3 %copy-start = (f32[3,25,4,8,128]{4,3,2,1,0:T(8,128)S(1)}, f32[3,25,4,8,128]{4,3,2,1,0:T(8,128)}, u32[]{:S(2)}) copy-start(f32[3,25,4,8,128]{4,3,2,1,0:T(8,128)} %refs_0_.3) | copy-start | bytes 3686404
  0.6 13.3 %copy-start.4 = (f32[4,8,128]{2,1,0:T(8,128)S(1)}, f32[4,8,128]{2,1,0:T(8,128)}, u32[]{:S(2)}) copy-start(f32[4,8,128]{2,1,0:T(8,128)} %param.8) | copy-start | bytes 49156
  0.7 13.3 %copy-start.3 = (f32[4,8,128]{2,1,0:T(8,128)S(1)}, f32[4,8,128]{2,1,0:T(8,128)}, u32[]{:S(2)}) copy-start(f32[4,8,128]{2,1,0:T(8,128)} %param.7) | copy-start | bytes 49156
  1.7 12.2 %collective-permute-start = (f32[200,128]{1,0:T(8,128)S(1)}, f32[200,128]{1,0:T(8,128)S(1)}, u32[]{:S(2)}, u32[]{:S(2)}) collective-permute-start(f32[200,128]{1,0:T(8,128)S(1)} %bitcast.20), channel_id=1, source_target_pairs={{0,120},{8,0},{16,8},{24,16},{32,24},{40,32},{48,40},{56,48},{64,5... | collective-permute-start | bytes 307208 | tf_op jit(solution)/shard_map/ppermute | solution.py:27
  7.8 6.1 %collective-permute-start.1 = (f32[100,128]{1,0:T(8,128)S(1)}, f32[100,128]{1,0:T(8,128)S(1)}, u32[]{:S(2)}, u32[]{:S(2)}) collective-permute-start(f32[100,128]{1,0:T(8,128)S(1)} %reshape.38), channel_id=1, source_target_pairs={{0,7},{1,0},{2,1},{3,2},{4,3},{5,4},{6,5},{7,6},{8,15},{9,8},{10,9... | collective-permute-start | bytes 153608 | tf_op jit(solution)/shard_map/ppermute | solution.py:27
  11.8 0.9 %copy-start.2 = (f32[150,150]{1,0:T(8,128)S(1)}, f32[150,150]{1,0:T(8,128)}, u32[]{:S(2)}) copy-start(f32[150,150]{1,0:T(8,128)} %refs_1_.1) | copy-start | bytes 270004
  16.7 9.0 %collective-permute-start.2 = (f32[200,128]{1,0:T(8,128)S(1)}, f32[200,128]{1,0:T(8,128)S(1)}, u32[]{:S(2)}, u32[]{:S(2)}) collective-permute-start(f32[200,128]{1,0:T(8,128)S(1)} %get-tuple-element.35.refs_6_), channel_id=1, source_target_pairs={{0,120},{8,16},{16,8},{24,32},{32,24},{40,48},{48,40},{56,64},{64,... | collective-permute-start | bytes 307208 | tf_op jit(solution)/shard_map/ppermute | solution.py:38
  18.3 7.3 %collective-permute-start.5 = (f32[200,128]{1,0:T(8,128)S(1)}, f32[200,128]{1,0:T(8,128)S(1)}, u32[]{:S(2)}, u32[]{:S(2)}) collective-permute-start(f32[200,128]{1,0:T(8,128)S(1)} %get-tuple-element.38.refs_5_), channel_id=1, source_target_pairs={{0,8},{8,0},{16,24},{24,16},{32,40},{40,32},{48,56},{56,48},{64,72... | collective-permute-start | bytes 307208 | tf_op jit(solution)/shard_map/ppermute | solution.py:32
  18.3 7.3 %collective-permute-start.3 = (f32[100,128]{1,0:T(8,128)S(1)}, f32[100,128]{1,0:T(8,128)S(1)}, u32[]{:S(2)}, u32[]{:S(2)}) collective-permute-start(f32[100,128]{1,0:T(8,128)S(1)} %get-tuple-element.36.refs_8_), channel_id=1, source_target_pairs={{0,7},{1,2},{2,1},{3,4},{4,3},{5,6},{6,5},{7,0},{8,15},{9,10},{10,... | collective-permute-start | bytes 153608 | tf_op jit(solution)/shard_map/ppermute | solution.py:38
  21.3 4.3 %collective-permute-start.4 = (f32[100,128]{1,0:T(8,128)S(1)}, f32[100,128]{1,0:T(8,128)S(1)}, u32[]{:S(2)}, u32[]{:S(2)}) collective-permute-start(f32[100,128]{1,0:T(8,128)S(1)} %get-tuple-element.37.refs_7_), channel_id=1, source_target_pairs={{0,1},{1,0},{2,3},{3,2},{4,5},{5,4},{6,7},{7,6},{8,9},{9,8},{10,11... | collective-permute-start | bytes 153608 | tf_op jit(solution)/shard_map/ppermute | solution.py:32
  28.6 10.2 %collective-permute-start.6 = (f32[200,128]{1,0:T(8,128)S(1)}, f32[200,128]{1,0:T(8,128)S(1)}, u32[]{:S(2)}, u32[]{:S(2)}) collective-permute-start(f32[200,128]{1,0:T(8,128)S(1)} %get-tuple-element.41.refs_7_), channel_id=1, source_target_pairs={{0,120},{8,16},{16,8},{24,32},{32,24},{40,48},{48,40},{56,64},{64,... | collective-permute-start | bytes 307208 | tf_op jit(solution)/shard_map/ppermute | solution.py:38
  32.1 6.7 %collective-permute-start.9 = (f32[200,128]{1,0:T(8,128)S(1)}, f32[200,128]{1,0:T(8,128)S(1)}, u32[]{:S(2)}, u32[]{:S(2)}) collective-permute-start(f32[200,128]{1,0:T(8,128)S(1)} %get-tuple-element.44.refs_6_), channel_id=1, source_target_pairs={{0,8},{8,0},{16,24},{24,16},{32,40},{40,32},{48,56},{56,48},{64,72... | collective-permute-start | bytes 307208 | tf_op jit(solution)/shard_map/ppermute | solution.py:32
  32.1 6.7 %collective-permute-start.7 = (f32[100,128]{1,0:T(8,128)S(1)}, f32[100,128]{1,0:T(8,128)S(1)}, u32[]{:S(2)}, u32[]{:S(2)}) collective-permute-start(f32[100,128]{1,0:T(8,128)S(1)} %get-tuple-element.42.refs_9_), channel_id=1, source_target_pairs={{0,7},{1,2},{2,1},{3,4},{4,3},{5,6},{6,5},{7,0},{8,15},{9,10},{10,... | collective-permute-start | bytes 153608 | tf_op jit(solution)/shard_map/ppermute | solution.py:38
  33.5 5.3 %collective-permute-start.8 = (f32[100,128]{1,0:T(8,128)S(1)}, f32[100,128]{1,0:T(8,128)S(1)}, u32[]{:S(2)}, u32[]{:S(2)}) collective-permute-start(f32[100,128]{1,0:T(8,128)S(1)} %get-tuple-element.43.refs_8_), channel_id=1, source_target_pairs={{0,1},{1,0},{2,3},{3,2},{4,5},{5,4},{6,7},{7,6},{8,9},{9,8},{10,11... | collective-permute-start | bytes 153608 | tf_op jit(solution)/shard_map/ppermute | solution.py:32
  38.9 23.7 %copy-start.5 = (f32[3,25]{1,0:T(4,128)S(1)}, f32[3,25]{1,0:T(4,128)}, u32[]{:S(2)}) copy-start(f32[3,25]{1,0:T(4,128)} %refs_0_.5) | copy-start | bytes 904
  43.7 10.2 %collective-permute-start.12 = (f32[264,128]{1,0:T(8,128)S(1)}, f32[264,128]{1,0:T(8,128)S(1)}, u32[]{:S(2)}, u32[]{:S(2)}) collective-permute-start(f32[264,128]{1,0:T(8,128)S(1)} %get-tuple-element.46.refs_0_), channel_id=1, source_target_pairs={{0,24},{8,16},{16,8},{24,0},{32,56},{40,48},{48,40},{56,32},{64,88... | collective-permute-start | bytes 405512 | tf_op jit(solution)/shard_map/ppermute | solution.py:516
  43.8 10.1 %collective-permute-start.11 = (f32[264,128]{1,0:T(8,128)S(1)}, f32[264,128]{1,0:T(8,128)S(1)}, u32[]{:S(2)}, u32[]{:S(2)}) collective-permute-start(f32[264,128]{1,0:T(8,128)S(1)} %get-tuple-element.46.refs_0_), channel_id=1, source_target_pairs={{0,16},{8,24},{16,0},{24,8},{32,48},{40,56},{48,32},{56,40},{64,80... | collective-permute-start | bytes 405512 | tf_op jit(solution)/shard_map/ppermute | solution.py:516
  46.3 7.6 %collective-permute-start.10 = (f32[264,128]{1,0:T(8,128)S(1)}, f32[264,128]{1,0:T(8,128)S(1)}, u32[]{:S(2)}, u32[]{:S(2)}) collective-permute-start(f32[264,128]{1,0:T(8,128)S(1)} %get-tuple-element.46.refs_0_), channel_id=1, source_target_pairs={{0,8},{8,0},{16,24},{24,16},{32,40},{40,32},{48,56},{56,48},{64,72... | collective-permute-start | bytes 405512 | tf_op jit(solution)/shard_map/ppermute | solution.py:516
  47.2 15.1 %all-to-all-start = ((f32[128,2,128]{2,1,0:T(2,128)}), f32[128,2,128]{2,1,0:T(2,128)S(1)}, u32[]{:S(2)}, u32[]{:S(2)}) async-start(f32[128,2,128]{2,1,0:T(2,128)} %bitcast.4), calls=%async_computation | async-start | bytes 262144 | tf_op jit(solution)/shard_map/all_to_all | solution.py:519
  52.7 8.4 %collective-permute-start.16 = (f32[200,128]{1,0:T(8,128)S(1)}, f32[200,128]{1,0:T(8,128)S(1)}, u32[]{:S(2)}, u32[]{:S(2)}) collective-permute-start(f32[200,128]{1,0:T(8,128)S(1)} %get-tuple-element.54), channel_id=1, source_target_pairs={{0,8},{8,16},{16,24},{24,32},{32,40},{40,48},{48,56},{56,64},{64,7... | collective-permute-start | bytes 307208 | tf_op jit(solution)/shard_map/ppermute | solution.py:27
  52.8 7.2 %collective-permute-start.17 = (f32[100,128]{1,0:T(8,128)S(1)}, f32[100,128]{1,0:T(8,128)S(1)}, u32[]{:S(2)}, u32[]{:S(2)}) collective-permute-start(f32[100,128]{1,0:T(8,128)S(1)} %get-tuple-element.55), channel_id=1, source_target_pairs={{0,1},{1,2},{2,3},{3,4},{4,5},{5,6},{6,7},{7,0},{8,9},{9,10},{10,1... | collective-permute-start | bytes 153608 | tf_op jit(solution)/shard_map/ppermute | solution.py:27
  54.0 8.3 %collective-permute-start.13 = (f32[32,128]{1,0:T(8,128)S(1)}, f32[32,128]{1,0:T(8,128)S(1)}, u32[]{:S(2)}, u32[]{:S(2)}) collective-permute-start(f32[32,128]{1,0:T(8,128)S(1)} %get-tuple-element.48), channel_id=1, source_target_pairs={{0,32},{8,40},{16,48},{24,56},{32,64},{40,72},{48,80},{56,88},{64,... | collective-permute-start | bytes 49160 | tf_op jit(solution)/shard_map/ppermute | solution.py:27
  55.6 6.8 %collective-permute-start.14 = (f32[32,128]{1,0:T(8,128)S(1)}, f32[32,128]{1,0:T(8,128)S(1)}, u32[]{:S(2)}, u32[]{:S(2)}) collective-permute-start(f32[32,128]{1,0:T(8,128)S(1)} %get-tuple-element.49), channel_id=1, source_target_pairs={{0,64},{8,72},{16,80},{24,88},{32,96},{40,104},{48,112},{56,120},{... | collective-permute-start | bytes 49160 | tf_op jit(solution)/shard_map/ppermute | solution.py:27
  58.9 3.7 %collective-permute-start.15 = (f32[32,128]{1,0:T(8,128)S(1)}, f32[32,128]{1,0:T(8,128)S(1)}, u32[]{:S(2)}, u32[]{:S(2)}) collective-permute-start(f32[32,128]{1,0:T(8,128)S(1)} %get-tuple-element.50), channel_id=1, source_target_pairs={{0,96},{8,104},{16,112},{24,120},{32,0},{40,8},{48,16},{56,24},{64... | collective-permute-start | bytes 49160 | tf_op jit(solution)/shard_map/ppermute | solution.py:27
  (1 other events, 0.9 us)

commit v8 on v7

--- a/solution.py
+++ b/solution.py
@@ -16,6 +16,7 @@
 CELLS = LX * LY
 FACE = A * CELLS
 ROWS = F * FACE
+TAIL = F * CELLS * B
 f32, bf16 = jnp.float32, jnp.bfloat16
 VM = pl.BlockSpec(memory_space=pltpu.VMEM)
 SM = pl.BlockSpec(memory_space=pltpu.SMEM)
@@ -44,29 +45,35 @@
     return hi, lo
 
 
-def apply_operator(v_ref, ux_ref, uy_ref, k_ref, m_ref, w_ref, out_ref, up_x, low_x, up_y, low_y, last_in, last_out, layer_done=None):
+def apply_operator(v_ref, ux_ref, uy_ref, k_ref, m_ref, w_ref, out_ref, up_x, low_x, up_y, low_y, last_in, last_out, by_nodes=False):
     w_all = w_ref[...]
     at_first = lax.broadcasted_iota(jnp.int32, (LY, LZ), 0) == 0
     last_in[LAST // B * LY :] = jnp.zeros((2 * LY, LZ), f32)
 
+    def block(ref, at, pitch, i):
+        if by_nodes:
+            return ref[pl.ds(at * A + i, B, stride=pitch), :]
+        return ref[(at + i) * B : (at + i + 1) * B, :]
+
     def face(f, x, y):
         if f == 0 and x == LX:
-            return ux_ref[pl.ds(y, B, stride=LY), :]
+            return block(ux_ref, 0, LY, y)
         if f == 1 and y == LY:
-            return uy_ref[pl.ds(x, B, stride=LX), :]
-        return v_ref[pl.ds(f * FACE + x * LY + y, B, stride=CELLS), :]
+            return block(uy_ref, 0, LX, x)
+        return block(v_ref, f * CELLS, CELLS, x * LY + y)
 
     def last_rows(f, x):
         if x == LX:
             return ux_ref[B * LY :, :]
-        at = f * FACE + B * CELLS + x * LY
+        at = (f * FACE + B * CELLS if by_nodes else TAIL + f * CELLS) + x * LY
         return v_ref[at : at + LY, :]
 
     def put(f, x, y, value):
-        out_ref[pl.ds(f * FACE + x * LY + y, B, stride=CELLS), :] = value
+        at = (f * CELLS + x * LY + y) * B
+        out_ref[at : at + B, :] = value
 
     def put_last(f, x, value):
-        at = f * FACE + B * CELLS + x * LY
+        at = TAIL + f * CELLS + x * LY
         out_ref[at : at + LY, :] = value
 
     filler = jnp.zeros((IN - OUT, LZ), f32)
@@ -100,9 +107,9 @@
             put(1, x, y, wly if y == 0 else wly + parts[y - 1][3])
             put(2, x, y, wlz + pltpu.roll(wuz, 1, 1))
             if x == 0 and low_x is not None:
-                low_x[pl.ds(y, B, stride=LY), :] = wlx
+                low_x[y * B : (y + 1) * B] = wlx
             if x == LX - 1:
-                up_x[pl.ds(y, B, stride=LY), :] = wux
+                up_x[y * B : (y + 1) * B] = wux
         tiles = [last_out[j * LY : (j + 1) * LY] for j in range(6)]
         put_last(0, x, tiles[0] if x == 0 else tiles[0] + last_carry)
         put_last(1, x, tiles[1] + jnp.where(at_first, 0.0, pltpu.roll(tiles[4], 1, 0)))
@@ -112,14 +119,12 @@
         if x == LX - 1:
             up_x[B * LY :] = tiles[3]
         if low_y is not None:
-            low_y[pl.ds(x, B, stride=LX), :] = parts[0][2]
+            low_y[x * B : (x + 1) * B] = parts[0][2]
             low_y[B * LX + x : B * LX + x + 1] = tiles[1][:1]
-        up_y[pl.ds(x, B, stride=LX), :] = parts[LY - 1][3]
+        up_y[x * B : (x + 1) * B] = parts[LY - 1][3]
         up_y[B * LX + x : B * LX + x + 1] = tiles[4][LY - 1 :]
         carry = [parts[y][1] for y in range(LY)]
         last_carry = tiles[3]
-        if layer_done is not None:
-            layer_done(x)
 
 
 def is_even(axis):
@@ -174,7 +179,7 @@
 
 def first_kernel(rhs_ref, hx_ref, hy_ref, k_ref, m_ref, w_ref,
                  p_ref, snx, sfx, sny, sfy, last_in, last_out, upx, lowx, upy, lowy):
-    apply_operator(rhs_ref, hx_ref, hy_ref, k_ref, m_ref, w_ref, p_ref, upx, lowx, upy, lowy, last_in, last_out)
+    apply_operator(rhs_ref, hx_ref, hy_ref, k_ref, m_ref, w_ref, p_ref, upx, lowx, upy, lowy, last_in, last_out, True)
     route(is_even("gx"), upx, lowx, snx, sfx)
     route(is_even("gy"), upy, lowy, sny, sfy)
 
@@ -184,12 +189,14 @@
     even_y = is_even("gy")
     v[...] = p_ref[...]
     below_x = jnp.where(even_x, rfx[...], rnx[...])
-    for a in range(A):
-        rows = slice(a * CELLS, a * CELLS + LY)
-        v[rows, :] = v[rows, :] + below_x[a * LY : (a + 1) * LY]
+    v[: B * LY] = v[: B * LY] + below_x[: B * LY]
+    v[TAIL : TAIL + LY] = v[TAIL : TAIL + LY] + below_x[B * LY :]
     below_y = jnp.where(even_y, rfy[...], rny[...])
-    first = pl.ds(FACE, A * LX, stride=LY)
-    v[first, :] = v[first, :] + below_y
+    for x in range(LX):
+        at = (CELLS + x * LY) * B
+        v[at : at + B] = v[at : at + B] + below_y[x * B : (x + 1) * B]
+        at = TAIL + CELLS + x * LY
+        v[at : at + 1] = v[at : at + 1] + below_y[B * LX + x : B * LX + x + 1]
     ux[...] = jnp.where(even_x, snx[...] + rnx[...], sfx[...] + rfx[...])
     uy[...] = jnp.where(even_y, sny[...] + rny[...], sfy[...] + rfy[...])
 
@@ -210,40 +217,50 @@
     route(is_even("gy"), upy, lowy, tny, tfy)
 
 
+def element_sum(ref, faces):
+    rows = []
+    for y in range(LY):
+        total = 0.0
+        for at in range(0, faces, LY):
+            first = (at + y) * B
+            total = total + (ref[first : first + 8] + ref[first + 8 : first + 16] + ref[first + 16 : first + B])
+        rows.append(row(total))
+    return jnp.concatenate(rows, 0) + node_sum(ref[faces * B :])
+
+
+def tile_of(ref, faces, f, a, x):
+    at = f * CELLS + x * LY
+    if a == B:
+        return ref[faces * B + at : faces * B + at + LY, :]
+    return ref[pl.ds(at * B + a, LY, stride=B), :]
+
+
 def products_kernel(v0_ref, v1_ref, sums_ref):
-    v0 = v0_ref[...]
-    v1 = v1_ref[...]
-    sums_ref[0:8] = node_sum(v0)
-    sums_ref[8:16] = node_sum(v1)
-    sums_ref[16:24] = node_sum(v0 * v0)
-    sums_ref[24:32] = node_sum(v0 * v1)
-    sums_ref[32:40] = node_sum(v1 * v1)
+    s0 = s1 = s00 = s01 = s11 = 0.0
+    for f in range(F):
+        for a in range(A):
+            for x in range(LX):
+                at = (f * A + a) * CELLS + x * LY
+                v0 = v0_ref[at : at + LY, :]
+                v1 = tile_of(v1_ref, F * CELLS, f, a, x)
+                s0, s1, s00, s01, s11 = s0 + v0, s1 + v1, s00 + v0 * v0, s01 + v0 * v1, s11 + v1 * v1
+    for k, s in enumerate((s0, s1, s00, s01, s11)):
+        sums_ref[8 * k : 8 * k + 8] = s
 
 
 def third_kernel(p_ref, v1_ref, rfx, rfy, rny, rnx, snx, sfx, sny, sfy, sums_ref, k_ref, m_ref, w_ref,
-                 v2_out, p2_out, upx, upy, loads_ref, mom_ref, v2_ref, p2_ref, ux, uy, last_in, last_out, v2_sem, p2_sem):
+                 v2_ref, p2_ref, upx, upy, loads_ref, mom_ref, ux, uy, last_in, last_out):
     assemble(p_ref, snx, sfx, sny, sfy, rnx, rfx, rny, rfy, v2_ref, ux, uy)
-    v2_copy = pltpu.make_async_copy(v2_ref, v2_out, v2_sem)
-    v2_copy.start()
     v1 = v1_ref[...]
     v2 = v2_ref[...]
     loads_ref[0:16] = sums_ref[0:16]
-    loads_ref[16:24] = node_sum(v2)
+    loads_ref[16:24] = element_sum(v2_ref, F * CELLS)
     m3 = node_sum(v1 * v2)
     m4 = node_sum(v2 * v2)
-    p2_copies = [
-        pltpu.make_async_copy(p2_ref.reshape(F * A, LX, LY, LZ).at[:, x], p2_out.at[:, x], p2_sem.at[x]) for x in range(LX)
-    ]
-
-    def layer_done(x):
-        p2_copies[x].start()
-
-    apply_operator(v2_ref, ux, uy, k_ref, m_ref, w_ref, p2_ref, upx, None, upy, None, last_in, last_out, layer_done)
-    p2 = p2_ref[...]
-    above = upx[...]
-    loads_ref[24:32] = node_sum(p2)
-    loads_ref[32:40] = node_sum(above)
-    energy = node_sum(v2_ref[...] * p2) + node_sum(ux[...] * above)
+    apply_operator(v2_ref, ux, uy, k_ref, m_ref, w_ref, p2_ref, upx, None, upy, None, last_in, last_out)
+    loads_ref[24:32] = element_sum(p2_ref, F * CELLS)
+    loads_ref[32:40] = element_sum(upx, LY)
+    energy = node_sum(v2_ref[...] * p2_ref[...]) + node_sum(ux[...] * upx[...])
     tail = row(uy[...] * upy[...])
     tile = jnp.concatenate(
         [row(sums_ref[16 + 8 * k : 24 + 8 * k]) for k in range(3)]
@@ -258,9 +275,6 @@
     for at in range(0, mom_ref.shape[0], 8):
         mom_ref[at : at + 8] = pair
     loads_ref[40:] = jnp.zeros((loads_ref.shape[0] - 40, LZ), f32)
-    v2_copy.wait()
-    for copy in p2_copies:
-        copy.wait()
 
 
 def weigh_kernel(own, near, far, both, *outs, table):
@@ -381,14 +395,10 @@
     return plain(iterate), plain(residual)
 
 
-def last_kernel(prolong_ref, got_ref, c0, c1, c2, c3, inv_ref, rhs_ref, v1_ref, v2_hbm, p2_hbm, rx_ref, ry_ref,
-                sol_hbm, res_hbm, coarse_ref, v2_ref, p2_ref, sol_ref, res_ref, in_sems, out_sems, *, table, ny):
-    fetches = []
-    for f in range(F):
-        rows = pl.ds(f * FACE, FACE)
-        for i, (src, dst) in enumerate(((v2_hbm, v2_ref), (p2_hbm, p2_ref))):
-            fetches.append(pltpu.make_async_copy(src.at[rows], dst.at[rows], in_sems.at[2 * f + i]))
-            fetches[-1].start()
+def last_kernel(prolong_ref, got_ref, c0, c1, c2, c3, inv_ref, rhs_hbm, v1_ref, v2_ref, p2_ref, rx_ref, ry_ref,
+                sol_hbm, res_hbm, coarse_ref, rhs_ref, sol_ref, res_ref, in_sem, out_sems, *, table, ny):
+    fetch = pltpu.make_async_copy(rhs_hbm, rhs_ref, in_sem)
+    fetch.start()
     x, d = conjugate_gradient(*moments(got_ref[...]))
     inv = inv_ref[0:1, 0:1]
     x = [t * inv for t in x]
@@ -407,23 +417,26 @@
     x = [jnp.broadcast_to(t, (LY, LZ)) for t in x]
     d = [jnp.broadcast_to(t, (LY, LZ)) for t in d]
     stores = []
+    fetch.wait()
     for f in range(F):
-        fetches[2 * f].wait()
-        fetches[2 * f + 1].wait()
         for a in range(A):
             at = (f * A + a) * CELLS
             spread = coarse * prolong_ref[f, a]
             for cell in range(LX):
                 rows = slice(at + cell * LY, at + (cell + 1) * LY)
-                v0, v1, v2 = rhs_ref[rows, :], v1_ref[rows, :], v2_ref[rows, :]
-                img = p2_ref[rows, :]
+                v0 = rhs_ref[rows, :]
+                v1, v2, img = (tile_of(ref, F * CELLS, f, a, cell) for ref in (v1_ref, v2_ref, p2_ref))
                 if f == 0 and cell == 0:
-                    img = img + rx_ref[a * LY : (a + 1) * LY, :]
+                    img = img + tile_of(rx_ref, LY, 0, a, 0)
                 sol_ref[rows, :] = x[0] * v0 + x[1] * v1 + x[2] * v2 + spread
                 res_ref[rows, :] = d[0] * v0 + d[1] * v1 + d[2] * v2 + d[3] * img
         if f == 1:
-            first = pl.ds(FACE, A * LX, stride=LY)
-            res_ref[first, :] = res_ref[first, :] + d[3][0:1] * ry_ref[...]
+            below = d[3][0:1] * ry_ref[...]
+            for cell in range(LX):
+                first = pl.ds(FACE + cell * LY, B, stride=CELLS)
+                res_ref[first, :] = res_ref[first, :] + below[cell * B : (cell + 1) * B]
+            first = pl.ds(FACE + B * CELLS, LX, stride=LY)
+            res_ref[first, :] = res_ref[first, :] + below[B * LX :]
         rows = pl.ds(f * FACE, FACE)
         for i, (src, dst) in enumerate(((sol_ref, sol_hbm), (res_ref, res_hbm))):
             stores.append(pltpu.make_async_copy(src.at[rows], dst.at[rows], out_sems.at[2 * f + i]))
@@ -504,13 +517,10 @@
     )
     r = swap(s)
     sums, = call(products_kernel, "products", [rhs2, v1], [struct(40, LZ)])
-    dma = pltpu.SemaphoreType.DMA
     peers = nx * ny * 2
     v2, p2, upx, upy, loads, mom = call(
         third_kernel, "third", [p1, v1, *r, *s, sums, k2, m2, w],
-        [pltpu.HBM((ROWS, LZ), f32), pltpu.HBM((F * A, LX, LY, LZ), f32), struct(vx, LZ), struct(vy, LZ)]
-        + [struct(peers + 8, LZ), struct(peers, LZ)],
-        [pltpu.VMEM((ROWS, LZ), f32)] * 2 + upper + [dma, pltpu.SemaphoreType.DMA((LX,))],
+        [struct(ROWS, LZ)] * 2 + [struct(vx, LZ), struct(vy, LZ), struct(peers + 8, LZ), struct(peers, LZ)], upper,
     )
     table = [float(t) for t in jacobi_weights(nx)]
     group = [lax.ppermute(loads, "gx", [(i, i ^ b) for i in range(nx)]) for b in (1, 2, 3)]
@@ -519,11 +529,10 @@
     got = lax.all_to_all(mom.reshape(-1, 2, LZ), ("gx", "gy"), 0, 0, tiled=True).reshape(mom.shape)
     rx = shifted(upx, "gx", 1)
     ry = shifted(upy, "gy", 1)
-    v2, p2 = (pltpu.with_memory_space_constraint(v, pltpu.HBM) for v in (v2, p2.reshape(ROWS, LZ)))
     sol, res, coarse = call(
-        last_kernel, "last", [(prolong, SM), got, *coarse, inv, rhs2, v1, (v2, ANY), (p2, ANY), rx, ry],
+        last_kernel, "last", [(prolong, SM), got, *coarse, inv, (pltpu.with_memory_space_constraint(rhs2, pltpu.HBM), ANY), v1, v2, p2, rx, ry],
         [pltpu.HBM((ROWS, LZ), f32)] * 2 + [struct(LY, LZ)],
-        [pltpu.VMEM((ROWS, LZ), f32)] * 4 + [pltpu.SemaphoreType.DMA((6,))] * 2, table=table, ny=ny,
+        [pltpu.VMEM((ROWS, LZ), f32)] * 3 + [pltpu.SemaphoreType.DMA, pltpu.SemaphoreType.DMA((6,))], table=table, ny=ny,
     )
     return sol.reshape(rhs.shape), res.reshape(rhs.shape), coarse[None]
 

time: 68.2 us -> 66.9 us (0.981)
  Pallas kernels: 17.4 us -> 13.8 us
  local copies, waits for them, and re-layouts: 1.86 us -> 4.18 us
    pallas_call x8, Pallas kernels: 17.4 us -> 13.8 us  [call(): pl.pallas_call(bound, out_shape=outs, in_specs=specs, out_specs=[ANY if i...]
    unnamed x12 -> x16, local copies, waits for them, and re-layouts: 1.84 us -> 4.16 us
  transfers between devices with their start and end apart: 19 -> 19, of which waited for: 6 -> 6; matrix products, arithmetic and copies ran while one was open for 0% -> 0% of each run, Pallas kernels for 2% -> 3%
where the time goes in v8:
time: 66.9 us; the launch traced here: 65.5 us
  starting transfers between devices  35 us (52%)
  Pallas kernels  13.8 us (21%)
  waiting for transfers between devices  11.6 us (17%)
  local copies, waits for them, and re-layouts  4.18 us (6%)
  between operations  0.95 us (1%)
    ppermute x7, starting transfers between devices, shifted(): return lax.ppermute(value, axis, [(i, (i + by) % n) for i in range(n)])  16.6 us
    pallas_call x8, Pallas kernels, call(): pl.pallas_call(bound, out_shape=outs, in_specs=specs, out_specs=[ANY if i...  13.8 us
    ppermute x4, starting transfers between devices, far_swap(): return lax.ppermute(value, axis, pairs)  9.56 us
    ppermute x4, waiting for transfers between devices, far_swap(): return lax.ppermute(value, axis, pairs)  9.04 us
    all_to_all x1, starting transfers between devices, shards(): lax.all_to_all(mom.reshape(-1, 2, LZ), ('gx', 'gy'), 0, 0, tiled=True)  5.55 us
    unnamed x16, local copies, waits for them, and re-layouts  4.16 us
    ppermute x3, starting transfers between devices, shards(): lax.ppermute(loads, 'gx', [(i, i ^ b) for i in range(nx)])  3.37 us
    ppermute x7, waiting for transfers between devices, shifted(): return lax.ppermute(value, axis, [(i, (i + by) % n) for i in range(n)])  1.38 us
  transfers between devices with their start and end apart: 19, of which 6 were waited for; matrix products, arithmetic and copies ran while one was open for 0% of the time, Pallas kernels for 3%

profile of v8, /device:TPU:0, one launch (start us, length us, event | category | flops | bytes accessed | tf_op | source)
XLA Modules:
  0.0 65.5 jit_solution(7516036725578319083)
XLA Ops:
  0.7 1.0 %edges.1 = (f32[25,8,128]{2,1,0:T(8,128)S(1)}, f32[25,4,128]{2,1,0:T(4,128)S(1)}) custom-call(f32[3,25,4,8,128]{4,3,2,1,0:T(8,128)} %refs_0_.3), custom_call_target="tpu_custom_call" | custom-call | tf_op jit(solution)/shard_map/edges/pallas_call | solution.py:481
  1.7 6.1 %collective-permute-start = (f32[200,128]{1,0:T(8,128)S(1)}, f32[200,128]{1,0:T(8,128)S(1)}, u32[]{:S(2)}, u32[]{:S(2)}) collective-permute-start(f32[200,128]{1,0:T(8,128)S(1)} %bitcast.19), channel_id=1, source_target_pairs={{0,120},{8,0},{16,8},{24,16},{32,24},{40,32},{48,40},{56,48},{64,5... | collective-permute-start | bytes 307208 | tf_op jit(solution)/shard_map/ppermute | solution.py:28
  7.8 3.1 %collective-permute-start.1 = (f32[100,128]{1,0:T(8,128)S(1)}, f32[100,128]{1,0:T(8,128)S(1)}, u32[]{:S(2)}, u32[]{:S(2)}) collective-permute-start(f32[100,128]{1,0:T(8,128)S(1)} %reshape.35), channel_id=1, source_target_pairs={{0,7},{1,0},{2,1},{3,2},{4,3},{5,4},{6,5},{7,6},{8,15},{9,8},{10,9... | collective-permute-start | bytes 153608 | tf_op jit(solution)/shard_map/ppermute | solution.py:28
  12.7 1.2 %weights.1 = (bf16[304,480]{1,0:T(8,128)(2,1)S(1)}, f32[8,128]{1,0:T(8,128)S(1)}) custom-call(f32[150,150]{1,0:T(8,128)S(1)} %copy-done.3, f32[150,150]{1,0:T(8,128)S(1)} %copy-done.4), custom_call_target="tpu_custom_call" | custom-call | tf_op jit(solution)/shard_map/weights/pallas_call | solution.py:481
  13.9 2.0 %first.1 = (f32[2400,128]{1,0:T(8,128)S(1)}, f32[200,128]{1,0:T(8,128)S(1)}, f32[200,128]{1,0:T(8,128)S(1)}, f32[100,128]{1,0:T(8,128)S(1)}, f32[100,128]{1,0:T(8,128)S(1)}) custom-call(f32[2400,128]{1,0:T(8,128)S(1)} %bitcast.10, f32[200,128]{1,0:T(8,128)S(1)} %collective-permute-done.refs_1_, f32[100,128]{1,0:T(8,128)S(1)} %collective-permute-done.1.refs_2_, ...), custom_call_target="tpu_custom_call" | custom-call | tf_op jit(solution)/shard_map/first/pallas_call | solution.py:481
  16.0 1.6 %collective-permute-start.2 = (f32[200,128]{1,0:T(8,128)S(1)}, f32[200,128]{1,0:T(8,128)S(1)}, u32[]{:S(2)}, u32[]{:S(2)}) collective-permute-start(f32[200,128]{1,0:T(8,128)S(1)} %get-tuple-element.35.refs_6_), channel_id=1, source_target_pairs={{0,120},{8,16},{16,8},{24,32},{32,24},{40,48},{48,40},{56,64},{64,... | collective-permute-start | bytes 307208 | tf_op jit(solution)/shard_map/ppermute | solution.py:39
  17.6 3.0 %collective-permute-start.3 = (f32[100,128]{1,0:T(8,128)S(1)}, f32[100,128]{1,0:T(8,128)S(1)}, u32[]{:S(2)}, u32[]{:S(2)}) collective-permute-start(f32[100,128]{1,0:T(8,128)S(1)} %get-tuple-element.36.refs_8_), channel_id=1, source_target_pairs={{0,7},{1,2},{2,1},{3,4},{4,3},{5,6},{6,5},{7,0},{8,15},{9,10},{10,... | collective-permute-start | bytes 153608 | tf_op jit(solution)/shard_map/ppermute | solution.py:39
  20.6 4.3 %collective-permute-done.3.refs_2_ = f32[100,128]{1,0:T(8,128)S(1)} collective-permute-done((f32[100,128]{1,0:T(8,128)S(1)}, f32[100,128]{1,0:T(8,128)S(1)}, u32[]{:S(2)}, u32[]{:S(2)}) %collective-permute-start.3) | collective-permute-done | bytes 51232 | tf_op jit(solution)/shard_map/ppermute | solution.py:39
  24.9 1.7 %second.1 = (f32[2400,128]{1,0:T(8,128)S(1)}, f32[2400,128]{1,0:T(8,128)S(1)}, f32[200,128]{1,0:T(8,128)S(1)}, f32[200,128]{1,0:T(8,128)S(1)}, f32[100,128]{1,0:T(8,128)S(1)}, /*index=5*/f32[100,128]{1,0:T(8,128)S(1)}) custom-call(f32[2400,128]{1,0:T(8,128)S(1)} %get-tuple-element.34.refs_0_, f32[200,128]{1,0:T(8,128)S(1)} %collective-permute-done.2.refs_1_, ...), custom_call_target="tpu_custom_call" | custom-call | tf_op jit(solution)/shard_map/second/pallas_call | solution.py:481
  26.7 3.5 %collective-permute-start.6 = (f32[200,128]{1,0:T(8,128)S(1)}, f32[200,128]{1,0:T(8,128)S(1)}, u32[]{:S(2)}, u32[]{:S(2)}) collective-permute-start(f32[200,128]{1,0:T(8,128)S(1)} %get-tuple-element.41.refs_7_), channel_id=1, source_target_pairs={{0,120},{8,16},{16,8},{24,32},{32,24},{40,48},{48,40},{56,64},{64,... | collective-permute-start | bytes 307208 | tf_op jit(solution)/shard_map/ppermute | solution.py:39
  30.2 1.4 %collective-permute-start.7 = (f32[100,128]{1,0:T(8,128)S(1)}, f32[100,128]{1,0:T(8,128)S(1)}, u32[]{:S(2)}, u32[]{:S(2)}) collective-permute-start(f32[100,128]{1,0:T(8,128)S(1)} %get-tuple-element.42.refs_9_), channel_id=1, source_target_pairs={{0,7},{1,2},{2,1},{3,4},{4,3},{5,6},{6,5},{7,0},{8,15},{9,10},{10,... | collective-permute-start | bytes 153608 | tf_op jit(solution)/shard_map/ppermute | solution.py:39
  32.1 4.7 %collective-permute-done.7.refs_3_ = f32[100,128]{1,0:T(8,128)S(1)} collective-permute-done((f32[100,128]{1,0:T(8,128)S(1)}, f32[100,128]{1,0:T(8,128)S(1)}, u32[]{:S(2)}, u32[]{:S(2)}) %collective-permute-start.7) | collective-permute-done | bytes 51232 | tf_op jit(solution)/shard_map/ppermute | solution.py:39
  36.9 2.9 %third.1 = (f32[2400,128]{1,0:T(8,128)S(1)}, f32[2400,128]{1,0:T(8,128)S(1)}, f32[200,128]{1,0:T(8,128)S(1)}, f32[100,128]{1,0:T(8,128)S(1)}, f32[264,128]{1,0:T(8,128)S(1)}, /*index=5*/f32[256,128]{1,0:T(8,128)}) custom-call(f32[2400,128]{1,0:T(8,128)S(1)} %get-tuple-element.39.refs_0_, f32[2400,128]{1,0:T(8,128)S(1)} %get-tuple-element.40.refs_1_.refs_8_, ...), custom_call_target="tpu_custom_call" | custom-call | tf_op jit(solution)/shard_map/third/pallas_call | solution.py:481
  39.8 1.0 %copy-done.1 = f32[2400,128]{1,0:T(8,128)} copy-done((f32[2400,128]{1,0:T(8,128)}, f32[2400,128]{1,0:T(8,128)S(1)}, u32[]{:S(2)}) %copy-start.1) | copy-done | bytes 1228824
  40.8 2.5 %collective-permute-start.11 = (f32[264,128]{1,0:T(8,128)S(1)}, f32[264,128]{1,0:T(8,128)S(1)}, u32[]{:S(2)}, u32[]{:S(2)}) collective-permute-start(f32[264,128]{1,0:T(8,128)S(1)} %get-tuple-element.46.refs_0_), channel_id=1, source_target_pairs={{0,16},{8,24},{16,0},{24,8},{32,48},{40,56},{48,32},{56,40},{64,80... | collective-permute-start | bytes 405512 | tf_op jit(solution)/shard_map/ppermute | solution.py:526
  44.2 5.5 %all-to-all-start = ((f32[128,2,128]{2,1,0:T(2,128)}), f32[128,2,128]{2,1,0:T(2,128)S(1)}, u32[]{:S(2)}, u32[]{:S(2)}) async-start(f32[128,2,128]{2,1,0:T(2,128)} %bitcast.4), calls=%async_computation | async-start | bytes 262144 | tf_op jit(solution)/shard_map/all_to_all | solution.py:529
  49.8 1.2 %collective-permute-start.17 = (f32[100,128]{1,0:T(8,128)S(1)}, f32[100,128]{1,0:T(8,128)S(1)}, u32[]{:S(2)}, u32[]{:S(2)}) collective-permute-start(f32[100,128]{1,0:T(8,128)S(1)} %get-tuple-element.55), channel_id=1, source_target_pairs={{0,1},{1,2},{2,3},{3,4},{4,5},{5,6},{6,7},{7,0},{8,9},{9,10},{10,1... | collective-permute-start | bytes 153608 | tf_op jit(solution)/shard_map/ppermute | solution.py:28
  51.1 1.7 %collective-permute-start.13 = (f32[32,128]{1,0:T(8,128)S(1)}, f32[32,128]{1,0:T(8,128)S(1)}, u32[]{:S(2)}, u32[]{:S(2)}) collective-permute-start(f32[32,128]{1,0:T(8,128)S(1)} %get-tuple-element.48), channel_id=1, source_target_pairs={{0,32},{8,40},{16,48},{24,56},{32,64},{40,72},{48,80},{56,88},{64,... | collective-permute-start | bytes 49160 | tf_op jit(solution)/shard_map/ppermute | solution.py:28
  52.8 3.2 %collective-permute-start.14 = (f32[32,128]{1,0:T(8,128)S(1)}, f32[32,128]{1,0:T(8,128)S(1)}, u32[]{:S(2)}, u32[]{:S(2)}) collective-permute-start(f32[32,128]{1,0:T(8,128)S(1)} %get-tuple-element.49), channel_id=1, source_target_pairs={{0,64},{8,72},{16,80},{24,88},{32,96},{40,104},{48,112},{56,120},{... | collective-permute-start | bytes 49160 | tf_op jit(solution)/shard_map/ppermute | solution.py:28
  56.0 1.2 %collective-permute-start.15 = (f32[32,128]{1,0:T(8,128)S(1)}, f32[32,128]{1,0:T(8,128)S(1)}, u32[]{:S(2)}, u32[]{:S(2)}) collective-permute-start(f32[32,128]{1,0:T(8,128)S(1)} %get-tuple-element.50), channel_id=1, source_target_pairs={{0,96},{8,104},{16,112},{24,120},{32,0},{40,8},{48,16},{56,24},{64... | collective-permute-start | bytes 49160 | tf_op jit(solution)/shard_map/ppermute | solution.py:28
  57.2 0.9 %collective-permute-done.16.refs_11_ = f32[200,128]{1,0:T(8,128)S(1)} collective-permute-done((f32[200,128]{1,0:T(8,128)S(1)}, f32[200,128]{1,0:T(8,128)S(1)}, u32[]{:S(2)}, u32[]{:S(2)}) %collective-permute-start.16) | collective-permute-done | bytes 102432 | tf_op jit(solution)/shard_map/ppermute | solution.py:28
  58.1 1.2 %all-to-all-done = f32[128,2,128]{2,1,0:T(2,128)S(1)} async-done(((f32[128,2,128]{2,1,0:T(2,128)}), f32[128,2,128]{2,1,0:T(2,128)S(1)}, u32[]{:S(2)}, u32[]{:S(2)}) %all-to-all-start) | async-done | bytes 131104 | tf_op jit(solution)/shard_map/all_to_all | solution.py:529
  59.7 1.3 %copy-done.2 = f32[2400,128]{1,0:T(8,128)S(1)} copy-done((f32[2400,128]{1,0:T(8,128)S(1)}, f32[2400,128]{1,0:T(8,128)}, u32[]{:S(2)}) %copy-start.2) | copy-done | bytes 1228824
  61.0 4.4 %last.1 = (f32[2400,128]{1,0:T(8,128)}, f32[2400,128]{1,0:T(8,128)}, f32[8,128]{1,0:T(8,128)}) custom-call(f32[3,25]{1,0:T(4,128)S(1)} %copy-done.7, f32[256,128]{1,0:T(8,128)S(1)} %bitcast.12, f32[32,128]{1,0:T(8,128)S(1)} %get-tuple-element.47.refs_2_, f32[32,128]{1,0:T(8,128)S(1)} %collective-permute-done.13.refs_3_, ...), custom_call_target="tpu_custom_call" | custom-call | tf_op jit(solution)/shard_map/last/pallas_call | solution.py:481
  (39 shorter events, 4.0 us)
Async XLA Ops:
  0.6 13.3 %copy-start = (f32[3,25,4,8,128]{4,3,2,1,0:T(8,128)S(1)}, f32[3,25,4,8,128]{4,3,2,1,0:T(8,128)}, u32[]{:S(2)}) copy-start(f32[3,25,4,8,128]{4,3,2,1,0:T(8,128)} %refs_0_.3) | copy-start | bytes 3686404
  0.6 13.3 %copy-start.6 = (f32[4,8,128]{2,1,0:T(8,128)S(1)}, f32[4,8,128]{2,1,0:T(8,128)}, u32[]{:S(2)}) copy-start(f32[4,8,128]{2,1,0:T(8,128)} %param.8) | copy-start | bytes 49156
  0.7 13.3 %copy-start.5 = (f32[4,8,128]{2,1,0:T(8,128)S(1)}, f32[4,8,128]{2,1,0:T(8,128)}, u32[]{:S(2)}) copy-start(f32[4,8,128]{2,1,0:T(8,128)} %param.7) | copy-start | bytes 49156
  1.7 12.2 %collective-permute-start = (f32[200,128]{1,0:T(8,128)S(1)}, f32[200,128]{1,0:T(8,128)S(1)}, u32[]{:S(2)}, u32[]{:S(2)}) collective-permute-start(f32[200,128]{1,0:T(8,128)S(1)} %bitcast.19), channel_id=1, source_target_pairs={{0,120},{8,0},{16,8},{24,16},{32,24},{40,32},{48,40},{56,48},{64,5... | collective-permute-start | bytes 307208 | tf_op jit(solution)/shard_map/ppermute | solution.py:28
  7.8 6.1 %collective-permute-start.1 = (f32[100,128]{1,0:T(8,128)S(1)}, f32[100,128]{1,0:T(8,128)S(1)}, u32[]{:S(2)}, u32[]{:S(2)}) collective-permute-start(f32[100,128]{1,0:T(8,128)S(1)} %reshape.35), channel_id=1, source_target_pairs={{0,7},{1,0},{2,1},{3,2},{4,3},{5,4},{6,5},{7,6},{8,15},{9,8},{10,9... | collective-permute-start | bytes 153608 | tf_op jit(solution)/shard_map/ppermute | solution.py:28
  16.0 9.0 %collective-permute-start.2 = (f32[200,128]{1,0:T(8,128)S(1)}, f32[200,128]{1,0:T(8,128)S(1)}, u32[]{:S(2)}, u32[]{:S(2)}) collective-permute-start(f32[200,128]{1,0:T(8,128)S(1)} %get-tuple-element.35.refs_6_), channel_id=1, source_target_pairs={{0,120},{8,16},{16,8},{24,32},{32,24},{40,48},{48,40},{56,64},{64,... | collective-permute-start | bytes 307208 | tf_op jit(solution)/shard_map/ppermute | solution.py:39
  17.6 7.3 %collective-permute-start.5 = (f32[200,128]{1,0:T(8,128)S(1)}, f32[200,128]{1,0:T(8,128)S(1)}, u32[]{:S(2)}, u32[]{:S(2)}) collective-permute-start(f32[200,128]{1,0:T(8,128)S(1)} %get-tuple-element.38.refs_5_), channel_id=1, source_target_pairs={{0,8},{8,0},{16,24},{24,16},{32,40},{40,32},{48,56},{56,48},{64,72... | collective-permute-start | bytes 307208 | tf_op jit(solution)/shard_map/ppermute | solution.py:33
  17.6 7.3 %collective-permute-start.3 = (f32[100,128]{1,0:T(8,128)S(1)}, f32[100,128]{1,0:T(8,128)S(1)}, u32[]{:S(2)}, u32[]{:S(2)}) collective-permute-start(f32[100,128]{1,0:T(8,128)S(1)} %get-tuple-element.36.refs_8_), channel_id=1, source_target_pairs={{0,7},{1,2},{2,1},{3,4},{4,3},{5,6},{6,5},{7,0},{8,15},{9,10},{10,... | collective-permute-start | bytes 153608 | tf_op jit(solution)/shard_map/ppermute | solution.py:39
  20.6 4.3 %collective-permute-start.4 = (f32[100,128]{1,0:T(8,128)S(1)}, f32[100,128]{1,0:T(8,128)S(1)}, u32[]{:S(2)}, u32[]{:S(2)}) collective-permute-start(f32[100,128]{1,0:T(8,128)S(1)} %get-tuple-element.37.refs_7_), channel_id=1, source_target_pairs={{0,1},{1,0},{2,3},{3,2},{4,5},{5,4},{6,7},{7,6},{8,9},{9,8},{10,11... | collective-permute-start | bytes 153608 | tf_op jit(solution)/shard_map/ppermute | solution.py:33
  26.7 10.2 %collective-permute-start.6 = (f32[200,128]{1,0:T(8,128)S(1)}, f32[200,128]{1,0:T(8,128)S(1)}, u32[]{:S(2)}, u32[]{:S(2)}) collective-permute-start(f32[200,128]{1,0:T(8,128)S(1)} %get-tuple-element.41.refs_7_), channel_id=1, source_target_pairs={{0,120},{8,16},{16,8},{24,32},{32,24},{40,48},{48,40},{56,64},{64,... | collective-permute-start | bytes 307208 | tf_op jit(solution)/shard_map/ppermute | solution.py:39
  30.2 6.7 %collective-permute-start.9 = (f32[200,128]{1,0:T(8,128)S(1)}, f32[200,128]{1,0:T(8,128)S(1)}, u32[]{:S(2)}, u32[]{:S(2)}) collective-permute-start(f32[200,128]{1,0:T(8,128)S(1)} %get-tuple-element.44.refs_6_), channel_id=1, source_target_pairs={{0,8},{8,0},{16,24},{24,16},{32,40},{40,32},{48,56},{56,48},{64,72... | collective-permute-start | bytes 307208 | tf_op jit(solution)/shard_map/ppermute | solution.py:33
  30.2 6.7 %collective-permute-start.7 = (f32[100,128]{1,0:T(8,128)S(1)}, f32[100,128]{1,0:T(8,128)S(1)}, u32[]{:S(2)}, u32[]{:S(2)}) collective-permute-start(f32[100,128]{1,0:T(8,128)S(1)} %get-tuple-element.42.refs_9_), channel_id=1, source_target_pairs={{0,7},{1,2},{2,1},{3,4},{4,3},{5,6},{6,5},{7,0},{8,15},{9,10},{10,... | collective-permute-start | bytes 153608 | tf_op jit(solution)/shard_map/ppermute | solution.py:39
  31.6 5.3 %collective-permute-start.8 = (f32[100,128]{1,0:T(8,128)S(1)}, f32[100,128]{1,0:T(8,128)S(1)}, u32[]{:S(2)}, u32[]{:S(2)}) collective-permute-start(f32[100,128]{1,0:T(8,128)S(1)} %get-tuple-element.43.refs_8_), channel_id=1, source_target_pairs={{0,1},{1,0},{2,3},{3,2},{4,5},{5,4},{6,7},{7,6},{8,9},{9,8},{10,11... | collective-permute-start | bytes 153608 | tf_op jit(solution)/shard_map/ppermute | solution.py:33
  36.9 22.8 %copy-start.7 = (f32[3,25]{1,0:T(4,128)S(1)}, f32[3,25]{1,0:T(4,128)}, u32[]{:S(2)}) copy-start(f32[3,25]{1,0:T(4,128)} %refs_0_.5) | copy-start | bytes 904
  40.8 10.2 %collective-permute-start.12 = (f32[264,128]{1,0:T(8,128)S(1)}, f32[264,128]{1,0:T(8,128)S(1)}, u32[]{:S(2)}, u32[]{:S(2)}) collective-permute-start(f32[264,128]{1,0:T(8,128)S(1)} %get-tuple-element.46.refs_0_), channel_id=1, source_target_pairs={{0,24},{8,16},{16,8},{24,0},{32,56},{40,48},{48,40},{56,32},{64,88... | collective-permute-start | bytes 405512 | tf_op jit(solution)/shard_map/ppermute | solution.py:526
  40.8 10.2 %collective-permute-start.11 = (f32[264,128]{1,0:T(8,128)S(1)}, f32[264,128]{1,0:T(8,128)S(1)}, u32[]{:S(2)}, u32[]{:S(2)}) collective-permute-start(f32[264,128]{1,0:T(8,128)S(1)} %get-tuple-element.46.refs_0_), channel_id=1, source_target_pairs={{0,16},{8,24},{16,0},{24,8},{32,48},{40,56},{48,32},{56,40},{64,80... | collective-permute-start | bytes 405512 | tf_op jit(solution)/shard_map/ppermute | solution.py:526
  43.3 7.7 %collective-permute-start.10 = (f32[264,128]{1,0:T(8,128)S(1)}, f32[264,128]{1,0:T(8,128)S(1)}, u32[]{:S(2)}, u32[]{:S(2)}) collective-permute-start(f32[264,128]{1,0:T(8,128)S(1)} %get-tuple-element.46.refs_0_), channel_id=1, source_target_pairs={{0,8},{8,0},{16,24},{24,16},{32,40},{40,32},{48,56},{56,48},{64,72... | collective-permute-start | bytes 405512 | tf_op jit(solution)/shard_map/ppermute | solution.py:526
  44.2 15.1 %all-to-all-start = ((f32[128,2,128]{2,1,0:T(2,128)}), f32[128,2,128]{2,1,0:T(2,128)S(1)}, u32[]{:S(2)}, u32[]{:S(2)}) async-start(f32[128,2,128]{2,1,0:T(2,128)} %bitcast.4), calls=%async_computation | async-start | bytes 262144 | tf_op jit(solution)/shard_map/all_to_all | solution.py:529
  49.7 8.4 %collective-permute-start.16 = (f32[200,128]{1,0:T(8,128)S(1)}, f32[200,128]{1,0:T(8,128)S(1)}, u32[]{:S(2)}, u32[]{:S(2)}) collective-permute-start(f32[200,128]{1,0:T(8,128)S(1)} %get-tuple-element.54), channel_id=1, source_target_pairs={{0,8},{8,16},{16,24},{24,32},{32,40},{40,48},{48,56},{56,64},{64,7... | collective-permute-start | bytes 307208 | tf_op jit(solution)/shard_map/ppermute | solution.py:28
  49.8 7.4 %collective-permute-start.17 = (f32[100,128]{1,0:T(8,128)S(1)}, f32[100,128]{1,0:T(8,128)S(1)}, u32[]{:S(2)}, u32[]{:S(2)}) collective-permute-start(f32[100,128]{1,0:T(8,128)S(1)} %get-tuple-element.55), channel_id=1, source_target_pairs={{0,1},{1,2},{2,3},{3,4},{4,5},{5,6},{6,7},{7,0},{8,9},{9,10},{10,1... | collective-permute-start | bytes 153608 | tf_op jit(solution)/shard_map/ppermute | solution.py:28
  51.1 8.2 %collective-permute-start.13 = (f32[32,128]{1,0:T(8,128)S(1)}, f32[32,128]{1,0:T(8,128)S(1)}, u32[]{:S(2)}, u32[]{:S(2)}) collective-permute-start(f32[32,128]{1,0:T(8,128)S(1)} %get-tuple-element.48), channel_id=1, source_target_pairs={{0,32},{8,40},{16,48},{24,56},{32,64},{40,72},{48,80},{56,88},{64,... | collective-permute-start | bytes 49160 | tf_op jit(solution)/shard_map/ppermute | solution.py:28
  52.8 6.8 %collective-permute-start.14 = (f32[32,128]{1,0:T(8,128)S(1)}, f32[32,128]{1,0:T(8,128)S(1)}, u32[]{:S(2)}, u32[]{:S(2)}) collective-permute-start(f32[32,128]{1,0:T(8,128)S(1)} %get-tuple-element.49), channel_id=1, source_target_pairs={{0,64},{8,72},{16,80},{24,88},{32,96},{40,104},{48,112},{56,120},{... | collective-permute-start | bytes 49160 | tf_op jit(solution)/shard_map/ppermute | solution.py:28
  56.0 3.8 %collective-permute-start.15 = (f32[32,128]{1,0:T(8,128)S(1)}, f32[32,128]{1,0:T(8,128)S(1)}, u32[]{:S(2)}, u32[]{:S(2)}) collective-permute-start(f32[32,128]{1,0:T(8,128)S(1)} %get-tuple-element.50), channel_id=1, source_target_pairs={{0,96},{8,104},{16,112},{24,120},{32,0},{40,8},{48,16},{56,24},{64... | collective-permute-start | bytes 49160 | tf_op jit(solution)/shard_map/ppermute | solution.py:28
  59.7 1.3 %copy-start.2 = (f32[2400,128]{1,0:T(8,128)S(1)}, f32[2400,128]{1,0:T(8,128)}, u32[]{:S(2)}) copy-start(f32[2400,128]{1,0:T(8,128)} %copy-done.1) | copy-start | bytes 3686404
  (3 other events, 2.9 us)

commit v9 on v8

--- a/solution.py
+++ b/solution.py
@@ -235,7 +235,9 @@
     return ref[pl.ds(at * B + a, LY, stride=B), :]
 
 
-def products_kernel(v0_ref, v1_ref, sums_ref):
+def products_kernel(v0_ref, v1_ref, sums_ref, v1_hbm, sem):
+    keep = pltpu.make_async_copy(v1_ref, v1_hbm, sem)
+    keep.start()
     s0 = s1 = s00 = s01 = s11 = 0.0
     for f in range(F):
         for a in range(A):
@@ -246,6 +248,7 @@
                 s0, s1, s00, s01, s11 = s0 + v0, s1 + v1, s00 + v0 * v0, s01 + v0 * v1, s11 + v1 * v1
     for k, s in enumerate((s0, s1, s00, s01, s11)):
         sums_ref[8 * k : 8 * k + 8] = s
+    keep.wait()
 
 
 def third_kernel(p_ref, v1_ref, rfx, rfy, rny, rnx, snx, sfx, sny, sfy, sums_ref, k_ref, m_ref, w_ref,
@@ -395,13 +398,15 @@
     return plain(iterate), plain(residual)
 
 
-def last_kernel(prolong_ref, got_ref, c0, c1, c2, c3, inv_ref, rhs_hbm, v1_ref, v2_ref, p2_ref, rx_ref, ry_ref,
-                sol_hbm, res_hbm, coarse_ref, rhs_ref, sol_ref, res_ref, in_sem, out_sems, *, table, ny):
-    fetch = pltpu.make_async_copy(rhs_hbm, rhs_ref, in_sem)
-    fetch.start()
+def coefficients_kernel(got_ref, inv_ref, rhs_hbm, v1_hbm, rhs_ref, v1_ref, coef_ref, edge_ref, sems, *, table, ny):
+    fetches = [pltpu.make_async_copy(rhs_hbm, rhs_ref, sems.at[0]), pltpu.make_async_copy(v1_hbm, v1_ref, sems.at[1])]
+    for fetch in fetches:
+        fetch.start()
     x, d = conjugate_gradient(*moments(got_ref[...]))
     inv = inv_ref[0:1, 0:1]
-    x = [t * inv for t in x]
+    for k, t in enumerate([t * inv for t in x] + d):
+        coef_ref[k : k + 1] = jnp.broadcast_to(t, (1, LZ))
+    coef_ref[7:8] = jnp.zeros((1, LZ), f32)
     below = lax.rem(lax.axis_index("gy") + ny - 1, ny)
     me = lax.axis_index("gx")
     nx = len(table)
@@ -409,15 +414,19 @@
     for offset, weight in enumerate(table):
         slab = lax.rem(me + nx - offset, nx)
         edge = edge + got_ref[pl.ds(2 * (slab * ny + below) + 1, 1), :] * weight
+    edge_ref[...] = jnp.concatenate([edge, jnp.zeros((LY - 1, LZ), f32)], 0)
+    for fetch in fetches:
+        fetch.wait()
+
+
+def last_kernel(prolong_ref, coef_ref, edge_ref, c0, c1, c2, c3, rhs_ref, v1_ref, v2_ref, p2_ref, rx_ref, ry_ref,
+                sol_hbm, res_hbm, coarse_ref, sol_ref, res_ref, out_sems):
+    coef = [jnp.broadcast_to(coef_ref[k : k + 1], (LY, LZ)) for k in range(7)]
+    x, d = coef[:3], coef[3:]
     circ = [c0[k * 8 : k * 8 + 8] + c1[k * 8 : k * 8 + 8] + c2[k * 8 : k * 8 + 8] + c3[k * 8 : k * 8 + 8] for k in range(4)]
-    at_first = lax.broadcasted_iota(jnp.int32, (LY, LZ), 0) == 0
-    circ[3] = circ[3] + jnp.where(at_first, jnp.broadcast_to(edge, (LY, LZ)), 0.0)
-    coarse = d[0] * circ[0] + d[1] * circ[1] + d[2] * circ[2] + d[3] * circ[3]
+    coarse = d[0] * circ[0] + d[1] * circ[1] + d[2] * circ[2] + d[3] * (circ[3] + edge_ref[...])
     coarse_ref[...] = coarse
-    x = [jnp.broadcast_to(t, (LY, LZ)) for t in x]
-    d = [jnp.broadcast_to(t, (LY, LZ)) for t in d]
     stores = []
-    fetch.wait()
     for f in range(F):
         for a in range(A):
             at = (f * A + a) * CELLS
@@ -516,7 +525,9 @@
         [struct(ROWS, LZ), struct(ROWS, LZ)] + sends, upper + edges,
     )
     r = swap(s)
-    sums, = call(products_kernel, "products", [rhs2, v1], [struct(40, LZ)])
+    sums, v1_kept = call(
+        products_kernel, "products", [rhs2, v1], [struct(40, LZ), pltpu.HBM((ROWS, LZ), f32)], [pltpu.SemaphoreType.DMA],
+    )
     peers = nx * ny * 2
     v2, p2, upx, upy, loads, mom = call(
         third_kernel, "third", [p1, v1, *r, *s, sums, k2, m2, w],
@@ -529,10 +540,15 @@
     got = lax.all_to_all(mom.reshape(-1, 2, LZ), ("gx", "gy"), 0, 0, tiled=True).reshape(mom.shape)
     rx = shifted(upx, "gx", 1)
     ry = shifted(upy, "gy", 1)
+    v0, v1_kept = (pltpu.with_memory_space_constraint(v, pltpu.HBM) for v in (rhs2, v1_kept))
+    v0, v1, coef, edge = call(
+        coefficients_kernel, "coefficients", [got, inv, (v0, ANY), (v1_kept, ANY)],
+        [struct(ROWS, LZ)] * 2 + [struct(8, LZ), struct(LY, LZ)], [pltpu.SemaphoreType.DMA((2,))], table=table, ny=ny,
+    )
     sol, res, coarse = call(
-        last_kernel, "last", [(prolong, SM), got, *coarse, inv, (pltpu.with_memory_space_constraint(rhs2, pltpu.HBM), ANY), v1, v2, p2, rx, ry],
+        last_kernel, "last", [(prolong, SM), coef, edge, *coarse, v0, v1, v2, p2, rx, ry],
         [pltpu.HBM((ROWS, LZ), f32)] * 2 + [struct(LY, LZ)],
-        [pltpu.VMEM((ROWS, LZ), f32)] * 3 + [pltpu.SemaphoreType.DMA, pltpu.SemaphoreType.DMA((6,))], table=table, ny=ny,
+        [pltpu.VMEM((ROWS, LZ), f32)] * 2 + [pltpu.SemaphoreType.DMA((6,))],
     )
     return sol.reshape(rhs.shape), res.reshape(rhs.shape), coarse[None]
 

time: 66.9 us -> 63.9 us (0.955)
  local copies, waits for them, and re-layouts: 4.18 us -> 1.86 us
  waiting for transfers between devices: 11.6 us -> 10.8 us
  Pallas kernels: 13.8 us -> 14.5 us
    unnamed x16 -> x12, local copies, waits for them, and re-layouts: 4.16 us -> 1.84 us
    ppermute x7, waiting for transfers between devices: 1.38 us -> 0.02 us  [shifted(): return lax.ppermute(value, axis, [(i, (i + by) % n) for i in range(n)])]
    all_to_all x1, waiting for transfers between devices: 1.19 us -> 2.24 us  [shards(): lax.all_to_all(mom.reshape(-1, 2, LZ), ('gx', 'gy'), 0, 0, tiled=True)]
    pallas_call x8 -> x9, Pallas kernels: 13.8 us -> 14.5 us  [call(): pl.pallas_call(bound, out_shape=outs, in_specs=specs, out_specs=[ANY if i...]
  transfers between devices with their start and end apart: 19 -> 19, of which waited for: 6 -> 3; matrix products, arithmetic and copies ran while one was open for 0% -> 0% of each run, Pallas kernels for 3% -> 6%
where the time goes in v9:
time: 63.9 us; the launch traced here: 63 us
  starting transfers between devices  34.9 us (55%)
  Pallas kernels  14.5 us (23%)
  waiting for transfers between devices  10.8 us (17%)
  local copies, waits for them, and re-layouts  1.86 us (3%)
  between operations  0.84 us (1%)
    ppermute x7, starting transfers between devices, shifted(): return lax.ppermute(value, axis, [(i, (i + by) % n) for i in range(n)])  16.4 us
    pallas_call x9, Pallas kernels, call(): pl.pallas_call(bound, out_shape=outs, in_specs=specs, out_specs=[ANY if i...  14.5 us
    ppermute x4, starting transfers between devices, far_swap(): return lax.ppermute(value, axis, pairs)  9.56 us
    ppermute x4, waiting for transfers between devices, far_swap(): return lax.ppermute(value, axis, pairs)  8.57 us
    all_to_all x1, starting transfers between devices, shards(): lax.all_to_all(mom.reshape(-1, 2, LZ), ('gx', 'gy'), 0, 0, tiled=True)  5.55 us
    ppermute x3, starting transfers between devices, shards(): lax.ppermute(loads, 'gx', [(i, i ^ b) for i in range(nx)])  3.37 us
    all_to_all x1, waiting for transfers between devices, shards(): lax.all_to_all(mom.reshape(-1, 2, LZ), ('gx', 'gy'), 0, 0, tiled=True)  2.24 us
    unnamed x12, local copies, waits for them, and re-layouts  1.84 us
  transfers between devices with their start and end apart: 19, of which 3 were waited for; matrix products, arithmetic and copies ran while one was open for 0% of the time, Pallas kernels for 6%

profile of v9, /device:TPU:0, one launch (start us, length us, event | category | flops | bytes accessed | tf_op | source)
XLA Modules:
  0.0 63.0 jit_solution(10939534839750338414)
XLA Ops:
  0.7 1.0 %edges.1 = (f32[25,8,128]{2,1,0:T(8,128)S(1)}, f32[25,4,128]{2,1,0:T(4,128)S(1)}) custom-call(f32[3,25,4,8,128]{4,3,2,1,0:T(8,128)} %refs_0_.3), custom_call_target="tpu_custom_call" | custom-call | tf_op jit(solution)/shard_map/edges/pallas_call | solution.py:490
  1.7 6.1 %collective-permute-start = (f32[200,128]{1,0:T(8,128)S(1)}, f32[200,128]{1,0:T(8,128)S(1)}, u32[]{:S(2)}, u32[]{:S(2)}) collective-permute-start(f32[200,128]{1,0:T(8,128)S(1)} %bitcast.19), channel_id=1, source_target_pairs={{0,120},{8,0},{16,8},{24,16},{32,24},{40,32},{48,40},{56,48},{64,5... | collective-permute-start | bytes 307208 | tf_op jit(solution)/shard_map/ppermute | solution.py:28
  7.8 3.1 %collective-permute-start.1 = (f32[100,128]{1,0:T(8,128)S(1)}, f32[100,128]{1,0:T(8,128)S(1)}, u32[]{:S(2)}, u32[]{:S(2)}) collective-permute-start(f32[100,128]{1,0:T(8,128)S(1)} %reshape.35), channel_id=1, source_target_pairs={{0,7},{1,0},{2,1},{3,2},{4,3},{5,4},{6,5},{7,6},{8,15},{9,8},{10,9... | collective-permute-start | bytes 153608 | tf_op jit(solution)/shard_map/ppermute | solution.py:28
  10.9 0.9 %copy-done.1 = f32[150,150]{1,0:T(8,128)S(1)} copy-done((f32[150,150]{1,0:T(8,128)S(1)}, f32[150,150]{1,0:T(8,128)}, u32[]{:S(2)}) %copy-start.1) | copy-done | bytes 90024
  12.7 1.2 %weights.1 = (bf16[304,480]{1,0:T(8,128)(2,1)S(1)}, f32[8,128]{1,0:T(8,128)S(1)}) custom-call(f32[150,150]{1,0:T(8,128)S(1)} %copy-done.1, f32[150,150]{1,0:T(8,128)S(1)} %copy-done.2), custom_call_target="tpu_custom_call" | custom-call | tf_op jit(solution)/shard_map/weights/pallas_call | solution.py:490
  13.9 2.0 %first.1 = (f32[2400,128]{1,0:T(8,128)S(1)}, f32[200,128]{1,0:T(8,128)S(1)}, f32[200,128]{1,0:T(8,128)S(1)}, f32[100,128]{1,0:T(8,128)S(1)}, f32[100,128]{1,0:T(8,128)S(1)}) custom-call(f32[2400,128]{1,0:T(8,128)S(1)} %bitcast.10, f32[200,128]{1,0:T(8,128)S(1)} %collective-permute-done.refs_1_, f32[100,128]{1,0:T(8,128)S(1)} %collective-permute-done.1.refs_2_, ...), custom_call_target="tpu_custom_call" | custom-call | tf_op jit(solution)/shard_map/first/pallas_call | solution.py:490
  16.0 1.6 %collective-permute-start.2 = (f32[200,128]{1,0:T(8,128)S(1)}, f32[200,128]{1,0:T(8,128)S(1)}, u32[]{:S(2)}, u32[]{:S(2)}) collective-permute-start(f32[200,128]{1,0:T(8,128)S(1)} %get-tuple-element.41.refs_6_), channel_id=1, source_target_pairs={{0,120},{8,16},{16,8},{24,32},{32,24},{40,48},{48,40},{56,64},{64,... | collective-permute-start | bytes 307208 | tf_op jit(solution)/shard_map/ppermute | solution.py:39
  17.6 3.0 %collective-permute-start.3 = (f32[100,128]{1,0:T(8,128)S(1)}, f32[100,128]{1,0:T(8,128)S(1)}, u32[]{:S(2)}, u32[]{:S(2)}) collective-permute-start(f32[100,128]{1,0:T(8,128)S(1)} %get-tuple-element.42.refs_8_), channel_id=1, source_target_pairs={{0,7},{1,2},{2,1},{3,4},{4,3},{5,6},{6,5},{7,0},{8,15},{9,10},{10,... | collective-permute-start | bytes 153608 | tf_op jit(solution)/shard_map/ppermute | solution.py:39
  20.7 4.3 %collective-permute-done.3.refs_2_ = f32[100,128]{1,0:T(8,128)S(1)} collective-permute-done((f32[100,128]{1,0:T(8,128)S(1)}, f32[100,128]{1,0:T(8,128)S(1)}, u32[]{:S(2)}, u32[]{:S(2)}) %collective-permute-start.3) | collective-permute-done | bytes 51232 | tf_op jit(solution)/shard_map/ppermute | solution.py:39
  24.9 1.7 %second.1 = (f32[2400,128]{1,0:T(8,128)S(1)}, f32[2400,128]{1,0:T(8,128)S(1)}, f32[200,128]{1,0:T(8,128)S(1)}, f32[200,128]{1,0:T(8,128)S(1)}, f32[100,128]{1,0:T(8,128)S(1)}, /*index=5*/f32[100,128]{1,0:T(8,128)S(1)}) custom-call(f32[2400,128]{1,0:T(8,128)S(1)} %get-tuple-element.40.refs_0_, f32[200,128]{1,0:T(8,128)S(1)} %collective-permute-done.2.refs_1_, ...), custom_call_target="tpu_custom_call" | custom-call | tf_op jit(solution)/shard_map/second/pallas_call | solution.py:490
  26.7 3.5 %collective-permute-start.6 = (f32[200,128]{1,0:T(8,128)S(1)}, f32[200,128]{1,0:T(8,128)S(1)}, u32[]{:S(2)}, u32[]{:S(2)}) collective-permute-start(f32[200,128]{1,0:T(8,128)S(1)} %get-tuple-element.47.refs_7_), channel_id=1, source_target_pairs={{0,120},{8,16},{16,8},{24,32},{32,24},{40,48},{48,40},{56,64},{64,... | collective-permute-start | bytes 307208 | tf_op jit(solution)/shard_map/ppermute | solution.py:39
  30.2 1.4 %collective-permute-start.7 = (f32[100,128]{1,0:T(8,128)S(1)}, f32[100,128]{1,0:T(8,128)S(1)}, u32[]{:S(2)}, u32[]{:S(2)}) collective-permute-start(f32[100,128]{1,0:T(8,128)S(1)} %get-tuple-element.48.refs_9_), channel_id=1, source_target_pairs={{0,7},{1,2},{2,1},{3,4},{4,3},{5,6},{6,5},{7,0},{8,15},{9,10},{10,... | collective-permute-start | bytes 153608 | tf_op jit(solution)/shard_map/ppermute | solution.py:39
  31.6 1.0 %products.1 = (f32[40,128]{1,0:T(8,128)S(1)}, f32[2400,128]{1,0:T(8,128)}) custom-call(f32[2400,128]{1,0:T(8,128)S(1)} %bitcast.11, f32[2400,128]{1,0:T(8,128)S(1)} %get-tuple-element.46.refs_1_), custom_call_target="tpu_custom_call" | custom-call | tf_op jit(solution)/shard_map/products/pallas_call | solution.py:490
  32.6 4.3 %collective-permute-done.7.refs_3_ = f32[100,128]{1,0:T(8,128)S(1)} collective-permute-done((f32[100,128]{1,0:T(8,128)S(1)}, f32[100,128]{1,0:T(8,128)S(1)}, u32[]{:S(2)}, u32[]{:S(2)}) %collective-permute-start.7) | collective-permute-done | bytes 51232 | tf_op jit(solution)/shard_map/ppermute | solution.py:39
  36.9 2.9 %third.1 = (f32[2400,128]{1,0:T(8,128)S(1)}, f32[2400,128]{1,0:T(8,128)S(1)}, f32[200,128]{1,0:T(8,128)S(1)}, f32[100,128]{1,0:T(8,128)S(1)}, f32[264,128]{1,0:T(8,128)S(1)}, /*index=5*/f32[256,128]{1,0:T(8,128)}) custom-call(f32[2400,128]{1,0:T(8,128)S(1)} %get-tuple-element.45.refs_0_, f32[2400,128]{1,0:T(8,128)S(1)} %get-tuple-element.46.refs_1_, ...), custom_call_target="tpu_custom_call" | custom-call | tf_op jit(solution)/shard_map/third/pallas_call | solution.py:490
  39.8 2.5 %collective-permute-start.11 = (f32[264,128]{1,0:T(8,128)S(1)}, f32[264,128]{1,0:T(8,128)S(1)}, u32[]{:S(2)}, u32[]{:S(2)}) collective-permute-start(f32[264,128]{1,0:T(8,128)S(1)} %get-tuple-element.57.refs_0_), channel_id=1, source_target_pairs={{0,16},{8,24},{16,0},{24,8},{32,48},{40,56},{48,32},{56,40},{64,80... | collective-permute-start | bytes 405512 | tf_op jit(solution)/shard_map/ppermute | solution.py:537
  43.1 5.5 %all-to-all-start = ((f32[128,2,128]{2,1,0:T(2,128)}), f32[128,2,128]{2,1,0:T(2,128)S(1)}, u32[]{:S(2)}, u32[]{:S(2)}) async-start(f32[128,2,128]{2,1,0:T(2,128)} %bitcast.4), calls=%async_computation | async-start | bytes 262144 | tf_op jit(solution)/shard_map/all_to_all | solution.py:540
  48.8 1.1 %collective-permute-start.17 = (f32[100,128]{1,0:T(8,128)S(1)}, f32[100,128]{1,0:T(8,128)S(1)}, u32[]{:S(2)}, u32[]{:S(2)}) collective-permute-start(f32[100,128]{1,0:T(8,128)S(1)} %get-tuple-element.67), channel_id=1, source_target_pairs={{0,1},{1,2},{2,3},{3,4},{4,5},{5,6},{6,7},{7,0},{8,9},{9,10},{10,1... | collective-permute-start | bytes 153608 | tf_op jit(solution)/shard_map/ppermute | solution.py:28
  49.9 1.7 %collective-permute-start.13 = (f32[32,128]{1,0:T(8,128)S(1)}, f32[32,128]{1,0:T(8,128)S(1)}, u32[]{:S(2)}, u32[]{:S(2)}) collective-permute-start(f32[32,128]{1,0:T(8,128)S(1)} %get-tuple-element.59), channel_id=1, source_target_pairs={{0,32},{8,40},{16,48},{24,56},{32,64},{40,72},{48,80},{56,88},{64,... | collective-permute-start | bytes 49160 | tf_op jit(solution)/shard_map/ppermute | solution.py:28
  51.6 3.2 %collective-permute-start.14 = (f32[32,128]{1,0:T(8,128)S(1)}, f32[32,128]{1,0:T(8,128)S(1)}, u32[]{:S(2)}, u32[]{:S(2)}) collective-permute-start(f32[32,128]{1,0:T(8,128)S(1)} %get-tuple-element.60), channel_id=1, source_target_pairs={{0,64},{8,72},{16,80},{24,88},{32,96},{40,104},{48,112},{56,120},{... | collective-permute-start | bytes 49160 | tf_op jit(solution)/shard_map/ppermute | solution.py:28
  54.8 1.2 %collective-permute-start.15 = (f32[32,128]{1,0:T(8,128)S(1)}, f32[32,128]{1,0:T(8,128)S(1)}, u32[]{:S(2)}, u32[]{:S(2)}) collective-permute-start(f32[32,128]{1,0:T(8,128)S(1)} %get-tuple-element.61), channel_id=1, source_target_pairs={{0,96},{8,104},{16,112},{24,120},{32,0},{40,8},{48,16},{56,24},{64... | collective-permute-start | bytes 49160 | tf_op jit(solution)/shard_map/ppermute | solution.py:28
  56.0 2.2 %all-to-all-done = f32[128,2,128]{2,1,0:T(2,128)S(1)} async-done(((f32[128,2,128]{2,1,0:T(2,128)}), f32[128,2,128]{2,1,0:T(2,128)S(1)}, u32[]{:S(2)}, u32[]{:S(2)}) %all-to-all-start) | async-done | bytes 131104 | tf_op jit(solution)/shard_map/all_to_all | solution.py:540
  58.2 1.7 %coefficients.1 = (f32[2400,128]{1,0:T(8,128)S(1)}, f32[2400,128]{1,0:T(8,128)S(1)}, f32[8,128]{1,0:T(8,128)S(1)}, f32[8,128]{1,0:T(8,128)S(1)}) custom-call(f32[256,128]{1,0:T(8,128)S(1)} %bitcast.12, f32[8,128]{1,0:T(8,128)S(1)} %get-tuple-element.53.refs_1_, f32[2400,128]{1,0:T(8,128)} %bitcast.9, f32[2400,128]{1,0:T(8,128)} %get-tuple-element.54.refs_3_), custom_call_target="tpu_custom_call" | custom-call | tf_op jit(solution)/shard_map/coefficients/pallas_call | solution.py:490
  60.0 2.9 %last.1 = (f32[2400,128]{1,0:T(8,128)}, f32[2400,128]{1,0:T(8,128)}, f32[8,128]{1,0:T(8,128)}) custom-call(f32[3,25]{1,0:T(4,128)S(1)} %copy-done.5, f32[8,128]{1,0:T(8,128)S(1)} %get-tuple-element.55.refs_1_, f32[8,128]{1,0:T(8,128)S(1)} %get-tuple-element.56.refs_2_, f32[32,128]{1,0:T(8,128)S(1)} %get-tuple-element.58.refs_3_, ...), custom_call_target="tpu_custom_call" | custom-call | tf_op jit(solution)/shard_map/last/pallas_call | solution.py:490
  (36 shorter events, 2.0 us)
Async XLA Ops:
  0.6 13.3 %copy-start = (f32[3,25,4,8,128]{4,3,2,1,0:T(8,128)S(1)}, f32[3,25,4,8,128]{4,3,2,1,0:T(8,128)}, u32[]{:S(2)}) copy-start(f32[3,25,4,8,128]{4,3,2,1,0:T(8,128)} %refs_0_.3) | copy-start | bytes 3686404
  0.6 13.3 %copy-start.4 = (f32[4,8,128]{2,1,0:T(8,128)S(1)}, f32[4,8,128]{2,1,0:T(8,128)}, u32[]{:S(2)}) copy-start(f32[4,8,128]{2,1,0:T(8,128)} %param.8) | copy-start | bytes 49156
  0.7 13.3 %copy-start.3 = (f32[4,8,128]{2,1,0:T(8,128)S(1)}, f32[4,8,128]{2,1,0:T(8,128)}, u32[]{:S(2)}) copy-start(f32[4,8,128]{2,1,0:T(8,128)} %param.7) | copy-start | bytes 49156
  1.7 12.2 %collective-permute-start = (f32[200,128]{1,0:T(8,128)S(1)}, f32[200,128]{1,0:T(8,128)S(1)}, u32[]{:S(2)}, u32[]{:S(2)}) collective-permute-start(f32[200,128]{1,0:T(8,128)S(1)} %bitcast.19), channel_id=1, source_target_pairs={{0,120},{8,0},{16,8},{24,16},{32,24},{40,32},{48,40},{56,48},{64,5... | collective-permute-start | bytes 307208 | tf_op jit(solution)/shard_map/ppermute | solution.py:28
  7.8 6.1 %collective-permute-start.1 = (f32[100,128]{1,0:T(8,128)S(1)}, f32[100,128]{1,0:T(8,128)S(1)}, u32[]{:S(2)}, u32[]{:S(2)}) collective-permute-start(f32[100,128]{1,0:T(8,128)S(1)} %reshape.35), channel_id=1, source_target_pairs={{0,7},{1,0},{2,1},{3,2},{4,3},{5,4},{6,5},{7,6},{8,15},{9,8},{10,9... | collective-permute-start | bytes 153608 | tf_op jit(solution)/shard_map/ppermute | solution.py:28
  11.8 0.9 %copy-start.2 = (f32[150,150]{1,0:T(8,128)S(1)}, f32[150,150]{1,0:T(8,128)}, u32[]{:S(2)}) copy-start(f32[150,150]{1,0:T(8,128)} %refs_1_.1) | copy-start | bytes 270004
  16.0 9.0 %collective-permute-start.2 = (f32[200,128]{1,0:T(8,128)S(1)}, f32[200,128]{1,0:T(8,128)S(1)}, u32[]{:S(2)}, u32[]{:S(2)}) collective-permute-start(f32[200,128]{1,0:T(8,128)S(1)} %get-tuple-element.41.refs_6_), channel_id=1, source_target_pairs={{0,120},{8,16},{16,8},{24,32},{32,24},{40,48},{48,40},{56,64},{64,... | collective-permute-start | bytes 307208 | tf_op jit(solution)/shard_map/ppermute | solution.py:39
  17.6 7.3 %collective-permute-start.5 = (f32[200,128]{1,0:T(8,128)S(1)}, f32[200,128]{1,0:T(8,128)S(1)}, u32[]{:S(2)}, u32[]{:S(2)}) collective-permute-start(f32[200,128]{1,0:T(8,128)S(1)} %get-tuple-element.44.refs_5_), channel_id=1, source_target_pairs={{0,8},{8,0},{16,24},{24,16},{32,40},{40,32},{48,56},{56,48},{64,72... | collective-permute-start | bytes 307208 | tf_op jit(solution)/shard_map/ppermute | solution.py:33
  17.6 7.3 %collective-permute-start.3 = (f32[100,128]{1,0:T(8,128)S(1)}, f32[100,128]{1,0:T(8,128)S(1)}, u32[]{:S(2)}, u32[]{:S(2)}) collective-permute-start(f32[100,128]{1,0:T(8,128)S(1)} %get-tuple-element.42.refs_8_), channel_id=1, source_target_pairs={{0,7},{1,2},{2,1},{3,4},{4,3},{5,6},{6,5},{7,0},{8,15},{9,10},{10,... | collective-permute-start | bytes 153608 | tf_op jit(solution)/shard_map/ppermute | solution.py:39
  20.6 4.3 %collective-permute-start.4 = (f32[100,128]{1,0:T(8,128)S(1)}, f32[100,128]{1,0:T(8,128)S(1)}, u32[]{:S(2)}, u32[]{:S(2)}) collective-permute-start(f32[100,128]{1,0:T(8,128)S(1)} %get-tuple-element.43.refs_7_), channel_id=1, source_target_pairs={{0,1},{1,0},{2,3},{3,2},{4,5},{5,4},{6,7},{7,6},{8,9},{9,8},{10,11... | collective-permute-start | bytes 153608 | tf_op jit(solution)/shard_map/ppermute | solution.py:33
  26.7 10.2 %collective-permute-start.6 = (f32[200,128]{1,0:T(8,128)S(1)}, f32[200,128]{1,0:T(8,128)S(1)}, u32[]{:S(2)}, u32[]{:S(2)}) collective-permute-start(f32[200,128]{1,0:T(8,128)S(1)} %get-tuple-element.47.refs_7_), channel_id=1, source_target_pairs={{0,120},{8,16},{16,8},{24,32},{32,24},{40,48},{48,40},{56,64},{64,... | collective-permute-start | bytes 307208 | tf_op jit(solution)/shard_map/ppermute | solution.py:39
  30.1 6.7 %collective-permute-start.9 = (f32[200,128]{1,0:T(8,128)S(1)}, f32[200,128]{1,0:T(8,128)S(1)}, u32[]{:S(2)}, u32[]{:S(2)}) collective-permute-start(f32[200,128]{1,0:T(8,128)S(1)} %get-tuple-element.50.refs_6_), channel_id=1, source_target_pairs={{0,8},{8,0},{16,24},{24,16},{32,40},{40,32},{48,56},{56,48},{64,72... | collective-permute-start | bytes 307208 | tf_op jit(solution)/shard_map/ppermute | solution.py:33
  30.2 6.7 %collective-permute-start.7 = (f32[100,128]{1,0:T(8,128)S(1)}, f32[100,128]{1,0:T(8,128)S(1)}, u32[]{:S(2)}, u32[]{:S(2)}) collective-permute-start(f32[100,128]{1,0:T(8,128)S(1)} %get-tuple-element.48.refs_9_), channel_id=1, source_target_pairs={{0,7},{1,2},{2,1},{3,4},{4,3},{5,6},{6,5},{7,0},{8,15},{9,10},{10,... | collective-permute-start | bytes 153608 | tf_op jit(solution)/shard_map/ppermute | solution.py:39
  31.6 5.3 %collective-permute-start.8 = (f32[100,128]{1,0:T(8,128)S(1)}, f32[100,128]{1,0:T(8,128)S(1)}, u32[]{:S(2)}, u32[]{:S(2)}) collective-permute-start(f32[100,128]{1,0:T(8,128)S(1)} %get-tuple-element.49.refs_8_), channel_id=1, source_target_pairs={{0,1},{1,0},{2,3},{3,2},{4,5},{5,4},{6,7},{7,6},{8,9},{9,8},{10,11... | collective-permute-start | bytes 153608 | tf_op jit(solution)/shard_map/ppermute | solution.py:33
  39.8 10.1 %collective-permute-start.12 = (f32[264,128]{1,0:T(8,128)S(1)}, f32[264,128]{1,0:T(8,128)S(1)}, u32[]{:S(2)}, u32[]{:S(2)}) collective-permute-start(f32[264,128]{1,0:T(8,128)S(1)} %get-tuple-element.57.refs_0_), channel_id=1, source_target_pairs={{0,24},{8,16},{16,8},{24,0},{32,56},{40,48},{48,40},{56,32},{64,88... | collective-permute-start | bytes 405512 | tf_op jit(solution)/shard_map/ppermute | solution.py:537
  39.8 10.1 %collective-permute-start.11 = (f32[264,128]{1,0:T(8,128)S(1)}, f32[264,128]{1,0:T(8,128)S(1)}, u32[]{:S(2)}, u32[]{:S(2)}) collective-permute-start(f32[264,128]{1,0:T(8,128)S(1)} %get-tuple-element.57.refs_0_), channel_id=1, source_target_pairs={{0,16},{8,24},{16,0},{24,8},{32,48},{40,56},{48,32},{56,40},{64,80... | collective-permute-start | bytes 405512 | tf_op jit(solution)/shard_map/ppermute | solution.py:537
  42.2 7.6 %collective-permute-start.10 = (f32[264,128]{1,0:T(8,128)S(1)}, f32[264,128]{1,0:T(8,128)S(1)}, u32[]{:S(2)}, u32[]{:S(2)}) collective-permute-start(f32[264,128]{1,0:T(8,128)S(1)} %get-tuple-element.57.refs_0_), channel_id=1, source_target_pairs={{0,8},{8,0},{16,24},{24,16},{32,40},{40,32},{48,56},{56,48},{64,72... | collective-permute-start | bytes 405512 | tf_op jit(solution)/shard_map/ppermute | solution.py:537
  43.1 15.1 %all-to-all-start = ((f32[128,2,128]{2,1,0:T(2,128)}), f32[128,2,128]{2,1,0:T(2,128)S(1)}, u32[]{:S(2)}, u32[]{:S(2)}) async-start(f32[128,2,128]{2,1,0:T(2,128)} %bitcast.4), calls=%async_computation | async-start | bytes 262144 | tf_op jit(solution)/shard_map/all_to_all | solution.py:540
  48.7 11.3 %collective-permute-start.16 = (f32[200,128]{1,0:T(8,128)S(1)}, f32[200,128]{1,0:T(8,128)S(1)}, u32[]{:S(2)}, u32[]{:S(2)}) collective-permute-start(f32[200,128]{1,0:T(8,128)S(1)} %get-tuple-element.66), channel_id=1, source_target_pairs={{0,8},{8,16},{16,24},{24,32},{32,40},{40,48},{48,56},{56,64},{64,7... | collective-permute-start | bytes 307208 | tf_op jit(solution)/shard_map/ppermute | solution.py:28
  48.8 11.2 %collective-permute-start.17 = (f32[100,128]{1,0:T(8,128)S(1)}, f32[100,128]{1,0:T(8,128)S(1)}, u32[]{:S(2)}, u32[]{:S(2)}) collective-permute-start(f32[100,128]{1,0:T(8,128)S(1)} %get-tuple-element.67), channel_id=1, source_target_pairs={{0,1},{1,2},{2,3},{3,4},{4,5},{5,6},{6,7},{7,0},{8,9},{9,10},{10,1... | collective-permute-start | bytes 153608 | tf_op jit(solution)/shard_map/ppermute | solution.py:28
  49.9 10.1 %collective-permute-start.13 = (f32[32,128]{1,0:T(8,128)S(1)}, f32[32,128]{1,0:T(8,128)S(1)}, u32[]{:S(2)}, u32[]{:S(2)}) collective-permute-start(f32[32,128]{1,0:T(8,128)S(1)} %get-tuple-element.59), channel_id=1, source_target_pairs={{0,32},{8,40},{16,48},{24,56},{32,64},{40,72},{48,80},{56,88},{64,... | collective-permute-start | bytes 49160 | tf_op jit(solution)/shard_map/ppermute | solution.py:28
  51.6 8.4 %collective-permute-start.14 = (f32[32,128]{1,0:T(8,128)S(1)}, f32[32,128]{1,0:T(8,128)S(1)}, u32[]{:S(2)}, u32[]{:S(2)}) collective-permute-start(f32[32,128]{1,0:T(8,128)S(1)} %get-tuple-element.60), channel_id=1, source_target_pairs={{0,64},{8,72},{16,80},{24,88},{32,96},{40,104},{48,112},{56,120},{... | collective-permute-start | bytes 49160 | tf_op jit(solution)/shard_map/ppermute | solution.py:28
  54.8 5.2 %collective-permute-start.15 = (f32[32,128]{1,0:T(8,128)S(1)}, f32[32,128]{1,0:T(8,128)S(1)}, u32[]{:S(2)}, u32[]{:S(2)}) collective-permute-start(f32[32,128]{1,0:T(8,128)S(1)} %get-tuple-element.61), channel_id=1, source_target_pairs={{0,96},{8,104},{16,112},{24,120},{32,0},{40,8},{48,16},{56,24},{64... | collective-permute-start | bytes 49160 | tf_op jit(solution)/shard_map/ppermute | solution.py:28
  58.2 1.8 %copy-start.5 = (f32[3,25]{1,0:T(4,128)S(1)}, f32[3,25]{1,0:T(4,128)}, u32[]{:S(2)}) copy-start(f32[3,25]{1,0:T(4,128)} %refs_0_.5) | copy-start | bytes 904
  (1 other events, 0.9 us)

commit v10 on v9

--- a/solution.py
+++ b/solution.py
@@ -21,6 +21,23 @@
 VM = pl.BlockSpec(memory_space=pltpu.VMEM)
 SM = pl.BlockSpec(memory_space=pltpu.SMEM)
 ANY = pl.BlockSpec(memory_space=pl.ANY)
+
+
+PARTS = (100, 100)
+
+
+class Parts:
+    def __init__(self, *refs):
+        self.refs = refs
+
+    def __getitem__(self, _):
+        return jnp.concatenate([ref[...] for ref in self.refs], 0)
+
+    def __setitem__(self, _, value):
+        at = 0
+        for ref in self.refs:
+            ref[...] = value[at : at + ref.shape[0]]
+            at += ref.shape[0]
 
 
 def shifted(value, axis, by):
@@ -178,9 +195,9 @@
 
 
 def first_kernel(rhs_ref, hx_ref, hy_ref, k_ref, m_ref, w_ref,
-                 p_ref, snx, sfx, sny, sfy, last_in, last_out, upx, lowx, upy, lowy):
+                 p_ref, sn0, sn1, sfx, sny, sfy, last_in, last_out, upx, lowx, upy, lowy):
     apply_operator(rhs_ref, hx_ref, hy_ref, k_ref, m_ref, w_ref, p_ref, upx, lowx, upy, lowy, last_in, last_out, True)
-    route(is_even("gx"), upx, lowx, snx, sfx)
+    route(is_even("gx"), upx, lowx, Parts(sn0, sn1), sfx)
     route(is_even("gy"), upy, lowy, sny, sfy)
 
 
@@ -209,11 +226,11 @@
     return jnp.sum(tile, 0, keepdims=True)
 
 
-def second_kernel(p_ref, rfx, rfy, rny, rnx, snx, sfx, sny, sfy, k_ref, m_ref, w_ref,
-                  v1_ref, p1_ref, tnx, tfx, tny, tfy, ux, uy, last_in, last_out, upx, lowx, upy, lowy):
-    assemble(p_ref, snx, sfx, sny, sfy, rnx, rfx, rny, rfy, v1_ref, ux, uy)
+def second_kernel(p_ref, rfx, rfy, rny, rn0, rn1, sn0, sn1, sfx, sny, sfy, k_ref, m_ref, w_ref,
+                  v1_ref, p1_ref, tn0, tn1, tfx, tny, tfy, ux, uy, last_in, last_out, upx, lowx, upy, lowy):
+    assemble(p_ref, Parts(sn0, sn1), sfx, sny, sfy, Parts(rn0, rn1), rfx, rny, rfy, v1_ref, ux, uy)
     apply_operator(v1_ref, ux, uy, k_ref, m_ref, w_ref, p1_ref, upx, lowx, upy, lowy, last_in, last_out)
-    route(is_even("gx"), upx, lowx, tnx, tfx)
+    route(is_even("gx"), upx, lowx, Parts(tn0, tn1), tfx)
     route(is_even("gy"), upy, lowy, tny, tfy)
 
 
@@ -251,9 +268,9 @@
     keep.wait()
 
 
-def third_kernel(p_ref, v1_ref, rfx, rfy, rny, rnx, snx, sfx, sny, sfy, sums_ref, k_ref, m_ref, w_ref,
+def third_kernel(p_ref, v1_ref, rfx, rfy, rny, rn0, rn1, sn0, sn1, sfx, sny, sfy, sums_ref, k_ref, m_ref, w_ref,
                  v2_ref, p2_ref, upx, upy, loads_ref, mom_ref, ux, uy, last_in, last_out):
-    assemble(p_ref, snx, sfx, sny, sfy, rnx, rfx, rny, rfy, v2_ref, ux, uy)
+    assemble(p_ref, Parts(sn0, sn1), sfx, sny, sfy, Parts(rn0, rn1), rfx, rny, rfy, v2_ref, ux, uy)
     v1 = v1_ref[...]
     v2 = v2_ref[...]
     loads_ref[0:16] = sums_ref[0:16]
@@ -476,7 +493,7 @@
     rhs2 = rhs.reshape(ROWS, LZ)
     k2 = kappa.reshape(CELLS, LZ)
     m2 = mass.reshape(CELLS, LZ)
-    sends = [struct(vx, LZ), struct(vx, LZ), struct(vy, LZ), struct(vy, LZ)]
+    sends = [struct(n, LZ) for n in PARTS] + [struct(vx, LZ), struct(vy, LZ), struct(vy, LZ)]
     upper = [pltpu.VMEM((vx, LZ), f32), pltpu.VMEM((vy, LZ), f32)] + [pltpu.VMEM((8 * LY, LZ), f32)] * 2
     edges = [pltpu.VMEM((vx, LZ), f32)] * 2 + [pltpu.VMEM((vy, LZ), f32)] * 2
 
@@ -498,11 +515,11 @@
         )(*ins)
 
     def swap(s):
-        far_x = far_swap(s[1], "gx")
-        far_y = far_swap(s[3], "gy")
-        near_y = near_swap(s[2], "gy")
-        near_x = near_swap(s[0], "gx")
-        return [far_x, far_y, near_y, near_x]
+        *near, far_x, near_y, far_y = s
+        far_x = far_swap(far_x, "gx")
+        far_y = far_swap(far_y, "gy")
+        near_y = near_swap(near_y, "gy")
+        return [far_x, far_y, near_y] + [near_swap(part, "gx") for part in near]
 
     hbm = pltpu.with_memory_space_constraint(rhs, pltpu.HBM)
     fx, fy = call(

time: 63.9 us -> 62.5 us (0.978)
  waiting for transfers between devices: 10.8 us -> 8.79 us
    ppermute x4, waiting for transfers between devices: 8.57 us -> 5.59 us  [far_swap(): return lax.ppermute(value, axis, pairs)]
    ppermute x4 -> x6, starting transfers between devices: 0.01 us -> 1.03 us  [near_swap(): return lax.ppermute(value, axis, [(i, i ^ 1) for i in range(n)])]
    ppermute x4 -> x6, waiting for transfers between devices: 0.01 us -> 0.94 us  [near_swap(): return lax.ppermute(value, axis, [(i, i ^ 1) for i in range(n)])]
    all_to_all x1, starting transfers between devices: 5.55 us -> 4.79 us  [shards(): lax.all_to_all(mom.reshape(-1, 2, LZ), ('gx', 'gy'), 0, 0, tiled=True)]
  transfers between devices with their start and end apart: 19 -> 21, of which waited for: 3 -> 4; matrix products, arithmetic and copies ran while one was open for 0% -> 0% of each run, Pallas kernels for 6% -> 6%
where the time goes in v10:
time: 62.5 us; the launch traced here: 61.6 us
  starting transfers between devices  35.3 us (56%)
  Pallas kernels  14.6 us (23%)
  waiting for transfers between devices  8.79 us (14%)
  local copies, waits for them, and re-layouts  1.86 us (3%)
  between operations  1.01 us (2%)
    ppermute x7, starting transfers between devices, shifted(): return lax.ppermute(value, axis, [(i, (i + by) % n) for i in range(n)])  16.4 us
    pallas_call x9, Pallas kernels, call(): pl.pallas_call(bound, out_shape=outs, in_specs=specs, out_specs=[ANY if i...  14.6 us
    ppermute x4, starting transfers between devices, far_swap(): return lax.ppermute(value, axis, pairs)  9.72 us
    ppermute x4, waiting for transfers between devices, far_swap(): return lax.ppermute(value, axis, pairs)  5.59 us
    all_to_all x1, starting transfers between devices, shards(): lax.all_to_all(mom.reshape(-1, 2, LZ), ('gx', 'gy'), 0, 0, tiled=True)  4.79 us
    ppermute x3, starting transfers between devices, shards(): lax.ppermute(loads, 'gx', [(i, i ^ b) for i in range(nx)])  3.37 us
    all_to_all x1, waiting for transfers between devices, shards(): lax.all_to_all(mom.reshape(-1, 2, LZ), ('gx', 'gy'), 0, 0, tiled=True)  2.24 us
    unnamed x12, local copies, waits for them, and re-layouts  1.84 us
  transfers between devices with their start and end apart: 21, of which 4 were waited for; matrix products, arithmetic and copies ran while one was open for 0% of the time, Pallas kernels for 6%

profile of v10, /device:TPU:0, one launch (start us, length us, event | category | flops | bytes accessed | tf_op | source)
XLA Modules:
  0.0 61.6 jit_solution(12121328028561864341)
XLA Ops:
  0.7 1.0 %edges.1 = (f32[25,8,128]{2,1,0:T(8,128)S(1)}, f32[25,4,128]{2,1,0:T(4,128)S(1)}) custom-call(f32[3,25,4,8,128]{4,3,2,1,0:T(8,128)} %refs_0_.3), custom_call_target="tpu_custom_call" | custom-call | tf_op jit(solution)/shard_map/edges/pallas_call | solution.py:507
  1.7 6.1 %collective-permute-start = (f32[200,128]{1,0:T(8,128)S(1)}, f32[200,128]{1,0:T(8,128)S(1)}, u32[]{:S(2)}, u32[]{:S(2)}) collective-permute-start(f32[200,128]{1,0:T(8,128)S(1)} %bitcast.19), channel_id=1, source_target_pairs={{0,120},{8,0},{16,8},{24,16},{32,24},{40,32},{48,40},{56,48},{64,5... | collective-permute-start | bytes 307208 | tf_op jit(solution)/shard_map/ppermute | solution.py:45
  7.8 3.1 %collective-permute-start.1 = (f32[100,128]{1,0:T(8,128)S(1)}, f32[100,128]{1,0:T(8,128)S(1)}, u32[]{:S(2)}, u32[]{:S(2)}) collective-permute-start(f32[100,128]{1,0:T(8,128)S(1)} %reshape.35), channel_id=1, source_target_pairs={{0,7},{1,0},{2,1},{3,2},{4,3},{5,4},{6,5},{7,6},{8,15},{9,8},{10,9... | collective-permute-start | bytes 153608 | tf_op jit(solution)/shard_map/ppermute | solution.py:45
  12.7 1.2 %weights.1 = (bf16[304,480]{1,0:T(8,128)(2,1)S(1)}, f32[8,128]{1,0:T(8,128)S(1)}) custom-call(f32[150,150]{1,0:T(8,128)S(1)} %copy-done.1, f32[150,150]{1,0:T(8,128)S(1)} %copy-done.2), custom_call_target="tpu_custom_call" | custom-call | tf_op jit(solution)/shard_map/weights/pallas_call | solution.py:507
  13.9 2.0 %first.1 = (f32[2400,128]{1,0:T(8,128)S(1)}, f32[100,128]{1,0:T(8,128)S(1)}, f32[100,128]{1,0:T(8,128)S(1)}, f32[200,128]{1,0:T(8,128)S(1)}, f32[100,128]{1,0:T(8,128)S(1)}, /*index=5*/f32[100,128]{1,0:T(8,128)S(1)}) custom-call(f32[2400,128]{1,0:T(8,128)S(1)} %bitcast.10, f32[200,128]{1,0:T(8,128)S(1)} %collective-permute-done.refs_1_, ...), custom_call_target="tpu_custom_call" | custom-call | tf_op jit(solution)/shard_map/first/pallas_call | solution.py:507
  16.0 1.6 %collective-permute-start.2 = (f32[200,128]{1,0:T(8,128)S(1)}, f32[200,128]{1,0:T(8,128)S(1)}, u32[]{:S(2)}, u32[]{:S(2)}) collective-permute-start(f32[200,128]{1,0:T(8,128)S(1)} %get-tuple-element.43.refs_8_), channel_id=1, source_target_pairs={{0,120},{8,16},{16,8},{24,32},{32,24},{40,48},{48,40},{56,64},{64,... | collective-permute-start | bytes 307208 | tf_op jit(solution)/shard_map/ppermute | solution.py:56
  17.6 3.0 %collective-permute-start.3 = (f32[100,128]{1,0:T(8,128)S(1)}, f32[100,128]{1,0:T(8,128)S(1)}, u32[]{:S(2)}, u32[]{:S(2)}) collective-permute-start(f32[100,128]{1,0:T(8,128)S(1)} %get-tuple-element.44.refs_10_), channel_id=1, source_target_pairs={{0,7},{1,2},{2,1},{3,4},{4,3},{5,6},{6,5},{7,0},{8,15},{9,10},{10,... | collective-permute-start | bytes 153608 | tf_op jit(solution)/shard_map/ppermute | solution.py:56
  21.2 2.7 %collective-permute-done.3.refs_2_ = f32[100,128]{1,0:T(8,128)S(1)} collective-permute-done((f32[100,128]{1,0:T(8,128)S(1)}, f32[100,128]{1,0:T(8,128)S(1)}, u32[]{:S(2)}, u32[]{:S(2)}) %collective-permute-start.3) | collective-permute-done | bytes 51232 | tf_op jit(solution)/shard_map/ppermute | solution.py:56
  23.9 0.9 %collective-permute-done.4.refs_3_ = f32[100,128]{1,0:T(8,128)S(1)} collective-permute-done((f32[100,128]{1,0:T(8,128)S(1)}, f32[100,128]{1,0:T(8,128)S(1)}, u32[]{:S(2)}, u32[]{:S(2)}) %collective-permute-start.4) | collective-permute-done | bytes 51232 | tf_op jit(solution)/shard_map/ppermute | solution.py:50
  24.8 1.8 %second.1 = (f32[2400,128]{1,0:T(8,128)S(1)}, f32[2400,128]{1,0:T(8,128)S(1)}, f32[100,128]{1,0:T(8,128)S(1)}, f32[100,128]{1,0:T(8,128)S(1)}, f32[200,128]{1,0:...) custom-call(f32[2400,128]{1,0:T(8,128)S(1)} %get-tuple-element.42.refs_0_, ...), custom_call_target="tpu_custom_call" | custom-call | tf_op jit(solution)/shard_map/second/pallas_call | solution.py:507
  26.6 3.3 %collective-permute-start.7 = (f32[200,128]{1,0:T(8,128)S(1)}, f32[200,128]{1,0:T(8,128)S(1)}, u32[]{:S(2)}, u32[]{:S(2)}) collective-permute-start(f32[200,128]{1,0:T(8,128)S(1)} %get-tuple-element.50.refs_9_), channel_id=1, source_target_pairs={{0,120},{8,16},{16,8},{24,32},{32,24},{40,48},{48,40},{56,64},{64,... | collective-permute-start | bytes 307208 | tf_op jit(solution)/shard_map/ppermute | solution.py:56
  29.8 1.8 %collective-permute-start.8 = (f32[100,128]{1,0:T(8,128)S(1)}, f32[100,128]{1,0:T(8,128)S(1)}, u32[]{:S(2)}, u32[]{:S(2)}) collective-permute-start(f32[100,128]{1,0:T(8,128)S(1)} %get-tuple-element.51.refs_11_), channel_id=1, source_target_pairs={{0,7},{1,2},{2,1},{3,4},{4,3},{5,6},{6,5},{7,0},{8,15},{9,10},{10,... | collective-permute-start | bytes 153608 | tf_op jit(solution)/shard_map/ppermute | solution.py:56
  32.1 1.0 %products.1 = (f32[40,128]{1,0:T(8,128)S(1)}, f32[2400,128]{1,0:T(8,128)}) custom-call(f32[2400,128]{1,0:T(8,128)S(1)} %bitcast.11, f32[2400,128]{1,0:T(8,128)S(1)} %get-tuple-element.49.refs_1_), custom_call_target="tpu_custom_call" | custom-call | tf_op jit(solution)/shard_map/products/pallas_call | solution.py:507
  33.2 2.9 %collective-permute-done.8.refs_3_ = f32[100,128]{1,0:T(8,128)S(1)} collective-permute-done((f32[100,128]{1,0:T(8,128)S(1)}, f32[100,128]{1,0:T(8,128)S(1)}, u32[]{:S(2)}, u32[]{:S(2)}) %collective-permute-start.8) | collective-permute-done | bytes 51232 | tf_op jit(solution)/shard_map/ppermute | solution.py:56
  36.1 2.9 %third.1 = (f32[2400,128]{1,0:T(8,128)S(1)}, f32[2400,128]{1,0:T(8,128)S(1)}, f32[200,128]{1,0:T(8,128)S(1)}, f32[100,128]{1,0:T(8,128)S(1)}, f32[264,128]{1,0:T(8,128)S(1)}, /*index=5*/f32[256,128]{1,0:T(8,128)}) custom-call(f32[2400,128]{1,0:T(8,128)S(1)} %get-tuple-element.48.refs_0_, f32[2400,128]{1,0:T(8,128)S(1)} %get-tuple-element.49.refs_1_, ...), custom_call_target="tpu_custom_call" | custom-call | tf_op jit(solution)/shard_map/third/pallas_call | solution.py:507
  39.4 3.0 %collective-permute-start.12 = (f32[264,128]{1,0:T(8,128)S(1)}, f32[264,128]{1,0:T(8,128)S(1)}, u32[]{:S(2)}, u32[]{:S(2)}) collective-permute-start(f32[264,128]{1,0:T(8,128)S(1)} %get-tuple-element.61.refs_0_), channel_id=1, source_target_pairs={{0,8},{8,0},{16,24},{24,16},{32,40},{40,32},{48,56},{56,48},{64,72... | collective-permute-start | bytes 405512 | tf_op jit(solution)/shard_map/ppermute | solution.py:554
  42.4 4.8 %all-to-all-start = ((f32[128,2,128]{2,1,0:T(2,128)}), f32[128,2,128]{2,1,0:T(2,128)S(1)}, u32[]{:S(2)}, u32[]{:S(2)}) async-start(f32[128,2,128]{2,1,0:T(2,128)} %bitcast.4), calls=%async_computation | async-start | bytes 262144 | tf_op jit(solution)/shard_map/all_to_all | solution.py:557
  47.2 1.0 %collective-permute-start.19 = (f32[100,128]{1,0:T(8,128)S(1)}, f32[100,128]{1,0:T(8,128)S(1)}, u32[]{:S(2)}, u32[]{:S(2)}) collective-permute-start(f32[100,128]{1,0:T(8,128)S(1)} %get-tuple-element.71), channel_id=1, source_target_pairs={{0,1},{1,2},{2,3},{3,4},{4,5},{5,6},{6,7},{7,0},{8,9},{9,10},{10,1... | collective-permute-start | bytes 153608 | tf_op jit(solution)/shard_map/ppermute | solution.py:45
  48.3 1.8 %collective-permute-start.15 = (f32[32,128]{1,0:T(8,128)S(1)}, f32[32,128]{1,0:T(8,128)S(1)}, u32[]{:S(2)}, u32[]{:S(2)}) collective-permute-start(f32[32,128]{1,0:T(8,128)S(1)} %get-tuple-element.63), channel_id=1, source_target_pairs={{0,32},{8,40},{16,48},{24,56},{32,64},{40,72},{48,80},{56,88},{64,... | collective-permute-start | bytes 49160 | tf_op jit(solution)/shard_map/ppermute | solution.py:45
  50.1 3.2 %collective-permute-start.16 = (f32[32,128]{1,0:T(8,128)S(1)}, f32[32,128]{1,0:T(8,128)S(1)}, u32[]{:S(2)}, u32[]{:S(2)}) collective-permute-start(f32[32,128]{1,0:T(8,128)S(1)} %get-tuple-element.64), channel_id=1, source_target_pairs={{0,64},{8,72},{16,80},{24,88},{32,96},{40,104},{48,112},{56,120},{... | collective-permute-start | bytes 49160 | tf_op jit(solution)/shard_map/ppermute | solution.py:45
  53.3 1.2 %collective-permute-start.17 = (f32[32,128]{1,0:T(8,128)S(1)}, f32[32,128]{1,0:T(8,128)S(1)}, u32[]{:S(2)}, u32[]{:S(2)}) collective-permute-start(f32[32,128]{1,0:T(8,128)S(1)} %get-tuple-element.65), channel_id=1, source_target_pairs={{0,96},{8,104},{16,112},{24,120},{32,0},{40,8},{48,16},{56,24},{64... | collective-permute-start | bytes 49160 | tf_op jit(solution)/shard_map/ppermute | solution.py:45
  54.5 2.2 %all-to-all-done = f32[128,2,128]{2,1,0:T(2,128)S(1)} async-done(((f32[128,2,128]{2,1,0:T(2,128)}), f32[128,2,128]{2,1,0:T(2,128)S(1)}, u32[]{:S(2)}, u32[]{:S(2)}) %all-to-all-start) | async-done | bytes 131104 | tf_op jit(solution)/shard_map/all_to_all | solution.py:557
  56.7 1.7 %coefficients.1 = (f32[2400,128]{1,0:T(8,128)S(1)}, f32[2400,128]{1,0:T(8,128)S(1)}, f32[8,128]{1,0:T(8,128)S(1)}, f32[8,128]{1,0:T(8,128)S(1)}) custom-call(f32[256,128]{1,0:T(8,128)S(1)} %bitcast.12, f32[8,128]{1,0:T(8,128)S(1)} %get-tuple-element.57.refs_1_, f32[2400,128]{1,0:T(8,128)} %bitcast.9, f32[2400,128]{1,0:T(8,128)} %get-tuple-element.58.refs_3_), custom_call_target="tpu_custom_call" | custom-call | tf_op jit(solution)/shard_map/coefficients/pallas_call | solution.py:507
  58.5 2.9 %last.1 = (f32[2400,128]{1,0:T(8,128)}, f32[2400,128]{1,0:T(8,128)}, f32[8,128]{1,0:T(8,128)}) custom-call(f32[3,25]{1,0:T(4,128)S(1)} %copy-done.5, f32[8,128]{1,0:T(8,128)S(1)} %get-tuple-element.59.refs_1_, f32[8,128]{1,0:T(8,128)S(1)} %get-tuple-element.60.refs_2_, f32[32,128]{1,0:T(8,128)S(1)} %get-tuple-element.62.refs_3_, ...), custom_call_target="tpu_custom_call" | custom-call | tf_op jit(solution)/shard_map/last/pallas_call | solution.py:507
  (40 shorter events, 3.5 us)
Async XLA Ops:
  0.6 13.3 %copy-start = (f32[3,25,4,8,128]{4,3,2,1,0:T(8,128)S(1)}, f32[3,25,4,8,128]{4,3,2,1,0:T(8,128)}, u32[]{:S(2)}) copy-start(f32[3,25,4,8,128]{4,3,2,1,0:T(8,128)} %refs_0_.3) | copy-start | bytes 3686404
  0.6 13.3 %copy-start.4 = (f32[4,8,128]{2,1,0:T(8,128)S(1)}, f32[4,8,128]{2,1,0:T(8,128)}, u32[]{:S(2)}) copy-start(f32[4,8,128]{2,1,0:T(8,128)} %param.8) | copy-start | bytes 49156
  0.7 13.3 %copy-start.3 = (f32[4,8,128]{2,1,0:T(8,128)S(1)}, f32[4,8,128]{2,1,0:T(8,128)}, u32[]{:S(2)}) copy-start(f32[4,8,128]{2,1,0:T(8,128)} %param.7) | copy-start | bytes 49156
  1.7 12.2 %collective-permute-start = (f32[200,128]{1,0:T(8,128)S(1)}, f32[200,128]{1,0:T(8,128)S(1)}, u32[]{:S(2)}, u32[]{:S(2)}) collective-permute-start(f32[200,128]{1,0:T(8,128)S(1)} %bitcast.19), channel_id=1, source_target_pairs={{0,120},{8,0},{16,8},{24,16},{32,24},{40,32},{48,40},{56,48},{64,5... | collective-permute-start | bytes 307208 | tf_op jit(solution)/shard_map/ppermute | solution.py:45
  7.8 6.1 %collective-permute-start.1 = (f32[100,128]{1,0:T(8,128)S(1)}, f32[100,128]{1,0:T(8,128)S(1)}, u32[]{:S(2)}, u32[]{:S(2)}) collective-permute-start(f32[100,128]{1,0:T(8,128)S(1)} %reshape.35), channel_id=1, source_target_pairs={{0,7},{1,0},{2,1},{3,2},{4,3},{5,4},{6,5},{7,6},{8,15},{9,8},{10,9... | collective-permute-start | bytes 153608 | tf_op jit(solution)/shard_map/ppermute | solution.py:45
  16.0 8.8 %collective-permute-start.2 = (f32[200,128]{1,0:T(8,128)S(1)}, f32[200,128]{1,0:T(8,128)S(1)}, u32[]{:S(2)}, u32[]{:S(2)}) collective-permute-start(f32[200,128]{1,0:T(8,128)S(1)} %get-tuple-element.43.refs_8_), channel_id=1, source_target_pairs={{0,120},{8,16},{16,8},{24,32},{32,24},{40,48},{48,40},{56,64},{64,... | collective-permute-start | bytes 307208 | tf_op jit(solution)/shard_map/ppermute | solution.py:56
  17.6 6.2 %collective-permute-start.3 = (f32[100,128]{1,0:T(8,128)S(1)}, f32[100,128]{1,0:T(8,128)S(1)}, u32[]{:S(2)}, u32[]{:S(2)}) collective-permute-start(f32[100,128]{1,0:T(8,128)S(1)} %get-tuple-element.44.refs_10_), channel_id=1, source_target_pairs={{0,7},{1,2},{2,1},{3,4},{4,3},{5,6},{6,5},{7,0},{8,15},{9,10},{10,... | collective-permute-start | bytes 153608 | tf_op jit(solution)/shard_map/ppermute | solution.py:56
  20.6 4.1 %collective-permute-start.4 = (f32[100,128]{1,0:T(8,128)S(1)}, f32[100,128]{1,0:T(8,128)S(1)}, u32[]{:S(2)}, u32[]{:S(2)}) collective-permute-start(f32[100,128]{1,0:T(8,128)S(1)} %get-tuple-element.45.refs_9_), channel_id=1, source_target_pairs={{0,1},{1,0},{2,3},{3,2},{4,5},{5,4},{6,7},{7,6},{8,9},{9,8},{10,11... | collective-permute-start | bytes 153608 | tf_op jit(solution)/shard_map/ppermute | solution.py:50
  20.6 4.1 %collective-permute-start.5 = (f32[100,128]{1,0:T(8,128)S(1)}, f32[100,128]{1,0:T(8,128)S(1)}, u32[]{:S(2)}, u32[]{:S(2)}) collective-permute-start(f32[100,128]{1,0:T(8,128)S(1)} %get-tuple-element.46.refs_6_), channel_id=1, source_target_pairs={{0,8},{8,0},{16,24},{24,16},{32,40},{40,32},{48,56},{56,48},{64,72... | collective-permute-start | bytes 153608 | tf_op jit(solution)/shard_map/ppermute | solution.py:50
  20.7 4.1 %collective-permute-start.6 = (f32[100,128]{1,0:T(8,128)S(1)}, f32[100,128]{1,0:T(8,128)S(1)}, u32[]{:S(2)}, u32[]{:S(2)}) collective-permute-start(f32[100,128]{1,0:T(8,128)S(1)} %get-tuple-element.47.refs_7_), channel_id=1, source_target_pairs={{0,8},{8,0},{16,24},{24,16},{32,40},{40,32},{48,56},{56,48},{64,72... | collective-permute-start | bytes 153608 | tf_op jit(solution)/shard_map/ppermute | solution.py:50
  26.6 9.5 %collective-permute-start.7 = (f32[200,128]{1,0:T(8,128)S(1)}, f32[200,128]{1,0:T(8,128)S(1)}, u32[]{:S(2)}, u32[]{:S(2)}) collective-permute-start(f32[200,128]{1,0:T(8,128)S(1)} %get-tuple-element.50.refs_9_), channel_id=1, source_target_pairs={{0,120},{8,16},{16,8},{24,32},{32,24},{40,48},{48,40},{56,64},{64,... | collective-permute-start | bytes 307208 | tf_op jit(solution)/shard_map/ppermute | solution.py:56
  29.8 6.2 %collective-permute-start.8 = (f32[100,128]{1,0:T(8,128)S(1)}, f32[100,128]{1,0:T(8,128)S(1)}, u32[]{:S(2)}, u32[]{:S(2)}) collective-permute-start(f32[100,128]{1,0:T(8,128)S(1)} %get-tuple-element.51.refs_11_), channel_id=1, source_target_pairs={{0,7},{1,2},{2,1},{3,4},{4,3},{5,6},{6,5},{7,0},{8,15},{9,10},{10,... | collective-permute-start | bytes 153608 | tf_op jit(solution)/shard_map/ppermute | solution.py:56
  31.6 4.5 %collective-permute-start.9 = (f32[100,128]{1,0:T(8,128)S(1)}, f32[100,128]{1,0:T(8,128)S(1)}, u32[]{:S(2)}, u32[]{:S(2)}) collective-permute-start(f32[100,128]{1,0:T(8,128)S(1)} %get-tuple-element.52.refs_10_), channel_id=1, source_target_pairs={{0,1},{1,0},{2,3},{3,2},{4,5},{5,4},{6,7},{7,6},{8,9},{9,8},{10,11... | collective-permute-start | bytes 153608 | tf_op jit(solution)/shard_map/ppermute | solution.py:50
  31.6 4.5 %collective-permute-start.10 = (f32[100,128]{1,0:T(8,128)S(1)}, f32[100,128]{1,0:T(8,128)S(1)}, u32[]{:S(2)}, u32[]{:S(2)}) collective-permute-start(f32[100,128]{1,0:T(8,128)S(1)} %get-tuple-element.53.refs_7_), channel_id=1, source_target_pairs={{0,8},{8,0},{16,24},{24,16},{32,40},{40,32},{48,56},{56,48},{64,72... | collective-permute-start | bytes 153608 | tf_op jit(solution)/shard_map/ppermute | solution.py:50
  31.6 4.5 %collective-permute-start.11 = (f32[100,128]{1,0:T(8,128)S(1)}, f32[100,128]{1,0:T(8,128)S(1)}, u32[]{:S(2)}, u32[]{:S(2)}) collective-permute-start(f32[100,128]{1,0:T(8,128)S(1)} %get-tuple-element.54.refs_8_), channel_id=1, source_target_pairs={{0,8},{8,0},{16,24},{24,16},{32,40},{40,32},{48,56},{56,48},{64,72... | collective-permute-start | bytes 153608 | tf_op jit(solution)/shard_map/ppermute | solution.py:50
  39.0 9.2 %collective-permute-start.14 = (f32[264,128]{1,0:T(8,128)S(1)}, f32[264,128]{1,0:T(8,128)S(1)}, u32[]{:S(2)}, u32[]{:S(2)}) collective-permute-start(f32[264,128]{1,0:T(8,128)S(1)} %get-tuple-element.61.refs_0_), channel_id=1, source_target_pairs={{0,24},{8,16},{16,8},{24,0},{32,56},{40,48},{48,40},{56,32},{64,88... | collective-permute-start | bytes 405512 | tf_op jit(solution)/shard_map/ppermute | solution.py:554
  39.0 9.2 %collective-permute-start.13 = (f32[264,128]{1,0:T(8,128)S(1)}, f32[264,128]{1,0:T(8,128)S(1)}, u32[]{:S(2)}, u32[]{:S(2)}) collective-permute-start(f32[264,128]{1,0:T(8,128)S(1)} %get-tuple-element.61.refs_0_), channel_id=1, source_target_pairs={{0,16},{8,24},{16,0},{24,8},{32,48},{40,56},{48,32},{56,40},{64,80... | collective-permute-start | bytes 405512 | tf_op jit(solution)/shard_map/ppermute | solution.py:554
  39.4 8.8 %collective-permute-start.12 = (f32[264,128]{1,0:T(8,128)S(1)}, f32[264,128]{1,0:T(8,128)S(1)}, u32[]{:S(2)}, u32[]{:S(2)}) collective-permute-start(f32[264,128]{1,0:T(8,128)S(1)} %get-tuple-element.61.refs_0_), channel_id=1, source_target_pairs={{0,8},{8,0},{16,24},{24,16},{32,40},{40,32},{48,56},{56,48},{64,72... | collective-permute-start | bytes 405512 | tf_op jit(solution)/shard_map/ppermute | solution.py:554
  42.4 14.4 %all-to-all-start = ((f32[128,2,128]{2,1,0:T(2,128)}), f32[128,2,128]{2,1,0:T(2,128)S(1)}, u32[]{:S(2)}, u32[]{:S(2)}) async-start(f32[128,2,128]{2,1,0:T(2,128)} %bitcast.4), calls=%async_computation | async-start | bytes 262144 | tf_op jit(solution)/shard_map/all_to_all | solution.py:557
  47.2 11.3 %collective-permute-start.18 = (f32[200,128]{1,0:T(8,128)S(1)}, f32[200,128]{1,0:T(8,128)S(1)}, u32[]{:S(2)}, u32[]{:S(2)}) collective-permute-start(f32[200,128]{1,0:T(8,128)S(1)} %get-tuple-element.70), channel_id=1, source_target_pairs={{0,8},{8,16},{16,24},{24,32},{32,40},{40,48},{48,56},{56,64},{64,7... | collective-permute-start | bytes 307208 | tf_op jit(solution)/shard_map/ppermute | solution.py:45
  47.2 11.2 %collective-permute-start.19 = (f32[100,128]{1,0:T(8,128)S(1)}, f32[100,128]{1,0:T(8,128)S(1)}, u32[]{:S(2)}, u32[]{:S(2)}) collective-permute-start(f32[100,128]{1,0:T(8,128)S(1)} %get-tuple-element.71), channel_id=1, source_target_pairs={{0,1},{1,2},{2,3},{3,4},{4,5},{5,6},{6,7},{7,0},{8,9},{9,10},{10,1... | collective-permute-start | bytes 153608 | tf_op jit(solution)/shard_map/ppermute | solution.py:45
  48.3 10.2 %collective-permute-start.15 = (f32[32,128]{1,0:T(8,128)S(1)}, f32[32,128]{1,0:T(8,128)S(1)}, u32[]{:S(2)}, u32[]{:S(2)}) collective-permute-start(f32[32,128]{1,0:T(8,128)S(1)} %get-tuple-element.63), channel_id=1, source_target_pairs={{0,32},{8,40},{16,48},{24,56},{32,64},{40,72},{48,80},{56,88},{64,... | collective-permute-start | bytes 49160 | tf_op jit(solution)/shard_map/ppermute | solution.py:45
  50.1 8.4 %collective-permute-start.16 = (f32[32,128]{1,0:T(8,128)S(1)}, f32[32,128]{1,0:T(8,128)S(1)}, u32[]{:S(2)}, u32[]{:S(2)}) collective-permute-start(f32[32,128]{1,0:T(8,128)S(1)} %get-tuple-element.64), channel_id=1, source_target_pairs={{0,64},{8,72},{16,80},{24,88},{32,96},{40,104},{48,112},{56,120},{... | collective-permute-start | bytes 49160 | tf_op jit(solution)/shard_map/ppermute | solution.py:45
  53.3 5.2 %collective-permute-start.17 = (f32[32,128]{1,0:T(8,128)S(1)}, f32[32,128]{1,0:T(8,128)S(1)}, u32[]{:S(2)}, u32[]{:S(2)}) collective-permute-start(f32[32,128]{1,0:T(8,128)S(1)} %get-tuple-element.65), channel_id=1, source_target_pairs={{0,96},{8,104},{16,112},{24,120},{32,0},{40,8},{48,16},{56,24},{64... | collective-permute-start | bytes 49160 | tf_op jit(solution)/shard_map/ppermute | solution.py:45
  (3 other events, 3.6 us)

commit v11 on v10

--- a/solution.py
+++ b/solution.py
@@ -269,7 +269,10 @@
 
 
 def third_kernel(p_ref, v1_ref, rfx, rfy, rny, rn0, rn1, sn0, sn1, sfx, sny, sfy, sums_ref, k_ref, m_ref, w_ref,
-                 v2_ref, p2_ref, upx, upy, loads_ref, mom_ref, ux, uy, last_in, last_out):
+                 v2_ref, p2_ref, upx_out, upy_out, loads_ref, mom_ref, ux, uy, last_in, last_out):
+    upx, upy = upx_out.at[: A * LY], upy_out.at[: A * LX]
+    upx_out[A * LY :] = jnp.zeros((upx_out.shape[0] - A * LY, LZ), f32)
+    upy_out[A * LX :] = jnp.zeros((upy_out.shape[0] - A * LX, LZ), f32)
     assemble(p_ref, Parts(sn0, sn1), sfx, sny, sfy, Parts(rn0, rn1), rfx, rny, rfy, v2_ref, ux, uy)
     v1 = v1_ref[...]
     v2 = v2_ref[...]
@@ -415,15 +418,24 @@
     return plain(iterate), plain(residual)
 
 
-def coefficients_kernel(got_ref, inv_ref, rhs_hbm, v1_hbm, rhs_ref, v1_ref, coef_ref, edge_ref, sems, *, table, ny):
-    fetches = [pltpu.make_async_copy(rhs_hbm, rhs_ref, sems.at[0]), pltpu.make_async_copy(v1_hbm, v1_ref, sems.at[1])]
-    for fetch in fetches:
-        fetch.start()
+def residual_kernel(got_ref, inv_ref, rhs_hbm, v1_hbm, v2_ref, p2_ref, rx_ref, ry_ref,
+                    part_ref, res_hbm, coef_ref, edge_ref, rhs_ref, v1_ref, res_ref, in_sems, out_sems, *, table, ny):
+    fetches = []
+    for f in range(F):
+        pairs = (
+            (rhs_hbm, rhs_ref, pl.ds(f * FACE, FACE)),
+            (v1_hbm, v1_ref, pl.ds(f * CELLS * B, CELLS * B)),
+            (v1_hbm, v1_ref, pl.ds(TAIL + f * CELLS, CELLS)),
+        )
+        fetches.append([pltpu.make_async_copy(src.at[r], dst.at[r], in_sems.at[3 * f + i]) for i, (src, dst, r) in enumerate(pairs)])
+        for fetch in fetches[f]:
+            fetch.start()
     x, d = conjugate_gradient(*moments(got_ref[...]))
     inv = inv_ref[0:1, 0:1]
-    for k, t in enumerate([t * inv for t in x] + d):
+    x = [t * inv for t in x]
+    for k, t in enumerate(d):
         coef_ref[k : k + 1] = jnp.broadcast_to(t, (1, LZ))
-    coef_ref[7:8] = jnp.zeros((1, LZ), f32)
+    coef_ref[4:8] = jnp.zeros((4, LZ), f32)
     below = lax.rem(lax.axis_index("gy") + ny - 1, ny)
     me = lax.axis_index("gx")
     nx = len(table)
@@ -432,14 +444,38 @@
         slab = lax.rem(me + nx - offset, nx)
         edge = edge + got_ref[pl.ds(2 * (slab * ny + below) + 1, 1), :] * weight
     edge_ref[...] = jnp.concatenate([edge, jnp.zeros((LY - 1, LZ), f32)], 0)
-    for fetch in fetches:
-        fetch.wait()
-
-
-def last_kernel(prolong_ref, coef_ref, edge_ref, c0, c1, c2, c3, rhs_ref, v1_ref, v2_ref, p2_ref, rx_ref, ry_ref,
-                sol_hbm, res_hbm, coarse_ref, sol_ref, res_ref, out_sems):
-    coef = [jnp.broadcast_to(coef_ref[k : k + 1], (LY, LZ)) for k in range(7)]
-    x, d = coef[:3], coef[3:]
+    x = [jnp.broadcast_to(t, (LY, LZ)) for t in x]
+    d = [jnp.broadcast_to(t, (LY, LZ)) for t in d]
+    stores = []
+    for f in range(F):
+        for fetch in fetches[f]:
+            fetch.wait()
+        for a in range(A):
+            for cell in range(LX):
+                at = (f * A + a) * CELLS + cell * LY
+                rows = slice(at, at + LY)
+                v0 = rhs_ref[rows, :]
+                v1, v2, img = (tile_of(ref, F * CELLS, f, a, cell) for ref in (v1_ref, v2_ref, p2_ref))
+                if f == 0 and cell == 0:
+                    img = img + tile_of(rx_ref, LY, 0, a, 0)
+                part_ref[rows, :] = x[0] * v0 + x[1] * v1 + x[2] * v2
+                res_ref[rows, :] = d[0] * v0 + d[1] * v1 + d[2] * v2 + d[3] * img
+        if f == 1:
+            add = d[3][0:1] * ry_ref[: A * LX]
+            for cell in range(LX):
+                first = pl.ds(FACE + cell * LY, B, stride=CELLS)
+                res_ref[first, :] = res_ref[first, :] + add[cell * B : (cell + 1) * B]
+            first = pl.ds(FACE + B * CELLS, LX, stride=LY)
+            res_ref[first, :] = res_ref[first, :] + add[B * LX :]
+        rows = pl.ds(f * FACE, FACE)
+        stores.append(pltpu.make_async_copy(res_ref.at[rows], res_hbm.at[rows], out_sems.at[f]))
+        stores[-1].start()
+    for store in stores:
+        store.wait()
+
+
+def last_kernel(prolong_ref, coef_ref, edge_ref, c0, c1, c2, c3, part_ref, sol_hbm, coarse_ref, sol_ref, out_sems):
+    d = [jnp.broadcast_to(coef_ref[k : k + 1], (LY, LZ)) for k in range(4)]
     circ = [c0[k * 8 : k * 8 + 8] + c1[k * 8 : k * 8 + 8] + c2[k * 8 : k * 8 + 8] + c3[k * 8 : k * 8 + 8] for k in range(4)]
     coarse = d[0] * circ[0] + d[1] * circ[1] + d[2] * circ[2] + d[3] * (circ[3] + edge_ref[...])
     coarse_ref[...] = coarse
@@ -450,23 +486,10 @@
             spread = coarse * prolong_ref[f, a]
             for cell in range(LX):
                 rows = slice(at + cell * LY, at + (cell + 1) * LY)
-                v0 = rhs_ref[rows, :]
-                v1, v2, img = (tile_of(ref, F * CELLS, f, a, cell) for ref in (v1_ref, v2_ref, p2_ref))
-                if f == 0 and cell == 0:
-                    img = img + tile_of(rx_ref, LY, 0, a, 0)
-                sol_ref[rows, :] = x[0] * v0 + x[1] * v1 + x[2] * v2 + spread
-                res_ref[rows, :] = d[0] * v0 + d[1] * v1 + d[2] * v2 + d[3] * img
-        if f == 1:
-            below = d[3][0:1] * ry_ref[...]
-            for cell in range(LX):
-                first = pl.ds(FACE + cell * LY, B, stride=CELLS)
-                res_ref[first, :] = res_ref[first, :] + below[cell * B : (cell + 1) * B]
-            first = pl.ds(FACE + B * CELLS, LX, stride=LY)
-            res_ref[first, :] = res_ref[first, :] + below[B * LX :]
+                sol_ref[rows, :] = part_ref[rows, :] + spread
         rows = pl.ds(f * FACE, FACE)
-        for i, (src, dst) in enumerate(((sol_ref, sol_hbm), (res_ref, res_hbm))):
-            stores.append(pltpu.make_async_copy(src.at[rows], dst.at[rows], out_sems.at[2 * f + i]))
-            stores[-1].start()
+        stores.append(pltpu.make_async_copy(sol_ref.at[rows], sol_hbm.at[rows], out_sems.at[f]))
+        stores[-1].start()
     for store in stores:
         store.wait()
 
@@ -548,7 +571,7 @@
     peers = nx * ny * 2
     v2, p2, upx, upy, loads, mom = call(
         third_kernel, "third", [p1, v1, *r, *s, sums, k2, m2, w],
-        [struct(ROWS, LZ)] * 2 + [struct(vx, LZ), struct(vy, LZ), struct(peers + 8, LZ), struct(peers, LZ)], upper,
+        [struct(ROWS, LZ)] * 2 + [struct(peers + 8, LZ)] * 3 + [struct(peers, LZ)], upper,
     )
     table = [float(t) for t in jacobi_weights(nx)]
     group = [lax.ppermute(loads, "gx", [(i, i ^ b) for i in range(nx)]) for b in (1, 2, 3)]
@@ -558,14 +581,14 @@
     rx = shifted(upx, "gx", 1)
     ry = shifted(upy, "gy", 1)
     v0, v1_kept = (pltpu.with_memory_space_constraint(v, pltpu.HBM) for v in (rhs2, v1_kept))
-    v0, v1, coef, edge = call(
-        coefficients_kernel, "coefficients", [got, inv, (v0, ANY), (v1_kept, ANY)],
-        [struct(ROWS, LZ)] * 2 + [struct(8, LZ), struct(LY, LZ)], [pltpu.SemaphoreType.DMA((2,))], table=table, ny=ny,
-    )
-    sol, res, coarse = call(
-        last_kernel, "last", [(prolong, SM), coef, edge, *coarse, v0, v1, v2, p2, rx, ry],
-        [pltpu.HBM((ROWS, LZ), f32)] * 2 + [struct(LY, LZ)],
-        [pltpu.VMEM((ROWS, LZ), f32)] * 2 + [pltpu.SemaphoreType.DMA((6,))],
+    part, res, coef, edge = call(
+        residual_kernel, "residual", [got, inv, (v0, ANY), (v1_kept, ANY), v2, p2, rx, ry],
+        [struct(ROWS, LZ), pltpu.HBM((ROWS, LZ), f32), struct(8, LZ), struct(LY, LZ)],
+        [pltpu.VMEM((ROWS, LZ), f32)] * 3 + [pltpu.SemaphoreType.DMA((9,)), pltpu.SemaphoreType.DMA((F,))], table=table, ny=ny,
+    )
+    sol, coarse = call(
+        last_kernel, "last", [(prolong, SM), coef, edge, *coarse, part],
+        [pltpu.HBM((ROWS, LZ), f32), struct(LY, LZ)], [pltpu.VMEM((ROWS, LZ), f32), pltpu.SemaphoreType.DMA((F,))],
     )
     return sol.reshape(rhs.shape), res.reshape(rhs.shape), coarse[None]
 

time: 62.5 us -> 68 us (1.088)
  starting transfers between devices: 35.3 us -> 38.5 us
  Pallas kernels: 14.6 us -> 15.8 us
  waiting for transfers between devices: 8.79 us -> 9.82 us
    all_to_all x1, starting transfers between devices: 4.79 us -> 9.43 us  [shards(): lax.all_to_all(mom.reshape(-1, 2, LZ), ('gx', 'gy'), 0, 0, tiled=True)]
    ppermute x7, starting transfers between devices: 16.4 us -> 14.9 us  [shifted(): return lax.ppermute(value, axis, [(i, (i + by) % n) for i in range(n)])]
    pallas_call x9, Pallas kernels: 14.6 us -> 15.8 us  [call(): pl.pallas_call(bound, out_shape=outs, in_specs=specs, out_specs=[ANY if i...]
    all_to_all x1, waiting for transfers between devices: 2.24 us -> 3.26 us  [shards(): lax.all_to_all(mom.reshape(-1, 2, LZ), ('gx', 'gy'), 0, 0, tiled=True)]
  transfers between devices with their start and end apart: 21 -> 21, of which waited for: 4 -> 4; matrix products, arithmetic and copies ran while one was open for 0% -> 0% of each run, Pallas kernels for 6% -> 9%
where the time goes in v11:
time: 68 us; the launch traced here: 67 us
  starting transfers between devices  38.5 us (57%)
  Pallas kernels  15.8 us (23%)
  waiting for transfers between devices  9.82 us (14%)
  local copies, waits for them, and re-layouts  1.86 us (3%)
  between operations  1 us (1%)
    pallas_call x9, Pallas kernels, call(): pl.pallas_call(bound, out_shape=outs, in_specs=specs, out_specs=[ANY if i...  15.8 us
    ppermute x7, starting transfers between devices, shifted(): return lax.ppermute(value, axis, [(i, (i + by) % n) for i in range(n)])  14.9 us
    ppermute x4, starting transfers between devices, far_swap(): return lax.ppermute(value, axis, pairs)  9.72 us
    all_to_all x1, starting transfers between devices, shards(): lax.all_to_all(mom.reshape(-1, 2, LZ), ('gx', 'gy'), 0, 0, tiled=True)  9.43 us
    ppermute x4, waiting for transfers between devices, far_swap(): return lax.ppermute(value, axis, pairs)  5.58 us
    ppermute x3, starting transfers between devices, shards(): lax.ppermute(loads, 'gx', [(i, i ^ b) for i in range(nx)])  3.37 us
    all_to_all x1, waiting for transfers between devices, shards(): lax.all_to_all(mom.reshape(-1, 2, LZ), ('gx', 'gy'), 0, 0, tiled=True)  3.26 us
    unnamed x12, local copies, waits for them, and re-layouts  1.84 us
  transfers between devices with their start and end apart: 21, of which 4 were waited for; matrix products, arithmetic and copies ran while one was open for 0% of the time, Pallas kernels for 9%

profile of v11, /device:TPU:0, one launch (start us, length us, event | category | flops | bytes accessed | tf_op | source)
XLA Modules:
  0.0 67.0 jit_solution(2977448973003759584)
XLA Ops:
  0.7 1.0 %edges.1 = (f32[25,8,128]{2,1,0:T(8,128)S(1)}, f32[25,4,128]{2,1,0:T(4,128)S(1)}) custom-call(f32[3,25,4,8,128]{4,3,2,1,0:T(8,128)} %refs_0_.3), custom_call_target="tpu_custom_call" | custom-call | tf_op jit(solution)/shard_map/edges/pallas_call | solution.py:530
  1.7 6.1 %collective-permute-start = (f32[200,128]{1,0:T(8,128)S(1)}, f32[200,128]{1,0:T(8,128)S(1)}, u32[]{:S(2)}, u32[]{:S(2)}) collective-permute-start(f32[200,128]{1,0:T(8,128)S(1)} %bitcast.19), channel_id=1, source_target_pairs={{0,120},{8,0},{16,8},{24,16},{32,24},{40,32},{48,40},{56,48},{64,5... | collective-permute-start | bytes 307208 | tf_op jit(solution)/shard_map/ppermute | solution.py:45
  7.8 3.1 %collective-permute-start.1 = (f32[100,128]{1,0:T(8,128)S(1)}, f32[100,128]{1,0:T(8,128)S(1)}, u32[]{:S(2)}, u32[]{:S(2)}) collective-permute-start(f32[100,128]{1,0:T(8,128)S(1)} %reshape.35), channel_id=1, source_target_pairs={{0,7},{1,0},{2,1},{3,2},{4,3},{5,4},{6,5},{7,6},{8,15},{9,8},{10,9... | collective-permute-start | bytes 153608 | tf_op jit(solution)/shard_map/ppermute | solution.py:45
  10.9 0.9 %copy-done.1 = f32[150,150]{1,0:T(8,128)S(1)} copy-done((f32[150,150]{1,0:T(8,128)S(1)}, f32[150,150]{1,0:T(8,128)}, u32[]{:S(2)}) %copy-start.1) | copy-done | bytes 90024
  12.7 1.2 %weights.1 = (bf16[304,480]{1,0:T(8,128)(2,1)S(1)}, f32[8,128]{1,0:T(8,128)S(1)}) custom-call(f32[150,150]{1,0:T(8,128)S(1)} %copy-done.1, f32[150,150]{1,0:T(8,128)S(1)} %copy-done.2), custom_call_target="tpu_custom_call" | custom-call | tf_op jit(solution)/shard_map/weights/pallas_call | solution.py:530
  13.9 2.0 %first.1 = (f32[2400,128]{1,0:T(8,128)S(1)}, f32[100,128]{1,0:T(8,128)S(1)}, f32[100,128]{1,0:T(8,128)S(1)}, f32[200,128]{1,0:T(8,128)S(1)}, f32[100,128]{1,0:T(8,128)S(1)}, /*index=5*/f32[100,128]{1,0:T(8,128)S(1)}) custom-call(f32[2400,128]{1,0:T(8,128)S(1)} %bitcast.10, f32[200,128]{1,0:T(8,128)S(1)} %collective-permute-done.refs_1_, ...), custom_call_target="tpu_custom_call" | custom-call | tf_op jit(solution)/shard_map/first/pallas_call | solution.py:530
  16.0 1.6 %collective-permute-start.2 = (f32[200,128]{1,0:T(8,128)S(1)}, f32[200,128]{1,0:T(8,128)S(1)}, u32[]{:S(2)}, u32[]{:S(2)}) collective-permute-start(f32[200,128]{1,0:T(8,128)S(1)} %get-tuple-element.42.refs_8_), channel_id=1, source_target_pairs={{0,120},{8,16},{16,8},{24,32},{32,24},{40,48},{48,40},{56,64},{64,... | collective-permute-start | bytes 307208 | tf_op jit(solution)/shard_map/ppermute | solution.py:56
  17.6 3.0 %collective-permute-start.3 = (f32[100,128]{1,0:T(8,128)S(1)}, f32[100,128]{1,0:T(8,128)S(1)}, u32[]{:S(2)}, u32[]{:S(2)}) collective-permute-start(f32[100,128]{1,0:T(8,128)S(1)} %get-tuple-element.43.refs_10_), channel_id=1, source_target_pairs={{0,7},{1,2},{2,1},{3,4},{4,3},{5,6},{6,5},{7,0},{8,15},{9,10},{10,... | collective-permute-start | bytes 153608 | tf_op jit(solution)/shard_map/ppermute | solution.py:56
  21.2 2.7 %collective-permute-done.3.refs_2_ = f32[100,128]{1,0:T(8,128)S(1)} collective-permute-done((f32[100,128]{1,0:T(8,128)S(1)}, f32[100,128]{1,0:T(8,128)S(1)}, u32[]{:S(2)}, u32[]{:S(2)}) %collective-permute-start.3) | collective-permute-done | bytes 51232 | tf_op jit(solution)/shard_map/ppermute | solution.py:56
  23.9 0.9 %collective-permute-done.4.refs_3_ = f32[100,128]{1,0:T(8,128)S(1)} collective-permute-done((f32[100,128]{1,0:T(8,128)S(1)}, f32[100,128]{1,0:T(8,128)S(1)}, u32[]{:S(2)}, u32[]{:S(2)}) %collective-permute-start.4) | collective-permute-done | bytes 51232 | tf_op jit(solution)/shard_map/ppermute | solution.py:50
  24.8 1.8 %second.1 = (f32[2400,128]{1,0:T(8,128)S(1)}, f32[2400,128]{1,0:T(8,128)S(1)}, f32[100,128]{1,0:T(8,128)S(1)}, f32[100,128]{1,0:T(8,128)S(1)}, f32[200,128]{1,0:...) custom-call(f32[2400,128]{1,0:T(8,128)S(1)} %get-tuple-element.41.refs_0_, ...), custom_call_target="tpu_custom_call" | custom-call | tf_op jit(solution)/shard_map/second/pallas_call | solution.py:530
  26.6 3.3 %collective-permute-start.7 = (f32[200,128]{1,0:T(8,128)S(1)}, f32[200,128]{1,0:T(8,128)S(1)}, u32[]{:S(2)}, u32[]{:S(2)}) collective-permute-start(f32[200,128]{1,0:T(8,128)S(1)} %get-tuple-element.49.refs_9_), channel_id=1, source_target_pairs={{0,120},{8,16},{16,8},{24,32},{32,24},{40,48},{48,40},{56,64},{64,... | collective-permute-start | bytes 307208 | tf_op jit(solution)/shard_map/ppermute | solution.py:56
  29.8 1.8 %collective-permute-start.8 = (f32[100,128]{1,0:T(8,128)S(1)}, f32[100,128]{1,0:T(8,128)S(1)}, u32[]{:S(2)}, u32[]{:S(2)}) collective-permute-start(f32[100,128]{1,0:T(8,128)S(1)} %get-tuple-element.50.refs_11_), channel_id=1, source_target_pairs={{0,7},{1,2},{2,1},{3,4},{4,3},{5,6},{6,5},{7,0},{8,15},{9,10},{10,... | collective-permute-start | bytes 153608 | tf_op jit(solution)/shard_map/ppermute | solution.py:56
  32.1 1.0 %products.1 = (f32[40,128]{1,0:T(8,128)S(1)}, f32[2400,128]{1,0:T(8,128)}) custom-call(f32[2400,128]{1,0:T(8,128)S(1)} %bitcast.11, f32[2400,128]{1,0:T(8,128)S(1)} %get-tuple-element.48.refs_1_), custom_call_target="tpu_custom_call" | custom-call | tf_op jit(solution)/shard_map/products/pallas_call | solution.py:530
  33.2 2.9 %collective-permute-done.8.refs_3_ = f32[100,128]{1,0:T(8,128)S(1)} collective-permute-done((f32[100,128]{1,0:T(8,128)S(1)}, f32[100,128]{1,0:T(8,128)S(1)}, u32[]{:S(2)}, u32[]{:S(2)}) %collective-permute-start.8) | collective-permute-done | bytes 51232 | tf_op jit(solution)/shard_map/ppermute | solution.py:56
  36.1 2.9 %third.1 = (f32[2400,128]{1,0:T(8,128)S(1)}, f32[2400,128]{1,0:T(8,128)S(1)}, f32[264,128]{1,0:T(8,128)}, f32[264,128]{1,0:T(8,128)S(1)}, f32[264,128]{1,0:T(8,128)S(1)}, /*index=5*/f32[256,128]{1,0:T(8,128)}) custom-call(f32[2400,128]{1,0:T(8,128)S(1)} %get-tuple-element.47.refs_0_, f32[2400,128]{1,0:T(8,128)S(1)} %get-tuple-element.48.refs_1_, ...), custom_call_target="tpu_custom_call" | custom-call | tf_op jit(solution)/shard_map/third/pallas_call | solution.py:530
  39.4 3.0 %collective-permute-start.14 = (f32[264,128]{1,0:T(8,128)S(1)}, f32[264,128]{1,0:T(8,128)S(1)}, u32[]{:S(2)}, u32[]{:S(2)}) collective-permute-start(f32[264,128]{1,0:T(8,128)S(1)} %get-tuple-element.64.refs_0_), channel_id=1, source_target_pairs={{0,8},{8,0},{16,24},{24,16},{32,40},{40,32},{48,56},{56,48},{64,72... | collective-permute-start | bytes 405512 | tf_op jit(solution)/shard_map/ppermute | solution.py:577
  42.6 9.4 %all-to-all-start = ((f32[128,2,128]{2,1,0:T(2,128)}), f32[128,2,128]{2,1,0:T(2,128)S(1)}, u32[]{:S(2)}, u32[]{:S(2)}) async-start(f32[128,2,128]{2,1,0:T(2,128)} %bitcast.4), calls=%async_computation | async-start | bytes 262144 | tf_op jit(solution)/shard_map/all_to_all | solution.py:580
  52.7 1.1 %collective-permute-start.17 = (f32[32,128]{1,0:T(8,128)}, f32[32,128]{1,0:T(8,128)S(1)}, u32[]{:S(2)}, u32[]{:S(2)}) collective-permute-start(f32[32,128]{1,0:T(8,128)} %get-tuple-element.66), channel_id=1, source_target_pairs={{0,32},{8,40},{16,48},{24,56},{32,64},{40,72},{48,80},{56,88},{64,... | collective-permute-start | bytes 49160 | tf_op jit(solution)/shard_map/ppermute | solution.py:45
  53.8 3.2 %collective-permute-start.18 = (f32[32,128]{1,0:T(8,128)}, f32[32,128]{1,0:T(8,128)S(1)}, u32[]{:S(2)}, u32[]{:S(2)}) collective-permute-start(f32[32,128]{1,0:T(8,128)} %get-tuple-element.67), channel_id=1, source_target_pairs={{0,64},{8,72},{16,80},{24,88},{32,96},{40,104},{48,112},{56,120},{... | collective-permute-start | bytes 49160 | tf_op jit(solution)/shard_map/ppermute | solution.py:45
  57.0 1.2 %collective-permute-start.19 = (f32[32,128]{1,0:T(8,128)}, f32[32,128]{1,0:T(8,128)S(1)}, u32[]{:S(2)}, u32[]{:S(2)}) collective-permute-start(f32[32,128]{1,0:T(8,128)} %get-tuple-element.68), channel_id=1, source_target_pairs={{0,96},{8,104},{16,112},{24,120},{32,0},{40,8},{48,16},{56,24},{64... | collective-permute-start | bytes 49160 | tf_op jit(solution)/shard_map/ppermute | solution.py:45
  58.2 3.3 %all-to-all-done = f32[128,2,128]{2,1,0:T(2,128)S(1)} async-done(((f32[128,2,128]{2,1,0:T(2,128)}), f32[128,2,128]{2,1,0:T(2,128)S(1)}, u32[]{:S(2)}, u32[]{:S(2)}) %all-to-all-start) | async-done | bytes 131104 | tf_op jit(solution)/shard_map/all_to_all | solution.py:580
  61.5 3.0 %residual.1 = (f32[2400,128]{1,0:T(8,128)S(1)}, f32[2400,128]{1,0:T(8,128)}, f32[8,128]{1,0:T(8,128)S(1)}, f32[8,128]{1,0:T(8,128)S(1)}) custom-call(f32[256,128]{1,0:T(8,128)S(1)} %bitcast.12, f32[8,128]{1,0:T(8,128)S(1)} %get-tuple-element.56.refs_1_, f32[2400,128]{1,0:T(8,128)} %bitcast.9, f32[2400,128]{1,0:T(8,128)} %get-tuple-element.57.refs_3_, ...), custom_call_target="tpu_custom_call" | custom-call | tf_op jit(solution)/shard_map/residual/pallas_call | solution.py:530
  64.5 2.2 %last.1 = (f32[2400,128]{1,0:T(8,128)}, f32[8,128]{1,0:T(8,128)}) custom-call(f32[3,25]{1,0:T(4,128)S(1)} %copy-done.5, f32[8,128]{1,0:T(8,128)S(1)} %get-tuple-element.62.refs_1_, f32[8,128]{1,0:T(8,128)S(1)} %get-tuple-element.63.refs_2_, f32[32,128]{1,0:T(8,128)S(1)} %get-tuple-element.65.refs_3_, f32[32,128]{1,0:T(8,128)S(1)} %collective-permute-done.17.refs_4_, ...), custom_call_target="tpu_custom_call" | custom-call | tf_op jit(solution)/shard_map/last/pallas_call | solution.py:530
  (40 shorter events, 3.3 us)
Async XLA Ops:
  0.6 13.3 %copy-start = (f32[3,25,4,8,128]{4,3,2,1,0:T(8,128)S(1)}, f32[3,25,4,8,128]{4,3,2,1,0:T(8,128)}, u32[]{:S(2)}) copy-start(f32[3,25,4,8,128]{4,3,2,1,0:T(8,128)} %refs_0_.3) | copy-start | bytes 3686404
  0.6 13.3 %copy-start.4 = (f32[4,8,128]{2,1,0:T(8,128)S(1)}, f32[4,8,128]{2,1,0:T(8,128)}, u32[]{:S(2)}) copy-start(f32[4,8,128]{2,1,0:T(8,128)} %param.8) | copy-start | bytes 49156
  0.7 13.3 %copy-start.3 = (f32[4,8,128]{2,1,0:T(8,128)S(1)}, f32[4,8,128]{2,1,0:T(8,128)}, u32[]{:S(2)}) copy-start(f32[4,8,128]{2,1,0:T(8,128)} %param.7) | copy-start | bytes 49156
  1.7 12.2 %collective-permute-start = (f32[200,128]{1,0:T(8,128)S(1)}, f32[200,128]{1,0:T(8,128)S(1)}, u32[]{:S(2)}, u32[]{:S(2)}) collective-permute-start(f32[200,128]{1,0:T(8,128)S(1)} %bitcast.19), channel_id=1, source_target_pairs={{0,120},{8,0},{16,8},{24,16},{32,24},{40,32},{48,40},{56,48},{64,5... | collective-permute-start | bytes 307208 | tf_op jit(solution)/shard_map/ppermute | solution.py:45
  7.8 6.1 %collective-permute-start.1 = (f32[100,128]{1,0:T(8,128)S(1)}, f32[100,128]{1,0:T(8,128)S(1)}, u32[]{:S(2)}, u32[]{:S(2)}) collective-permute-start(f32[100,128]{1,0:T(8,128)S(1)} %reshape.35), channel_id=1, source_target_pairs={{0,7},{1,0},{2,1},{3,2},{4,3},{5,4},{6,5},{7,6},{8,15},{9,8},{10,9... | collective-permute-start | bytes 153608 | tf_op jit(solution)/shard_map/ppermute | solution.py:45
  16.0 8.8 %collective-permute-start.2 = (f32[200,128]{1,0:T(8,128)S(1)}, f32[200,128]{1,0:T(8,128)S(1)}, u32[]{:S(2)}, u32[]{:S(2)}) collective-permute-start(f32[200,128]{1,0:T(8,128)S(1)} %get-tuple-element.42.refs_8_), channel_id=1, source_target_pairs={{0,120},{8,16},{16,8},{24,32},{32,24},{40,48},{48,40},{56,64},{64,... | collective-permute-start | bytes 307208 | tf_op jit(solution)/shard_map/ppermute | solution.py:56
  17.6 6.2 %collective-permute-start.3 = (f32[100,128]{1,0:T(8,128)S(1)}, f32[100,128]{1,0:T(8,128)S(1)}, u32[]{:S(2)}, u32[]{:S(2)}) collective-permute-start(f32[100,128]{1,0:T(8,128)S(1)} %get-tuple-element.43.refs_10_), channel_id=1, source_target_pairs={{0,7},{1,2},{2,1},{3,4},{4,3},{5,6},{6,5},{7,0},{8,15},{9,10},{10,... | collective-permute-start | bytes 153608 | tf_op jit(solution)/shard_map/ppermute | solution.py:56
  20.6 4.1 %collective-permute-start.4 = (f32[100,128]{1,0:T(8,128)S(1)}, f32[100,128]{1,0:T(8,128)S(1)}, u32[]{:S(2)}, u32[]{:S(2)}) collective-permute-start(f32[100,128]{1,0:T(8,128)S(1)} %get-tuple-element.44.refs_9_), channel_id=1, source_target_pairs={{0,1},{1,0},{2,3},{3,2},{4,5},{5,4},{6,7},{7,6},{8,9},{9,8},{10,11... | collective-permute-start | bytes 153608 | tf_op jit(solution)/shard_map/ppermute | solution.py:50
  20.6 4.1 %collective-permute-start.5 = (f32[100,128]{1,0:T(8,128)S(1)}, f32[100,128]{1,0:T(8,128)S(1)}, u32[]{:S(2)}, u32[]{:S(2)}) collective-permute-start(f32[100,128]{1,0:T(8,128)S(1)} %get-tuple-element.45.refs_6_), channel_id=1, source_target_pairs={{0,8},{8,0},{16,24},{24,16},{32,40},{40,32},{48,56},{56,48},{64,72... | collective-permute-start | bytes 153608 | tf_op jit(solution)/shard_map/ppermute | solution.py:50
  20.7 4.1 %collective-permute-start.6 = (f32[100,128]{1,0:T(8,128)S(1)}, f32[100,128]{1,0:T(8,128)S(1)}, u32[]{:S(2)}, u32[]{:S(2)}) collective-permute-start(f32[100,128]{1,0:T(8,128)S(1)} %get-tuple-element.46.refs_7_), channel_id=1, source_target_pairs={{0,8},{8,0},{16,24},{24,16},{32,40},{40,32},{48,56},{56,48},{64,72... | collective-permute-start | bytes 153608 | tf_op jit(solution)/shard_map/ppermute | solution.py:50
  26.6 9.5 %collective-permute-start.7 = (f32[200,128]{1,0:T(8,128)S(1)}, f32[200,128]{1,0:T(8,128)S(1)}, u32[]{:S(2)}, u32[]{:S(2)}) collective-permute-start(f32[200,128]{1,0:T(8,128)S(1)} %get-tuple-element.49.refs_9_), channel_id=1, source_target_pairs={{0,120},{8,16},{16,8},{24,32},{32,24},{40,48},{48,40},{56,64},{64,... | collective-permute-start | bytes 307208 | tf_op jit(solution)/shard_map/ppermute | solution.py:56
  29.8 6.2 %collective-permute-start.8 = (f32[100,128]{1,0:T(8,128)S(1)}, f32[100,128]{1,0:T(8,128)S(1)}, u32[]{:S(2)}, u32[]{:S(2)}) collective-permute-start(f32[100,128]{1,0:T(8,128)S(1)} %get-tuple-element.50.refs_11_), channel_id=1, source_target_pairs={{0,7},{1,2},{2,1},{3,4},{4,3},{5,6},{6,5},{7,0},{8,15},{9,10},{10,... | collective-permute-start | bytes 153608 | tf_op jit(solution)/shard_map/ppermute | solution.py:56
  31.6 4.5 %collective-permute-start.9 = (f32[100,128]{1,0:T(8,128)S(1)}, f32[100,128]{1,0:T(8,128)S(1)}, u32[]{:S(2)}, u32[]{:S(2)}) collective-permute-start(f32[100,128]{1,0:T(8,128)S(1)} %get-tuple-element.51.refs_10_), channel_id=1, source_target_pairs={{0,1},{1,0},{2,3},{3,2},{4,5},{5,4},{6,7},{7,6},{8,9},{9,8},{10,11... | collective-permute-start | bytes 153608 | tf_op jit(solution)/shard_map/ppermute | solution.py:50
  31.6 4.5 %collective-permute-start.10 = (f32[100,128]{1,0:T(8,128)S(1)}, f32[100,128]{1,0:T(8,128)S(1)}, u32[]{:S(2)}, u32[]{:S(2)}) collective-permute-start(f32[100,128]{1,0:T(8,128)S(1)} %get-tuple-element.52.refs_7_), channel_id=1, source_target_pairs={{0,8},{8,0},{16,24},{24,16},{32,40},{40,32},{48,56},{56,48},{64,72... | collective-permute-start | bytes 153608 | tf_op jit(solution)/shard_map/ppermute | solution.py:50
  31.6 4.5 %collective-permute-start.11 = (f32[100,128]{1,0:T(8,128)S(1)}, f32[100,128]{1,0:T(8,128)S(1)}, u32[]{:S(2)}, u32[]{:S(2)}) collective-permute-start(f32[100,128]{1,0:T(8,128)S(1)} %get-tuple-element.53.refs_8_), channel_id=1, source_target_pairs={{0,8},{8,0},{16,24},{24,16},{32,40},{40,32},{48,56},{56,48},{64,72... | collective-permute-start | bytes 153608 | tf_op jit(solution)/shard_map/ppermute | solution.py:50
  39.0 13.1 %collective-permute-start.16 = (f32[264,128]{1,0:T(8,128)S(1)}, f32[264,128]{1,0:T(8,128)S(1)}, u32[]{:S(2)}, u32[]{:S(2)}) collective-permute-start(f32[264,128]{1,0:T(8,128)S(1)} %get-tuple-element.64.refs_0_), channel_id=1, source_target_pairs={{0,24},{8,16},{16,8},{24,0},{32,56},{40,48},{48,40},{56,32},{64,88... | collective-permute-start | bytes 405512 | tf_op jit(solution)/shard_map/ppermute | solution.py:577
  39.0 13.1 %collective-permute-start.15 = (f32[264,128]{1,0:T(8,128)S(1)}, f32[264,128]{1,0:T(8,128)S(1)}, u32[]{:S(2)}, u32[]{:S(2)}) collective-permute-start(f32[264,128]{1,0:T(8,128)S(1)} %get-tuple-element.64.refs_0_), channel_id=1, source_target_pairs={{0,16},{8,24},{16,0},{24,8},{32,48},{40,56},{48,32},{56,40},{64,80... | collective-permute-start | bytes 405512 | tf_op jit(solution)/shard_map/ppermute | solution.py:577
  39.4 12.7 %collective-permute-start.14 = (f32[264,128]{1,0:T(8,128)S(1)}, f32[264,128]{1,0:T(8,128)S(1)}, u32[]{:S(2)}, u32[]{:S(2)}) collective-permute-start(f32[264,128]{1,0:T(8,128)S(1)} %get-tuple-element.64.refs_0_), channel_id=1, source_target_pairs={{0,8},{8,0},{16,24},{24,16},{32,40},{40,32},{48,56},{56,48},{64,72... | collective-permute-start | bytes 405512 | tf_op jit(solution)/shard_map/ppermute | solution.py:577
  42.4 19.1 %collective-permute-start.12 = (f32[264,128]{1,0:T(8,128)}, f32[264,128]{1,0:T(8,128)S(1)}, u32[]{:S(2)}, u32[]{:S(2)}) collective-permute-start(f32[264,128]{1,0:T(8,128)} %get-tuple-element.60), channel_id=1, source_target_pairs={{0,8},{8,16},{16,24},{24,32},{32,40},{40,48},{48,56},{56,64},{64,7... | collective-permute-start | bytes 405512 | tf_op jit(solution)/shard_map/ppermute | solution.py:45
  42.4 19.1 %collective-permute-start.13 = (f32[264,128]{1,0:T(8,128)S(1)}, f32[264,128]{1,0:T(8,128)S(1)}, u32[]{:S(2)}, u32[]{:S(2)}) collective-permute-start(f32[264,128]{1,0:T(8,128)S(1)} %get-tuple-element.61), channel_id=1, source_target_pairs={{0,1},{1,2},{2,3},{3,4},{4,5},{5,6},{6,7},{7,0},{8,9},{9,10},{10,1... | collective-permute-start | bytes 405512 | tf_op jit(solution)/shard_map/ppermute | solution.py:45
  42.6 18.9 %all-to-all-start = ((f32[128,2,128]{2,1,0:T(2,128)}), f32[128,2,128]{2,1,0:T(2,128)S(1)}, u32[]{:S(2)}, u32[]{:S(2)}) async-start(f32[128,2,128]{2,1,0:T(2,128)} %bitcast.4), calls=%async_computation | async-start | bytes 262144 | tf_op jit(solution)/shard_map/all_to_all | solution.py:580
  52.7 11.8 %collective-permute-start.17 = (f32[32,128]{1,0:T(8,128)}, f32[32,128]{1,0:T(8,128)S(1)}, u32[]{:S(2)}, u32[]{:S(2)}) collective-permute-start(f32[32,128]{1,0:T(8,128)} %get-tuple-element.66), channel_id=1, source_target_pairs={{0,32},{8,40},{16,48},{24,56},{32,64},{40,72},{48,80},{56,88},{64,... | collective-permute-start | bytes 49160 | tf_op jit(solution)/shard_map/ppermute | solution.py:45
  53.8 10.7 %collective-permute-start.18 = (f32[32,128]{1,0:T(8,128)}, f32[32,128]{1,0:T(8,128)S(1)}, u32[]{:S(2)}, u32[]{:S(2)}) collective-permute-start(f32[32,128]{1,0:T(8,128)} %get-tuple-element.67), channel_id=1, source_target_pairs={{0,64},{8,72},{16,80},{24,88},{32,96},{40,104},{48,112},{56,120},{... | collective-permute-start | bytes 49160 | tf_op jit(solution)/shard_map/ppermute | solution.py:45
  57.0 7.5 %collective-permute-start.19 = (f32[32,128]{1,0:T(8,128)}, f32[32,128]{1,0:T(8,128)S(1)}, u32[]{:S(2)}, u32[]{:S(2)}) collective-permute-start(f32[32,128]{1,0:T(8,128)} %get-tuple-element.68), channel_id=1, source_target_pairs={{0,96},{8,104},{16,112},{24,120},{32,0},{40,8},{48,16},{56,24},{64... | collective-permute-start | bytes 49160 | tf_op jit(solution)/shard_map/ppermute | solution.py:45
  (3 other events, 4.9 us)

commit v12 on v10

--- a/solution.py
+++ b/solution.py
@@ -16,6 +16,7 @@
 CELLS = LX * LY
 FACE = A * CELLS
 ROWS = F * FACE
+LOADS = 40
 TAIL = F * CELLS * B
 f32, bf16 = jnp.float32, jnp.bfloat16
 VM = pl.BlockSpec(memory_space=pltpu.VMEM)
@@ -269,7 +270,8 @@
 
 
 def third_kernel(p_ref, v1_ref, rfx, rfy, rny, rn0, rn1, sn0, sn1, sfx, sny, sfy, sums_ref, k_ref, m_ref, w_ref,
-                 v2_ref, p2_ref, upx, upy, loads_ref, mom_ref, ux, uy, last_in, last_out):
+                 v2_ref, p2_ref, upy, loads_ref, mom_ref, ux, uy, last_in, last_out):
+    upx = loads_ref.at[LOADS : LOADS + A * LY]
     assemble(p_ref, Parts(sn0, sn1), sfx, sny, sfy, Parts(rn0, rn1), rfx, rny, rfy, v2_ref, ux, uy)
     v1 = v1_ref[...]
     v2 = v2_ref[...]
@@ -294,29 +296,18 @@
     pair = jnp.concatenate([packed, row(upy[...])] * 4, 0)
     for at in range(0, mom_ref.shape[0], 8):
         mom_ref[at : at + 8] = pair
-    loads_ref[40:] = jnp.zeros((loads_ref.shape[0] - 40, LZ), f32)
-
-
-def weigh_kernel(own, near, far, both, *outs, table):
+    used = LOADS + A * LY
+    loads_ref[used:] = jnp.zeros((loads_ref.shape[0] - used, LZ), f32)
+
+
+def weigh_kernel(own, below, above, second_above, *outs, table):
     nx = len(table)
-    q = lax.rem(lax.axis_index("gx"), 4)
-    low, high = lax.rem(q, 2) == 0, q < 2
-    one, two = jnp.where(low, 1, -1), jnp.where(high, 2, -2)
-    sources = ((own, 0, (0,)), (near, one, (1, -1)), (far, two, (2, -2)), (both, one + two, (3, 1, -1, -3)))
-
-    def pick(at, shift, span):
-        value = jnp.float32(table[(at - span[0]) % nx])
-        for s in span[1:]:
-            value = jnp.where(shift == s, table[(at - s) % nx], value)
-        return value
-
     for z, out in enumerate(outs):
         total = [0.0] * 4
-        for ref, shift, span in sources:
-            w = pick(4 * z, shift, span)
+        for ref, at in ((own, 0), (below, -1), (above, 1), (second_above, 2)):
             for k in range(4):
-                total[k] = total[k] + ref[k * 8 : k * 8 + 8] * w
-            total[3] = total[3] + ref[32:40] * pick(4 * z - 1, shift, span)
+                total[k] = total[k] + ref[k * 8 : k * 8 + 8] * table[(4 * z - at) % nx]
+            total[3] = total[3] + ref[32:40] * table[(4 * z - at - 1) % nx]
         for k in range(4):
             out[k * 8 : k * 8 + 8] = total[k]
 
@@ -436,8 +427,9 @@
         fetch.wait()
 
 
-def last_kernel(prolong_ref, coef_ref, edge_ref, c0, c1, c2, c3, rhs_ref, v1_ref, v2_ref, p2_ref, rx_ref, ry_ref,
+def last_kernel(prolong_ref, coef_ref, edge_ref, c0, c1, c2, c3, rhs_ref, v1_ref, v2_ref, p2_ref, below_ref, ry_ref,
                 sol_hbm, res_hbm, coarse_ref, sol_ref, res_ref, out_sems):
+    rx_ref = below_ref.at[LOADS : LOADS + A * LY]
     coef = [jnp.broadcast_to(coef_ref[k : k + 1], (LY, LZ)) for k in range(7)]
     x, d = coef[:3], coef[3:]
     circ = [c0[k * 8 : k * 8 + 8] + c1[k * 8 : k * 8 + 8] + c2[k * 8 : k * 8 + 8] + c3[k * 8 : k * 8 + 8] for k in range(4)]
@@ -546,16 +538,15 @@
         products_kernel, "products", [rhs2, v1], [struct(40, LZ), pltpu.HBM((ROWS, LZ), f32)], [pltpu.SemaphoreType.DMA],
     )
     peers = nx * ny * 2
-    v2, p2, upx, upy, loads, mom = call(
+    v2, p2, upy, loads, mom = call(
         third_kernel, "third", [p1, v1, *r, *s, sums, k2, m2, w],
-        [struct(ROWS, LZ)] * 2 + [struct(vx, LZ), struct(vy, LZ), struct(peers + 8, LZ), struct(peers, LZ)], upper,
+        [struct(ROWS, LZ)] * 2 + [struct(vy, LZ), struct(max(peers + 8, LOADS + vx), LZ), struct(peers, LZ)], upper,
     )
     table = [float(t) for t in jacobi_weights(nx)]
-    group = [lax.ppermute(loads, "gx", [(i, i ^ b) for i in range(nx)]) for b in (1, 2, 3)]
-    pieces = call(weigh_kernel, "weigh", [loads, *group], [struct(32, LZ)] * (nx // 4), table=table)
+    window = [shifted(loads, "gx", by) for by in (1, -1, -2)]
+    pieces = call(weigh_kernel, "weigh", [loads, *window], [struct(32, LZ)] * (nx // 4), table=table)
     coarse = [pieces[0]] + [shifted(p, "gx", 4 * z) for z, p in enumerate(pieces) if z]
     got = lax.all_to_all(mom.reshape(-1, 2, LZ), ("gx", "gy"), 0, 0, tiled=True).reshape(mom.shape)
-    rx = shifted(upx, "gx", 1)
     ry = shifted(upy, "gy", 1)
     v0, v1_kept = (pltpu.with_memory_space_constraint(v, pltpu.HBM) for v in (rhs2, v1_kept))
     v0, v1, coef, edge = call(
@@ -563,7 +554,7 @@
         [struct(ROWS, LZ)] * 2 + [struct(8, LZ), struct(LY, LZ)], [pltpu.SemaphoreType.DMA((2,))], table=table, ny=ny,
     )
     sol, res, coarse = call(
-        last_kernel, "last", [(prolong, SM), coef, edge, *coarse, v0, v1, v2, p2, rx, ry],
+        last_kernel, "last", [(prolong, SM), coef, edge, *coarse, v0, v1, v2, p2, window[0], ry],
         [pltpu.HBM((ROWS, LZ), f32)] * 2 + [struct(LY, LZ)],
         [pltpu.VMEM((ROWS, LZ), f32)] * 2 + [pltpu.SemaphoreType.DMA((6,))],
     )

time: 62.5 us -> 64.6 us (1.034)
  starting transfers between devices: 35.3 us -> 36.8 us
    all_to_all x1, starting transfers between devices: 4.79 us -> 8.19 us  [shards(): lax.all_to_all(mom.reshape(-1, 2, LZ), ('gx', 'gy'), 0, 0, tiled=True)]
    ppermute x3 -> x0, starting transfers between devices: 3.37 us -> none  [shards(): lax.ppermute(loads, 'gx', [(i, i ^ b) for i in range(nx)])]
    ppermute x7 -> x9, starting transfers between devices: 16.4 us -> 17.8 us  [shifted(): return lax.ppermute(value, axis, [(i, (i + by) % n) for i in range(n)])]
  transfers between devices with their start and end apart: 21 -> 20, of which waited for: 4 -> 4; matrix products, arithmetic and copies ran while one was open for 0% -> 0% of each run, Pallas kernels for 6% -> 6%
where the time goes in v12:
time: 64.6 us; the launch traced here: 63.4 us
  starting transfers between devices  36.8 us (57%)
  Pallas kernels  14.8 us (23%)
  waiting for transfers between devices  8.98 us (14%)
  local copies, waits for them, and re-layouts  1.86 us (3%)
  between operations  0.99 us (2%)
    ppermute x9, starting transfers between devices, shifted(): return lax.ppermute(value, axis, [(i, (i + by) % n) for i in range(n)])  17.8 us
    pallas_call x9, Pallas kernels, call(): pl.pallas_call(bound, out_shape=outs, in_specs=specs, out_specs=[ANY if i...  14.8 us
    ppermute x4, starting transfers between devices, far_swap(): return lax.ppermute(value, axis, pairs)  9.72 us
    all_to_all x1, starting transfers between devices, shards(): lax.all_to_all(mom.reshape(-1, 2, LZ), ('gx', 'gy'), 0, 0, tiled=True)  8.19 us
    ppermute x4, waiting for transfers between devices, far_swap(): return lax.ppermute(value, axis, pairs)  5.59 us
    all_to_all x1, waiting for transfers between devices, shards(): lax.all_to_all(mom.reshape(-1, 2, LZ), ('gx', 'gy'), 0, 0, tiled=True)  2.43 us
    unnamed x12, local copies, waits for them, and re-layouts  1.84 us
  transfers between devices with their start and end apart: 20, of which 4 were waited for; matrix products, arithmetic and copies ran while one was open for 0% of the time, Pallas kernels for 6%

profile of v12, /device:TPU:0, one launch (start us, length us, event | category | flops | bytes accessed | tf_op | source)
XLA Modules:
  0.0 63.4 jit_solution(3792124007575769700)
XLA Ops:
  0.7 1.0 %edges.1 = (f32[25,8,128]{2,1,0:T(8,128)S(1)}, f32[25,4,128]{2,1,0:T(4,128)S(1)}) custom-call(f32[3,25,4,8,128]{4,3,2,1,0:T(8,128)} %refs_0_.3), custom_call_target="tpu_custom_call" | custom-call | tf_op jit(solution)/shard_map/edges/pallas_call | solution.py:499
  1.7 6.1 %collective-permute-start = (f32[200,128]{1,0:T(8,128)S(1)}, f32[200,128]{1,0:T(8,128)S(1)}, u32[]{:S(2)}, u32[]{:S(2)}) collective-permute-start(f32[200,128]{1,0:T(8,128)S(1)} %bitcast.19), channel_id=1, source_target_pairs={{0,120},{8,0},{16,8},{24,16},{32,24},{40,32},{48,40},{56,48},{64,5... | collective-permute-start | bytes 307208 | tf_op jit(solution)/shard_map/ppermute | solution.py:46
  7.8 3.1 %collective-permute-start.1 = (f32[100,128]{1,0:T(8,128)S(1)}, f32[100,128]{1,0:T(8,128)S(1)}, u32[]{:S(2)}, u32[]{:S(2)}) collective-permute-start(f32[100,128]{1,0:T(8,128)S(1)} %reshape.35), channel_id=1, source_target_pairs={{0,7},{1,0},{2,1},{3,2},{4,3},{5,4},{6,5},{7,6},{8,15},{9,8},{10,9... | collective-permute-start | bytes 153608 | tf_op jit(solution)/shard_map/ppermute | solution.py:46
  10.9 0.9 %copy-done.1 = f32[150,150]{1,0:T(8,128)S(1)} copy-done((f32[150,150]{1,0:T(8,128)S(1)}, f32[150,150]{1,0:T(8,128)}, u32[]{:S(2)}) %copy-start.1) | copy-done | bytes 90024
  12.7 1.2 %weights.1 = (bf16[304,480]{1,0:T(8,128)(2,1)S(1)}, f32[8,128]{1,0:T(8,128)S(1)}) custom-call(f32[150,150]{1,0:T(8,128)S(1)} %copy-done.1, f32[150,150]{1,0:T(8,128)S(1)} %copy-done.2), custom_call_target="tpu_custom_call" | custom-call | tf_op jit(solution)/shard_map/weights/pallas_call | solution.py:499
  13.9 2.1 %first.1 = (f32[2400,128]{1,0:T(8,128)S(1)}, f32[100,128]{1,0:T(8,128)S(1)}, f32[100,128]{1,0:T(8,128)S(1)}, f32[200,128]{1,0:T(8,128)S(1)}, f32[100,128]{1,0:T(8,128)S(1)}, /*index=5*/f32[100,128]{1,0:T(8,128)S(1)}) custom-call(f32[2400,128]{1,0:T(8,128)S(1)} %bitcast.10, f32[200,128]{1,0:T(8,128)S(1)} %collective-permute-done.refs_1_, ...), custom_call_target="tpu_custom_call" | custom-call | tf_op jit(solution)/shard_map/first/pallas_call | solution.py:499
  16.1 1.6 %collective-permute-start.2 = (f32[200,128]{1,0:T(8,128)S(1)}, f32[200,128]{1,0:T(8,128)S(1)}, u32[]{:S(2)}, u32[]{:S(2)}) collective-permute-start(f32[200,128]{1,0:T(8,128)S(1)} %get-tuple-element.42.refs_8_), channel_id=1, source_target_pairs={{0,120},{8,16},{16,8},{24,32},{32,24},{40,48},{48,40},{56,64},{64,... | collective-permute-start | bytes 307208 | tf_op jit(solution)/shard_map/ppermute | solution.py:57
  17.7 3.0 %collective-permute-start.3 = (f32[100,128]{1,0:T(8,128)S(1)}, f32[100,128]{1,0:T(8,128)S(1)}, u32[]{:S(2)}, u32[]{:S(2)}) collective-permute-start(f32[100,128]{1,0:T(8,128)S(1)} %get-tuple-element.43.refs_10_), channel_id=1, source_target_pairs={{0,7},{1,2},{2,1},{3,4},{4,3},{5,6},{6,5},{7,0},{8,15},{9,10},{10,... | collective-permute-start | bytes 153608 | tf_op jit(solution)/shard_map/ppermute | solution.py:57
  21.3 2.7 %collective-permute-done.3.refs_2_ = f32[100,128]{1,0:T(8,128)S(1)} collective-permute-done((f32[100,128]{1,0:T(8,128)S(1)}, f32[100,128]{1,0:T(8,128)S(1)}, u32[]{:S(2)}, u32[]{:S(2)}) %collective-permute-start.3) | collective-permute-done | bytes 51232 | tf_op jit(solution)/shard_map/ppermute | solution.py:57
  24.0 0.9 %collective-permute-done.4.refs_3_ = f32[100,128]{1,0:T(8,128)S(1)} collective-permute-done((f32[100,128]{1,0:T(8,128)S(1)}, f32[100,128]{1,0:T(8,128)S(1)}, u32[]{:S(2)}, u32[]{:S(2)}) %collective-permute-start.4) | collective-permute-done | bytes 51232 | tf_op jit(solution)/shard_map/ppermute | solution.py:51
  24.9 1.8 %second.1 = (f32[2400,128]{1,0:T(8,128)S(1)}, f32[2400,128]{1,0:T(8,128)S(1)}, f32[100,128]{1,0:T(8,128)S(1)}, f32[100,128]{1,0:T(8,128)S(1)}, f32[200,128]{1,0:...) custom-call(f32[2400,128]{1,0:T(8,128)S(1)} %get-tuple-element.41.refs_0_, ...), custom_call_target="tpu_custom_call" | custom-call | tf_op jit(solution)/shard_map/second/pallas_call | solution.py:499
  26.7 3.3 %collective-permute-start.7 = (f32[200,128]{1,0:T(8,128)S(1)}, f32[200,128]{1,0:T(8,128)S(1)}, u32[]{:S(2)}, u32[]{:S(2)}) collective-permute-start(f32[200,128]{1,0:T(8,128)S(1)} %get-tuple-element.49.refs_9_), channel_id=1, source_target_pairs={{0,120},{8,16},{16,8},{24,32},{32,24},{40,48},{48,40},{56,64},{64,... | collective-permute-start | bytes 307208 | tf_op jit(solution)/shard_map/ppermute | solution.py:57
  30.0 1.8 %collective-permute-start.8 = (f32[100,128]{1,0:T(8,128)S(1)}, f32[100,128]{1,0:T(8,128)S(1)}, u32[]{:S(2)}, u32[]{:S(2)}) collective-permute-start(f32[100,128]{1,0:T(8,128)S(1)} %get-tuple-element.50.refs_11_), channel_id=1, source_target_pairs={{0,7},{1,2},{2,1},{3,4},{4,3},{5,6},{6,5},{7,0},{8,15},{9,10},{10,... | collective-permute-start | bytes 153608 | tf_op jit(solution)/shard_map/ppermute | solution.py:57
  32.3 1.0 %products.1 = (f32[40,128]{1,0:T(8,128)S(1)}, f32[2400,128]{1,0:T(8,128)}) custom-call(f32[2400,128]{1,0:T(8,128)S(1)} %bitcast.11, f32[2400,128]{1,0:T(8,128)S(1)} %get-tuple-element.48.refs_1_), custom_call_target="tpu_custom_call" | custom-call | tf_op jit(solution)/shard_map/products/pallas_call | solution.py:499
  33.3 2.9 %collective-permute-done.8.refs_3_ = f32[100,128]{1,0:T(8,128)S(1)} collective-permute-done((f32[100,128]{1,0:T(8,128)S(1)}, f32[100,128]{1,0:T(8,128)S(1)}, u32[]{:S(2)}, u32[]{:S(2)}) %collective-permute-start.8) | collective-permute-done | bytes 51232 | tf_op jit(solution)/shard_map/ppermute | solution.py:57
  36.2 3.0 %third.1 = (f32[2400,128]{1,0:T(8,128)S(1)}, f32[2400,128]{1,0:T(8,128)S(1)}, f32[100,128]{1,0:T(8,128)S(1)}, f32[264,128]{1,0:T(8,128)S(1)}, f32[256,128]{1,0:T(8,128)}) custom-call(f32[2400,128]{1,0:T(8,128)S(1)} %get-tuple-element.47.refs_0_, f32[2400,128]{1,0:T(8,128)S(1)} %get-tuple-element.48.refs_1_, f32[200,128]{1,0:T(8,128)S(1)} %collective-permute-done.7.refs_2_, ...), custom_call_target="tpu_custom_call" | custom-call | tf_op jit(solution)/shard_map/third/pallas_call | solution.py:499
  40.8 8.2 %all-to-all-start = ((f32[128,2,128]{2,1,0:T(2,128)}), f32[128,2,128]{2,1,0:T(2,128)S(1)}, u32[]{:S(2)}, u32[]{:S(2)}) async-start(f32[128,2,128]{2,1,0:T(2,128)} %bitcast.4), calls=%async_computation | async-start | bytes 262144 | tf_op jit(solution)/shard_map/all_to_all | solution.py:549
  49.0 1.0 %collective-permute-start.18 = (f32[100,128]{1,0:T(8,128)S(1)}, f32[100,128]{1,0:T(8,128)S(1)}, u32[]{:S(2)}, u32[]{:S(2)}) collective-permute-start(f32[100,128]{1,0:T(8,128)S(1)} %get-tuple-element.69), channel_id=1, source_target_pairs={{0,1},{1,2},{2,3},{3,4},{4,5},{5,6},{6,7},{7,0},{8,9},{9,10},{10,1... | collective-permute-start | bytes 153608 | tf_op jit(solution)/shard_map/ppermute | solution.py:46
  50.1 1.7 %collective-permute-start.15 = (f32[32,128]{1,0:T(8,128)S(1)}, f32[32,128]{1,0:T(8,128)S(1)}, u32[]{:S(2)}, u32[]{:S(2)}) collective-permute-start(f32[32,128]{1,0:T(8,128)S(1)} %get-tuple-element.62), channel_id=1, source_target_pairs={{0,32},{8,40},{16,48},{24,56},{32,64},{40,72},{48,80},{56,88},{64,... | collective-permute-start | bytes 49160 | tf_op jit(solution)/shard_map/ppermute | solution.py:46
  51.7 3.2 %collective-permute-start.16 = (f32[32,128]{1,0:T(8,128)S(1)}, f32[32,128]{1,0:T(8,128)S(1)}, u32[]{:S(2)}, u32[]{:S(2)}) collective-permute-start(f32[32,128]{1,0:T(8,128)S(1)} %get-tuple-element.63), channel_id=1, source_target_pairs={{0,64},{8,72},{16,80},{24,88},{32,96},{40,104},{48,112},{56,120},{... | collective-permute-start | bytes 49160 | tf_op jit(solution)/shard_map/ppermute | solution.py:46
  54.9 1.2 %collective-permute-start.17 = (f32[32,128]{1,0:T(8,128)S(1)}, f32[32,128]{1,0:T(8,128)S(1)}, u32[]{:S(2)}, u32[]{:S(2)}) collective-permute-start(f32[32,128]{1,0:T(8,128)S(1)} %get-tuple-element.64), channel_id=1, source_target_pairs={{0,96},{8,104},{16,112},{24,120},{32,0},{40,8},{48,16},{56,24},{64... | collective-permute-start | bytes 49160 | tf_op jit(solution)/shard_map/ppermute | solution.py:46
  56.1 2.4 %all-to-all-done = f32[128,2,128]{2,1,0:T(2,128)S(1)} async-done(((f32[128,2,128]{2,1,0:T(2,128)}), f32[128,2,128]{2,1,0:T(2,128)S(1)}, u32[]{:S(2)}, u32[]{:S(2)}) %all-to-all-start) | async-done | bytes 131104 | tf_op jit(solution)/shard_map/all_to_all | solution.py:549
  58.6 1.7 %coefficients.1 = (f32[2400,128]{1,0:T(8,128)S(1)}, f32[2400,128]{1,0:T(8,128)S(1)}, f32[8,128]{1,0:T(8,128)S(1)}, f32[8,128]{1,0:T(8,128)S(1)}) custom-call(f32[256,128]{1,0:T(8,128)S(1)} %bitcast.12, f32[8,128]{1,0:T(8,128)S(1)} %get-tuple-element.56.refs_1_, f32[2400,128]{1,0:T(8,128)} %bitcast.9, f32[2400,128]{1,0:T(8,128)} %get-tuple-element.57.refs_3_), custom_call_target="tpu_custom_call" | custom-call | tf_op jit(solution)/shard_map/coefficients/pallas_call | solution.py:499
  60.4 2.9 %last.1 = (f32[2400,128]{1,0:T(8,128)}, f32[2400,128]{1,0:T(8,128)}, f32[8,128]{1,0:T(8,128)}) custom-call(f32[3,25]{1,0:T(4,128)S(1)} %copy-done.5, f32[8,128]{1,0:T(8,128)S(1)} %get-tuple-element.58.refs_1_, f32[8,128]{1,0:T(8,128)S(1)} %get-tuple-element.59.refs_2_, f32[32,128]{1,0:T(8,128)S(1)} %get-tuple-element.61.refs_3_, ...), custom_call_target="tpu_custom_call" | custom-call | tf_op jit(solution)/shard_map/last/pallas_call | solution.py:499
  (38 shorter events, 3.6 us)
Async XLA Ops:
  0.6 13.3 %copy-start = (f32[3,25,4,8,128]{4,3,2,1,0:T(8,128)S(1)}, f32[3,25,4,8,128]{4,3,2,1,0:T(8,128)}, u32[]{:S(2)}) copy-start(f32[3,25,4,8,128]{4,3,2,1,0:T(8,128)} %refs_0_.3) | copy-start | bytes 3686404
  0.6 13.3 %copy-start.4 = (f32[4,8,128]{2,1,0:T(8,128)S(1)}, f32[4,8,128]{2,1,0:T(8,128)}, u32[]{:S(2)}) copy-start(f32[4,8,128]{2,1,0:T(8,128)} %param.8) | copy-start | bytes 49156
  0.7 13.3 %copy-start.3 = (f32[4,8,128]{2,1,0:T(8,128)S(1)}, f32[4,8,128]{2,1,0:T(8,128)}, u32[]{:S(2)}) copy-start(f32[4,8,128]{2,1,0:T(8,128)} %param.7) | copy-start | bytes 49156
  1.7 12.2 %collective-permute-start = (f32[200,128]{1,0:T(8,128)S(1)}, f32[200,128]{1,0:T(8,128)S(1)}, u32[]{:S(2)}, u32[]{:S(2)}) collective-permute-start(f32[200,128]{1,0:T(8,128)S(1)} %bitcast.19), channel_id=1, source_target_pairs={{0,120},{8,0},{16,8},{24,16},{32,24},{40,32},{48,40},{56,48},{64,5... | collective-permute-start | bytes 307208 | tf_op jit(solution)/shard_map/ppermute | solution.py:46
  7.8 6.1 %collective-permute-start.1 = (f32[100,128]{1,0:T(8,128)S(1)}, f32[100,128]{1,0:T(8,128)S(1)}, u32[]{:S(2)}, u32[]{:S(2)}) collective-permute-start(f32[100,128]{1,0:T(8,128)S(1)} %reshape.35), channel_id=1, source_target_pairs={{0,7},{1,0},{2,1},{3,2},{4,3},{5,4},{6,5},{7,6},{8,15},{9,8},{10,9... | collective-permute-start | bytes 153608 | tf_op jit(solution)/shard_map/ppermute | solution.py:46
  16.1 8.8 %collective-permute-start.2 = (f32[200,128]{1,0:T(8,128)S(1)}, f32[200,128]{1,0:T(8,128)S(1)}, u32[]{:S(2)}, u32[]{:S(2)}) collective-permute-start(f32[200,128]{1,0:T(8,128)S(1)} %get-tuple-element.42.refs_8_), channel_id=1, source_target_pairs={{0,120},{8,16},{16,8},{24,32},{32,24},{40,48},{48,40},{56,64},{64,... | collective-permute-start | bytes 307208 | tf_op jit(solution)/shard_map/ppermute | solution.py:57
  17.7 6.2 %collective-permute-start.3 = (f32[100,128]{1,0:T(8,128)S(1)}, f32[100,128]{1,0:T(8,128)S(1)}, u32[]{:S(2)}, u32[]{:S(2)}) collective-permute-start(f32[100,128]{1,0:T(8,128)S(1)} %get-tuple-element.43.refs_10_), channel_id=1, source_target_pairs={{0,7},{1,2},{2,1},{3,4},{4,3},{5,6},{6,5},{7,0},{8,15},{9,10},{10,... | collective-permute-start | bytes 153608 | tf_op jit(solution)/shard_map/ppermute | solution.py:57
  20.7 4.1 %collective-permute-start.4 = (f32[100,128]{1,0:T(8,128)S(1)}, f32[100,128]{1,0:T(8,128)S(1)}, u32[]{:S(2)}, u32[]{:S(2)}) collective-permute-start(f32[100,128]{1,0:T(8,128)S(1)} %get-tuple-element.44.refs_9_), channel_id=1, source_target_pairs={{0,1},{1,0},{2,3},{3,2},{4,5},{5,4},{6,7},{7,6},{8,9},{9,8},{10,11... | collective-permute-start | bytes 153608 | tf_op jit(solution)/shard_map/ppermute | solution.py:51
  20.7 4.1 %collective-permute-start.5 = (f32[100,128]{1,0:T(8,128)S(1)}, f32[100,128]{1,0:T(8,128)S(1)}, u32[]{:S(2)}, u32[]{:S(2)}) collective-permute-start(f32[100,128]{1,0:T(8,128)S(1)} %get-tuple-element.45.refs_6_), channel_id=1, source_target_pairs={{0,8},{8,0},{16,24},{24,16},{32,40},{40,32},{48,56},{56,48},{64,72... | collective-permute-start | bytes 153608 | tf_op jit(solution)/shard_map/ppermute | solution.py:51
  20.8 4.1 %collective-permute-start.6 = (f32[100,128]{1,0:T(8,128)S(1)}, f32[100,128]{1,0:T(8,128)S(1)}, u32[]{:S(2)}, u32[]{:S(2)}) collective-permute-start(f32[100,128]{1,0:T(8,128)S(1)} %get-tuple-element.46.refs_7_), channel_id=1, source_target_pairs={{0,8},{8,0},{16,24},{24,16},{32,40},{40,32},{48,56},{56,48},{64,72... | collective-permute-start | bytes 153608 | tf_op jit(solution)/shard_map/ppermute | solution.py:51
  26.7 9.5 %collective-permute-start.7 = (f32[200,128]{1,0:T(8,128)S(1)}, f32[200,128]{1,0:T(8,128)S(1)}, u32[]{:S(2)}, u32[]{:S(2)}) collective-permute-start(f32[200,128]{1,0:T(8,128)S(1)} %get-tuple-element.49.refs_9_), channel_id=1, source_target_pairs={{0,120},{8,16},{16,8},{24,32},{32,24},{40,48},{48,40},{56,64},{64,... | collective-permute-start | bytes 307208 | tf_op jit(solution)/shard_map/ppermute | solution.py:57
  30.0 6.2 %collective-permute-start.8 = (f32[100,128]{1,0:T(8,128)S(1)}, f32[100,128]{1,0:T(8,128)S(1)}, u32[]{:S(2)}, u32[]{:S(2)}) collective-permute-start(f32[100,128]{1,0:T(8,128)S(1)} %get-tuple-element.50.refs_11_), channel_id=1, source_target_pairs={{0,7},{1,2},{2,1},{3,4},{4,3},{5,6},{6,5},{7,0},{8,15},{9,10},{10,... | collective-permute-start | bytes 153608 | tf_op jit(solution)/shard_map/ppermute | solution.py:57
  31.8 4.5 %collective-permute-start.9 = (f32[100,128]{1,0:T(8,128)S(1)}, f32[100,128]{1,0:T(8,128)S(1)}, u32[]{:S(2)}, u32[]{:S(2)}) collective-permute-start(f32[100,128]{1,0:T(8,128)S(1)} %get-tuple-element.51.refs_10_), channel_id=1, source_target_pairs={{0,1},{1,0},{2,3},{3,2},{4,5},{5,4},{6,7},{7,6},{8,9},{9,8},{10,11... | collective-permute-start | bytes 153608 | tf_op jit(solution)/shard_map/ppermute | solution.py:51
  31.8 4.5 %collective-permute-start.10 = (f32[100,128]{1,0:T(8,128)S(1)}, f32[100,128]{1,0:T(8,128)S(1)}, u32[]{:S(2)}, u32[]{:S(2)}) collective-permute-start(f32[100,128]{1,0:T(8,128)S(1)} %get-tuple-element.52.refs_7_), channel_id=1, source_target_pairs={{0,8},{8,0},{16,24},{24,16},{32,40},{40,32},{48,56},{56,48},{64,72... | collective-permute-start | bytes 153608 | tf_op jit(solution)/shard_map/ppermute | solution.py:51
  31.8 4.5 %collective-permute-start.11 = (f32[100,128]{1,0:T(8,128)S(1)}, f32[100,128]{1,0:T(8,128)S(1)}, u32[]{:S(2)}, u32[]{:S(2)}) collective-permute-start(f32[100,128]{1,0:T(8,128)S(1)} %get-tuple-element.53.refs_8_), channel_id=1, source_target_pairs={{0,8},{8,0},{16,24},{24,16},{32,40},{40,32},{48,56},{56,48},{64,72... | collective-permute-start | bytes 153608 | tf_op jit(solution)/shard_map/ppermute | solution.py:51
  39.2 10.8 %collective-permute-start.14 = (f32[264,128]{1,0:T(8,128)S(1)}, f32[264,128]{1,0:T(8,128)S(1)}, u32[]{:S(2)}, u32[]{:S(2)}) collective-permute-start(f32[264,128]{1,0:T(8,128)S(1)} %get-tuple-element.60.refs_0_), channel_id=1, source_target_pairs={{0,112},{8,120},{16,0},{24,8},{32,16},{40,24},{48,32},{56,40},{64,... | collective-permute-start | bytes 405512 | tf_op jit(solution)/shard_map/ppermute | solution.py:46
  39.8 10.2 %collective-permute-start.13 = (f32[264,128]{1,0:T(8,128)S(1)}, f32[264,128]{1,0:T(8,128)S(1)}, u32[]{:S(2)}, u32[]{:S(2)}) collective-permute-start(f32[264,128]{1,0:T(8,128)S(1)} %get-tuple-element.60.refs_0_), channel_id=1, source_target_pairs={{0,120},{8,0},{16,8},{24,16},{32,24},{40,32},{48,40},{56,48},{64,5... | collective-permute-start | bytes 405512 | tf_op jit(solution)/shard_map/ppermute | solution.py:46
  40.7 9.3 %collective-permute-start.12 = (f32[264,128]{1,0:T(8,128)S(1)}, f32[264,128]{1,0:T(8,128)S(1)}, u32[]{:S(2)}, u32[]{:S(2)}) collective-permute-start(f32[264,128]{1,0:T(8,128)S(1)} %get-tuple-element.60.refs_0_), channel_id=1, source_target_pairs={{0,8},{8,16},{16,24},{24,32},{32,40},{40,48},{48,56},{56,64},{64,7... | collective-permute-start | bytes 405512 | tf_op jit(solution)/shard_map/ppermute | solution.py:46
  40.8 17.8 %all-to-all-start = ((f32[128,2,128]{2,1,0:T(2,128)}), f32[128,2,128]{2,1,0:T(2,128)S(1)}, u32[]{:S(2)}, u32[]{:S(2)}) async-start(f32[128,2,128]{2,1,0:T(2,128)} %bitcast.4), calls=%async_computation | async-start | bytes 262144 | tf_op jit(solution)/shard_map/all_to_all | solution.py:549
  49.0 11.3 %collective-permute-start.18 = (f32[100,128]{1,0:T(8,128)S(1)}, f32[100,128]{1,0:T(8,128)S(1)}, u32[]{:S(2)}, u32[]{:S(2)}) collective-permute-start(f32[100,128]{1,0:T(8,128)S(1)} %get-tuple-element.69), channel_id=1, source_target_pairs={{0,1},{1,2},{2,3},{3,4},{4,5},{5,6},{6,7},{7,0},{8,9},{9,10},{10,1... | collective-permute-start | bytes 153608 | tf_op jit(solution)/shard_map/ppermute | solution.py:46
  50.1 10.3 %collective-permute-start.15 = (f32[32,128]{1,0:T(8,128)S(1)}, f32[32,128]{1,0:T(8,128)S(1)}, u32[]{:S(2)}, u32[]{:S(2)}) collective-permute-start(f32[32,128]{1,0:T(8,128)S(1)} %get-tuple-element.62), channel_id=1, source_target_pairs={{0,32},{8,40},{16,48},{24,56},{32,64},{40,72},{48,80},{56,88},{64,... | collective-permute-start | bytes 49160 | tf_op jit(solution)/shard_map/ppermute | solution.py:46
  51.7 8.6 %collective-permute-start.16 = (f32[32,128]{1,0:T(8,128)S(1)}, f32[32,128]{1,0:T(8,128)S(1)}, u32[]{:S(2)}, u32[]{:S(2)}) collective-permute-start(f32[32,128]{1,0:T(8,128)S(1)} %get-tuple-element.63), channel_id=1, source_target_pairs={{0,64},{8,72},{16,80},{24,88},{32,96},{40,104},{48,112},{56,120},{... | collective-permute-start | bytes 49160 | tf_op jit(solution)/shard_map/ppermute | solution.py:46
  54.9 5.4 %collective-permute-start.17 = (f32[32,128]{1,0:T(8,128)S(1)}, f32[32,128]{1,0:T(8,128)S(1)}, u32[]{:S(2)}, u32[]{:S(2)}) collective-permute-start(f32[32,128]{1,0:T(8,128)S(1)} %get-tuple-element.64), channel_id=1, source_target_pairs={{0,96},{8,104},{16,112},{24,120},{32,0},{40,8},{48,16},{56,24},{64... | collective-permute-start | bytes 49160 | tf_op jit(solution)/shard_map/ppermute | solution.py:46
  58.6 1.8 %copy-start.5 = (f32[3,25]{1,0:T(4,128)S(1)}, f32[3,25]{1,0:T(4,128)}, u32[]{:S(2)}) copy-start(f32[3,25]{1,0:T(4,128)} %refs_0_.5) | copy-start | bytes 904
  (2 other events, 1.8 us)

commit v13 on v10

--- a/solution.py
+++ b/solution.py
@@ -16,6 +16,7 @@
 CELLS = LX * LY
 FACE = A * CELLS
 ROWS = F * FACE
+HALF, SHORT = LZ // 2, LZ // 2 + 8
 TAIL = F * CELLS * B
 f32, bf16 = jnp.float32, jnp.bfloat16
 VM = pl.BlockSpec(memory_space=pltpu.VMEM)
@@ -286,12 +287,13 @@
         [row(sums_ref[16 + 8 * k : 24 + 8 * k]) for k in range(3)]
         + [row(m3), row(m4), row(energy) + tail, jnp.zeros((2, LZ), f32)], 0,
     )
-    for lanes in (64, 32, 16):
-        tile = tile + pltpu.roll(tile, lanes, 1)
     lane = lax.broadcasted_iota(jnp.int32, (8, LZ), 1)
     moment = lax.broadcasted_iota(jnp.int32, (8, LZ), 0)
-    packed = row(jnp.where(lax.div(lane, 16) == moment, tile, 0.0))
-    pair = jnp.concatenate([packed, row(upy[...])] * 4, 0)
+    sums = jnp.broadcast_to(jnp.sum(tile, axis=1, keepdims=True), (8, LZ))
+    packed = row(jnp.where(lane == HALF + moment, sums, 0.0))
+    edge = row(upy[...])
+    pair = [jnp.where(lane[:1] < HALF, edge, packed), pltpu.roll(edge, HALF, 1)]
+    pair = jnp.concatenate(pair * 4, 0)[:, :SHORT]
     for at in range(0, mom_ref.shape[0], 8):
         mom_ref[at : at + 8] = pair
     loads_ref[40:] = jnp.zeros((loads_ref.shape[0] - 40, LZ), f32)
@@ -348,26 +350,20 @@
 
 
 def moments(got):
-    zero = jnp.zeros((8, LZ), f32)
+    zero = jnp.zeros((8, SHORT), f32)
     pairs = [(got[at : at + 8], zero) for at in range(0, got.shape[0], 8)]
     while len(pairs) > 1:
         pairs = [pair_add(a, b) for a, b in zip(pairs[::2], pairs[1::2])]
     h, l = pairs[0]
     rows = [(h[r : r + 1], l[r : r + 1]) for r in (0, 2, 4, 6)]
     t = pair_add(pair_add(rows[0], rows[1]), pair_add(rows[2], rows[3]))
-    level = [t] + [tuple(pltpu.roll(p, LZ - 16 * k, 1) for p in t) for k in range(1, 6)]
-    inside = lax.broadcasted_iota(jnp.int32, (1, LZ), 1) < 16
-
-    def total(value):
-        return jnp.sum(jnp.where(inside, value, 0.0), axis=1, keepdims=True)
-
-    c = total(level[1][0]) / total(level[0][0])
-    minus = jnp.broadcast_to(-c, (1, LZ))
+    level = [tuple(p[:, HALF + k : HALF + k + 1] for p in t) for k in range(6)]
+    c = level[1][0] / level[0][0]
     heads = [level[0]]
     while len(level) > 1:
-        level = [pair_add(up, pair_times(at, minus)) for at, up in zip(level, level[1:])]
+        level = [pair_add(up, pair_times(at, -c)) for at, up in zip(level, level[1:])]
         heads.append(level[0])
-    return c, [total(p[0] + p[1]) for p in heads]
+    return c, [p[0] + p[1] for p in heads]
 
 
 def conjugate_gradient(c, m):
@@ -427,10 +423,11 @@
     below = lax.rem(lax.axis_index("gy") + ny - 1, ny)
     me = lax.axis_index("gx")
     nx = len(table)
-    edge = jnp.zeros((1, LZ), f32)
+    edge = [jnp.zeros((1, SHORT), f32)] * 2
     for offset, weight in enumerate(table):
         slab = lax.rem(me + nx - offset, nx)
-        edge = edge + got_ref[pl.ds(2 * (slab * ny + below) + 1, 1), :] * weight
+        edge = [e + got_ref[pl.ds(2 * (slab * ny + below) + i, 1), :] * weight for i, e in enumerate(edge)]
+    edge = jnp.concatenate([e[:, :HALF] for e in edge], 1)
     edge_ref[...] = jnp.concatenate([edge, jnp.zeros((LY - 1, LZ), f32)], 0)
     for fetch in fetches:
         fetch.wait()
@@ -548,13 +545,13 @@
     peers = nx * ny * 2
     v2, p2, upx, upy, loads, mom = call(
         third_kernel, "third", [p1, v1, *r, *s, sums, k2, m2, w],
-        [struct(ROWS, LZ)] * 2 + [struct(vx, LZ), struct(vy, LZ), struct(peers + 8, LZ), struct(peers, LZ)], upper,
+        [struct(ROWS, LZ)] * 2 + [struct(vx, LZ), struct(vy, LZ), struct(152, LZ), struct(peers, SHORT)], upper,
     )
     table = [float(t) for t in jacobi_weights(nx)]
     group = [lax.ppermute(loads, "gx", [(i, i ^ b) for i in range(nx)]) for b in (1, 2, 3)]
     pieces = call(weigh_kernel, "weigh", [loads, *group], [struct(32, LZ)] * (nx // 4), table=table)
     coarse = [pieces[0]] + [shifted(p, "gx", 4 * z) for z, p in enumerate(pieces) if z]
-    got = lax.all_to_all(mom.reshape(-1, 2, LZ), ("gx", "gy"), 0, 0, tiled=True).reshape(mom.shape)
+    got = lax.all_to_all(mom.reshape(-1, 2, SHORT), ("gx", "gy"), 0, 0, tiled=True).reshape(mom.shape)
     rx = shifted(upx, "gx", 1)
     ry = shifted(upy, "gy", 1)
     v0, v1_kept = (pltpu.with_memory_space_constraint(v, pltpu.HBM) for v in (rhs2, v1_kept))

time: 62.5 us -> 67.8 us (1.085)
  starting transfers between devices: 35.3 us -> 39.1 us
  Pallas kernels: 14.6 us -> 15.6 us
    all_to_all x1, starting transfers between devices: 4.79 us -> 8.73 us  [shards(): lax.all_to_all(mom.reshape(-1, 2, SHORT), ('gx', 'gy'), 0, 0, tiled=True)]
    pallas_call x9, Pallas kernels: 14.6 us -> 15.6 us  [call(): pl.pallas_call(bound, out_shape=outs, in_specs=specs, out_specs=[ANY if i...]
  transfers between devices with their start and end apart: 21 -> 21, of which waited for: 4 -> 4; matrix products, arithmetic and copies ran while one was open for 0% -> 0% of each run, Pallas kernels for 6% -> 8%
where the time goes in v13:
time: 67.8 us; the launch traced here: 66.6 us
  starting transfers between devices  39.1 us (58%)
  Pallas kernels  15.6 us (23%)
  waiting for transfers between devices  8.97 us (13%)
  local copies, waits for them, and re-layouts  1.86 us (3%)
  between operations  1 us (1%)
    ppermute x7, starting transfers between devices, shifted(): return lax.ppermute(value, axis, [(i, (i + by) % n) for i in range(n)])  16.3 us
    pallas_call x9, Pallas kernels, call(): pl.pallas_call(bound, out_shape=outs, in_specs=specs, out_specs=[ANY if i...  15.6 us
    ppermute x4, starting transfers between devices, far_swap(): return lax.ppermute(value, axis, pairs)  9.72 us
    all_to_all x1, starting transfers between devices, shards(): lax.all_to_all(mom.reshape(-1, 2, SHORT), ('gx', 'gy'), 0, 0, tiled=True)  8.73 us
    ppermute x4, waiting for transfers between devices, far_swap(): return lax.ppermute(value, axis, pairs)  5.59 us
    ppermute x3, starting transfers between devices, shards(): lax.ppermute(loads, 'gx', [(i, i ^ b) for i in range(nx)])  3.37 us
    all_to_all x1, waiting for transfers between devices, shards(): lax.all_to_all(mom.reshape(-1, 2, SHORT), ('gx', 'gy'), 0, 0, tiled=True)  2.41 us
    unnamed x12, local copies, waits for them, and re-layouts  1.84 us
  transfers between devices with their start and end apart: 21, of which 4 were waited for; matrix products, arithmetic and copies ran while one was open for 0% of the time, Pallas kernels for 8%

profile of v13, /device:TPU:0, one launch (start us, length us, event | category | flops | bytes accessed | tf_op | source)
XLA Modules:
  0.0 66.6 jit_solution(2740408145289521607)
XLA Ops:
  0.7 1.0 %edges.1 = (f32[25,8,128]{2,1,0:T(8,128)S(1)}, f32[25,4,128]{2,1,0:T(4,128)S(1)}) custom-call(f32[3,25,4,8,128]{4,3,2,1,0:T(8,128)} %refs_0_.3), custom_call_target="tpu_custom_call" | custom-call | tf_op jit(solution)/shard_map/edges/pallas_call | solution.py:504
  1.7 6.1 %collective-permute-start = (f32[200,128]{1,0:T(8,128)S(1)}, f32[200,128]{1,0:T(8,128)S(1)}, u32[]{:S(2)}, u32[]{:S(2)}) collective-permute-start(f32[200,128]{1,0:T(8,128)S(1)} %bitcast.19), channel_id=1, source_target_pairs={{0,120},{8,0},{16,8},{24,16},{32,24},{40,32},{48,40},{56,48},{64,5... | collective-permute-start | bytes 307208 | tf_op jit(solution)/shard_map/ppermute | solution.py:46
  7.8 3.1 %collective-permute-start.1 = (f32[100,128]{1,0:T(8,128)S(1)}, f32[100,128]{1,0:T(8,128)S(1)}, u32[]{:S(2)}, u32[]{:S(2)}) collective-permute-start(f32[100,128]{1,0:T(8,128)S(1)} %reshape.35), channel_id=1, source_target_pairs={{0,7},{1,0},{2,1},{3,2},{4,3},{5,4},{6,5},{7,6},{8,15},{9,8},{10,9... | collective-permute-start | bytes 153608 | tf_op jit(solution)/shard_map/ppermute | solution.py:46
  12.7 1.2 %weights.1 = (bf16[304,480]{1,0:T(8,128)(2,1)S(1)}, f32[8,128]{1,0:T(8,128)S(1)}) custom-call(f32[150,150]{1,0:T(8,128)S(1)} %copy-done.1, f32[150,150]{1,0:T(8,128)S(1)} %copy-done.2), custom_call_target="tpu_custom_call" | custom-call | tf_op jit(solution)/shard_map/weights/pallas_call | solution.py:504
  13.9 2.0 %first.1 = (f32[2400,128]{1,0:T(8,128)S(1)}, f32[100,128]{1,0:T(8,128)S(1)}, f32[100,128]{1,0:T(8,128)S(1)}, f32[200,128]{1,0:T(8,128)S(1)}, f32[100,128]{1,0:T(8,128)S(1)}, /*index=5*/f32[100,128]{1,0:T(8,128)S(1)}) custom-call(f32[2400,128]{1,0:T(8,128)S(1)} %bitcast.10, f32[200,128]{1,0:T(8,128)S(1)} %collective-permute-done.refs_1_, ...), custom_call_target="tpu_custom_call" | custom-call | tf_op jit(solution)/shard_map/first/pallas_call | solution.py:504
  16.0 1.6 %collective-permute-start.2 = (f32[200,128]{1,0:T(8,128)S(1)}, f32[200,128]{1,0:T(8,128)S(1)}, u32[]{:S(2)}, u32[]{:S(2)}) collective-permute-start(f32[200,128]{1,0:T(8,128)S(1)} %get-tuple-element.43.refs_8_), channel_id=1, source_target_pairs={{0,120},{8,16},{16,8},{24,32},{32,24},{40,48},{48,40},{56,64},{64,... | collective-permute-start | bytes 307208 | tf_op jit(solution)/shard_map/ppermute | solution.py:57
  17.6 3.0 %collective-permute-start.3 = (f32[100,128]{1,0:T(8,128)S(1)}, f32[100,128]{1,0:T(8,128)S(1)}, u32[]{:S(2)}, u32[]{:S(2)}) collective-permute-start(f32[100,128]{1,0:T(8,128)S(1)} %get-tuple-element.44.refs_10_), channel_id=1, source_target_pairs={{0,7},{1,2},{2,1},{3,4},{4,3},{5,6},{6,5},{7,0},{8,15},{9,10},{10,... | collective-permute-start | bytes 153608 | tf_op jit(solution)/shard_map/ppermute | solution.py:57
  21.2 2.7 %collective-permute-done.3.refs_2_ = f32[100,128]{1,0:T(8,128)S(1)} collective-permute-done((f32[100,128]{1,0:T(8,128)S(1)}, f32[100,128]{1,0:T(8,128)S(1)}, u32[]{:S(2)}, u32[]{:S(2)}) %collective-permute-start.3) | collective-permute-done | bytes 51232 | tf_op jit(solution)/shard_map/ppermute | solution.py:57
  24.8 1.7 %second.1 = (f32[2400,128]{1,0:T(8,128)S(1)}, f32[2400,128]{1,0:T(8,128)S(1)}, f32[100,128]{1,0:T(8,128)S(1)}, f32[100,128]{1,0:T(8,128)S(1)}, f32[200,128]{1,0:...) custom-call(f32[2400,128]{1,0:T(8,128)S(1)} %get-tuple-element.42.refs_0_, ...), custom_call_target="tpu_custom_call" | custom-call | tf_op jit(solution)/shard_map/second/pallas_call | solution.py:504
  26.5 3.3 %collective-permute-start.7 = (f32[200,128]{1,0:T(8,128)S(1)}, f32[200,128]{1,0:T(8,128)S(1)}, u32[]{:S(2)}, u32[]{:S(2)}) collective-permute-start(f32[200,128]{1,0:T(8,128)S(1)} %get-tuple-element.50.refs_9_), channel_id=1, source_target_pairs={{0,120},{8,16},{16,8},{24,32},{32,24},{40,48},{48,40},{56,64},{64,... | collective-permute-start | bytes 307208 | tf_op jit(solution)/shard_map/ppermute | solution.py:57
  29.8 1.8 %collective-permute-start.8 = (f32[100,128]{1,0:T(8,128)S(1)}, f32[100,128]{1,0:T(8,128)S(1)}, u32[]{:S(2)}, u32[]{:S(2)}) collective-permute-start(f32[100,128]{1,0:T(8,128)S(1)} %get-tuple-element.51.refs_11_), channel_id=1, source_target_pairs={{0,7},{1,2},{2,1},{3,4},{4,3},{5,6},{6,5},{7,0},{8,15},{9,10},{10,... | collective-permute-start | bytes 153608 | tf_op jit(solution)/shard_map/ppermute | solution.py:57
  32.1 1.0 %products.1 = (f32[40,128]{1,0:T(8,128)S(1)}, f32[2400,128]{1,0:T(8,128)}) custom-call(f32[2400,128]{1,0:T(8,128)S(1)} %bitcast.11, f32[2400,128]{1,0:T(8,128)S(1)} %get-tuple-element.49.refs_1_), custom_call_target="tpu_custom_call" | custom-call | tf_op jit(solution)/shard_map/products/pallas_call | solution.py:504
  33.2 2.9 %collective-permute-done.8.refs_3_ = f32[100,128]{1,0:T(8,128)S(1)} collective-permute-done((f32[100,128]{1,0:T(8,128)S(1)}, f32[100,128]{1,0:T(8,128)S(1)}, u32[]{:S(2)}, u32[]{:S(2)}) %collective-permute-start.8) | collective-permute-done | bytes 51232 | tf_op jit(solution)/shard_map/ppermute | solution.py:57
  36.1 2.7 %third.1 = (f32[2400,128]{1,0:T(8,128)S(1)}, f32[2400,128]{1,0:T(8,128)S(1)}, f32[200,128]{1,0:T(8,128)S(1)}, f32[100,128]{1,0:T(8,128)S(1)}, f32[152,128]{1,0:T(8,128)S(1)}, /*index=5*/f32[256,72]{1,0:T(8,128)}) custom-call(f32[2400,128]{1,0:T(8,128)S(1)} %get-tuple-element.48.refs_0_, f32[2400,128]{1,0:T(8,128)S(1)} %get-tuple-element.49.refs_1_, ...), custom_call_target="tpu_custom_call" | custom-call | tf_op jit(solution)/shard_map/third/pallas_call | solution.py:504
  38.8 1.7 %collective-permute-start.13 = (f32[152,128]{1,0:T(8,128)S(1)}, f32[152,128]{1,0:T(8,128)S(1)}, u32[]{:S(2)}, u32[]{:S(2)}) collective-permute-start(f32[152,128]{1,0:T(8,128)S(1)} %get-tuple-element.61.refs_0_), channel_id=1, source_target_pairs={{0,16},{8,24},{16,0},{24,8},{32,48},{40,56},{48,32},{56,40},{64,80... | collective-permute-start | bytes 233480 | tf_op jit(solution)/shard_map/ppermute | solution.py:551
  40.5 1.6 %collective-permute-start.12 = (f32[152,128]{1,0:T(8,128)S(1)}, f32[152,128]{1,0:T(8,128)S(1)}, u32[]{:S(2)}, u32[]{:S(2)}) collective-permute-start(f32[152,128]{1,0:T(8,128)S(1)} %get-tuple-element.61.refs_0_), channel_id=1, source_target_pairs={{0,8},{8,0},{16,24},{24,16},{32,40},{40,32},{48,56},{56,48},{64,72... | collective-permute-start | bytes 233480 | tf_op jit(solution)/shard_map/ppermute | solution.py:551
  42.2 8.7 %all-to-all-start = ((f32[128,2,72]{2,1,0:T(2,128)}), f32[128,2,72]{2,1,0:T(2,128)S(1)}, u32[]{:S(2)}, u32[]{:S(2)}) async-start(f32[128,2,72]{2,1,0:T(2,128)} %bitcast.4), calls=%async_computation | async-start | bytes 262144 | tf_op jit(solution)/shard_map/all_to_all | solution.py:554
  50.9 1.0 %collective-permute-start.19 = (f32[100,128]{1,0:T(8,128)S(1)}, f32[100,128]{1,0:T(8,128)S(1)}, u32[]{:S(2)}, u32[]{:S(2)}) collective-permute-start(f32[100,128]{1,0:T(8,128)S(1)} %get-tuple-element.71), channel_id=1, source_target_pairs={{0,1},{1,2},{2,3},{3,4},{4,5},{5,6},{6,7},{7,0},{8,9},{9,10},{10,1... | collective-permute-start | bytes 153608 | tf_op jit(solution)/shard_map/ppermute | solution.py:46
  52.0 1.7 %collective-permute-start.15 = (f32[32,128]{1,0:T(8,128)S(1)}, f32[32,128]{1,0:T(8,128)S(1)}, u32[]{:S(2)}, u32[]{:S(2)}) collective-permute-start(f32[32,128]{1,0:T(8,128)S(1)} %get-tuple-element.63), channel_id=1, source_target_pairs={{0,32},{8,40},{16,48},{24,56},{32,64},{40,72},{48,80},{56,88},{64,... | collective-permute-start | bytes 49160 | tf_op jit(solution)/shard_map/ppermute | solution.py:46
  53.7 3.2 %collective-permute-start.16 = (f32[32,128]{1,0:T(8,128)S(1)}, f32[32,128]{1,0:T(8,128)S(1)}, u32[]{:S(2)}, u32[]{:S(2)}) collective-permute-start(f32[32,128]{1,0:T(8,128)S(1)} %get-tuple-element.64), channel_id=1, source_target_pairs={{0,64},{8,72},{16,80},{24,88},{32,96},{40,104},{48,112},{56,120},{... | collective-permute-start | bytes 49160 | tf_op jit(solution)/shard_map/ppermute | solution.py:46
  56.9 1.2 %collective-permute-start.17 = (f32[32,128]{1,0:T(8,128)S(1)}, f32[32,128]{1,0:T(8,128)S(1)}, u32[]{:S(2)}, u32[]{:S(2)}) collective-permute-start(f32[32,128]{1,0:T(8,128)S(1)} %get-tuple-element.65), channel_id=1, source_target_pairs={{0,96},{8,104},{16,112},{24,120},{32,0},{40,8},{48,16},{56,24},{64... | collective-permute-start | bytes 49160 | tf_op jit(solution)/shard_map/ppermute | solution.py:46
  58.1 2.4 %all-to-all-done = f32[128,2,72]{2,1,0:T(2,128)S(1)} async-done(((f32[128,2,72]{2,1,0:T(2,128)}), f32[128,2,72]{2,1,0:T(2,128)S(1)}, u32[]{:S(2)}, u32[]{:S(2)}) %all-to-all-start) | async-done | bytes 73760 | tf_op jit(solution)/shard_map/all_to_all | solution.py:554
  60.5 3.0 %coefficients.1 = (f32[2400,128]{1,0:T(8,128)S(1)}, f32[2400,128]{1,0:T(8,128)S(1)}, f32[8,128]{1,0:T(8,128)S(1)}, f32[8,128]{1,0:T(8,128)S(1)}) custom-call(f32[256,72]{1,0:T(8,128)S(1)} %bitcast.12, f32[8,128]{1,0:T(8,128)S(1)} %get-tuple-element.57.refs_1_, f32[2400,128]{1,0:T(8,128)} %bitcast.9, f32[2400,128]{1,0:T(8,128)} %get-tuple-element.58.refs_3_), custom_call_target="tpu_custom_call" | custom-call | tf_op jit(solution)/shard_map/coefficients/pallas_call | solution.py:504
  63.5 2.9 %last.1 = (f32[2400,128]{1,0:T(8,128)}, f32[2400,128]{1,0:T(8,128)}, f32[8,128]{1,0:T(8,128)}) custom-call(f32[3,25]{1,0:T(4,128)S(1)} %copy-done.5, f32[8,128]{1,0:T(8,128)S(1)} %get-tuple-element.59.refs_1_, f32[8,128]{1,0:T(8,128)S(1)} %get-tuple-element.60.refs_2_, f32[32,128]{1,0:T(8,128)S(1)} %get-tuple-element.62.refs_3_, ...), custom_call_target="tpu_custom_call" | custom-call | tf_op jit(solution)/shard_map/last/pallas_call | solution.py:504
  (40 shorter events, 3.9 us)
Async XLA Ops:
  0.6 13.3 %copy-start = (f32[3,25,4,8,128]{4,3,2,1,0:T(8,128)S(1)}, f32[3,25,4,8,128]{4,3,2,1,0:T(8,128)}, u32[]{:S(2)}) copy-start(f32[3,25,4,8,128]{4,3,2,1,0:T(8,128)} %refs_0_.3) | copy-start | bytes 3686404
  0.6 13.3 %copy-start.4 = (f32[4,8,128]{2,1,0:T(8,128)S(1)}, f32[4,8,128]{2,1,0:T(8,128)}, u32[]{:S(2)}) copy-start(f32[4,8,128]{2,1,0:T(8,128)} %param.8) | copy-start | bytes 49156
  0.7 13.3 %copy-start.3 = (f32[4,8,128]{2,1,0:T(8,128)S(1)}, f32[4,8,128]{2,1,0:T(8,128)}, u32[]{:S(2)}) copy-start(f32[4,8,128]{2,1,0:T(8,128)} %param.7) | copy-start | bytes 49156
  1.7 12.2 %collective-permute-start = (f32[200,128]{1,0:T(8,128)S(1)}, f32[200,128]{1,0:T(8,128)S(1)}, u32[]{:S(2)}, u32[]{:S(2)}) collective-permute-start(f32[200,128]{1,0:T(8,128)S(1)} %bitcast.19), channel_id=1, source_target_pairs={{0,120},{8,0},{16,8},{24,16},{32,24},{40,32},{48,40},{56,48},{64,5... | collective-permute-start | bytes 307208 | tf_op jit(solution)/shard_map/ppermute | solution.py:46
  7.8 6.1 %collective-permute-start.1 = (f32[100,128]{1,0:T(8,128)S(1)}, f32[100,128]{1,0:T(8,128)S(1)}, u32[]{:S(2)}, u32[]{:S(2)}) collective-permute-start(f32[100,128]{1,0:T(8,128)S(1)} %reshape.35), channel_id=1, source_target_pairs={{0,7},{1,0},{2,1},{3,2},{4,3},{5,4},{6,5},{7,6},{8,15},{9,8},{10,9... | collective-permute-start | bytes 153608 | tf_op jit(solution)/shard_map/ppermute | solution.py:46
  16.0 8.8 %collective-permute-start.2 = (f32[200,128]{1,0:T(8,128)S(1)}, f32[200,128]{1,0:T(8,128)S(1)}, u32[]{:S(2)}, u32[]{:S(2)}) collective-permute-start(f32[200,128]{1,0:T(8,128)S(1)} %get-tuple-element.43.refs_8_), channel_id=1, source_target_pairs={{0,120},{8,16},{16,8},{24,32},{32,24},{40,48},{48,40},{56,64},{64,... | collective-permute-start | bytes 307208 | tf_op jit(solution)/shard_map/ppermute | solution.py:57
  17.6 6.2 %collective-permute-start.3 = (f32[100,128]{1,0:T(8,128)S(1)}, f32[100,128]{1,0:T(8,128)S(1)}, u32[]{:S(2)}, u32[]{:S(2)}) collective-permute-start(f32[100,128]{1,0:T(8,128)S(1)} %get-tuple-element.44.refs_10_), channel_id=1, source_target_pairs={{0,7},{1,2},{2,1},{3,4},{4,3},{5,6},{6,5},{7,0},{8,15},{9,10},{10,... | collective-permute-start | bytes 153608 | tf_op jit(solution)/shard_map/ppermute | solution.py:57
  20.6 4.1 %collective-permute-start.4 = (f32[100,128]{1,0:T(8,128)S(1)}, f32[100,128]{1,0:T(8,128)S(1)}, u32[]{:S(2)}, u32[]{:S(2)}) collective-permute-start(f32[100,128]{1,0:T(8,128)S(1)} %get-tuple-element.45.refs_9_), channel_id=1, source_target_pairs={{0,1},{1,0},{2,3},{3,2},{4,5},{5,4},{6,7},{7,6},{8,9},{9,8},{10,11... | collective-permute-start | bytes 153608 | tf_op jit(solution)/shard_map/ppermute | solution.py:51
  20.6 4.1 %collective-permute-start.5 = (f32[100,128]{1,0:T(8,128)S(1)}, f32[100,128]{1,0:T(8,128)S(1)}, u32[]{:S(2)}, u32[]{:S(2)}) collective-permute-start(f32[100,128]{1,0:T(8,128)S(1)} %get-tuple-element.46.refs_6_), channel_id=1, source_target_pairs={{0,8},{8,0},{16,24},{24,16},{32,40},{40,32},{48,56},{56,48},{64,72... | collective-permute-start | bytes 153608 | tf_op jit(solution)/shard_map/ppermute | solution.py:51
  20.7 4.1 %collective-permute-start.6 = (f32[100,128]{1,0:T(8,128)S(1)}, f32[100,128]{1,0:T(8,128)S(1)}, u32[]{:S(2)}, u32[]{:S(2)}) collective-permute-start(f32[100,128]{1,0:T(8,128)S(1)} %get-tuple-element.47.refs_7_), channel_id=1, source_target_pairs={{0,8},{8,0},{16,24},{24,16},{32,40},{40,32},{48,56},{56,48},{64,72... | collective-permute-start | bytes 153608 | tf_op jit(solution)/shard_map/ppermute | solution.py:51
  26.5 9.5 %collective-permute-start.7 = (f32[200,128]{1,0:T(8,128)S(1)}, f32[200,128]{1,0:T(8,128)S(1)}, u32[]{:S(2)}, u32[]{:S(2)}) collective-permute-start(f32[200,128]{1,0:T(8,128)S(1)} %get-tuple-element.50.refs_9_), channel_id=1, source_target_pairs={{0,120},{8,16},{16,8},{24,32},{32,24},{40,48},{48,40},{56,64},{64,... | collective-permute-start | bytes 307208 | tf_op jit(solution)/shard_map/ppermute | solution.py:57
  29.8 6.2 %collective-permute-start.8 = (f32[100,128]{1,0:T(8,128)S(1)}, f32[100,128]{1,0:T(8,128)S(1)}, u32[]{:S(2)}, u32[]{:S(2)}) collective-permute-start(f32[100,128]{1,0:T(8,128)S(1)} %get-tuple-element.51.refs_11_), channel_id=1, source_target_pairs={{0,7},{1,2},{2,1},{3,4},{4,3},{5,6},{6,5},{7,0},{8,15},{9,10},{10,... | collective-permute-start | bytes 153608 | tf_op jit(solution)/shard_map/ppermute | solution.py:57
  31.6 4.5 %collective-permute-start.9 = (f32[100,128]{1,0:T(8,128)S(1)}, f32[100,128]{1,0:T(8,128)S(1)}, u32[]{:S(2)}, u32[]{:S(2)}) collective-permute-start(f32[100,128]{1,0:T(8,128)S(1)} %get-tuple-element.52.refs_10_), channel_id=1, source_target_pairs={{0,1},{1,0},{2,3},{3,2},{4,5},{5,4},{6,7},{7,6},{8,9},{9,8},{10,11... | collective-permute-start | bytes 153608 | tf_op jit(solution)/shard_map/ppermute | solution.py:51
  31.6 4.5 %collective-permute-start.10 = (f32[100,128]{1,0:T(8,128)S(1)}, f32[100,128]{1,0:T(8,128)S(1)}, u32[]{:S(2)}, u32[]{:S(2)}) collective-permute-start(f32[100,128]{1,0:T(8,128)S(1)} %get-tuple-element.53.refs_7_), channel_id=1, source_target_pairs={{0,8},{8,0},{16,24},{24,16},{32,40},{40,32},{48,56},{56,48},{64,72... | collective-permute-start | bytes 153608 | tf_op jit(solution)/shard_map/ppermute | solution.py:51
  31.6 4.5 %collective-permute-start.11 = (f32[100,128]{1,0:T(8,128)S(1)}, f32[100,128]{1,0:T(8,128)S(1)}, u32[]{:S(2)}, u32[]{:S(2)}) collective-permute-start(f32[100,128]{1,0:T(8,128)S(1)} %get-tuple-element.54.refs_8_), channel_id=1, source_target_pairs={{0,8},{8,0},{16,24},{24,16},{32,40},{40,32},{48,56},{56,48},{64,72... | collective-permute-start | bytes 153608 | tf_op jit(solution)/shard_map/ppermute | solution.py:51
  38.8 24.7 %collective-permute-start.18 = (f32[200,128]{1,0:T(8,128)S(1)}, f32[200,128]{1,0:T(8,128)S(1)}, u32[]{:S(2)}, u32[]{:S(2)}) collective-permute-start(f32[200,128]{1,0:T(8,128)S(1)} %get-tuple-element.70), channel_id=1, source_target_pairs={{0,8},{8,16},{16,24},{24,32},{32,40},{40,48},{48,56},{56,64},{64,7... | collective-permute-start | bytes 307208 | tf_op jit(solution)/shard_map/ppermute | solution.py:46
  38.8 13.1 %collective-permute-start.14 = (f32[152,128]{1,0:T(8,128)S(1)}, f32[152,128]{1,0:T(8,128)S(1)}, u32[]{:S(2)}, u32[]{:S(2)}) collective-permute-start(f32[152,128]{1,0:T(8,128)S(1)} %get-tuple-element.61.refs_0_), channel_id=1, source_target_pairs={{0,24},{8,16},{16,8},{24,0},{32,56},{40,48},{48,40},{56,32},{64,88... | collective-permute-start | bytes 233480 | tf_op jit(solution)/shard_map/ppermute | solution.py:551
  38.8 13.1 %collective-permute-start.13 = (f32[152,128]{1,0:T(8,128)S(1)}, f32[152,128]{1,0:T(8,128)S(1)}, u32[]{:S(2)}, u32[]{:S(2)}) collective-permute-start(f32[152,128]{1,0:T(8,128)S(1)} %get-tuple-element.61.refs_0_), channel_id=1, source_target_pairs={{0,16},{8,24},{16,0},{24,8},{32,48},{40,56},{48,32},{56,40},{64,80... | collective-permute-start | bytes 233480 | tf_op jit(solution)/shard_map/ppermute | solution.py:551
  40.5 11.4 %collective-permute-start.12 = (f32[152,128]{1,0:T(8,128)S(1)}, f32[152,128]{1,0:T(8,128)S(1)}, u32[]{:S(2)}, u32[]{:S(2)}) collective-permute-start(f32[152,128]{1,0:T(8,128)S(1)} %get-tuple-element.61.refs_0_), channel_id=1, source_target_pairs={{0,8},{8,0},{16,24},{24,16},{32,40},{40,32},{48,56},{56,48},{64,72... | collective-permute-start | bytes 233480 | tf_op jit(solution)/shard_map/ppermute | solution.py:551
  42.2 18.3 %all-to-all-start = ((f32[128,2,72]{2,1,0:T(2,128)}), f32[128,2,72]{2,1,0:T(2,128)S(1)}, u32[]{:S(2)}, u32[]{:S(2)}) async-start(f32[128,2,72]{2,1,0:T(2,128)} %bitcast.4), calls=%async_computation | async-start | bytes 262144 | tf_op jit(solution)/shard_map/all_to_all | solution.py:554
  50.9 12.6 %collective-permute-start.19 = (f32[100,128]{1,0:T(8,128)S(1)}, f32[100,128]{1,0:T(8,128)S(1)}, u32[]{:S(2)}, u32[]{:S(2)}) collective-permute-start(f32[100,128]{1,0:T(8,128)S(1)} %get-tuple-element.71), channel_id=1, source_target_pairs={{0,1},{1,2},{2,3},{3,4},{4,5},{5,6},{6,7},{7,0},{8,9},{9,10},{10,1... | collective-permute-start | bytes 153608 | tf_op jit(solution)/shard_map/ppermute | solution.py:46
  52.0 11.5 %collective-permute-start.15 = (f32[32,128]{1,0:T(8,128)S(1)}, f32[32,128]{1,0:T(8,128)S(1)}, u32[]{:S(2)}, u32[]{:S(2)}) collective-permute-start(f32[32,128]{1,0:T(8,128)S(1)} %get-tuple-element.63), channel_id=1, source_target_pairs={{0,32},{8,40},{16,48},{24,56},{32,64},{40,72},{48,80},{56,88},{64,... | collective-permute-start | bytes 49160 | tf_op jit(solution)/shard_map/ppermute | solution.py:46
  53.7 9.8 %collective-permute-start.16 = (f32[32,128]{1,0:T(8,128)S(1)}, f32[32,128]{1,0:T(8,128)S(1)}, u32[]{:S(2)}, u32[]{:S(2)}) collective-permute-start(f32[32,128]{1,0:T(8,128)S(1)} %get-tuple-element.64), channel_id=1, source_target_pairs={{0,64},{8,72},{16,80},{24,88},{32,96},{40,104},{48,112},{56,120},{... | collective-permute-start | bytes 49160 | tf_op jit(solution)/shard_map/ppermute | solution.py:46
  56.9 6.6 %collective-permute-start.17 = (f32[32,128]{1,0:T(8,128)S(1)}, f32[32,128]{1,0:T(8,128)S(1)}, u32[]{:S(2)}, u32[]{:S(2)}) collective-permute-start(f32[32,128]{1,0:T(8,128)S(1)} %get-tuple-element.65), channel_id=1, source_target_pairs={{0,96},{8,104},{16,112},{24,120},{32,0},{40,8},{48,16},{56,24},{64... | collective-permute-start | bytes 49160 | tf_op jit(solution)/shard_map/ppermute | solution.py:46
  (3 other events, 4.9 us)

commit v14 on v10

--- a/solution.py
+++ b/solution.py
@@ -227,7 +227,7 @@
 
 
 def second_kernel(p_ref, rfx, rfy, rny, rn0, rn1, sn0, sn1, sfx, sny, sfy, k_ref, m_ref, w_ref,
-                  v1_ref, p1_ref, tn0, tn1, tfx, tny, tfy, ux, uy, last_in, last_out, upx, lowx, upy, lowy):
+                  v1_ref, p1_ref, tn0, tn1, tfx, tny, tfy, ux, uy, upx, upy, last_in, last_out, lowx, lowy):
     assemble(p_ref, Parts(sn0, sn1), sfx, sny, sfy, Parts(rn0, rn1), rfx, rny, rfy, v1_ref, ux, uy)
     apply_operator(v1_ref, ux, uy, k_ref, m_ref, w_ref, p1_ref, upx, lowx, upy, lowy, last_in, last_out)
     route(is_even("gx"), upx, lowx, Parts(tn0, tn1), tfx)
@@ -252,7 +252,7 @@
     return ref[pl.ds(at * B + a, LY, stride=B), :]
 
 
-def products_kernel(v0_ref, v1_ref, sums_ref, v1_hbm, sem):
+def products_kernel(v0_ref, v1_ref, p1_ref, ux, uy, upx, upy, sums_ref, v1_hbm, sem):
     keep = pltpu.make_async_copy(v1_ref, v1_hbm, sem)
     keep.start()
     s0 = s1 = s00 = s01 = s11 = 0.0
@@ -265,17 +265,18 @@
                 s0, s1, s00, s01, s11 = s0 + v0, s1 + v1, s00 + v0 * v0, s01 + v0 * v1, s11 + v1 * v1
     for k, s in enumerate((s0, s1, s00, s01, s11)):
         sums_ref[8 * k : 8 * k + 8] = s
+    energy = node_sum(v1_ref[...] * p1_ref[...]) + node_sum(ux[...] * upx[...])
+    sums_ref[40:48] = energy
+    sums_ref[40:41] = sums_ref[40:41] + row(uy[...] * upy[...])
     keep.wait()
 
 
-def third_kernel(p_ref, v1_ref, rfx, rfy, rny, rn0, rn1, sn0, sn1, sfx, sny, sfy, sums_ref, k_ref, m_ref, w_ref,
+def third_kernel(p_ref, rfx, rfy, rny, rn0, rn1, sn0, sn1, sfx, sny, sfy, sums_ref, k_ref, m_ref, w_ref,
                  v2_ref, p2_ref, upx, upy, loads_ref, mom_ref, ux, uy, last_in, last_out):
     assemble(p_ref, Parts(sn0, sn1), sfx, sny, sfy, Parts(rn0, rn1), rfx, rny, rfy, v2_ref, ux, uy)
-    v1 = v1_ref[...]
     v2 = v2_ref[...]
     loads_ref[0:16] = sums_ref[0:16]
     loads_ref[16:24] = element_sum(v2_ref, F * CELLS)
-    m3 = node_sum(v1 * v2)
     m4 = node_sum(v2 * v2)
     apply_operator(v2_ref, ux, uy, k_ref, m_ref, w_ref, p2_ref, upx, None, upy, None, last_in, last_out)
     loads_ref[24:32] = element_sum(p2_ref, F * CELLS)
@@ -283,14 +284,13 @@
     energy = node_sum(v2_ref[...] * p2_ref[...]) + node_sum(ux[...] * upx[...])
     tail = row(uy[...] * upy[...])
     tile = jnp.concatenate(
-        [row(sums_ref[16 + 8 * k : 24 + 8 * k]) for k in range(3)]
-        + [row(m3), row(m4), row(energy) + tail, jnp.zeros((2, LZ), f32)], 0,
-    )
-    for lanes in (64, 32, 16):
-        tile = tile + pltpu.roll(tile, lanes, 1)
+        [row(sums_ref[16 + 8 * k : 24 + 8 * k]) for k in range(4)]
+        + [row(m4), row(energy) + tail, jnp.zeros((2, LZ), f32)], 0,
+    )
     lane = lax.broadcasted_iota(jnp.int32, (8, LZ), 1)
     moment = lax.broadcasted_iota(jnp.int32, (8, LZ), 0)
-    packed = row(jnp.where(lax.div(lane, 16) == moment, tile, 0.0))
+    sums = jnp.broadcast_to(jnp.sum(tile, axis=1, keepdims=True), (8, LZ))
+    packed = row(jnp.where(lane == 16 * moment, sums, 0.0))
     pair = jnp.concatenate([packed, row(upy[...])] * 4, 0)
     for at in range(0, mom_ref.shape[0], 8):
         mom_ref[at : at + 8] = pair
@@ -537,17 +537,17 @@
         first_kernel, "first", [rhs2, hx, hy, k2, m2, w], [struct(ROWS, LZ)] + sends, upper[2:] + edges,
     )
     r = swap(s)
-    v1, p1, *s = call(
+    v1, p1, *s, ux1, uy1, upx1, upy1 = call(
         second_kernel, "second", [p0, *r, *s, k2, m2, w],
-        [struct(ROWS, LZ), struct(ROWS, LZ)] + sends, upper + edges,
+        [struct(ROWS, LZ), struct(ROWS, LZ)] + sends + [struct(vx, LZ), struct(vy, LZ)] * 2, upper[2:] + [edges[1], edges[3]],
     )
     r = swap(s)
     sums, v1_kept = call(
-        products_kernel, "products", [rhs2, v1], [struct(40, LZ), pltpu.HBM((ROWS, LZ), f32)], [pltpu.SemaphoreType.DMA],
+        products_kernel, "products", [rhs2, v1, p1, ux1, uy1, upx1, upy1], [struct(48, LZ), pltpu.HBM((ROWS, LZ), f32)], [pltpu.SemaphoreType.DMA],
     )
     peers = nx * ny * 2
     v2, p2, upx, upy, loads, mom = call(
-        third_kernel, "third", [p1, v1, *r, *s, sums, k2, m2, w],
+        third_kernel, "third", [p1, *r, *s, sums, k2, m2, w],
         [struct(ROWS, LZ)] * 2 + [struct(vx, LZ), struct(vy, LZ), struct(peers + 8, LZ), struct(peers, LZ)], upper,
     )
     table = [float(t) for t in jacobi_weights(nx)]

time: 62.5 us -> 62.6 us (level)
  no operation moved by 1% of the time
where the time goes in v14:
time: 62.6 us; the launch traced here: 61.6 us
  starting transfers between devices  35.3 us (56%)
  Pallas kernels  14.6 us (23%)
  waiting for transfers between devices  8.79 us (14%)
  local copies, waits for them, and re-layouts  1.86 us (3%)
  between operations  1.01 us (2%)
    ppermute x7, starting transfers between devices, shifted(): return lax.ppermute(value, axis, [(i, (i + by) % n) for i in range(n)])  16.4 us
    pallas_call x9, Pallas kernels, call(): pl.pallas_call(bound, out_shape=outs, in_specs=specs, out_specs=[ANY if i...  14.6 us
    ppermute x4, starting transfers between devices, far_swap(): return lax.ppermute(value, axis, pairs)  9.72 us
    ppermute x4, waiting for transfers between devices, far_swap(): return lax.ppermute(value, axis, pairs)  5.59 us
    all_to_all x1, starting transfers between devices, shards(): lax.all_to_all(mom.reshape(-1, 2, LZ), ('gx', 'gy'), 0, 0, tiled=True)  4.79 us
    ppermute x3, starting transfers between devices, shards(): lax.ppermute(loads, 'gx', [(i, i ^ b) for i in range(nx)])  3.37 us
    all_to_all x1, waiting for transfers between devices, shards(): lax.all_to_all(mom.reshape(-1, 2, LZ), ('gx', 'gy'), 0, 0, tiled=True)  2.24 us
    unnamed x12, local copies, waits for them, and re-layouts  1.84 us
  transfers between devices with their start and end apart: 21, of which 4 were waited for; matrix products, arithmetic and copies ran while one was open for 0% of the time, Pallas kernels for 6%

profile of v14, /device:TPU:0, one launch (start us, length us, event | category | flops | bytes accessed | tf_op | source)
XLA Modules:
  0.0 61.6 jit_solution(632920037550454386)
XLA Ops:
  0.7 1.0 %edges.1 = (f32[25,8,128]{2,1,0:T(8,128)S(1)}, f32[25,4,128]{2,1,0:T(4,128)S(1)}) custom-call(f32[3,25,4,8,128]{4,3,2,1,0:T(8,128)} %refs_0_.3), custom_call_target="tpu_custom_call" | custom-call | tf_op jit(solution)/shard_map/edges/pallas_call | solution.py:507
  1.7 6.1 %collective-permute-start = (f32[200,128]{1,0:T(8,128)S(1)}, f32[200,128]{1,0:T(8,128)S(1)}, u32[]{:S(2)}, u32[]{:S(2)}) collective-permute-start(f32[200,128]{1,0:T(8,128)S(1)} %bitcast.19), channel_id=1, source_target_pairs={{0,120},{8,0},{16,8},{24,16},{32,24},{40,32},{48,40},{56,48},{64,5... | collective-permute-start | bytes 307208 | tf_op jit(solution)/shard_map/ppermute | solution.py:45
  7.8 3.1 %collective-permute-start.1 = (f32[100,128]{1,0:T(8,128)S(1)}, f32[100,128]{1,0:T(8,128)S(1)}, u32[]{:S(2)}, u32[]{:S(2)}) collective-permute-start(f32[100,128]{1,0:T(8,128)S(1)} %reshape.35), channel_id=1, source_target_pairs={{0,7},{1,0},{2,1},{3,2},{4,3},{5,4},{6,5},{7,6},{8,15},{9,8},{10,9... | collective-permute-start | bytes 153608 | tf_op jit(solution)/shard_map/ppermute | solution.py:45
  12.7 1.2 %weights.1 = (bf16[304,480]{1,0:T(8,128)(2,1)S(1)}, f32[8,128]{1,0:T(8,128)S(1)}) custom-call(f32[150,150]{1,0:T(8,128)S(1)} %copy-done.1, f32[150,150]{1,0:T(8,128)S(1)} %copy-done.2), custom_call_target="tpu_custom_call" | custom-call | tf_op jit(solution)/shard_map/weights/pallas_call | solution.py:507
  13.9 2.1 %first.1 = (f32[2400,128]{1,0:T(8,128)S(1)}, f32[100,128]{1,0:T(8,128)S(1)}, f32[100,128]{1,0:T(8,128)S(1)}, f32[200,128]{1,0:T(8,128)S(1)}, f32[100,128]{1,0:T(8,128)S(1)}, /*index=5*/f32[100,128]{1,0:T(8,128)S(1)}) custom-call(f32[2400,128]{1,0:T(8,128)S(1)} %bitcast.10, f32[200,128]{1,0:T(8,128)S(1)} %collective-permute-done.refs_1_, ...), custom_call_target="tpu_custom_call" | custom-call | tf_op jit(solution)/shard_map/first/pallas_call | solution.py:507
  16.1 1.6 %collective-permute-start.2 = (f32[200,128]{1,0:T(8,128)S(1)}, f32[200,128]{1,0:T(8,128)S(1)}, u32[]{:S(2)}, u32[]{:S(2)}) collective-permute-start(f32[200,128]{1,0:T(8,128)S(1)} %get-tuple-element.47.refs_8_), channel_id=1, source_target_pairs={{0,120},{8,16},{16,8},{24,32},{32,24},{40,48},{48,40},{56,64},{64,... | collective-permute-start | bytes 307208 | tf_op jit(solution)/shard_map/ppermute | solution.py:56
  17.7 3.0 %collective-permute-start.3 = (f32[100,128]{1,0:T(8,128)S(1)}, f32[100,128]{1,0:T(8,128)S(1)}, u32[]{:S(2)}, u32[]{:S(2)}) collective-permute-start(f32[100,128]{1,0:T(8,128)S(1)} %get-tuple-element.48.refs_10_), channel_id=1, source_target_pairs={{0,7},{1,2},{2,1},{3,4},{4,3},{5,6},{6,5},{7,0},{8,15},{9,10},{10,... | collective-permute-start | bytes 153608 | tf_op jit(solution)/shard_map/ppermute | solution.py:56
  21.3 2.7 %collective-permute-done.3.refs_2_ = f32[100,128]{1,0:T(8,128)S(1)} collective-permute-done((f32[100,128]{1,0:T(8,128)S(1)}, f32[100,128]{1,0:T(8,128)S(1)}, u32[]{:S(2)}, u32[]{:S(2)}) %collective-permute-start.3) | collective-permute-done | bytes 51232 | tf_op jit(solution)/shard_map/ppermute | solution.py:56
  24.0 0.9 %collective-permute-done.4.refs_3_ = f32[100,128]{1,0:T(8,128)S(1)} collective-permute-done((f32[100,128]{1,0:T(8,128)S(1)}, f32[100,128]{1,0:T(8,128)S(1)}, u32[]{:S(2)}, u32[]{:S(2)}) %collective-permute-start.4) | collective-permute-done | bytes 51232 | tf_op jit(solution)/shard_map/ppermute | solution.py:50
  24.9 1.8 %second.1 = (f32[2400,128]{1,0:T(8,128)S(1)}, f32[2400,128]{1,0:T(8,128)S(1)}, f32[100,128]{1,0:T(8,128)S(1)}, f32[100,128]{1,0:T(8,128)S(1)}, f32[200,128]{1,0:...) custom-call(f32[2400,128]{1,0:T(8,128)S(1)} %get-tuple-element.46.re, ...), custom_call_target="tpu_custom_call" | custom-call | tf_op jit(solution)/shard_map/second/pallas_call | solution.py:507
  26.7 3.3 %collective-permute-start.7 = (f32[200,128]{1,0:T(8,128)S(1)}, f32[200,128]{1,0:T(8,128)S(1)}, u32[]{:S(2)}, u32[]{:S(2)}) collective-permute-start(f32[200,128]{1,0:T(8,128)S(1)} %get-tuple-element.53.refs_8_), channel_id=1, source_target_pairs={{0,120},{8,16},{16,8},{24,32},{32,24},{40,48},{48,40},{56,64},{64,... | collective-permute-start | bytes 307208 | tf_op jit(solution)/shard_map/ppermute | solution.py:56
  30.0 1.8 %collective-permute-start.8 = (f32[100,128]{1,0:T(8,128)S(1)}, f32[100,128]{1,0:T(8,128)S(1)}, u32[]{:S(2)}, u32[]{:S(2)}) collective-permute-start(f32[100,128]{1,0:T(8,128)S(1)} %get-tuple-element.54.refs_10_), channel_id=1, source_target_pairs={{0,7},{1,2},{2,1},{3,4},{4,3},{5,6},{6,5},{7,0},{8,15},{9,10},{10,... | collective-permute-start | bytes 153608 | tf_op jit(solution)/shard_map/ppermute | solution.py:56
  32.3 1.0 %products.1 = (f32[48,128]{1,0:T(8,128)S(1)}, f32[2400,128]{1,0:T(8,128)}) custom-call(f32[2400,128]{1,0:T(8,128)S(1)} %bitcast.11, f32[2400,128]{1,0:T(8,128)S(1)} %get-tuple-element.58.refs_1_, f32[2400,128]{1,0:T(8,128)S(1)} %get-tuple-element.52.refs_2_.refs_0_, f32[200,128]{1,0:T(8,128)S(1)} %get-tuple-element.59.refs_3_, ...), custom_call_target="tpu_custom_call" | custom-call | tf_op jit(solution)/shard_map/products/pallas_call | solution.py:507
  33.3 2.9 %collective-permute-done.8.refs_2_ = f32[100,128]{1,0:T(8,128)S(1)} collective-permute-done((f32[100,128]{1,0:T(8,128)S(1)}, f32[100,128]{1,0:T(8,128)S(1)}, u32[]{:S(2)}, u32[]{:S(2)}) %collective-permute-start.8) | collective-permute-done | bytes 51232 | tf_op jit(solution)/shard_map/ppermute | solution.py:56
  36.3 2.8 %third.1 = (f32[2400,128]{1,0:T(8,128)S(1)}, f32[2400,128]{1,0:T(8,128)S(1)}, f32[200,128]{1,0:T(8,128)S(1)}, f32[100,128]{1,0:T(8,128)S(1)}, f32[264,128]{1,0:T(8,128)S(1)}, /*index=5*/f32[256,128]{1,0:T(8,128)}) custom-call(f32[2400,128]{1,0:T(8,128)S(1)} %get-tuple-element.52.refs_2_.refs_0_, f32[200,128]{1,0:T(8,128)S(1)} %collective-permute-done.7.refs_1_, ...), custom_call_target="tpu_custom_call" | custom-call | tf_op jit(solution)/shard_map/third/pallas_call | solution.py:507
  39.5 3.0 %collective-permute-start.12 = (f32[264,128]{1,0:T(8,128)S(1)}, f32[264,128]{1,0:T(8,128)S(1)}, u32[]{:S(2)}, u32[]{:S(2)}) collective-permute-start(f32[264,128]{1,0:T(8,128)S(1)} %get-tuple-element.69.refs_0_), channel_id=1, source_target_pairs={{0,8},{8,0},{16,24},{24,16},{32,40},{40,32},{48,56},{56,48},{64,72... | collective-permute-start | bytes 405512 | tf_op jit(solution)/shard_map/ppermute | solution.py:554
  42.4 4.8 %all-to-all-start = ((f32[128,2,128]{2,1,0:T(2,128)}), f32[128,2,128]{2,1,0:T(2,128)S(1)}, u32[]{:S(2)}, u32[]{:S(2)}) async-start(f32[128,2,128]{2,1,0:T(2,128)} %bitcast.4), calls=%async_computation | async-start | bytes 262144 | tf_op jit(solution)/shard_map/all_to_all | solution.py:557
  47.3 1.0 %collective-permute-start.19 = (f32[100,128]{1,0:T(8,128)S(1)}, f32[100,128]{1,0:T(8,128)S(1)}, u32[]{:S(2)}, u32[]{:S(2)}) collective-permute-start(f32[100,128]{1,0:T(8,128)S(1)} %get-tuple-element.79), channel_id=1, source_target_pairs={{0,1},{1,2},{2,3},{3,4},{4,5},{5,6},{6,7},{7,0},{8,9},{9,10},{10,1... | collective-permute-start | bytes 153608 | tf_op jit(solution)/shard_map/ppermute | solution.py:45
  48.3 1.8 %collective-permute-start.15 = (f32[32,128]{1,0:T(8,128)S(1)}, f32[32,128]{1,0:T(8,128)S(1)}, u32[]{:S(2)}, u32[]{:S(2)}) collective-permute-start(f32[32,128]{1,0:T(8,128)S(1)} %get-tuple-element.71), channel_id=1, source_target_pairs={{0,32},{8,40},{16,48},{24,56},{32,64},{40,72},{48,80},{56,88},{64,... | collective-permute-start | bytes 49160 | tf_op jit(solution)/shard_map/ppermute | solution.py:45
  50.1 3.2 %collective-permute-start.16 = (f32[32,128]{1,0:T(8,128)S(1)}, f32[32,128]{1,0:T(8,128)S(1)}, u32[]{:S(2)}, u32[]{:S(2)}) collective-permute-start(f32[32,128]{1,0:T(8,128)S(1)} %get-tuple-element.72), channel_id=1, source_target_pairs={{0,64},{8,72},{16,80},{24,88},{32,96},{40,104},{48,112},{56,120},{... | collective-permute-start | bytes 49160 | tf_op jit(solution)/shard_map/ppermute | solution.py:45
  53.3 1.2 %collective-permute-start.17 = (f32[32,128]{1,0:T(8,128)S(1)}, f32[32,128]{1,0:T(8,128)S(1)}, u32[]{:S(2)}, u32[]{:S(2)}) collective-permute-start(f32[32,128]{1,0:T(8,128)S(1)} %get-tuple-element.73), channel_id=1, source_target_pairs={{0,96},{8,104},{16,112},{24,120},{32,0},{40,8},{48,16},{56,24},{64... | collective-permute-start | bytes 49160 | tf_op jit(solution)/shard_map/ppermute | solution.py:45
  54.5 2.2 %all-to-all-done = f32[128,2,128]{2,1,0:T(2,128)S(1)} async-done(((f32[128,2,128]{2,1,0:T(2,128)}), f32[128,2,128]{2,1,0:T(2,128)S(1)}, u32[]{:S(2)}, u32[]{:S(2)}) %all-to-all-start) | async-done | bytes 131104 | tf_op jit(solution)/shard_map/all_to_all | solution.py:557
  56.8 1.7 %coefficients.1 = (f32[2400,128]{1,0:T(8,128)S(1)}, f32[2400,128]{1,0:T(8,128)S(1)}, f32[8,128]{1,0:T(8,128)S(1)}, f32[8,128]{1,0:T(8,128)S(1)}) custom-call(f32[256,128]{1,0:T(8,128)S(1)} %bitcast.12, f32[8,128]{1,0:T(8,128)S(1)} %get-tuple-element.65.refs_1_, f32[2400,128]{1,0:T(8,128)} %bitcast.9, f32[2400,128]{1,0:T(8,128)} %get-tuple-element.66.refs_3_), custom_call_target="tpu_custom_call" | custom-call | tf_op jit(solution)/shard_map/coefficients/pallas_call | solution.py:507
  58.6 2.9 %last.1 = (f32[2400,128]{1,0:T(8,128)}, f32[2400,128]{1,0:T(8,128)}, f32[8,128]{1,0:T(8,128)}) custom-call(f32[3,25]{1,0:T(4,128)S(1)} %copy-done.5, f32[8,128]{1,0:T(8,128)S(1)} %get-tuple-element.67.refs_1_, f32[8,128]{1,0:T(8,128)S(1)} %get-tuple-element.68.refs_2_, f32[32,128]{1,0:T(8,128)S(1)} %get-tuple-element.70.refs_3_, ...), custom_call_target="tpu_custom_call" | custom-call | tf_op jit(solution)/shard_map/last/pallas_call | solution.py:507
  (40 shorter events, 3.5 us)
Async XLA Ops:
  0.6 13.3 %copy-start = (f32[3,25,4,8,128]{4,3,2,1,0:T(8,128)S(1)}, f32[3,25,4,8,128]{4,3,2,1,0:T(8,128)}, u32[]{:S(2)}) copy-start(f32[3,25,4,8,128]{4,3,2,1,0:T(8,128)} %refs_0_.3) | copy-start | bytes 3686404
  0.6 13.3 %copy-start.4 = (f32[4,8,128]{2,1,0:T(8,128)S(1)}, f32[4,8,128]{2,1,0:T(8,128)}, u32[]{:S(2)}) copy-start(f32[4,8,128]{2,1,0:T(8,128)} %param.8) | copy-start | bytes 49156
  0.7 13.3 %copy-start.3 = (f32[4,8,128]{2,1,0:T(8,128)S(1)}, f32[4,8,128]{2,1,0:T(8,128)}, u32[]{:S(2)}) copy-start(f32[4,8,128]{2,1,0:T(8,128)} %param.7) | copy-start | bytes 49156
  1.7 12.2 %collective-permute-start = (f32[200,128]{1,0:T(8,128)S(1)}, f32[200,128]{1,0:T(8,128)S(1)}, u32[]{:S(2)}, u32[]{:S(2)}) collective-permute-start(f32[200,128]{1,0:T(8,128)S(1)} %bitcast.19), channel_id=1, source_target_pairs={{0,120},{8,0},{16,8},{24,16},{32,24},{40,32},{48,40},{56,48},{64,5... | collective-permute-start | bytes 307208 | tf_op jit(solution)/shard_map/ppermute | solution.py:45
  7.8 6.1 %collective-permute-start.1 = (f32[100,128]{1,0:T(8,128)S(1)}, f32[100,128]{1,0:T(8,128)S(1)}, u32[]{:S(2)}, u32[]{:S(2)}) collective-permute-start(f32[100,128]{1,0:T(8,128)S(1)} %reshape.35), channel_id=1, source_target_pairs={{0,7},{1,0},{2,1},{3,2},{4,3},{5,4},{6,5},{7,6},{8,15},{9,8},{10,9... | collective-permute-start | bytes 153608 | tf_op jit(solution)/shard_map/ppermute | solution.py:45
  16.1 8.8 %collective-permute-start.2 = (f32[200,128]{1,0:T(8,128)S(1)}, f32[200,128]{1,0:T(8,128)S(1)}, u32[]{:S(2)}, u32[]{:S(2)}) collective-permute-start(f32[200,128]{1,0:T(8,128)S(1)} %get-tuple-element.47.refs_8_), channel_id=1, source_target_pairs={{0,120},{8,16},{16,8},{24,32},{32,24},{40,48},{48,40},{56,64},{64,... | collective-permute-start | bytes 307208 | tf_op jit(solution)/shard_map/ppermute | solution.py:56
  17.7 6.2 %collective-permute-start.3 = (f32[100,128]{1,0:T(8,128)S(1)}, f32[100,128]{1,0:T(8,128)S(1)}, u32[]{:S(2)}, u32[]{:S(2)}) collective-permute-start(f32[100,128]{1,0:T(8,128)S(1)} %get-tuple-element.48.refs_10_), channel_id=1, source_target_pairs={{0,7},{1,2},{2,1},{3,4},{4,3},{5,6},{6,5},{7,0},{8,15},{9,10},{10,... | collective-permute-start | bytes 153608 | tf_op jit(solution)/shard_map/ppermute | solution.py:56
  20.7 4.1 %collective-permute-start.4 = (f32[100,128]{1,0:T(8,128)S(1)}, f32[100,128]{1,0:T(8,128)S(1)}, u32[]{:S(2)}, u32[]{:S(2)}) collective-permute-start(f32[100,128]{1,0:T(8,128)S(1)} %get-tuple-element.49.refs_9_), channel_id=1, source_target_pairs={{0,1},{1,0},{2,3},{3,2},{4,5},{5,4},{6,7},{7,6},{8,9},{9,8},{10,11... | collective-permute-start | bytes 153608 | tf_op jit(solution)/shard_map/ppermute | solution.py:50
  20.8 4.1 %collective-permute-start.5 = (f32[100,128]{1,0:T(8,128)S(1)}, f32[100,128]{1,0:T(8,128)S(1)}, u32[]{:S(2)}, u32[]{:S(2)}) collective-permute-start(f32[100,128]{1,0:T(8,128)S(1)} %get-tuple-element.50.refs_6_), channel_id=1, source_target_pairs={{0,8},{8,0},{16,24},{24,16},{32,40},{40,32},{48,56},{56,48},{64,72... | collective-permute-start | bytes 153608 | tf_op jit(solution)/shard_map/ppermute | solution.py:50
  20.8 4.1 %collective-permute-start.6 = (f32[100,128]{1,0:T(8,128)S(1)}, f32[100,128]{1,0:T(8,128)S(1)}, u32[]{:S(2)}, u32[]{:S(2)}) collective-permute-start(f32[100,128]{1,0:T(8,128)S(1)} %get-tuple-element.51.refs_7_), channel_id=1, source_target_pairs={{0,8},{8,0},{16,24},{24,16},{32,40},{40,32},{48,56},{56,48},{64,72... | collective-permute-start | bytes 153608 | tf_op jit(solution)/shard_map/ppermute | solution.py:50
  26.7 9.5 %collective-permute-start.7 = (f32[200,128]{1,0:T(8,128)S(1)}, f32[200,128]{1,0:T(8,128)S(1)}, u32[]{:S(2)}, u32[]{:S(2)}) collective-permute-start(f32[200,128]{1,0:T(8,128)S(1)} %get-tuple-element.53.refs_8_), channel_id=1, source_target_pairs={{0,120},{8,16},{16,8},{24,32},{32,24},{40,48},{48,40},{56,64},{64,... | collective-permute-start | bytes 307208 | tf_op jit(solution)/shard_map/ppermute | solution.py:56
  30.0 6.2 %collective-permute-start.8 = (f32[100,128]{1,0:T(8,128)S(1)}, f32[100,128]{1,0:T(8,128)S(1)}, u32[]{:S(2)}, u32[]{:S(2)}) collective-permute-start(f32[100,128]{1,0:T(8,128)S(1)} %get-tuple-element.54.refs_10_), channel_id=1, source_target_pairs={{0,7},{1,2},{2,1},{3,4},{4,3},{5,6},{6,5},{7,0},{8,15},{9,10},{10,... | collective-permute-start | bytes 153608 | tf_op jit(solution)/shard_map/ppermute | solution.py:56
  31.8 4.5 %collective-permute-start.9 = (f32[100,128]{1,0:T(8,128)S(1)}, f32[100,128]{1,0:T(8,128)S(1)}, u32[]{:S(2)}, u32[]{:S(2)}) collective-permute-start(f32[100,128]{1,0:T(8,128)S(1)} %get-tuple-element.55.refs_9_), channel_id=1, source_target_pairs={{0,1},{1,0},{2,3},{3,2},{4,5},{5,4},{6,7},{7,6},{8,9},{9,8},{10,11... | collective-permute-start | bytes 153608 | tf_op jit(solution)/shard_map/ppermute | solution.py:50
  31.8 4.5 %collective-permute-start.10 = (f32[100,128]{1,0:T(8,128)S(1)}, f32[100,128]{1,0:T(8,128)S(1)}, u32[]{:S(2)}, u32[]{:S(2)}) collective-permute-start(f32[100,128]{1,0:T(8,128)S(1)} %get-tuple-element.56.refs_6_), channel_id=1, source_target_pairs={{0,8},{8,0},{16,24},{24,16},{32,40},{40,32},{48,56},{56,48},{64,72... | collective-permute-start | bytes 153608 | tf_op jit(solution)/shard_map/ppermute | solution.py:50
  31.8 4.5 %collective-permute-start.11 = (f32[100,128]{1,0:T(8,128)S(1)}, f32[100,128]{1,0:T(8,128)S(1)}, u32[]{:S(2)}, u32[]{:S(2)}) collective-permute-start(f32[100,128]{1,0:T(8,128)S(1)} %get-tuple-element.57.refs_7_), channel_id=1, source_target_pairs={{0,8},{8,0},{16,24},{24,16},{32,40},{40,32},{48,56},{56,48},{64,72... | collective-permute-start | bytes 153608 | tf_op jit(solution)/shard_map/ppermute | solution.py:50
  39.1 9.2 %collective-permute-start.14 = (f32[264,128]{1,0:T(8,128)S(1)}, f32[264,128]{1,0:T(8,128)S(1)}, u32[]{:S(2)}, u32[]{:S(2)}) collective-permute-start(f32[264,128]{1,0:T(8,128)S(1)} %get-tuple-element.69.refs_0_), channel_id=1, source_target_pairs={{0,24},{8,16},{16,8},{24,0},{32,56},{40,48},{48,40},{56,32},{64,88... | collective-permute-start | bytes 405512 | tf_op jit(solution)/shard_map/ppermute | solution.py:554
  39.1 9.2 %collective-permute-start.13 = (f32[264,128]{1,0:T(8,128)S(1)}, f32[264,128]{1,0:T(8,128)S(1)}, u32[]{:S(2)}, u32[]{:S(2)}) collective-permute-start(f32[264,128]{1,0:T(8,128)S(1)} %get-tuple-element.69.refs_0_), channel_id=1, source_target_pairs={{0,16},{8,24},{16,0},{24,8},{32,48},{40,56},{48,32},{56,40},{64,80... | collective-permute-start | bytes 405512 | tf_op jit(solution)/shard_map/ppermute | solution.py:554
  39.5 8.8 %collective-permute-start.12 = (f32[264,128]{1,0:T(8,128)S(1)}, f32[264,128]{1,0:T(8,128)S(1)}, u32[]{:S(2)}, u32[]{:S(2)}) collective-permute-start(f32[264,128]{1,0:T(8,128)S(1)} %get-tuple-element.69.refs_0_), channel_id=1, source_target_pairs={{0,8},{8,0},{16,24},{24,16},{32,40},{40,32},{48,56},{56,48},{64,72... | collective-permute-start | bytes 405512 | tf_op jit(solution)/shard_map/ppermute | solution.py:554
  42.4 14.4 %all-to-all-start = ((f32[128,2,128]{2,1,0:T(2,128)}), f32[128,2,128]{2,1,0:T(2,128)S(1)}, u32[]{:S(2)}, u32[]{:S(2)}) async-start(f32[128,2,128]{2,1,0:T(2,128)} %bitcast.4), calls=%async_computation | async-start | bytes 262144 | tf_op jit(solution)/shard_map/all_to_all | solution.py:557
  47.2 11.3 %collective-permute-start.18 = (f32[200,128]{1,0:T(8,128)S(1)}, f32[200,128]{1,0:T(8,128)S(1)}, u32[]{:S(2)}, u32[]{:S(2)}) collective-permute-start(f32[200,128]{1,0:T(8,128)S(1)} %get-tuple-element.78), channel_id=1, source_target_pairs={{0,8},{8,16},{16,24},{24,32},{32,40},{40,48},{48,56},{56,64},{64,7... | collective-permute-start | bytes 307208 | tf_op jit(solution)/shard_map/ppermute | solution.py:45
  47.3 11.2 %collective-permute-start.19 = (f32[100,128]{1,0:T(8,128)S(1)}, f32[100,128]{1,0:T(8,128)S(1)}, u32[]{:S(2)}, u32[]{:S(2)}) collective-permute-start(f32[100,128]{1,0:T(8,128)S(1)} %get-tuple-element.79), channel_id=1, source_target_pairs={{0,1},{1,2},{2,3},{3,4},{4,5},{5,6},{6,7},{7,0},{8,9},{9,10},{10,1... | collective-permute-start | bytes 153608 | tf_op jit(solution)/shard_map/ppermute | solution.py:45
  48.3 10.2 %collective-permute-start.15 = (f32[32,128]{1,0:T(8,128)S(1)}, f32[32,128]{1,0:T(8,128)S(1)}, u32[]{:S(2)}, u32[]{:S(2)}) collective-permute-start(f32[32,128]{1,0:T(8,128)S(1)} %get-tuple-element.71), channel_id=1, source_target_pairs={{0,32},{8,40},{16,48},{24,56},{32,64},{40,72},{48,80},{56,88},{64,... | collective-permute-start | bytes 49160 | tf_op jit(solution)/shard_map/ppermute | solution.py:45
  50.1 8.4 %collective-permute-start.16 = (f32[32,128]{1,0:T(8,128)S(1)}, f32[32,128]{1,0:T(8,128)S(1)}, u32[]{:S(2)}, u32[]{:S(2)}) collective-permute-start(f32[32,128]{1,0:T(8,128)S(1)} %get-tuple-element.72), channel_id=1, source_target_pairs={{0,64},{8,72},{16,80},{24,88},{32,96},{40,104},{48,112},{56,120},{... | collective-permute-start | bytes 49160 | tf_op jit(solution)/shard_map/ppermute | solution.py:45
  53.3 5.2 %collective-permute-start.17 = (f32[32,128]{1,0:T(8,128)S(1)}, f32[32,128]{1,0:T(8,128)S(1)}, u32[]{:S(2)}, u32[]{:S(2)}) collective-permute-start(f32[32,128]{1,0:T(8,128)S(1)} %get-tuple-element.73), channel_id=1, source_target_pairs={{0,96},{8,104},{16,112},{24,120},{32,0},{40,8},{48,16},{56,24},{64... | collective-permute-start | bytes 49160 | tf_op jit(solution)/shard_map/ppermute | solution.py:45
  (3 other events, 3.6 us)

commit v15 on v10

--- a/solution.py
+++ b/solution.py
@@ -444,8 +444,8 @@
     coarse = d[0] * circ[0] + d[1] * circ[1] + d[2] * circ[2] + d[3] * (circ[3] + edge_ref[...])
     coarse_ref[...] = coarse
     stores = []
-    for f in range(F):
-        for a in range(A):
+    for part, (begin, end) in enumerate(((0, 8), (8, A), (A, 2 * A), (2 * A, 3 * A))):
+        for f, a in (divmod(n, A) for n in range(begin, end)):
             at = (f * A + a) * CELLS
             spread = coarse * prolong_ref[f, a]
             for cell in range(LX):
@@ -456,16 +456,16 @@
                     img = img + tile_of(rx_ref, LY, 0, a, 0)
                 sol_ref[rows, :] = x[0] * v0 + x[1] * v1 + x[2] * v2 + spread
                 res_ref[rows, :] = d[0] * v0 + d[1] * v1 + d[2] * v2 + d[3] * img
-        if f == 1:
+        if begin == A:
             below = d[3][0:1] * ry_ref[...]
             for cell in range(LX):
                 first = pl.ds(FACE + cell * LY, B, stride=CELLS)
                 res_ref[first, :] = res_ref[first, :] + below[cell * B : (cell + 1) * B]
             first = pl.ds(FACE + B * CELLS, LX, stride=LY)
             res_ref[first, :] = res_ref[first, :] + below[B * LX :]
-        rows = pl.ds(f * FACE, FACE)
+        rows = pl.ds(begin * CELLS, (end - begin) * CELLS)
         for i, (src, dst) in enumerate(((sol_ref, sol_hbm), (res_ref, res_hbm))):
-            stores.append(pltpu.make_async_copy(src.at[rows], dst.at[rows], out_sems.at[2 * f + i]))
+            stores.append(pltpu.make_async_copy(src.at[rows], dst.at[rows], out_sems.at[2 * part + i]))
             stores[-1].start()
     for store in stores:
         store.wait()
@@ -565,7 +565,7 @@
     sol, res, coarse = call(
         last_kernel, "last", [(prolong, SM), coef, edge, *coarse, v0, v1, v2, p2, rx, ry],
         [pltpu.HBM((ROWS, LZ), f32)] * 2 + [struct(LY, LZ)],
-        [pltpu.VMEM((ROWS, LZ), f32)] * 2 + [pltpu.SemaphoreType.DMA((6,))],
+        [pltpu.VMEM((ROWS, LZ), f32)] * 2 + [pltpu.SemaphoreType.DMA((8,))],
     )
     return sol.reshape(rhs.shape), res.reshape(rhs.shape), coarse[None]
 

time: 62.5 us -> 62.6 us (level)
  no operation moved by 1% of the time
where the time goes in v15:
time: 62.6 us; the launch traced here: 61.6 us
  starting transfers between devices  35.3 us (56%)
  Pallas kernels  14.6 us (23%)
  waiting for transfers between devices  8.79 us (14%)
  local copies, waits for them, and re-layouts  1.86 us (3%)
  between operations  1.01 us (2%)
    ppermute x7, starting transfers between devices, shifted(): return lax.ppermute(value, axis, [(i, (i + by) % n) for i in range(n)])  16.4 us
    pallas_call x9, Pallas kernels, call(): pl.pallas_call(bound, out_shape=outs, in_specs=specs, out_specs=[ANY if i...  14.6 us
    ppermute x4, starting transfers between devices, far_swap(): return lax.ppermute(value, axis, pairs)  9.72 us
    ppermute x4, waiting for transfers between devices, far_swap(): return lax.ppermute(value, axis, pairs)  5.59 us
    all_to_all x1, starting transfers between devices, shards(): lax.all_to_all(mom.reshape(-1, 2, LZ), ('gx', 'gy'), 0, 0, tiled=True)  4.79 us
    ppermute x3, starting transfers between devices, shards(): lax.ppermute(loads, 'gx', [(i, i ^ b) for i in range(nx)])  3.37 us
    all_to_all x1, waiting for transfers between devices, shards(): lax.all_to_all(mom.reshape(-1, 2, LZ), ('gx', 'gy'), 0, 0, tiled=True)  2.24 us
    unnamed x12, local copies, waits for them, and re-layouts  1.84 us
  transfers between devices with their start and end apart: 21, of which 4 were waited for; matrix products, arithmetic and copies ran while one was open for 0% of the time, Pallas kernels for 6%

profile of v15, /device:TPU:0, one launch (start us, length us, event | category | flops | bytes accessed | tf_op | source)
XLA Modules:
  0.0 61.6 jit_solution(11377566218850622721)
XLA Ops:
  0.7 1.0 %edges.1 = (f32[25,8,128]{2,1,0:T(8,128)S(1)}, f32[25,4,128]{2,1,0:T(4,128)S(1)}) custom-call(f32[3,25,4,8,128]{4,3,2,1,0:T(8,128)} %refs_0_.3), custom_call_target="tpu_custom_call" | custom-call | tf_op jit(solution)/shard_map/edges/pallas_call | solution.py:507
  1.7 6.1 %collective-permute-start = (f32[200,128]{1,0:T(8,128)S(1)}, f32[200,128]{1,0:T(8,128)S(1)}, u32[]{:S(2)}, u32[]{:S(2)}) collective-permute-start(f32[200,128]{1,0:T(8,128)S(1)} %bitcast.19), channel_id=1, source_target_pairs={{0,120},{8,0},{16,8},{24,16},{32,24},{40,32},{48,40},{56,48},{64,5... | collective-permute-start | bytes 307208 | tf_op jit(solution)/shard_map/ppermute | solution.py:45
  7.8 3.1 %collective-permute-start.1 = (f32[100,128]{1,0:T(8,128)S(1)}, f32[100,128]{1,0:T(8,128)S(1)}, u32[]{:S(2)}, u32[]{:S(2)}) collective-permute-start(f32[100,128]{1,0:T(8,128)S(1)} %reshape.35), channel_id=1, source_target_pairs={{0,7},{1,0},{2,1},{3,2},{4,3},{5,4},{6,5},{7,6},{8,15},{9,8},{10,9... | collective-permute-start | bytes 153608 | tf_op jit(solution)/shard_map/ppermute | solution.py:45
  12.7 1.2 %weights.1 = (bf16[304,480]{1,0:T(8,128)(2,1)S(1)}, f32[8,128]{1,0:T(8,128)S(1)}) custom-call(f32[150,150]{1,0:T(8,128)S(1)} %copy-done.1, f32[150,150]{1,0:T(8,128)S(1)} %copy-done.2), custom_call_target="tpu_custom_call" | custom-call | tf_op jit(solution)/shard_map/weights/pallas_call | solution.py:507
  13.9 2.0 %first.1 = (f32[2400,128]{1,0:T(8,128)S(1)}, f32[100,128]{1,0:T(8,128)S(1)}, f32[100,128]{1,0:T(8,128)S(1)}, f32[200,128]{1,0:T(8,128)S(1)}, f32[100,128]{1,0:T(8,128)S(1)}, /*index=5*/f32[100,128]{1,0:T(8,128)S(1)}) custom-call(f32[2400,128]{1,0:T(8,128)S(1)} %bitcast.10, f32[200,128]{1,0:T(8,128)S(1)} %collective-permute-done.refs_1_, ...), custom_call_target="tpu_custom_call" | custom-call | tf_op jit(solution)/shard_map/first/pallas_call | solution.py:507
  16.0 1.6 %collective-permute-start.2 = (f32[200,128]{1,0:T(8,128)S(1)}, f32[200,128]{1,0:T(8,128)S(1)}, u32[]{:S(2)}, u32[]{:S(2)}) collective-permute-start(f32[200,128]{1,0:T(8,128)S(1)} %get-tuple-element.43.refs_8_), channel_id=1, source_target_pairs={{0,120},{8,16},{16,8},{24,32},{32,24},{40,48},{48,40},{56,64},{64,... | collective-permute-start | bytes 307208 | tf_op jit(solution)/shard_map/ppermute | solution.py:56
  17.6 3.0 %collective-permute-start.3 = (f32[100,128]{1,0:T(8,128)S(1)}, f32[100,128]{1,0:T(8,128)S(1)}, u32[]{:S(2)}, u32[]{:S(2)}) collective-permute-start(f32[100,128]{1,0:T(8,128)S(1)} %get-tuple-element.44.refs_10_), channel_id=1, source_target_pairs={{0,7},{1,2},{2,1},{3,4},{4,3},{5,6},{6,5},{7,0},{8,15},{9,10},{10,... | collective-permute-start | bytes 153608 | tf_op jit(solution)/shard_map/ppermute | solution.py:56
  21.2 2.7 %collective-permute-done.3.refs_2_ = f32[100,128]{1,0:T(8,128)S(1)} collective-permute-done((f32[100,128]{1,0:T(8,128)S(1)}, f32[100,128]{1,0:T(8,128)S(1)}, u32[]{:S(2)}, u32[]{:S(2)}) %collective-permute-start.3) | collective-permute-done | bytes 51232 | tf_op jit(solution)/shard_map/ppermute | solution.py:56
  23.9 0.9 %collective-permute-done.4.refs_3_ = f32[100,128]{1,0:T(8,128)S(1)} collective-permute-done((f32[100,128]{1,0:T(8,128)S(1)}, f32[100,128]{1,0:T(8,128)S(1)}, u32[]{:S(2)}, u32[]{:S(2)}) %collective-permute-start.4) | collective-permute-done | bytes 51232 | tf_op jit(solution)/shard_map/ppermute | solution.py:50
  24.8 1.8 %second.1 = (f32[2400,128]{1,0:T(8,128)S(1)}, f32[2400,128]{1,0:T(8,128)S(1)}, f32[100,128]{1,0:T(8,128)S(1)}, f32[100,128]{1,0:T(8,128)S(1)}, f32[200,128]{1,0:...) custom-call(f32[2400,128]{1,0:T(8,128)S(1)} %get-tuple-element.42.refs_0_, ...), custom_call_target="tpu_custom_call" | custom-call | tf_op jit(solution)/shard_map/second/pallas_call | solution.py:507
  26.6 3.3 %collective-permute-start.7 = (f32[200,128]{1,0:T(8,128)S(1)}, f32[200,128]{1,0:T(8,128)S(1)}, u32[]{:S(2)}, u32[]{:S(2)}) collective-permute-start(f32[200,128]{1,0:T(8,128)S(1)} %get-tuple-element.50.refs_9_), channel_id=1, source_target_pairs={{0,120},{8,16},{16,8},{24,32},{32,24},{40,48},{48,40},{56,64},{64,... | collective-permute-start | bytes 307208 | tf_op jit(solution)/shard_map/ppermute | solution.py:56
  29.8 1.8 %collective-permute-start.8 = (f32[100,128]{1,0:T(8,128)S(1)}, f32[100,128]{1,0:T(8,128)S(1)}, u32[]{:S(2)}, u32[]{:S(2)}) collective-permute-start(f32[100,128]{1,0:T(8,128)S(1)} %get-tuple-element.51.refs_11_), channel_id=1, source_target_pairs={{0,7},{1,2},{2,1},{3,4},{4,3},{5,6},{6,5},{7,0},{8,15},{9,10},{10,... | collective-permute-start | bytes 153608 | tf_op jit(solution)/shard_map/ppermute | solution.py:56
  32.1 1.0 %products.1 = (f32[40,128]{1,0:T(8,128)S(1)}, f32[2400,128]{1,0:T(8,128)}) custom-call(f32[2400,128]{1,0:T(8,128)S(1)} %bitcast.11, f32[2400,128]{1,0:T(8,128)S(1)} %get-tuple-element.49.refs_1_), custom_call_target="tpu_custom_call" | custom-call | tf_op jit(solution)/shard_map/products/pallas_call | solution.py:507
  33.2 2.9 %collective-permute-done.8.refs_3_ = f32[100,128]{1,0:T(8,128)S(1)} collective-permute-done((f32[100,128]{1,0:T(8,128)S(1)}, f32[100,128]{1,0:T(8,128)S(1)}, u32[]{:S(2)}, u32[]{:S(2)}) %collective-permute-start.8) | collective-permute-done | bytes 51232 | tf_op jit(solution)/shard_map/ppermute | solution.py:56
  36.1 2.9 %third.1 = (f32[2400,128]{1,0:T(8,128)S(1)}, f32[2400,128]{1,0:T(8,128)S(1)}, f32[200,128]{1,0:T(8,128)S(1)}, f32[100,128]{1,0:T(8,128)S(1)}, f32[264,128]{1,0:T(8,128)S(1)}, /*index=5*/f32[256,128]{1,0:T(8,128)}) custom-call(f32[2400,128]{1,0:T(8,128)S(1)} %get-tuple-element.48.refs_0_, f32[2400,128]{1,0:T(8,128)S(1)} %get-tuple-element.49.refs_1_, ...), custom_call_target="tpu_custom_call" | custom-call | tf_op jit(solution)/shard_map/third/pallas_call | solution.py:507
  39.4 3.0 %collective-permute-start.12 = (f32[264,128]{1,0:T(8,128)S(1)}, f32[264,128]{1,0:T(8,128)S(1)}, u32[]{:S(2)}, u32[]{:S(2)}) collective-permute-start(f32[264,128]{1,0:T(8,128)S(1)} %get-tuple-element.61.refs_0_), channel_id=1, source_target_pairs={{0,8},{8,0},{16,24},{24,16},{32,40},{40,32},{48,56},{56,48},{64,72... | collective-permute-start | bytes 405512 | tf_op jit(solution)/shard_map/ppermute | solution.py:554
  42.4 4.8 %all-to-all-start = ((f32[128,2,128]{2,1,0:T(2,128)}), f32[128,2,128]{2,1,0:T(2,128)S(1)}, u32[]{:S(2)}, u32[]{:S(2)}) async-start(f32[128,2,128]{2,1,0:T(2,128)} %bitcast.4), calls=%async_computation | async-start | bytes 262144 | tf_op jit(solution)/shard_map/all_to_all | solution.py:557
  47.2 1.0 %collective-permute-start.19 = (f32[100,128]{1,0:T(8,128)S(1)}, f32[100,128]{1,0:T(8,128)S(1)}, u32[]{:S(2)}, u32[]{:S(2)}) collective-permute-start(f32[100,128]{1,0:T(8,128)S(1)} %get-tuple-element.71), channel_id=1, source_target_pairs={{0,1},{1,2},{2,3},{3,4},{4,5},{5,6},{6,7},{7,0},{8,9},{9,10},{10,1... | collective-permute-start | bytes 153608 | tf_op jit(solution)/shard_map/ppermute | solution.py:45
  48.3 1.8 %collective-permute-start.15 = (f32[32,128]{1,0:T(8,128)S(1)}, f32[32,128]{1,0:T(8,128)S(1)}, u32[]{:S(2)}, u32[]{:S(2)}) collective-permute-start(f32[32,128]{1,0:T(8,128)S(1)} %get-tuple-element.63), channel_id=1, source_target_pairs={{0,32},{8,40},{16,48},{24,56},{32,64},{40,72},{48,80},{56,88},{64,... | collective-permute-start | bytes 49160 | tf_op jit(solution)/shard_map/ppermute | solution.py:45
  50.1 3.2 %collective-permute-start.16 = (f32[32,128]{1,0:T(8,128)S(1)}, f32[32,128]{1,0:T(8,128)S(1)}, u32[]{:S(2)}, u32[]{:S(2)}) collective-permute-start(f32[32,128]{1,0:T(8,128)S(1)} %get-tuple-element.64), channel_id=1, source_target_pairs={{0,64},{8,72},{16,80},{24,88},{32,96},{40,104},{48,112},{56,120},{... | collective-permute-start | bytes 49160 | tf_op jit(solution)/shard_map/ppermute | solution.py:45
  53.3 1.2 %collective-permute-start.17 = (f32[32,128]{1,0:T(8,128)S(1)}, f32[32,128]{1,0:T(8,128)S(1)}, u32[]{:S(2)}, u32[]{:S(2)}) collective-permute-start(f32[32,128]{1,0:T(8,128)S(1)} %get-tuple-element.65), channel_id=1, source_target_pairs={{0,96},{8,104},{16,112},{24,120},{32,0},{40,8},{48,16},{56,24},{64... | collective-permute-start | bytes 49160 | tf_op jit(solution)/shard_map/ppermute | solution.py:45
  54.5 2.2 %all-to-all-done = f32[128,2,128]{2,1,0:T(2,128)S(1)} async-done(((f32[128,2,128]{2,1,0:T(2,128)}), f32[128,2,128]{2,1,0:T(2,128)S(1)}, u32[]{:S(2)}, u32[]{:S(2)}) %all-to-all-start) | async-done | bytes 131104 | tf_op jit(solution)/shard_map/all_to_all | solution.py:557
  56.7 1.7 %coefficients.1 = (f32[2400,128]{1,0:T(8,128)S(1)}, f32[2400,128]{1,0:T(8,128)S(1)}, f32[8,128]{1,0:T(8,128)S(1)}, f32[8,128]{1,0:T(8,128)S(1)}) custom-call(f32[256,128]{1,0:T(8,128)S(1)} %bitcast.12, f32[8,128]{1,0:T(8,128)S(1)} %get-tuple-element.57.refs_1_, f32[2400,128]{1,0:T(8,128)} %bitcast.9, f32[2400,128]{1,0:T(8,128)} %get-tuple-element.58.refs_3_), custom_call_target="tpu_custom_call" | custom-call | tf_op jit(solution)/shard_map/coefficients/pallas_call | solution.py:507
  58.5 2.9 %last.1 = (f32[2400,128]{1,0:T(8,128)}, f32[2400,128]{1,0:T(8,128)}, f32[8,128]{1,0:T(8,128)}) custom-call(f32[3,25]{1,0:T(4,128)S(1)} %copy-done.5, f32[8,128]{1,0:T(8,128)S(1)} %get-tuple-element.59.refs_1_, f32[8,128]{1,0:T(8,128)S(1)} %get-tuple-element.60.refs_2_, f32[32,128]{1,0:T(8,128)S(1)} %get-tuple-element.62.refs_3_, ...), custom_call_target="tpu_custom_call" | custom-call | tf_op jit(solution)/shard_map/last/pallas_call | solution.py:507
  (40 shorter events, 3.5 us)
Async XLA Ops:
  0.6 13.3 %copy-start = (f32[3,25,4,8,128]{4,3,2,1,0:T(8,128)S(1)}, f32[3,25,4,8,128]{4,3,2,1,0:T(8,128)}, u32[]{:S(2)}) copy-start(f32[3,25,4,8,128]{4,3,2,1,0:T(8,128)} %refs_0_.3) | copy-start | bytes 3686404
  0.6 13.3 %copy-start.4 = (f32[4,8,128]{2,1,0:T(8,128)S(1)}, f32[4,8,128]{2,1,0:T(8,128)}, u32[]{:S(2)}) copy-start(f32[4,8,128]{2,1,0:T(8,128)} %param.8) | copy-start | bytes 49156
  0.7 13.3 %copy-start.3 = (f32[4,8,128]{2,1,0:T(8,128)S(1)}, f32[4,8,128]{2,1,0:T(8,128)}, u32[]{:S(2)}) copy-start(f32[4,8,128]{2,1,0:T(8,128)} %param.7) | copy-start | bytes 49156
  1.7 12.2 %collective-permute-start = (f32[200,128]{1,0:T(8,128)S(1)}, f32[200,128]{1,0:T(8,128)S(1)}, u32[]{:S(2)}, u32[]{:S(2)}) collective-permute-start(f32[200,128]{1,0:T(8,128)S(1)} %bitcast.19), channel_id=1, source_target_pairs={{0,120},{8,0},{16,8},{24,16},{32,24},{40,32},{48,40},{56,48},{64,5... | collective-permute-start | bytes 307208 | tf_op jit(solution)/shard_map/ppermute | solution.py:45
  7.8 6.1 %collective-permute-start.1 = (f32[100,128]{1,0:T(8,128)S(1)}, f32[100,128]{1,0:T(8,128)S(1)}, u32[]{:S(2)}, u32[]{:S(2)}) collective-permute-start(f32[100,128]{1,0:T(8,128)S(1)} %reshape.35), channel_id=1, source_target_pairs={{0,7},{1,0},{2,1},{3,2},{4,3},{5,4},{6,5},{7,6},{8,15},{9,8},{10,9... | collective-permute-start | bytes 153608 | tf_op jit(solution)/shard_map/ppermute | solution.py:45
  16.0 8.8 %collective-permute-start.2 = (f32[200,128]{1,0:T(8,128)S(1)}, f32[200,128]{1,0:T(8,128)S(1)}, u32[]{:S(2)}, u32[]{:S(2)}) collective-permute-start(f32[200,128]{1,0:T(8,128)S(1)} %get-tuple-element.43.refs_8_), channel_id=1, source_target_pairs={{0,120},{8,16},{16,8},{24,32},{32,24},{40,48},{48,40},{56,64},{64,... | collective-permute-start | bytes 307208 | tf_op jit(solution)/shard_map/ppermute | solution.py:56
  17.6 6.2 %collective-permute-start.3 = (f32[100,128]{1,0:T(8,128)S(1)}, f32[100,128]{1,0:T(8,128)S(1)}, u32[]{:S(2)}, u32[]{:S(2)}) collective-permute-start(f32[100,128]{1,0:T(8,128)S(1)} %get-tuple-element.44.refs_10_), channel_id=1, source_target_pairs={{0,7},{1,2},{2,1},{3,4},{4,3},{5,6},{6,5},{7,0},{8,15},{9,10},{10,... | collective-permute-start | bytes 153608 | tf_op jit(solution)/shard_map/ppermute | solution.py:56
  20.6 4.1 %collective-permute-start.4 = (f32[100,128]{1,0:T(8,128)S(1)}, f32[100,128]{1,0:T(8,128)S(1)}, u32[]{:S(2)}, u32[]{:S(2)}) collective-permute-start(f32[100,128]{1,0:T(8,128)S(1)} %get-tuple-element.45.refs_9_), channel_id=1, source_target_pairs={{0,1},{1,0},{2,3},{3,2},{4,5},{5,4},{6,7},{7,6},{8,9},{9,8},{10,11... | collective-permute-start | bytes 153608 | tf_op jit(solution)/shard_map/ppermute | solution.py:50
  20.6 4.1 %collective-permute-start.5 = (f32[100,128]{1,0:T(8,128)S(1)}, f32[100,128]{1,0:T(8,128)S(1)}, u32[]{:S(2)}, u32[]{:S(2)}) collective-permute-start(f32[100,128]{1,0:T(8,128)S(1)} %get-tuple-element.46.refs_6_), channel_id=1, source_target_pairs={{0,8},{8,0},{16,24},{24,16},{32,40},{40,32},{48,56},{56,48},{64,72... | collective-permute-start | bytes 153608 | tf_op jit(solution)/shard_map/ppermute | solution.py:50
  20.7 4.1 %collective-permute-start.6 = (f32[100,128]{1,0:T(8,128)S(1)}, f32[100,128]{1,0:T(8,128)S(1)}, u32[]{:S(2)}, u32[]{:S(2)}) collective-permute-start(f32[100,128]{1,0:T(8,128)S(1)} %get-tuple-element.47.refs_7_), channel_id=1, source_target_pairs={{0,8},{8,0},{16,24},{24,16},{32,40},{40,32},{48,56},{56,48},{64,72... | collective-permute-start | bytes 153608 | tf_op jit(solution)/shard_map/ppermute | solution.py:50
  26.6 9.5 %collective-permute-start.7 = (f32[200,128]{1,0:T(8,128)S(1)}, f32[200,128]{1,0:T(8,128)S(1)}, u32[]{:S(2)}, u32[]{:S(2)}) collective-permute-start(f32[200,128]{1,0:T(8,128)S(1)} %get-tuple-element.50.refs_9_), channel_id=1, source_target_pairs={{0,120},{8,16},{16,8},{24,32},{32,24},{40,48},{48,40},{56,64},{64,... | collective-permute-start | bytes 307208 | tf_op jit(solution)/shard_map/ppermute | solution.py:56
  29.8 6.2 %collective-permute-start.8 = (f32[100,128]{1,0:T(8,128)S(1)}, f32[100,128]{1,0:T(8,128)S(1)}, u32[]{:S(2)}, u32[]{:S(2)}) collective-permute-start(f32[100,128]{1,0:T(8,128)S(1)} %get-tuple-element.51.refs_11_), channel_id=1, source_target_pairs={{0,7},{1,2},{2,1},{3,4},{4,3},{5,6},{6,5},{7,0},{8,15},{9,10},{10,... | collective-permute-start | bytes 153608 | tf_op jit(solution)/shard_map/ppermute | solution.py:56
  31.6 4.5 %collective-permute-start.9 = (f32[100,128]{1,0:T(8,128)S(1)}, f32[100,128]{1,0:T(8,128)S(1)}, u32[]{:S(2)}, u32[]{:S(2)}) collective-permute-start(f32[100,128]{1,0:T(8,128)S(1)} %get-tuple-element.52.refs_10_), channel_id=1, source_target_pairs={{0,1},{1,0},{2,3},{3,2},{4,5},{5,4},{6,7},{7,6},{8,9},{9,8},{10,11... | collective-permute-start | bytes 153608 | tf_op jit(solution)/shard_map/ppermute | solution.py:50
  31.6 4.5 %collective-permute-start.10 = (f32[100,128]{1,0:T(8,128)S(1)}, f32[100,128]{1,0:T(8,128)S(1)}, u32[]{:S(2)}, u32[]{:S(2)}) collective-permute-start(f32[100,128]{1,0:T(8,128)S(1)} %get-tuple-element.53.refs_7_), channel_id=1, source_target_pairs={{0,8},{8,0},{16,24},{24,16},{32,40},{40,32},{48,56},{56,48},{64,72... | collective-permute-start | bytes 153608 | tf_op jit(solution)/shard_map/ppermute | solution.py:50
  31.6 4.5 %collective-permute-start.11 = (f32[100,128]{1,0:T(8,128)S(1)}, f32[100,128]{1,0:T(8,128)S(1)}, u32[]{:S(2)}, u32[]{:S(2)}) collective-permute-start(f32[100,128]{1,0:T(8,128)S(1)} %get-tuple-element.54.refs_8_), channel_id=1, source_target_pairs={{0,8},{8,0},{16,24},{24,16},{32,40},{40,32},{48,56},{56,48},{64,72... | collective-permute-start | bytes 153608 | tf_op jit(solution)/shard_map/ppermute | solution.py:50
  39.0 9.2 %collective-permute-start.14 = (f32[264,128]{1,0:T(8,128)S(1)}, f32[264,128]{1,0:T(8,128)S(1)}, u32[]{:S(2)}, u32[]{:S(2)}) collective-permute-start(f32[264,128]{1,0:T(8,128)S(1)} %get-tuple-element.61.refs_0_), channel_id=1, source_target_pairs={{0,24},{8,16},{16,8},{24,0},{32,56},{40,48},{48,40},{56,32},{64,88... | collective-permute-start | bytes 405512 | tf_op jit(solution)/shard_map/ppermute | solution.py:554
  39.0 9.2 %collective-permute-start.13 = (f32[264,128]{1,0:T(8,128)S(1)}, f32[264,128]{1,0:T(8,128)S(1)}, u32[]{:S(2)}, u32[]{:S(2)}) collective-permute-start(f32[264,128]{1,0:T(8,128)S(1)} %get-tuple-element.61.refs_0_), channel_id=1, source_target_pairs={{0,16},{8,24},{16,0},{24,8},{32,48},{40,56},{48,32},{56,40},{64,80... | collective-permute-start | bytes 405512 | tf_op jit(solution)/shard_map/ppermute | solution.py:554
  39.4 8.8 %collective-permute-start.12 = (f32[264,128]{1,0:T(8,128)S(1)}, f32[264,128]{1,0:T(8,128)S(1)}, u32[]{:S(2)}, u32[]{:S(2)}) collective-permute-start(f32[264,128]{1,0:T(8,128)S(1)} %get-tuple-element.61.refs_0_), channel_id=1, source_target_pairs={{0,8},{8,0},{16,24},{24,16},{32,40},{40,32},{48,56},{56,48},{64,72... | collective-permute-start | bytes 405512 | tf_op jit(solution)/shard_map/ppermute | solution.py:554
  42.4 14.4 %all-to-all-start = ((f32[128,2,128]{2,1,0:T(2,128)}), f32[128,2,128]{2,1,0:T(2,128)S(1)}, u32[]{:S(2)}, u32[]{:S(2)}) async-start(f32[128,2,128]{2,1,0:T(2,128)} %bitcast.4), calls=%async_computation | async-start | bytes 262144 | tf_op jit(solution)/shard_map/all_to_all | solution.py:557
  47.2 11.3 %collective-permute-start.18 = (f32[200,128]{1,0:T(8,128)S(1)}, f32[200,128]{1,0:T(8,128)S(1)}, u32[]{:S(2)}, u32[]{:S(2)}) collective-permute-start(f32[200,128]{1,0:T(8,128)S(1)} %get-tuple-element.70), channel_id=1, source_target_pairs={{0,8},{8,16},{16,24},{24,32},{32,40},{40,48},{48,56},{56,64},{64,7... | collective-permute-start | bytes 307208 | tf_op jit(solution)/shard_map/ppermute | solution.py:45
  47.2 11.2 %collective-permute-start.19 = (f32[100,128]{1,0:T(8,128)S(1)}, f32[100,128]{1,0:T(8,128)S(1)}, u32[]{:S(2)}, u32[]{:S(2)}) collective-permute-start(f32[100,128]{1,0:T(8,128)S(1)} %get-tuple-element.71), channel_id=1, source_target_pairs={{0,1},{1,2},{2,3},{3,4},{4,5},{5,6},{6,7},{7,0},{8,9},{9,10},{10,1... | collective-permute-start | bytes 153608 | tf_op jit(solution)/shard_map/ppermute | solution.py:45
  48.3 10.2 %collective-permute-start.15 = (f32[32,128]{1,0:T(8,128)S(1)}, f32[32,128]{1,0:T(8,128)S(1)}, u32[]{:S(2)}, u32[]{:S(2)}) collective-permute-start(f32[32,128]{1,0:T(8,128)S(1)} %get-tuple-element.63), channel_id=1, source_target_pairs={{0,32},{8,40},{16,48},{24,56},{32,64},{40,72},{48,80},{56,88},{64,... | collective-permute-start | bytes 49160 | tf_op jit(solution)/shard_map/ppermute | solution.py:45
  50.1 8.4 %collective-permute-start.16 = (f32[32,128]{1,0:T(8,128)S(1)}, f32[32,128]{1,0:T(8,128)S(1)}, u32[]{:S(2)}, u32[]{:S(2)}) collective-permute-start(f32[32,128]{1,0:T(8,128)S(1)} %get-tuple-element.64), channel_id=1, source_target_pairs={{0,64},{8,72},{16,80},{24,88},{32,96},{40,104},{48,112},{56,120},{... | collective-permute-start | bytes 49160 | tf_op jit(solution)/shard_map/ppermute | solution.py:45
  53.3 5.2 %collective-permute-start.17 = (f32[32,128]{1,0:T(8,128)S(1)}, f32[32,128]{1,0:T(8,128)S(1)}, u32[]{:S(2)}, u32[]{:S(2)}) collective-permute-start(f32[32,128]{1,0:T(8,128)S(1)} %get-tuple-element.65), channel_id=1, source_target_pairs={{0,96},{8,104},{16,112},{24,120},{32,0},{40,8},{48,16},{56,24},{64... | collective-permute-start | bytes 49160 | tf_op jit(solution)/shard_map/ppermute | solution.py:45
  (3 other events, 3.6 us)
